TPU v7x, 32 devices: a whole 2x2x4 slice. The times are simulated.
32 devices in a mesh: dp: 4 (over y, core), fsdp: 8 (over z, x).
Axes of the slice: x: 2, y: 2, z: 4, core: 2. Of those that a mesh axis runs over, the one named last changes fastest.
Arguments:
- inputs: bfloat16 [64, 256, 1024], P(('dp', 'fsdp')), may hold values from -6 to 6
- image_ids: int32 [64, 256], P(('dp', 'fsdp')), may hold values from -1 to 7, as said below
- cotangent: bfloat16 [64, 256, 1024], P(('dp', 'fsdp')), may hold values from -6 to 6
- gains: bfloat16 [32, 64], P(('dp', 'fsdp')), may hold values from 0.25 to 1.75
- biases: bfloat16 [32, 320], P(('dp', 'fsdp')), may hold values from -2 to 2
- w_qkv: bfloat16 [32, 98304], P(('dp', 'fsdp')), may hold values from -0.1875 to 0.1875
- w_out: bfloat16 [32, 32768], P(('dp', 'fsdp')), may hold values from -0.5 to 0.5
- w_in: bfloat16 [32, 131072], P(('dp', 'fsdp')), may hold values from -0.1875 to 0.1875
- w_mlp: bfloat16 [32, 131072], P(('dp', 'fsdp')), may hold values from -0.09375 to 0.09375
Outputs:
- block_out: bfloat16 [64, 256, 1024], P(('dp', 'fsdp'))
- grad_inputs: float32 [64, 256, 1024], P(('dp', 'fsdp'))
- grad_gains: float32 [32, 64], P(('dp', 'fsdp'))
- grad_biases: float32 [32, 320], P(('dp', 'fsdp'))
- grad_w_qkv: float32 [32, 98304], P(('dp', 'fsdp'))
- grad_w_out: float32 [32, 32768], P(('dp', 'fsdp'))
- grad_w_in: float32 [32, 131072], P(('dp', 'fsdp'))
- grad_w_mlp: float32 [32, 131072], P(('dp', 'fsdp'))
Inputs may be any that keep to these rules, and one draw needn't show every extreme that they name: `image_ids`: -1 marks padding, which takes the last 1 to 64 positions of every row; the other positions hold their image's number within the row, counted from 0 in order, each image one run of positions; every row holds images 0 to 7.
All inputs are finite; a program needn't handle non-finite values.
Results may differ from a plain program's by a relative error of at most 0.014.
Values may be sent and summed in bfloat16 or wider, within the bound.
No kernel may reach another device: no remote copies, remote signals or barrier semaphores. Data moves between devices by JAX's collectives and lax.ppermute only.
A program may use at most 192 MiB of HBM per device.

v0:
```python
import jax
import jax.numpy as jnp
from jax import lax
from jax.sharding import PartitionSpec as P

D = 1024
FF = 4096
HEADS = 16
HEAD_DIM = 64


eps = 1e-06


def normalize(values):
    centre = values - jnp.mean(values, axis=-1, keepdims=True)
    inverse = lax.rsqrt(jnp.mean(centre * centre, axis=-1, keepdims=True) + eps)
    return (centre * inverse, inverse)


def norm_back(grad_norm, normed, inverse):
    return inverse * (
        grad_norm
        - jnp.mean(grad_norm, axis=-1, keepdims=True)
        - normed * jnp.mean(grad_norm * normed, axis=-1, keepdims=True)
    )


def unpack(gathered):
    gain_flat, bias_flat, qkv_flat, out_flat, in_flat, mlp_flat = gathered
    return (
        gain_flat.reshape(-1).astype(jnp.float32),
        bias_flat.reshape(-1).astype(jnp.float32),
        qkv_flat.reshape(-1).reshape(D, 3 * D),
        out_flat.reshape(-1).reshape(D, D),
        in_flat.reshape(-1).reshape(D, FF),
        mlp_flat.reshape(-1).reshape(FF, D),
    )


def spread_flat(members, template):
    joined = jnp.concatenate([member.reshape(-1) for member in members])
    outer = lax.axis_size("dp")
    inner = lax.axis_size("fsdp")
    return joined.reshape(outer, inner, template.shape[1])


def owned_rows(summed):
    return summed.reshape(1, summed.shape[-1])


def masked_scores(queries, keys_all, same_image, scale):
    raw = (
        jnp.einsum("rqhd,rkhd->rhqk", queries, keys_all, preferred_element_type=jnp.float32) * scale
    )
    return jnp.where(same_image, raw, -1000000000.0)


def column_sums(values):
    return jnp.sum(values.astype(jnp.float32), axis=0)


def per_device(inputs, image_ids, cotangent, gains, biases, w_qkv, w_out, w_in, w_mlp):
    gathered = (
        lax.all_gather(gains, ("dp", "fsdp"), axis=0, tiled=True),
        lax.all_gather(biases, ("dp", "fsdp"), axis=0, tiled=True),
        lax.all_gather(w_qkv, ("dp", "fsdp"), axis=0, tiled=True),
        lax.all_gather(w_out, ("dp", "fsdp"), axis=0, tiled=True),
        lax.all_gather(w_in, ("dp", "fsdp"), axis=0, tiled=True),
        lax.all_gather(w_mlp, ("dp", "fsdp"), axis=0, tiled=True),
    )
    gain_vec, bias_vec, matrix_qkv, matrix_out, matrix_in, matrix_mlp = unpack(gathered)
    blocks, length = image_ids.shape
    count = blocks * length
    scale = HEAD_DIM ** (-0.5)
    tokens = inputs.astype(jnp.float32).reshape(count, D)
    normed_one, inverse_one = normalize(tokens)
    entry = (normed_one * gain_vec[:D] + bias_vec[:D]).astype(jnp.bfloat16)
    bias_qkv = jnp.concatenate(
        [bias_vec[D : 2 * D], jnp.zeros((D,), jnp.float32), bias_vec[2 * D : 3 * D]]
    )
    project = (jnp.dot(entry, matrix_qkv, preferred_element_type=jnp.float32) + bias_qkv).astype(
        jnp.bfloat16
    )
    queries = project[:, :D].reshape(blocks, length, HEADS, HEAD_DIM)
    keys_all = project[:, D : 2 * D].reshape(blocks, length, HEADS, HEAD_DIM)
    values = project[:, 2 * D :].reshape(blocks, length, HEADS, HEAD_DIM)
    same_image = (image_ids[:, :, None] == image_ids[:, None, :])[:, None]
    scores = masked_scores(queries, keys_all, same_image, scale)
    ceiling = jnp.max(scores, axis=-1, keepdims=True)
    expo = jnp.exp(scores - ceiling)
    totals = jnp.sum(expo, axis=-1, keepdims=True)
    log_total = ceiling + jnp.log(totals)
    probs_low = (expo / totals).astype(jnp.bfloat16)
    mixed = (
        jnp.einsum("rhqk,rkhd->rqhd", probs_low, values, preferred_element_type=jnp.float32)
        .reshape(count, D)
        .astype(jnp.bfloat16)
    )
    middle = tokens + (
        jnp.dot(mixed, matrix_out, preferred_element_type=jnp.float32) + bias_vec[3 * D : 4 * D]
    )
    normed_two, inverse_two = normalize(middle)
    second = (normed_two * gain_vec[D:] + bias_vec[4 * D : 5 * D]).astype(jnp.bfloat16)
    hidden = jnp.dot(second, matrix_in, preferred_element_type=jnp.float32) + bias_vec[6 * D :]
    active, gelu_pull = jax.vjp(lambda point: jax.nn.gelu(point, approximate=False), hidden)
    active = active.astype(jnp.bfloat16)
    result = middle + (
        jnp.dot(active, matrix_mlp, preferred_element_type=jnp.float32) + bias_vec[5 * D : 6 * D]
    )
    output = result.reshape(blocks, length, D).astype(jnp.bfloat16)
    source = (
        lax.all_gather(gains, ("dp", "fsdp"), axis=0, tiled=True),
        lax.all_gather(biases, ("dp", "fsdp"), axis=0, tiled=True),
        lax.all_gather(w_qkv, ("dp", "fsdp"), axis=0, tiled=True),
        lax.all_gather(w_out, ("dp", "fsdp"), axis=0, tiled=True),
        lax.all_gather(w_in, ("dp", "fsdp"), axis=0, tiled=True),
        lax.all_gather(w_mlp, ("dp", "fsdp"), axis=0, tiled=True),
    )
    gain_vec, bias_vec, matrix_qkv, matrix_out, matrix_in, matrix_mlp = unpack(source)
    keep_rows = (image_ids.reshape(count, 1) >= 0).astype(jnp.float32)
    grad_out = cotangent.astype(jnp.float32).reshape(count, D) * keep_rows
    grad_top = grad_out.astype(jnp.bfloat16)
    grad_bias_mlp = column_sums(grad_top)
    grad_mlp = jnp.einsum("nf,nd->fd", active, grad_top, preferred_element_type=jnp.float32)
    grad_active = jnp.einsum("nd,fd->nf", grad_top, matrix_mlp, preferred_element_type=jnp.float32)
    grad_hidden = gelu_pull(grad_active)[0].astype(jnp.bfloat16)
    grad_bias_in = column_sums(grad_hidden)
    grad_in = jnp.einsum("nd,nf->df", second, grad_hidden, preferred_element_type=jnp.float32)
    grad_second = jnp.einsum(
        "nf,df->nd", grad_hidden, matrix_in, preferred_element_type=jnp.float32
    )
    grad_gain_two = jnp.sum(grad_second * normed_two, axis=0)
    grad_shift_two = jnp.sum(grad_second, axis=0)
    grad_middle = grad_out + norm_back(grad_second * gain_vec[D:], normed_two, inverse_two)
    grad_branch = grad_middle.astype(jnp.bfloat16)
    grad_bias_out = column_sums(grad_branch)
    grad_out_matrix = jnp.einsum(
        "nd,ne->de", mixed, grad_branch, preferred_element_type=jnp.float32
    )
    grad_mixed = (
        jnp.einsum("ne,de->nd", grad_branch, matrix_out, preferred_element_type=jnp.float32)
        .astype(jnp.bfloat16)
        .reshape(blocks, length, HEADS, HEAD_DIM)
    )
    probs_again = jnp.exp(masked_scores(queries, keys_all, same_image, scale) - log_total)
    grad_probs = jnp.einsum(
        "rqhd,rkhd->rhqk", grad_mixed, values, preferred_element_type=jnp.float32
    )
    grad_values = jnp.einsum(
        "rhqk,rqhd->rkhd",
        probs_again.astype(jnp.bfloat16),
        grad_mixed,
        preferred_element_type=jnp.float32,
    )
    grad_scores = (
        probs_again * (grad_probs - jnp.sum(probs_again * grad_probs, axis=-1, keepdims=True))
    ).astype(jnp.bfloat16)
    grad_queries = (
        jnp.einsum("rhqk,rkhd->rqhd", grad_scores, keys_all, preferred_element_type=jnp.float32)
        * scale
    )
    grad_keys = (
        jnp.einsum("rhqk,rqhd->rkhd", grad_scores, queries, preferred_element_type=jnp.float32)
        * scale
    )
    grad_project = jnp.concatenate(
        [
            grad_queries.reshape(count, D),
            grad_keys.reshape(count, D),
            grad_values.reshape(count, D),
        ],
        axis=1,
    ).astype(jnp.bfloat16)
    grad_bias_qkv = column_sums(grad_project)
    grad_qkv = jnp.einsum("nd,ne->de", entry, grad_project, preferred_element_type=jnp.float32)
    grad_entry = jnp.einsum(
        "ne,de->nd", grad_project, matrix_qkv, preferred_element_type=jnp.float32
    )
    grad_gain_one = jnp.sum(grad_entry * normed_one, axis=0)
    grad_shift_one = jnp.sum(grad_entry, axis=0)
    grad_inputs = grad_middle + norm_back(grad_entry * gain_vec[:D], normed_one, inverse_one)
    flat_gains = spread_flat([grad_gain_one, grad_gain_two], gathered[0])
    flat_biases = spread_flat(
        [
            grad_shift_one,
            grad_bias_qkv[:D],
            grad_bias_qkv[2 * D :],
            grad_bias_out,
            grad_shift_two,
            grad_bias_mlp,
            grad_bias_in,
        ],
        gathered[1],
    )
    flat_qkv = spread_flat([grad_qkv], gathered[2])
    flat_out = spread_flat([grad_out_matrix], gathered[3])
    inner_sums = (
        lax.psum_scatter(flat_gains, "fsdp", scatter_dimension=1, tiled=True),
        lax.psum_scatter(flat_biases, "fsdp", scatter_dimension=1, tiled=True),
        lax.psum_scatter(flat_qkv, "fsdp", scatter_dimension=1, tiled=True),
        lax.psum_scatter(flat_out, "fsdp", scatter_dimension=1, tiled=True),
        lax.psum_scatter(
            spread_flat([grad_in], gathered[4]), "fsdp", scatter_dimension=1, tiled=True
        ),
        lax.psum_scatter(
            spread_flat([grad_mlp], gathered[5]), "fsdp", scatter_dimension=1, tiled=True
        ),
    )
    results = (
        lax.psum_scatter(
            inner_sums[0].astype(jnp.bfloat16), "dp", scatter_dimension=0, tiled=True
        ).astype(jnp.float32),
        lax.psum_scatter(
            inner_sums[1].astype(jnp.bfloat16), "dp", scatter_dimension=0, tiled=True
        ).astype(jnp.float32),
        lax.psum_scatter(
            inner_sums[2].astype(jnp.bfloat16), "dp", scatter_dimension=0, tiled=True
        ).astype(jnp.float32),
        lax.psum_scatter(
            inner_sums[3].astype(jnp.bfloat16), "dp", scatter_dimension=0, tiled=True
        ).astype(jnp.float32),
        lax.psum_scatter(
            inner_sums[4].astype(jnp.bfloat16), "dp", scatter_dimension=0, tiled=True
        ).astype(jnp.float32),
        lax.psum_scatter(
            inner_sums[5].astype(jnp.bfloat16), "dp", scatter_dimension=0, tiled=True
        ).astype(jnp.float32),
    )
    return (
        output,
        grad_inputs.reshape(blocks, length, D),
        owned_rows(results[0]),
        owned_rows(results[1]),
        owned_rows(results[2]),
        owned_rows(results[3]),
        owned_rows(results[4]),
        owned_rows(results[5]),
    )


def solution(mesh):
    placed = (
        P(("dp", "fsdp"), None, None),
        P(("dp", "fsdp"), None),
        P(("dp", "fsdp"), None, None),
        P(("dp", "fsdp"), None),
        P(("dp", "fsdp"), None),
        P(("dp", "fsdp"), None),
        P(("dp", "fsdp"), None),
        P(("dp", "fsdp"), None),
        P(("dp", "fsdp"), None),
    )
    return jax.shard_map(
        per_device,
        mesh=mesh,
        in_specs=placed,
        out_specs=(
            P(("dp", "fsdp"), None, None),
            P(("dp", "fsdp"), None, None),
            P(("dp", "fsdp"), None),
            P(("dp", "fsdp"), None),
            P(("dp", "fsdp"), None),
            P(("dp", "fsdp"), None),
            P(("dp", "fsdp"), None),
            P(("dp", "fsdp"), None),
        ),
        check_vma=False,
    )
```

profile of v0, /device:TPU:8, one launch (start us, length us, event | category | flops | bytes accessed | tf_op | source)
XLA Modules:
  0.0 2774.2 jit_solution(13148850172513429802)
XLA Ops:
  10.1 66.4 %all-gather.1 = bf16[32,1,320]{2,1,0:T(2,128)(2,1)S(1)} all-gather(bf16[1,1,320]{2,1,0:T(2,128)(2,1)} %bitcast.162), channel_id=1, replica_groups=mesh['dp'=4,'fsdp'=8] {'dp','fsdp'}, dimensions={0}, use_global_device_ids=true | all-gather | bytes 21120 | tf_op jit(solution)/shard_map/all_gather | solution.py:66
  76.6 63.5 %all-gather = bf16[32,1,64]{2,1,0:T(2,128)(2,1)S(1)} all-gather(bf16[1,1,64]{2,1,0:T(2,128)(2,1)} %bitcast.163), channel_id=1, replica_groups=mesh['dp'=4,'fsdp'=8] {'dp','fsdp'}, dimensions={0}, use_global_device_ids=true | all-gather | bytes 4224 | tf_op jit(solution)/shard_map/all_gather | solution.py:65
  152.5 12.7 reduce.6
  171.6 38.7 %reduce.5 = bf16[32,98304]{1,0:T(8,128)(2,1)} reduce(bf16[32,1,98304]{2,1,0:T(2,128)(2,1)} %all-gather.11.cloned.1.call-done, bf16[]{:T(256)} %constant.144), dimensions={1}, to_apply=%all-gather.2.reduce_sub_computation | reduce | bytes 12582914 | tf_op jit(solution)/shard_map/all_gather | solution.py:67
  210.3 7.4 reshape_reshape.28
  217.7 6.4 add_convert_fusion.1
  253.5 33.8 %all-gather.15.cloned.1.call-done = bf16[32,1,131072]{2,1,0:T(2,128)(2,1)} async-done(((bf16[1,1,131072]{2,1,0:T(2,128)(2,1)}), bf16[32,1,131072]{2,1,0:T(2,128)(2,1)}) %all-gather.15.cloned.1.call-update) | async-done | bytes 8388624 | tf_op jit(solution)/shard_map/all_gather | solution.py:69
  287.3 49.8 %reduce.8 = bf16[32,131072]{1,0:T(8,128)(2,1)} reduce(bf16[32,1,131072]{2,1,0:T(2,128)(2,1)} %all-gather.15.cloned.1.call-done, bf16[]{:T(256)} %constant.144), dimensions={1}, to_apply=%all-gather.4.reduce_sub_computation | reduce | bytes 16777218 | tf_op jit(solution)/shard_map/all_gather | solution.py:69
  337.1 9.3 reshape_reshape.30
  346.4 56.8 %all-gather.17.cloned.1.call-done = bf16[32,1,131072]{2,1,0:T(2,128)(2,1)} async-done(((bf16[1,1,131072]{2,1,0:T(2,128)(2,1)}), bf16[32,1,131072]{2,1,0:T(2,128)(2,1)}) %all-gather.17.cloned.1.call-update) | async-done | bytes 8388624 | tf_op jit(solution)/shard_map/all_gather | solution.py:70
  403.3 49.8 %reduce.9 = bf16[32,131072]{1,0:T(8,128)(2,1)} reduce(bf16[32,1,131072]{2,1,0:T(2,128)(2,1)} %all-gather.17.cloned.1.call-done, bf16[]{:T(256)} %constant.144), dimensions={1}, to_apply=%all-gather.5.reduce_sub_computation | reduce | bytes 16777218 | tf_op jit(solution)/shard_map/all_gather | solution.py:70
  453.1 8.9 reshape_reshape.31
  462.0 7.3 fusion.53
  469.3 26.1 convert_reduce_fusion
  495.5 5.0 multiply_reduce_fusion.1
  510.2 5.9 multiply_reduce_fusion
  529.0 8.8 fusion.52
  537.8 10.0 multiply_convert_fusion.1
  554.7 5.9 fusion.27
  561.0 10.5 fusion.59
  571.5 9.8 reshape_reshape.32
  581.3 16.4 copy.103
  602.6 6.9 copy.105
  609.4 12.1 reshape_reshape.34
  621.5 21.0 copy.107
  642.5 8.4 fusion.60
  650.9 12.1 reshape_reshape.35
  663.0 20.9 copy.109
  683.8 1920.3 %all-reduce.19 = (bf16[4,8,64]{2,0,1:T(4,128)(2,1)S(1)}, bf16[4,8,320]{2,0,1:T(4,128)(2,1)S(1)}, bf16[4,8,98304]{2,0,1:T(4,128)(2,1)}, bf16[4,8,32768]{2,0,1:T(4...) all-reduce(f32[4,8,64]{2,0,1:T(4,128)S(1)} %copy.99, ...), channel_id=2, replica_groups=mesh['dp'=4,'fsdp'=8] {'fsdp'}, use_global_device_ids=true, to_apply=%region_13.14.clone | all-reduce | flops 12595200 | bytes 75571200
  2605.3 6.0 all-reduce.13
  2636.0 10.1 add_convert_fusion.2
  2646.1 110.0 %all-reduce.18.cloned.1.call-done = (bf16[4,1,98304]{2,1,0:T(2,128)(2,1)}, bf16[4,1,32768]{2,1,0:T(2,128)(2,1)}, bf16[4,1,131072]{2,1,0:T(2,128)(2,1)}, bf16[4,1,131072]{2,1,0:T(2,128)(2,1)}) async-done(((bf16[4,1,98304]{2,1,0:T(2,128)(2,1)}, bf16[4,1,32768]{2,1,0:T(2,128)(2,1)}, bf16[4,1,131072]{2,1,0:T(2,128)(2,1)}, bf16[4,1,131072]{2,1,0:T(2,128)(2,1)}), (bf16[4,1,98304]{2,1,0:T(2,128)(2,1)}, ...) | async-done | bytes 3145744
  (197 shorter events, 122.6 us)
Async XLA Ops:
  7.2 141.9 %copy-start.27 = (s32[2,256]{1,0:T(2,128)S(1)}, s32[2,256]{1,0:T(2,128)}, u32[]{:S(2)}) copy-start(s32[2,256]{1,0:T(2,128)} %param.10) | copy-start | bytes 6148
  7.2 143.9 %copy-start.1 = (bf16[2,256,1024]{2,1,0:T(8,128)(2,1)S(1)}, bf16[2,256,1024]{2,1,0:T(8,128)(2,1)}, u32[]{:S(2)}) copy-start(bf16[2,256,1024]{2,1,0:T(8,128)(2,1)} %param.9) | copy-start | bytes 3145732
  7.2 142.0 %copy-start.17 = (bf16[2,256,1024]{2,1,0:T(8,128)(2,1)S(1)}, bf16[2,256,1024]{2,1,0:T(8,128)(2,1)}, u32[]{:S(2)}) copy-start(bf16[2,256,1024]{2,1,0:T(8,128)(2,1)} %param.11) | copy-start | bytes 3145732
  7.2 145.3 %all-gather.13.cloned.1.call-start = ((), (), s32[]{:S(2)}) async-start(), calls=%async_computation.1 | async-start | bytes 4325376 | tf_op jit(solution)/shard_map/all_gather | solution.py:68
  7.9 163.7 %all-gather.11.cloned.1.call-start = ((), (), s32[]{:S(2)}) async-start(), calls=%async_computation | async-start | bytes 12976128 | tf_op jit(solution)/shard_map/all_gather | solution.py:67
  8.7 278.6 %all-gather.15.cloned.1.call-start = ((), (), s32[]{:S(2)}) async-start(), calls=%async_computation.2 | async-start | bytes 17301504 | tf_op jit(solution)/shard_map/all_gather | solution.py:69
  9.4 393.9 %all-gather.17.cloned.1.call-start = ((), (), s32[]{:S(2)}) async-start(), calls=%async_computation.3 | async-start | bytes 17301504 | tf_op jit(solution)/shard_map/all_gather | solution.py:70
  10.0 2746.2 %all-reduce.18.cloned.1.call-start = ((), (), s32[]{:S(2)}) async-start(), calls=%async_computation.4 | async-start | bytes 12582912
  140.3 12.2 copy-start.25
  149.0 3.5 copy-start.28
  210.3 7.4 copy-start.24
  231.3 7.2 copy-start.19
  238.5 6.9 copy-start.7
  245.4 3.2 copy-start
  462.0 7.3 copy-start.11
  462.0 7.3 copy-start.23
  462.0 33.5 %slice-start.2 = ((s8[8388608]{0:T(1024)(128)(4,1)}), s8[4194304]{0:T(1024)(128)(4,1)S(1)}, s32[]{:S(2)}) async-start(s8[8388608]{0:T(1024)(128)(4,1)} %bitcast.139), calls=%async_computation.7 | async-start | bytes 8388608
  469.2 26.2 copy-start.12
  469.3 26.2 slice-start.3
  495.4 5.1 copy-start.35
  495.5 5.1 copy-start.18
  495.5 5.1 copy-start.31
  500.6 3.2 copy-start.14
  510.2 13.7 slice-start
  516.1 4.6 copy-start.10
  516.1 7.8 slice-start.1
  537.8 10.0 copy-start.20
  549.1 3.5 slice-start.4
  552.1 8.5 copy-start.15
  554.7 6.2 copy-start.30
  621.5 21.0 copy-start.21
  621.5 21.0 copy-start.22
  (16 other events, 34.6 us)
Sparse Core Ops, SparseCore 0:
  11.0 63.4 all-gather.12
  77.5 94.0 all-gather.10
  174.6 112.6 all-gather.14
  290.2 113.0 all-gather.16
  2635.5 120.6 all-reduce.17
where the time goes:
time: 2780 us; the launch traced here: 2770 us
  blocking collectives  2060 us (74%)
  waiting for transfers between devices  207 us (7%)
  other arithmetic  195 us (7%)
  local copies, waits for them, and re-layouts  193 us (7%)
  matrix products  108 us (4%)
    unnamed x2, blocking collectives  1930 us
    unnamed x6, waiting for transfers between devices  113 us
    another operation x8, local copies, waits for them, and re-layouts, spread_flat(): return joined.reshape(outer, inner, template.shape[1])  104 us
    all_gather x1, blocking collectives, per_device(): lax.all_gather(biases, ('dp', 'fsdp'), axis=0, tiled=True)  66.4 us
    all_gather x1, blocking collectives, per_device(): lax.all_gather(gains, ('dp', 'fsdp'), axis=0, tiled=True)  63.5 us
    all_gather x1, waiting for transfers between devices, per_device(): lax.all_gather(w_mlp, ('dp', 'fsdp'), axis=0, tiled=True)  56.8 us
  transfers between devices with their start and end apart: 5, of which 4 were waited for; matrix products, arithmetic and copies ran while one was open for 6% of the time, Pallas kernels for 0%

commit v1 on v0

v1 whole, which is shorter than its diff:
```python
import jax
import jax.numpy as jnp
from jax import lax
from jax.experimental import pallas as pl
from jax.experimental.pallas import tpu as pltpu
from jax.sharding import PartitionSpec as P

D = 1024
FF = 4096
HEADS = 16
HEAD_DIM = 64
AXES = ("dp", "fsdp")


eps = 1e-06


def normalize(values):
    centre = values - jnp.mean(values, axis=-1, keepdims=True)
    inverse = lax.rsqrt(jnp.mean(centre * centre, axis=-1, keepdims=True) + eps)
    return (centre * inverse, inverse)


def norm_back(grad_norm, normed, inverse):
    return inverse * (
        grad_norm
        - jnp.mean(grad_norm, axis=-1, keepdims=True)
        - normed * jnp.mean(grad_norm * normed, axis=-1, keepdims=True)
    )


def masked_scores(queries, keys_all, same_image, scale):
    raw = (
        jnp.einsum("rqhd,rkhd->rhqk", queries, keys_all, preferred_element_type=jnp.float32) * scale
    )
    return jnp.where(same_image, raw, -1000000000.0)


def column_sums(values):
    return jnp.sum(values.astype(jnp.float32), axis=0)


class Plan:
    def __init__(self, mesh):
        outer, inner = mesh.shape["dp"], mesh.shape["fsdp"]
        ys = outer // 2
        xs = min(ys, inner)
        zs = inner // xs
        self.devices = outer * inner
        self.half = self.devices // 2

        def bits(size, unit):
            found = []
            while size > 1:
                size //= 2
                found.append(size * unit)
            return found

        xbits = bits(xs, 1)
        zbits = bits(zs, xs)
        self.core = inner
        ybits = bits(ys, 2 * inner)
        self.orders = (zbits + xbits + ybits, zbits + ybits + xbits)
        self.stages = len(self.orders[0])

    def pairs(self, stage):
        return [
            (i, i ^ self.orders[1 if i & self.core else 0][stage]) for i in range(self.devices)
        ]

    def core_pairs(self):
        return [(i, i ^ self.core) for i in range(self.devices)]

    def masks(self, which):
        found = [0]
        for bit in self.orders[which]:
            found = found + [mask ^ bit for mask in found]
        return found

    def positions(self, me):
        tables = jnp.array(
            [
                self.masks(0) + [mask ^ self.core for mask in self.masks(1)],
                self.masks(1) + [mask ^ self.core for mask in self.masks(0)],
            ],
            jnp.int32,
        )
        mine = jnp.where((me & self.core) > 0, tables[1], tables[0])
        return mine ^ me


def gather(plan, block):
    held = block[None]
    for stage in range(plan.stages):
        held = jnp.concatenate([held, lax.ppermute(held, AXES, plan.pairs(stage))], 0)
    return held, lax.ppermute(held, AXES, plan.core_pairs())


def total(parts):
    result = parts[0].astype(jnp.float32)
    for part in parts[1:]:
        result = result + part.astype(jnp.float32)
    return result


def scatter_sum(plan, keep, send):
    parts = [keep, lax.ppermute(send, AXES, plan.core_pairs())]
    count = plan.half
    for stage in reversed(range(plan.stages)):
        count //= 2
        outgoing = total([part[count : 2 * count] for part in parts]).astype(jnp.bfloat16)
        parts.append(lax.ppermute(outgoing, AXES, plan.pairs(stage)))
    return total([part[0] for part in parts])


def one_hot(order):
    return (order[:, None] == jnp.arange(order.shape[0])[None, :]).astype(jnp.bfloat16)


def assemble(order, own, other):
    half, rows, width = own.shape
    shape = (half, rows, width) if rows % 16 == 0 else (half, 16, rows * width // 16)

    def body(order_ref, own_ref, other_ref, out_ref, sems):
        copies = []
        for place in range(2 * half):
            source = own_ref.at[place] if place < half else other_ref.at[place - half]
            copies.append(
                pltpu.make_async_copy(source, out_ref.at[order_ref[place]], sems.at[place])
            )
        for copy in copies:
            copy.start()
        for copy in copies:
            copy.wait()

    return pl.pallas_call(
        body,
        out_shape=jax.ShapeDtypeStruct((2 * half, *shape[1:]), own.dtype),
        in_specs=[
            pl.BlockSpec(memory_space=pltpu.SMEM),
            pl.BlockSpec(memory_space=pl.ANY),
            pl.BlockSpec(memory_space=pl.ANY),
        ],
        out_specs=pl.BlockSpec(memory_space=pl.ANY),
        scratch_shapes=[pltpu.SemaphoreType.DMA((2 * half,))],
    )(order, own.reshape(shape), other.reshape(shape)).reshape(2 * half * rows, width)


def disassemble(order, matrix):
    blocks = order.shape[0]
    half = blocks // 2
    rows, width = matrix.shape[0] // blocks, matrix.shape[1]
    shape = (rows, width) if rows % 16 == 0 else (16, rows * width // 16)

    def body(order_ref, in_ref, own_ref, other_ref, sems):
        copies = []
        for place in range(blocks):
            target = own_ref.at[place] if place < half else other_ref.at[place - half]
            copies.append(
                pltpu.make_async_copy(in_ref.at[order_ref[place]], target, sems.at[place])
            )
        for copy in copies:
            copy.start()
        for copy in copies:
            copy.wait()

    own, other = pl.pallas_call(
        body,
        out_shape=[jax.ShapeDtypeStruct((half, *shape), matrix.dtype)] * 2,
        in_specs=[pl.BlockSpec(memory_space=pltpu.SMEM), pl.BlockSpec(memory_space=pl.ANY)],
        out_specs=[pl.BlockSpec(memory_space=pl.ANY)] * 2,
        scratch_shapes=[pltpu.SemaphoreType.DMA((blocks,))],
    )(order, matrix.reshape(blocks, *shape))
    return own.reshape(half, rows, width), other.reshape(half, rows, width)


def per_device(plan, inputs, image_ids, cotangent, gains, biases, w_qkv, w_out, w_in, w_mlp):
    me = lax.axis_index(AXES)
    order = plan.positions(me)
    gain_dev, bias_dev = gains.shape[1], biases.shape[1]
    small = jnp.concatenate([gains, biases], 1)
    rows = D // plan.devices
    first = jnp.concatenate([w_qkv.reshape(rows, 3 * D), w_out.reshape(rows, D)], 1)
    small_own, small_other = gather(plan, small)
    first_own, first_other = gather(plan, first)
    in_own, in_other = gather(plan, w_in.reshape(rows, FF))
    mlp_own, mlp_other = gather(plan, w_mlp.reshape(FF // plan.devices, D))
    placed = jnp.concatenate([small_own, small_other], 0)[:, 0]
    small_all = lax.dot_general(
        one_hot(order), placed, (((0,), (0,)), ((), ())), preferred_element_type=jnp.float32
    )
    gain_vec = small_all[:, :gain_dev].reshape(-1)
    bias_vec = small_all[:, gain_dev:].reshape(-1)
    matrix_first = assemble(order, first_own, first_other)
    matrix_qkv = matrix_first[:, : 3 * D]
    matrix_out = matrix_first[:, 3 * D :]
    matrix_in = assemble(order, in_own, in_other)
    matrix_mlp = assemble(order, mlp_own, mlp_other)
    blocks, length = image_ids.shape
    count = blocks * length
    scale = HEAD_DIM ** (-0.5)
    tokens = inputs.astype(jnp.float32).reshape(count, D)
    normed_one, inverse_one = normalize(tokens)
    entry = (normed_one * gain_vec[:D] + bias_vec[:D]).astype(jnp.bfloat16)
    bias_qkv = jnp.concatenate(
        [bias_vec[D : 2 * D], jnp.zeros((D,), jnp.float32), bias_vec[2 * D : 3 * D]]
    )
    project = (jnp.dot(entry, matrix_qkv, preferred_element_type=jnp.float32) + bias_qkv).astype(
        jnp.bfloat16
    )
    queries = project[:, :D].reshape(blocks, length, HEADS, HEAD_DIM)
    keys_all = project[:, D : 2 * D].reshape(blocks, length, HEADS, HEAD_DIM)
    values = project[:, 2 * D :].reshape(blocks, length, HEADS, HEAD_DIM)
    same_image = (image_ids[:, :, None] == image_ids[:, None, :])[:, None]
    scores = masked_scores(queries, keys_all, same_image, scale)
    ceiling = jnp.max(scores, axis=-1, keepdims=True)
    expo = jnp.exp(scores - ceiling)
    totals = jnp.sum(expo, axis=-1, keepdims=True)
    log_total = ceiling + jnp.log(totals)
    probs_low = (expo / totals).astype(jnp.bfloat16)
    mixed = (
        jnp.einsum("rhqk,rkhd->rqhd", probs_low, values, preferred_element_type=jnp.float32)
        .reshape(count, D)
        .astype(jnp.bfloat16)
    )
    middle = tokens + (
        jnp.dot(mixed, matrix_out, preferred_element_type=jnp.float32) + bias_vec[3 * D : 4 * D]
    )
    normed_two, inverse_two = normalize(middle)
    second = (normed_two * gain_vec[D:] + bias_vec[4 * D : 5 * D]).astype(jnp.bfloat16)
    hidden = jnp.dot(second, matrix_in, preferred_element_type=jnp.float32) + bias_vec[6 * D :]
    active, gelu_pull = jax.vjp(lambda point: jax.nn.gelu(point, approximate=False), hidden)
    active = active.astype(jnp.bfloat16)
    result = middle + (
        jnp.dot(active, matrix_mlp, preferred_element_type=jnp.float32) + bias_vec[5 * D : 6 * D]
    )
    output = result.reshape(blocks, length, D).astype(jnp.bfloat16)
    keep_rows = (image_ids.reshape(count, 1) >= 0).astype(jnp.float32)
    grad_out = cotangent.astype(jnp.float32).reshape(count, D) * keep_rows
    grad_top = grad_out.astype(jnp.bfloat16)
    grad_bias_mlp = column_sums(grad_top)
    grad_mlp = jnp.einsum(
        "nf,nd->fd", active, grad_top, preferred_element_type=jnp.float32
    ).astype(jnp.bfloat16)
    sum_mlp = scatter_sum(plan, *disassemble(order, grad_mlp))
    grad_active = jnp.einsum("nd,fd->nf", grad_top, matrix_mlp, preferred_element_type=jnp.float32)
    grad_hidden = gelu_pull(grad_active)[0].astype(jnp.bfloat16)
    grad_bias_in = column_sums(grad_hidden)
    grad_in = jnp.einsum(
        "nd,nf->df", second, grad_hidden, preferred_element_type=jnp.float32
    ).astype(jnp.bfloat16)
    sum_in = scatter_sum(plan, *disassemble(order, grad_in))
    grad_second = jnp.einsum(
        "nf,df->nd", grad_hidden, matrix_in, preferred_element_type=jnp.float32
    )
    grad_gain_two = jnp.sum(grad_second * normed_two, axis=0)
    grad_shift_two = jnp.sum(grad_second, axis=0)
    grad_middle = grad_out + norm_back(grad_second * gain_vec[D:], normed_two, inverse_two)
    grad_branch = grad_middle.astype(jnp.bfloat16)
    grad_bias_out = column_sums(grad_branch)
    grad_out_matrix = jnp.einsum(
        "nd,ne->de", mixed, grad_branch, preferred_element_type=jnp.float32
    ).astype(jnp.bfloat16)
    grad_mixed = (
        jnp.einsum("ne,de->nd", grad_branch, matrix_out, preferred_element_type=jnp.float32)
        .astype(jnp.bfloat16)
        .reshape(blocks, length, HEADS, HEAD_DIM)
    )
    probs_again = jnp.exp(masked_scores(queries, keys_all, same_image, scale) - log_total)
    grad_probs = jnp.einsum(
        "rqhd,rkhd->rhqk", grad_mixed, values, preferred_element_type=jnp.float32
    )
    grad_values = jnp.einsum(
        "rhqk,rqhd->rkhd",
        probs_again.astype(jnp.bfloat16),
        grad_mixed,
        preferred_element_type=jnp.float32,
    )
    grad_scores = (
        probs_again * (grad_probs - jnp.sum(probs_again * grad_probs, axis=-1, keepdims=True))
    ).astype(jnp.bfloat16)
    grad_queries = (
        jnp.einsum("rhqk,rkhd->rqhd", grad_scores, keys_all, preferred_element_type=jnp.float32)
        * scale
    )
    grad_keys = (
        jnp.einsum("rhqk,rqhd->rkhd", grad_scores, queries, preferred_element_type=jnp.float32)
        * scale
    )
    grad_project = jnp.concatenate(
        [
            grad_queries.reshape(count, D),
            grad_keys.reshape(count, D),
            grad_values.reshape(count, D),
        ],
        axis=1,
    ).astype(jnp.bfloat16)
    grad_bias_qkv = column_sums(grad_project)
    grad_qkv = jnp.einsum(
        "nd,ne->de", entry, grad_project, preferred_element_type=jnp.float32
    ).astype(jnp.bfloat16)
    sum_first = scatter_sum(
        plan, *disassemble(order, jnp.concatenate([grad_qkv, grad_out_matrix], 1))
    )
    grad_entry = jnp.einsum(
        "ne,de->nd", grad_project, matrix_qkv, preferred_element_type=jnp.float32
    )
    grad_gain_one = jnp.sum(grad_entry * normed_one, axis=0)
    grad_shift_one = jnp.sum(grad_entry, axis=0)
    grad_inputs = grad_middle + norm_back(grad_entry * gain_vec[:D], normed_one, inverse_one)
    flat_gains = jnp.concatenate([grad_gain_one, grad_gain_two]).reshape(-1, gain_dev)
    flat_biases = jnp.concatenate(
        [
            grad_shift_one,
            grad_bias_qkv[:D],
            grad_bias_qkv[2 * D :],
            grad_bias_out,
            grad_shift_two,
            grad_bias_mlp,
            grad_bias_in,
        ]
    ).reshape(-1, bias_dev)
    flat_small = jnp.concatenate([flat_gains, flat_biases], 1).astype(jnp.bfloat16)
    moved = jnp.dot(one_hot(order), flat_small, preferred_element_type=jnp.float32)
    moved = moved.astype(jnp.bfloat16)[:, None]
    sum_small = scatter_sum(plan, moved[: plan.half], moved[plan.half :])
    return (
        output,
        grad_inputs.reshape(blocks, length, D),
        sum_small[:, :gain_dev],
        sum_small[:, gain_dev:],
        sum_first[:, : 3 * D].reshape(1, -1),
        sum_first[:, 3 * D :].reshape(1, -1),
        sum_in.reshape(1, -1),
        sum_mlp.reshape(1, -1),
    )


def solution(mesh):
    plan = Plan(mesh)
    whole = P(AXES, None, None)
    flat = P(AXES, None)

    def body(*arrays):
        return per_device(plan, *arrays)

    return jax.shard_map(
        body,
        mesh=mesh,
        in_specs=(whole, flat, whole, flat, flat, flat, flat, flat, flat),
        out_specs=(whole, whole, flat, flat, flat, flat, flat, flat),
        check_vma=False,
    )
```

time: 2780 us -> 2080 us (0.75)
  blocking collectives: 2060 us -> 0 us
  Pallas kernels: 0 us -> 1540 us
  local copies, waits for them, and re-layouts: 193 us -> 63.4 us
  other arithmetic: 195 us -> 76.6 us
  starting transfers between devices: 0.19 us -> 58.4 us
    unnamed x2 -> x0, blocking collectives: 1930 us -> none
    pallas_call x0 -> x6, Pallas kernels: none -> 1540 us  [the longest x3 769 us: disassemble(): pl.pallas_call(body, out_shape=[jax.ShapeDtypeStruct((half, *shape), matr...]
    ppermute x0 -> x40, waiting for transfers between devices: none -> 207 us  [the longest x16 114 us: scatter_sum(): parts.append(lax.ppermute(outgoing, AXES, plan.pairs(stage)))]
    all_gather x4 -> x0, other arithmetic: 151 us -> none  [the longest x1 49.8 us: per_device(): lax.all_gather(w_in, ('dp', 'fsdp'), axis=0, tiled=True)]
    another operation x12 -> x2, local copies, waits for them, and re-layouts: 132 us -> 0.23 us  [gather(): held = block[None]]
    all_gather x2 -> x0, blocking collectives: 130 us -> none  [the longest x1 66.4 us: per_device(): lax.all_gather(biases, ('dp', 'fsdp'), axis=0, tiled=True)]
    unnamed x6 -> x0, waiting for transfers between devices: 113 us -> none
    all_gather x4 -> x0, waiting for transfers between devices: 94.7 us -> none  [the longest x1 56.8 us: per_device(): lax.all_gather(w_mlp, ('dp', 'fsdp'), axis=0, tiled=True)]
  transfers between devices with their start and end apart: 5 -> 40, of which waited for: 4 -> 22; matrix products, arithmetic and copies ran while one was open for 6% -> 7% of each run, Pallas kernels for 0% -> 37%
where the time goes in v1:
time: 2080 us; the launch traced here: 2060 us
  Pallas kernels  1540 us (74%)
  waiting for transfers between devices  207 us (10%)
  matrix products  117 us (6%)
  other arithmetic  76.6 us (4%)
  local copies, waits for them, and re-layouts  63.4 us (3%)
  starting transfers between devices  58.4 us (3%)
    pallas_call x3, Pallas kernels, disassemble(): pl.pallas_call(body, out_shape=[jax.ShapeDtypeStruct((half, *shape), matr...  769 us
    pallas_call x3, Pallas kernels, assemble(): pl.pallas_call(body, out_shape=jax.ShapeDtypeStruct((2 * half, *shape[1:]...  769 us
    ppermute x16, waiting for transfers between devices, scatter_sum(): parts.append(lax.ppermute(outgoing, AXES, plan.pairs(stage)))  114 us
    ppermute x16, waiting for transfers between devices, gather(): lax.ppermute(held, AXES, plan.pairs(stage))  92.7 us
  transfers between devices with their start and end apart: 40, of which 22 were waited for; matrix products, arithmetic and copies ran while one was open for 7% of the time, Pallas kernels for 37%

profile of v1, /device:TPU:8, one launch (start us, length us, event | category | flops | bytes accessed | tf_op | source)
XLA Modules:
  0.0 2061.8 jit_solution(11994685059669379144)
XLA Ops:
  23.5 16.9 collective-permute-done.5
  44.9 10.3 collective-permute-done.6
  62.1 9.3 collective-permute-done.2
  84.9 10.3 collective-permute-done.11
  101.9 7.4 collective-permute-done.8
  121.3 15.1 collective-permute-done.17
  142.6 6.9 collective-permute-done.13
  158.9 12.9 collective-permute-done.18
  175.1 256.2 %shard_map.161 = bf16[32,32,4096]{2,1,0:T(8,128)(2,1)} custom-call(s32[32]{0:T(128)} %copy-done.33, bf16[16,32,4096]{2,1,0:T(8,128)(2,1)} %constant_dynamic-update-slice_fusion.own_ref, bf16[16,32,4096]{2,1,0:T(8,128)(2,1)} %collective-permute-done.9.other_ref), custom_call_target="tpu_custom_call" | custom-call | tf_op jit(solution)/shard_map/pallas_call | solution.py:136
  431.3 6.8 add_convert_fusion.1
  467.5 256.2 %shard_map.162 = bf16[32,32,4096]{2,1,0:T(8,128)(2,1)} custom-call(s32[32]{0:T(128)} %copy-done.33, bf16[16,32,4096]{2,1,0:T(8,128)(2,1)} %constant_dynamic-update-slice_fusion.5.own_ref, bf16[16,32,4096]{2,1,0:T(8,128)(2,1)} %collective-permute-done.14.other_ref), custom_call_target="tpu_custom_call" | custom-call | tf_op jit(solution)/shard_map/pallas_call | solution.py:136
  728.0 7.1 fusion.89
  735.1 256.2 %shard_map.163 = bf16[32,128,1024]{2,1,0:T(8,128)(2,1)} custom-call(s32[32]{0:T(128)} %copy-done.33, bf16[16,128,1024]{2,1,0:T(8,128)(2,1)} %constant_dynamic-update-slice_fusion.10.own_ref, bf16[16,128,1024]{2,1,0:T(8,128)(2,1)} %collective-permute-done.19.other_ref), custom_call_target="tpu_custom_call" | custom-call | tf_op jit(solution)/shard_map/pallas_call | solution.py:136
  991.3 27.9 %fusion.90 = (bf16[4096]{0:T(1024)(128)(2,1)S(1)}, bf16[512,4096]{1,0:T(8,128)(2,1)S(1)}, f32[512,4096]{1,0:T(8,128)}) fusion(f32[512,4096]{1,0:T(8,128)} %fusion.89, f32[4096]{0:T(1024)S(1)} %slice.438, bf16[512,1024]{1,0:T(8,128)(2,1)} %bitcast.219, bf16[4096,1024]{1,0:T(8,128)(2,1)} %bitcast.199), kind=kOutput, calls=%fused_computation.208 | convolution fusion | flops 4450152448 | bytes 30433280 | tf_op jit(solution)/shard_map/nd,fd->nf/dot_general | solution.py:246
  1019.2 7.6 multiply_reduce_fusion.1
  1034.5 7.5 convolution_convert_fusion.1
  1053.8 5.6 multiply_reduce_fusion
  1069.0 5.4 fusion.31
  1074.4 5.4 convolution_convert_fusion.2
  1079.8 9.8 multiply_convert_fusion.1
  1089.6 256.3 %shard_map.165 = (bf16[16,32,4096]{2,1,0:T(8,128)(2,1)}, bf16[16,32,4096]{2,1,0:T(8,128)(2,1)}) custom-call(s32[32]{0:T(128)} %copy-done.33, bf16[32,32,4096]{2,1,0:T(8,128)(2,1)} %bitcast.209), custom_call_target="tpu_custom_call" | custom-call | tf_op jit(solution)/shard_map/pallas_call | solution.py:167
  1346.0 9.1 convolution_convert_fusion
  1355.1 256.3 %shard_map.166 = (bf16[16,128,1024]{2,1,0:T(8,128)(2,1)}, bf16[16,128,1024]{2,1,0:T(8,128)(2,1)}) custom-call(s32[32]{0:T(128)} %copy-done.33, bf16[32,128,1024]{2,1,0:T(8,128)(2,1)} %bitcast.210), custom_call_target="tpu_custom_call" | custom-call | tf_op jit(solution)/shard_map/pallas_call | solution.py:167
  1612.0 6.9 pad_maximum_fusion
  1621.4 256.3 %shard_map.164 = (bf16[16,32,4096]{2,1,0:T(8,128)(2,1)}, bf16[16,32,4096]{2,1,0:T(8,128)(2,1)}) custom-call(s32[32]{0:T(128)} %copy-done.33, bf16[32,32,4096]{2,1,0:T(8,128)(2,1)} %bitcast.198), custom_call_target="tpu_custom_call" | custom-call | tf_op jit(solution)/shard_map/pallas_call | solution.py:167
  1878.8 10.3 add_convert_fusion.8
  1915.1 11.8 collective-permute-done.36
  1930.9 29.8 %collective-permute-done.26 = bf16[8,32,4096]{2,1,0:T(8,128)(2,1)S(1)} collective-permute-done((bf16[8,32,4096]{2,1,0:T(8,128)(2,1)S(1)}, bf16[8,32,4096]{2,1,0:T(8,128)(2,1)S(1)}, u32[]{:S(2)}, u32[]{:S(2)}) %collective-permute-start.26) | collective-permute-done | bytes 2097184 | tf_op jit(solution)/shard_map/ppermute | solution.py:112
  1964.4 29.9 %collective-permute-done.31 = bf16[8,32,4096]{2,1,0:T(8,128)(2,1)S(1)} collective-permute-done((bf16[8,32,4096]{2,1,0:T(8,128)(2,1)S(1)}, bf16[8,32,4096]{2,1,0:T(8,128)(2,1)S(1)}, u32[]{:S(2)}, u32[]{:S(2)}) %collective-permute-start.31) | collective-permute-done | bytes 2097184 | tf_op jit(solution)/shard_map/ppermute | solution.py:112
  2003.0 7.9 collective-permute-done.32
  2016.8 15.1 collective-permute-done.28
  2042.8 10.6 collective-permute-done.29
  (310 shorter events, 218.9 us)
Async XLA Ops:
  1.6 56.2 %collective-permute-start = (bf16[1,1,384]{2,0,1:T(2,128)(2,1)S(1)}, bf16[1,1,384]{2,0,1:T(2,128)(2,1)S(1)}, u32[]{:S(2)}, u32[]{:S(2)}) collective-permute-start(bf16[1,1,384]{2,0,1:T(2,128)(2,1)S(1)} %maximum_bitcast_fusion.1), channel_id=1, source_target_pairs={{0,4},{1,5},{2,6},{3,7},{4,0},{5,1},{6,2},{7,3},{8,12},{9,13},{10,... | collective-permute-start | bytes 2312 | tf_op jit(solution)/shard_map/ppermute | solution.py:95
  6.8 75.3 %collective-permute-start.15 = (bf16[1,128,1024]{2,1,0:T(8,128)(2,1)S(1)}, bf16[1,128,1024]{2,1,0:T(8,128)(2,1)S(1)}, u32[]{:S(2)}, u32[]{:S(2)}) collective-permute-start(bf16[1,128,1024]{2,1,0:T(8,128)(2,1)S(1)} %broadcast_in_dim_reshape.7), channel_id=1, source_target_pairs={{0,4},{1,5},{2,6},{3,7},{4,0},{5,1},{6,2},{7,3},{8,12},{9,13},{10,... | collective-permute-start | bytes 786440 | tf_op jit(solution)/shard_map/ppermute | solution.py:95
  9.8 69.7 %collective-permute-start.10 = (bf16[1,32,4096]{2,1,0:T(8,128)(2,1)S(1)}, bf16[1,32,4096]{2,1,0:T(8,128)(2,1)S(1)}, u32[]{:S(2)}, u32[]{:S(2)}) collective-permute-start(bf16[1,32,4096]{2,1,0:T(8,128)(2,1)S(1)} %broadcast_in_dim_reshape.6), channel_id=1, source_target_pairs={{0,4},{1,5},{2,6},{3,7},{4,0},{5,1},{6,2},{7,3},{8,12},{9,13},{10,... | collective-permute-start | bytes 786440 | tf_op jit(solution)/shard_map/ppermute | solution.py:95
  18.3 22.1 %collective-permute-start.5 = (bf16[1,32,4096]{2,1,0:T(8,128)(2,1)S(1)}, bf16[1,32,4096]{2,1,0:T(8,128)(2,1)S(1)}, u32[]{:S(2)}, u32[]{:S(2)}) collective-permute-start(bf16[1,32,4096]{2,1,0:T(8,128)(2,1)S(1)} %maximum_bitcast_fusion), channel_id=1, source_target_pairs={{0,4},{1,5},{2,6},{3,7},{4,0},{5,1},{6,2},{7,3},{8,12},{9,13},{10,... | collective-permute-start | bytes 786440 | tf_op jit(solution)/shard_map/ppermute | solution.py:95
  40.5 14.7 collective-permute-start.6
  56.3 20.2 collective-permute-start.7
  77.9 31.4 %collective-permute-start.8 = (bf16[8,32,4096]{2,1,0:T(8,128)(2,1)S(1)}, bf16[8,32,4096]{2,1,0:T(8,128)(2,1)S(1)}, u32[]{:S(2)}, u32[]{:S(2)}) collective-permute-start(bf16[8,32,4096]{2,1,0:T(8,128)(2,1)S(1)} %pad_maximum_fusion.1), channel_id=1, source_target_pairs={{0,16},{1,17},{2,18},{3,19},{4,20},{5,21},{6,22},{7,23},{8,9},{9,8... | collective-permute-start | bytes 6291464 | tf_op jit(solution)/shard_map/ppermute | solution.py:95
  80.3 14.9 collective-permute-start.11
  82.9 28.3 %collective-permute-start.16 = (bf16[2,128,1024]{2,1,0:T(8,128)(2,1)}, bf16[2,128,1024]{2,1,0:T(8,128)(2,1)S(1)}, u32[]{:S(2)}, u32[]{:S(2)}) collective-permute-start(bf16[2,128,1024]{2,1,0:T(8,128)(2,1)} %pad_maximum_fusion.9), channel_id=1, source_target_pairs={{0,2},{1,3},{2,0},{3,1},{4,6},{5,7},{6,4},{7,5},{8,10},{9,11},{10,... | collective-permute-start | bytes 1572872 | tf_op jit(solution)/shard_map/ppermute | solution.py:95
  97.2 18.6 collective-permute-start.12
  110.8 64.3 %collective-permute-start.9 = (bf16[16,32,4096]{2,1,0:T(8,128)(2,1)}, bf16[16,32,4096]{2,1,0:T(8,128)(2,1)}, u32[]{:S(2)}, u32[]{:S(2)}) collective-permute-start(bf16[16,32,4096]{2,1,0:T(8,128)(2,1)} %constant_dynamic-update-slice_fusion.own_ref), channel_id=1, source_target_pairs={{0,8},{1,9},{2,10},{3,11},{4,12},{5,13},{6,14},{7,15},{8,0},{9,1},... | collective-permute-start | bytes 12582920 | tf_op jit(solution)/shard_map/ppermute | solution.py:96
  112.4 24.1 %collective-permute-start.17 = (bf16[4,128,1024]{2,1,0:T(8,128)(2,1)}, bf16[4,128,1024]{2,1,0:T(8,128)(2,1)}, u32[]{:S(2)}, u32[]{:S(2)}) collective-permute-start(bf16[4,128,1024]{2,1,0:T(8,128)(2,1)} %pad_maximum_fusion.6), channel_id=1, source_target_pairs={{0,1},{1,0},{2,3},{3,2},{4,5},{5,4},{6,7},{7,6},{8,24},{9,25},{10,... | collective-permute-start | bytes 3145736 | tf_op jit(solution)/shard_map/ppermute | solution.py:95
  118.5 31.0 %collective-permute-start.13 = (bf16[8,32,4096]{2,1,0:T(8,128)(2,1)}, bf16[8,32,4096]{2,1,0:T(8,128)(2,1)}, u32[]{:S(2)}, u32[]{:S(2)}) collective-permute-start(bf16[8,32,4096]{2,1,0:T(8,128)(2,1)} %pad_maximum_fusion.2), channel_id=1, source_target_pairs={{0,16},{1,17},{2,18},{3,19},{4,20},{5,21},{6,22},{7,23},{8,9},{9,8... | collective-permute-start | bytes 6291464 | tf_op jit(solution)/shard_map/ppermute | solution.py:95
  137.9 34.0 %collective-permute-start.18 = (bf16[8,128,1024]{2,1,0:T(8,128)(2,1)S(1)}, bf16[8,128,1024]{2,1,0:T(8,128)(2,1)S(1)}, u32[]{:S(2)}, u32[]{:S(2)}) collective-permute-start(bf16[8,128,1024]{2,1,0:T(8,128)(2,1)S(1)} %pad_maximum_fusion.3), channel_id=1, source_target_pairs={{0,16},{1,17},{2,18},{3,19},{4,20},{5,21},{6,22},{7,23},{8,9},{9,8... | collective-permute-start | bytes 6291464 | tf_op jit(solution)/shard_map/ppermute | solution.py:95
  152.7 314.7 %collective-permute-start.14 = (bf16[16,32,4096]{2,1,0:T(8,128)(2,1)}, bf16[16,32,4096]{2,1,0:T(8,128)(2,1)}, u32[]{:S(2)}, u32[]{:S(2)}) collective-permute-start(bf16[16,32,4096]{2,1,0:T(8,128)(2,1)} %constant_dynamic-update-slice_fusion.5.own_ref), channel_id=1, source_target_pairs={{0,8},{1,9},{2,10},{3,11},{4,12},{5,13},{6,14},{7,15},{8,0},{9,1},... | collective-permute-start | bytes 12582920 | tf_op jit(solution)/shard_map/ppermute | solution.py:96
  173.4 561.7 %collective-permute-start.19 = (bf16[16,128,1024]{2,1,0:T(8,128)(2,1)}, bf16[16,128,1024]{2,1,0:T(8,128)(2,1)}, u32[]{:S(2)}, u32[]{:S(2)}) collective-permute-start(bf16[16,128,1024]{2,1,0:T(8,128)(2,1)} %constant_dynamic-update-slice_fusion.10.own_ref), channel_id=1, source_target_pairs={{0,8},{1,9},{2,10},{3,11},{4,12},{5,13},{6,14},{7,15},{8,0},{9,1},... | collective-permute-start | bytes 12582920 | tf_op jit(solution)/shard_map/ppermute | solution.py:96
  1611.4 286.8 %collective-permute-start.35 = (bf16[16,128,1024]{2,1,0:T(8,128)(2,1)}, bf16[16,128,1024]{2,1,0:T(8,128)(2,1)}, u32[]{:S(2)}, u32[]{:S(2)}) collective-permute-start(bf16[16,128,1024]{2,1,0:T(8,128)(2,1)} %get-tuple-element.19), channel_id=1, source_target_pairs={{0,8},{1,9},{2,10},{3,11},{4,12},{5,13},{6,14},{7,15},{8,0},{9,1},... | collective-permute-start | bytes 12582920 | tf_op jit(solution)/shard_map/ppermute | solution.py:107
  1611.5 294.3 %collective-permute-start.30 = (bf16[16,32,4096]{2,1,0:T(8,128)(2,1)}, bf16[16,32,4096]{2,1,0:T(8,128)(2,1)}, u32[]{:S(2)}, u32[]{:S(2)}) collective-permute-start(bf16[16,32,4096]{2,1,0:T(8,128)(2,1)} %get-tuple-element.17), channel_id=1, source_target_pairs={{0,8},{1,9},{2,10},{3,11},{4,12},{5,13},{6,14},{7,15},{8,0},{9,1},... | collective-permute-start | bytes 12582920 | tf_op jit(solution)/shard_map/ppermute | solution.py:107
  1877.7 24.5 %collective-permute-start.25 = (bf16[16,32,4096]{2,1,0:T(8,128)(2,1)}, bf16[16,32,4096]{2,1,0:T(8,128)(2,1)}, u32[]{:S(2)}, u32[]{:S(2)}) collective-permute-start(bf16[16,32,4096]{2,1,0:T(8,128)(2,1)} %get-tuple-element.15), channel_id=1, source_target_pairs={{0,8},{1,9},{2,10},{3,11},{4,12},{5,13},{6,14},{7,15},{8,0},{9,1},... | collective-permute-start | bytes 12582920 | tf_op jit(solution)/shard_map/ppermute | solution.py:107
  1896.4 13.0 collective-permute-start.23
  1900.8 26.1 %collective-permute-start.36 = (bf16[8,128,1024]{2,1,0:T(8,128)(2,1)S(1)}, bf16[8,128,1024]{2,1,0:T(8,128)(2,1)S(1)}, u32[]{:S(2)}, u32[]{:S(2)}) collective-permute-start(bf16[8,128,1024]{2,1,0:T(8,128)(2,1)S(1)} %add_convert_fusion.2), channel_id=1, source_target_pairs={{0,16},{1,17},{2,18},{3,19},{4,20},{5,21},{6,22},{7,23},{8,9},{9,8... | collective-permute-start | bytes 6291464 | tf_op jit(solution)/shard_map/ppermute | solution.py:112
  1904.6 56.0 %collective-permute-start.26 = (bf16[8,32,4096]{2,1,0:T(8,128)(2,1)S(1)}, bf16[8,32,4096]{2,1,0:T(8,128)(2,1)S(1)}, u32[]{:S(2)}, u32[]{:S(2)}) collective-permute-start(bf16[8,32,4096]{2,1,0:T(8,128)(2,1)S(1)} %add_convert_fusion.4), channel_id=1, source_target_pairs={{0,16},{1,17},{2,18},{3,19},{4,20},{5,21},{6,22},{7,23},{8,9},{9,8... | collective-permute-start | bytes 6291464 | tf_op jit(solution)/shard_map/ppermute | solution.py:112
  1908.2 86.1 %collective-permute-start.31 = (bf16[8,32,4096]{2,1,0:T(8,128)(2,1)S(1)}, bf16[8,32,4096]{2,1,0:T(8,128)(2,1)S(1)}, u32[]{:S(2)}, u32[]{:S(2)}) collective-permute-start(bf16[8,32,4096]{2,1,0:T(8,128)(2,1)S(1)} %add_convert_fusion.3), channel_id=1, source_target_pairs={{0,16},{1,17},{2,18},{3,19},{4,20},{5,21},{6,22},{7,23},{8,9},{9,8... | collective-permute-start | bytes 6291464 | tf_op jit(solution)/shard_map/ppermute | solution.py:112
  1928.8 69.3 %collective-permute-start.37 = (bf16[4,128,1024]{2,1,0:T(8,128)(2,1)S(1)}, bf16[4,128,1024]{2,1,0:T(8,128)(2,1)S(1)}, u32[]{:S(2)}, u32[]{:S(2)}) collective-permute-start(bf16[4,128,1024]{2,1,0:T(8,128)(2,1)S(1)} %add_convert_fusion.5), channel_id=1, source_target_pairs={{0,1},{1,0},{2,3},{3,2},{4,5},{5,4},{6,7},{7,6},{8,24},{9,25},{10,... | collective-permute-start | bytes 3145736 | tf_op jit(solution)/shard_map/ppermute | solution.py:112
  1962.3 37.5 %collective-permute-start.27 = (bf16[4,32,4096]{2,1,0:T(8,128)(2,1)S(1)}, bf16[4,32,4096]{2,1,0:T(8,128)(2,1)S(1)}, u32[]{:S(2)}, u32[]{:S(2)}) collective-permute-start(bf16[4,32,4096]{2,1,0:T(8,128)(2,1)S(1)} %add_convert_fusion.7), channel_id=1, source_target_pairs={{0,1},{1,0},{2,3},{3,2},{4,5},{5,4},{6,7},{7,6},{8,24},{9,25},{10,... | collective-permute-start | bytes 3145736 | tf_op jit(solution)/shard_map/ppermute | solution.py:112
  1996.0 14.9 collective-permute-start.32
  1999.5 14.9 collective-permute-start.38
  2001.2 30.7 %collective-permute-start.28 = (bf16[2,32,4096]{2,1,0:T(8,128)(2,1)S(1)}, bf16[2,32,4096]{2,1,0:T(8,128)(2,1)S(1)}, u32[]{:S(2)}, u32[]{:S(2)}) collective-permute-start(bf16[2,32,4096]{2,1,0:T(8,128)(2,1)S(1)} %add_convert_fusion.12), channel_id=1, source_target_pairs={{0,2},{1,3},{2,0},{3,1},{4,6},{5,7},{6,4},{7,5},{8,10},{9,11},{10,... | collective-permute-start | bytes 1572872 | tf_op jit(solution)/shard_map/ppermute | solution.py:112
  2012.4 25.9 %collective-permute-start.33 = (bf16[2,32,4096]{2,1,0:T(8,128)(2,1)S(1)}, bf16[2,32,4096]{2,1,0:T(8,128)(2,1)S(1)}, u32[]{:S(2)}, u32[]{:S(2)}) collective-permute-start(bf16[2,32,4096]{2,1,0:T(8,128)(2,1)S(1)} %add_convert_fusion.11), channel_id=1, source_target_pairs={{0,2},{1,3},{2,0},{3,1},{4,6},{5,7},{6,4},{7,5},{8,10},{9,11},{10,... | collective-permute-start | bytes 1572872 | tf_op jit(solution)/shard_map/ppermute | solution.py:112
  2015.6 38.9 %collective-permute-start.39 = (bf16[1,128,1024]{2,1,0:T(8,128)(2,1)S(1)}, bf16[1,128,1024]{2,1,0:T(8,128)(2,1)S(1)}, u32[]{:S(2)}, u32[]{:S(2)}) collective-permute-start(bf16[1,128,1024]{2,1,0:T(8,128)(2,1)S(1)} %add_convert_fusion.13), channel_id=1, source_target_pairs={{0,4},{1,5},{2,6},{3,7},{4,0},{5,1},{6,2},{7,3},{8,12},{9,13},{10,... | collective-permute-start | bytes 786440 | tf_op jit(solution)/shard_map/ppermute | solution.py:112
  2033.0 20.3 collective-permute-start.29
  2039.4 17.7 collective-permute-start.34
  (58 other events, 2855.3 us)

commit v2 on v1

v2 whole, which is shorter than its diff:
```python
import jax
import jax.numpy as jnp
from jax import lax
from jax.experimental import pallas as pl
from jax.experimental.pallas import tpu as pltpu
from jax.sharding import PartitionSpec as P

D = 1024
FF = 4096
HEADS = 16
HEAD_DIM = 64
SEQ = 256
AXES = ("dp", "fsdp")
BLOCKS = 32
GROUP = 4
WIDE = GROUP * HEAD_DIM
TILE = 512
CHUNK = 32
BF = jnp.bfloat16
F32 = jnp.float32

eps = 1e-06
ANY = pl.BlockSpec(memory_space=pl.ANY)
VMEM = pl.BlockSpec(memory_space=pltpu.VMEM)
SMEM = pl.BlockSpec(memory_space=pltpu.SMEM)


class Plan:
    def __init__(self, mesh):
        outer, inner = mesh.shape["dp"], mesh.shape["fsdp"]
        ys = outer // 2
        xs = min(ys, inner)
        zs = inner // xs
        self.devices = outer * inner
        self.half = self.devices // 2

        def bits(size, unit):
            found = []
            while size > 1:
                size //= 2
                found.append(size * unit)
            return found

        xbits = bits(xs, 1)
        zbits = bits(zs, xs)
        self.core = inner
        ybits = bits(ys, 2 * inner)
        self.orders = (zbits + xbits + ybits, zbits + ybits + xbits)
        self.stages = len(self.orders[0])

    def pairs(self, stage):
        return [
            (i, i ^ self.orders[1 if i & self.core else 0][stage]) for i in range(self.devices)
        ]

    def core_pairs(self):
        return [(i, i ^ self.core) for i in range(self.devices)]

    def masks(self, which):
        found = [0]
        for bit in self.orders[which]:
            found = found + [mask ^ bit for mask in found]
        return found

    def positions(self, me):
        tables = jnp.array(
            [
                self.masks(0) + [mask ^ self.core for mask in self.masks(1)],
                self.masks(1) + [mask ^ self.core for mask in self.masks(0)],
            ],
            jnp.int32,
        )
        mine = jnp.where((me & self.core) > 0, tables[1], tables[0])
        return mine ^ me


def gather(plan, block):
    held = block[None]
    for stage in range(plan.stages):
        held = jnp.concatenate([held, lax.ppermute(held, AXES, plan.pairs(stage))], 0)
    return held, lax.ppermute(held, AXES, plan.core_pairs())


def total(parts):
    result = parts[0].astype(F32)
    for part in parts[1:]:
        result = result + part.astype(F32)
    return result


def scatter_sum(plan, keep, send):
    parts = [keep, lax.ppermute(send, AXES, plan.core_pairs())]
    count = plan.half
    for stage in reversed(range(plan.stages)):
        count //= 2
        outgoing = total([part[count : 2 * count] for part in parts]).astype(BF)
        parts.append(lax.ppermute(outgoing, AXES, plan.pairs(stage)))
    return total([part[0] for part in parts])


def one_hot(order):
    return (order[:, None] == jnp.arange(order.shape[0])[None, :]).astype(BF)


def to_blocks(order, own, other):
    half, rows, width = own.shape
    if 2 * half == BLOCKS:
        return order, own, other
    joined = jnp.concatenate([own, other], 0).reshape(2 * half, rows * width)
    spread = lax.dot_general(
        one_hot(order), joined, (((0,), (0,)), ((), ())), preferred_element_type=BF
    ).reshape(2, BLOCKS // 2, -1, width)
    return jnp.arange(BLOCKS, dtype=jnp.int32), spread[0], spread[1]


def from_blocks(order, own, other):
    count = order.shape[0]
    if count == BLOCKS:
        return own, other
    half, _, width = own.shape
    joined = jnp.concatenate([own, other], 0).reshape(count, -1)
    moved = jnp.dot(one_hot(order), joined, preferred_element_type=BF).reshape(count, -1, width)
    return moved[: count // 2], moved[count // 2 :]


def params(limit):
    return pltpu.CompilerParams(vmem_limit_bytes=limit << 20)


def rows_of(ref, number, rows):
    return ref.at[pl.ds(pl.multiple_of(number * rows, rows), rows), :]


def fetches(order_ref, own_ref, other_ref, held_ref, sems, width=None):
    half, rows, _ = own_ref.shape
    copies = []
    for place in range(2 * half):
        source = own_ref.at[place] if place < half else other_ref.at[place - half]
        if width is not None:
            source = source.at[:, pl.ds(0, width)]
        number = order_ref[place]
        copies.append(
            pltpu.make_async_copy(source, rows_of(held_ref, number, rows), sems.at[number])
        )
    return copies


def stores(order_ref, held_ref, own_ref, other_ref, sems):
    half, rows, _ = own_ref.shape
    copies = []
    for place in list(range(half, 2 * half)) + list(range(half)):
        target = own_ref.at[place] if place < half else other_ref.at[place - half]
        copies.append(
            pltpu.make_async_copy(
                rows_of(held_ref, order_ref[place], rows), target, sems.at[place]
            )
        )
    return copies


def norm_parts(values):
    centre = values - jnp.mean(values, axis=-1, keepdims=True)
    inverse = lax.rsqrt(jnp.mean(centre * centre, axis=-1, keepdims=True) + eps)
    return centre * inverse, inverse


def norm_back(grad_norm, normed, inverse):
    return inverse * (
        grad_norm
        - jnp.mean(grad_norm, axis=-1, keepdims=True)
        - normed * jnp.mean(grad_norm * normed, axis=-1, keepdims=True)
    )


def span(index, size):
    return pl.ds(pl.multiple_of(index * size, size), size)


def dot(a, b):
    return jnp.dot(a, b, preferred_element_type=F32)


def dot_nt(a, b):
    return lax.dot_general(a, b, (((1,), (1,)), ((), ())), preferred_element_type=F32)


def dot_tn(a, b):
    return lax.dot_general(a, b, (((0,), (0,)), ((), ())), preferred_element_type=F32)


def stacked(values):
    head = lax.broadcasted_iota(jnp.int32, values.shape, 1) // HEAD_DIM
    zero = jnp.zeros_like(values)
    return jnp.concatenate([jnp.where(head == h, values, zero) for h in range(GROUP)], 0)


def unstacked(values):
    rows = values.shape[0] // GROUP
    head = lax.broadcasted_iota(jnp.int32, (rows, values.shape[1]), 1) // HEAD_DIM
    result = values[:rows]
    for h in range(1, GROUP):
        result = jnp.where(head == h, values[h * rows : (h + 1) * rows], result)
    return result


def attend_kernel(
    order_ref, vec_ref, x_ref, idr_ref, idc_ref, own_ref, other_ref,
    entry_ref, project_ref, probs_ref, mixed_ref, middle_ref, second_ref,
    held, project, probs, sems, out_sems,
):
    copies = fetches(order_ref, own_ref, other_ref, held, sems)
    for copy in copies:
        copy.start()
    count = x_ref.shape[0]

    @pl.loop(0, count // CHUNK)
    def _(i):
        normed, _ = norm_parts(x_ref[span(i, CHUNK), :].astype(F32))
        entry_ref[span(i, CHUNK), :] = (normed * vec_ref[0:1, :] + vec_ref[2:3, :]).astype(BF)

    for copy in copies:
        copy.wait()

    @pl.loop(0, 3 * D // TILE)
    def _(i):
        third = i // (D // TILE)
        column = span(lax.rem(i, D // TILE), TILE)
        bias_row = jnp.where(third == 0, 3, 4)
        bias = jnp.where(third == 1, 0.0, vec_ref[pl.ds(bias_row, 1), column])
        project[:, span(i, TILE)] = (dot(entry_ref[...], held[:, span(i, TILE)]) + bias).astype(BF)

    project_out = pltpu.make_async_copy(project, project_ref, out_sems.at[0])
    project_out.start()
    groups = D // WIDE

    @pl.loop(0, (count // SEQ) * groups)
    def _(i):
        row, group = i // groups, lax.rem(i, groups)
        rows = span(row, SEQ)
        queries = project[rows, span(group, WIDE)] * BF(HEAD_DIM**-0.5)
        keys = project[rows, span(groups + group, WIDE)]
        values = project[rows, span(2 * groups + group, WIDE)]
        scores = dot_nt(stacked(queries), keys)
        same = idc_ref[rows, :] == idr_ref[pl.ds(row, 1), :]
        scores = jnp.where(same[None], scores.reshape(GROUP, SEQ, SEQ), -1e9)
        expo = jnp.exp(scores - jnp.max(scores, axis=-1, keepdims=True))
        low = (expo / jnp.sum(expo, axis=-1, keepdims=True)).astype(BF)
        low = low.reshape(GROUP * SEQ, SEQ)
        probs[i] = low
        pltpu.make_async_copy(probs.at[i], probs_ref.at[i], out_sems.at[1 + i]).start()
        mixed_ref[rows, span(group, WIDE)] = unstacked(dot(low, values)).astype(BF)

    @pl.loop(0, D // TILE)
    def _(i):
        columns = span(i, TILE)
        branch = dot(mixed_ref[...], held[:, span(3 * D // TILE + i, TILE)])
        middle_ref[:, columns] = x_ref[:, columns].astype(F32) + (branch + vec_ref[5:6, columns])

    @pl.loop(0, count // CHUNK)
    def _(i):
        normed, _ = norm_parts(middle_ref[span(i, CHUNK), :])
        second_ref[span(i, CHUNK), :] = (normed * vec_ref[1:2, :] + vec_ref[6:7, :]).astype(BF)

    project_out.wait()
    for i in range((count // SEQ) * groups):
        pltpu.make_async_copy(probs.at[i], probs_ref.at[i], out_sems.at[1 + i]).wait()


def attend(order, vec, x, ids, own, other):
    count = x.shape[0]
    steps = (count // SEQ) * (D // WIDE)
    shape = jax.ShapeDtypeStruct
    return pl.pallas_call(
        attend_kernel,
        out_shape=[
            shape((count, D), BF),
            shape((count, 3 * D), BF),
            shape((steps, GROUP * SEQ, SEQ), BF),
            shape((count, D), BF),
            shape((count, D), F32),
            shape((count, D), BF),
        ],
        in_specs=[SMEM, VMEM, VMEM, VMEM, VMEM, ANY, ANY],
        out_specs=[VMEM, ANY, ANY, VMEM, VMEM, VMEM],
        scratch_shapes=[
            pltpu.VMEM((D, 4 * D), BF),
            pltpu.VMEM((count, 3 * D), BF),
            pltpu.VMEM((steps, GROUP * SEQ, SEQ), BF),
            pltpu.SemaphoreType.DMA((BLOCKS,)),
            pltpu.SemaphoreType.DMA((1 + steps,)),
        ],
        compiler_params=params(48),
        name="attend",
    )(order, vec, x, ids, ids.reshape(count, 1), own, other)


def rise_kernel(
    order_ref, spot_ref, bias_ref, second_ref, top_ref, own_ref, other_ref,
    active_ref, slope_ref, gown_ref, gother_ref,
    held, grads, sems, out_sems,
):
    step = pl.program_id(0)
    half, rows, _ = gown_ref.shape

    @pl.when(step == 0)
    def _():
        copies = fetches(order_ref, own_ref, other_ref, held, sems)
        for copy in copies:
            copy.start()
        for copy in copies:
            copy.wait()

    hidden = dot(second_ref[...], held[:, span(step, TILE)]) + bias_ref[...]
    cdf = 0.5 + 0.5 * lax.erf(hidden * (0.5**0.5))
    slope = cdf + hidden * jnp.exp(-0.5 * hidden * hidden) * 0.3989422804014327
    active = (hidden * cdf).astype(BF)
    active_ref[...] = active
    slope_ref[...] = slope.astype(BF)
    grads[span(step, TILE), :] = dot_tn(active, top_ref[...]).astype(BF)
    for block in range(TILE // rows):
        number = step * (TILE // rows) + block
        place = spot_ref[number]

        @pl.when(place < half)
        def _():
            pltpu.make_async_copy(
                rows_of(grads, number, rows), gown_ref.at[place], out_sems.at[number]
            ).start()

        @pl.when(place >= half)
        def _():
            pltpu.make_async_copy(
                rows_of(grads, number, rows), gother_ref.at[place - half], out_sems.at[number]
            ).start()

    @pl.when(step == FF // TILE - 1)
    def _():
        for number in range(2 * half):
            pltpu.make_async_copy(
                rows_of(grads, number, rows), gown_ref.at[0], out_sems.at[number]
            ).wait()


def rise(order, spot, bias, second, top, own, other):
    count = second.shape[0]
    shape = jax.ShapeDtypeStruct
    whole = pl.BlockSpec((count, D), lambda t: (0, 0))
    columns = pl.BlockSpec((count, TILE), lambda t: (0, t))
    grad = shape((BLOCKS // 2, FF // BLOCKS, D), BF)
    return pl.pallas_call(
        rise_kernel,
        grid=(FF // TILE,),
        out_shape=[shape((count, FF), BF), shape((count, FF), BF), grad, grad],
        in_specs=[SMEM, SMEM, pl.BlockSpec((1, TILE), lambda t: (0, t)), whole, whole, ANY, ANY],
        out_specs=[columns, columns, ANY, ANY],
        scratch_shapes=[
            pltpu.VMEM((D, FF), BF),
            pltpu.VMEM((FF, D), BF),
            pltpu.SemaphoreType.DMA((BLOCKS,)),
            pltpu.SemaphoreType.DMA((BLOCKS,)),
        ],
        compiler_params=params(48),
        name="rise",
    )(order, spot, bias, second, top, own, other)


def fall_kernel(
    order_ref, top_ref, slope_ref, second_ref, mown_ref, mother_ref, iown_ref, iother_ref,
    gsecond_ref, bias_ref, gown_ref, gother_ref,
    mheld, iheld, turned, grads, msems, isems, out_sems,
):
    step = pl.program_id(0)
    rows = mown_ref.shape[1]

    @pl.when(step == 0)
    def _():
        for copy in fetches(order_ref, mown_ref, mother_ref, mheld, msems):
            copy.start()
        for copy in fetches(order_ref, iown_ref, iother_ref, iheld, isems):
            copy.start()
        turned[...] = second_ref[...].T

    for block in range(TILE // rows):
        number = step * (TILE // rows) + block
        pltpu.make_async_copy(
            mown_ref.at[0], rows_of(mheld, number, rows), msems.at[number]
        ).wait()
    grad_active = dot_nt(top_ref[...], mheld[span(step, TILE), :])
    grad_hidden = (grad_active * slope_ref[...].astype(F32)).astype(BF)
    bias_ref[...] = jnp.sum(grad_hidden.astype(F32), axis=0, keepdims=True)
    grads[:, span(step, TILE)] = dot(turned[...], grad_hidden).astype(BF)

    @pl.when(step == 0)
    def _():
        for copy in fetches(order_ref, iown_ref, iother_ref, iheld, isems):
            copy.wait()
        gsecond_ref[...] = jnp.zeros_like(gsecond_ref)

    gsecond_ref[...] += dot_nt(grad_hidden, iheld[:, span(step, TILE)])

    @pl.when(step == FF // TILE - 1)
    def _():
        copies = stores(order_ref, grads, gown_ref, gother_ref, out_sems)
        for copy in copies:
            copy.start()
        for copy in copies:
            copy.wait()


def fall(order, top, slope, second, mlp, win):
    count = second.shape[0]
    shape = jax.ShapeDtypeStruct
    whole = pl.BlockSpec((count, D), lambda t: (0, 0))
    grad = shape((BLOCKS // 2, D // BLOCKS, FF), BF)
    return pl.pallas_call(
        fall_kernel,
        grid=(FF // TILE,),
        out_shape=[shape((count, D), F32), shape((1, FF), F32), grad, grad],
        in_specs=[
            SMEM, whole, pl.BlockSpec((count, TILE), lambda t: (0, t)), whole, ANY, ANY, ANY, ANY,
        ],
        out_specs=[whole, pl.BlockSpec((1, TILE), lambda t: (0, t)), ANY, ANY],
        scratch_shapes=[
            pltpu.VMEM((FF, D), BF),
            pltpu.VMEM((D, FF), BF),
            pltpu.VMEM((D, count), BF),
            pltpu.VMEM((D, FF), BF),
            pltpu.SemaphoreType.DMA((BLOCKS,)),
            pltpu.SemaphoreType.DMA((BLOCKS,)),
            pltpu.SemaphoreType.DMA((BLOCKS,)),
        ],
        compiler_params=params(56),
        name="fall",
    )(order, top, slope, second, *mlp, *win)


def unattend_kernel(
    order_ref, vec_ref, gsecond_ref, middle_ref, top_ref, mixed_ref, entry_ref, project_ref,
    probs_ref, own_ref, other_ref,
    gmiddle_ref, gproject_ref, sums_ref, gown_ref, gother_ref,
    held, branch, gmixed, turned, grads, sems, out_sems,
):
    copies = fetches(order_ref, own_ref, other_ref, held, sems)
    for copy in copies:
        copy.start()
    count = middle_ref.shape[0]
    sums_ref[...] = jnp.zeros_like(sums_ref)

    @pl.loop(0, count // CHUNK)
    def _(i):
        rows = span(i, CHUNK)
        normed, inverse = norm_parts(middle_ref[rows, :])
        grad = gsecond_ref[rows, :]
        sums_ref[0:1, :] += jnp.sum(grad * normed, axis=0, keepdims=True)
        sums_ref[1:2, :] += jnp.sum(grad, axis=0, keepdims=True)
        top = top_ref[rows, :].astype(F32)
        sums_ref[3:4, :] += jnp.sum(top, axis=0, keepdims=True)
        gmiddle = top + norm_back(grad * vec_ref[1:2, :], normed, inverse)
        gmiddle_ref[rows, :] = gmiddle
        low = gmiddle.astype(BF)
        branch[rows, :] = low
        sums_ref[2:3, :] += jnp.sum(low.astype(F32), axis=0, keepdims=True)

    turned[...] = mixed_ref[...].T
    for copy in copies:
        copy.wait()

    @pl.loop(0, D // TILE)
    def _(i):
        columns = span(i, TILE)
        grads[:, span(3 * D // TILE + i, TILE)] = dot(turned[...], branch[:, columns]).astype(BF)
        gmixed[:, columns] = dot_nt(branch[...], held[columns, 3 * D :]).astype(BF)

    turned[...] = entry_ref[...].T
    groups = D // WIDE

    @pl.loop(0, (count // SEQ) * groups)
    def _(i):
        row, group = i // groups, lax.rem(i, groups)
        rows = span(row, SEQ)
        scale = HEAD_DIM**-0.5
        queries = stacked(project_ref[rows, span(group, WIDE)] * BF(scale))
        keys = project_ref[rows, span(groups + group, WIDE)]
        values = project_ref[rows, span(2 * groups + group, WIDE)]
        gmix = stacked(gmixed[rows, span(group, WIDE)])
        low = probs_ref[i]
        gprobs = dot_nt(gmix, values)
        gvalues = dot_tn(low, gmix)
        weight = low.astype(F32)
        inner = jnp.sum(weight * gprobs, axis=-1, keepdims=True)
        gscores = (weight * (gprobs - inner)).astype(BF)
        gqueries = unstacked(dot(gscores, keys)) * scale
        gkeys = dot_tn(gscores, queries)
        gproject_ref[rows, span(group, WIDE)] = gqueries.astype(BF)
        gproject_ref[rows, span(groups + group, WIDE)] = gkeys.astype(BF)
        gproject_ref[rows, span(2 * groups + group, WIDE)] = gvalues.astype(BF)

    @pl.loop(0, 3 * D // TILE)
    def _(i):
        gpart = gproject_ref[:, span(i, TILE)]
        grads[:, span(i, TILE)] = dot(turned[...], gpart).astype(BF)
        third = i // (D // TILE)
        column = span(lax.rem(i, D // TILE), TILE)
        sums_ref[pl.ds(4 + third, 1), column] = jnp.sum(gpart.astype(F32), axis=0, keepdims=True)

    copies = stores(order_ref, grads, gown_ref, gother_ref, out_sems)
    for copy in copies:
        copy.start()
    for copy in copies:
        copy.wait()


def unattend(order, vec, gsecond, middle, top, mixed, entry, project, probs, first):
    count = middle.shape[0]
    shape = jax.ShapeDtypeStruct
    grad = shape((BLOCKS // 2, D // BLOCKS, 4 * D), BF)
    return pl.pallas_call(
        unattend_kernel,
        out_shape=[
            shape((count, D), F32), shape((count, 3 * D), BF), shape((8, D), F32), grad, grad,
        ],
        in_specs=[SMEM] + [VMEM] * 8 + [ANY] * 2,
        out_specs=[VMEM] * 3 + [ANY] * 2,
        scratch_shapes=[
            pltpu.VMEM((D, 4 * D), BF),
            pltpu.VMEM((count, D), BF),
            pltpu.VMEM((count, D), BF),
            pltpu.VMEM((D, count), BF),
            pltpu.VMEM((D, 4 * D), BF),
            pltpu.SemaphoreType.DMA((BLOCKS,)),
            pltpu.SemaphoreType.DMA((BLOCKS,)),
        ],
        compiler_params=params(56),
        name="unattend",
    )(order, vec, gsecond, middle, top, mixed, entry, project, probs, *first)


def enter_kernel(
    order_ref, vec_ref, x_ref, gmiddle_ref, gproject_ref, own_ref, other_ref,
    ginputs_ref, sums_ref,
    held, gentry, sems,
):
    copies = fetches(order_ref, own_ref, other_ref, held, sems, 3 * D)
    for copy in copies:
        copy.start()
    count = x_ref.shape[0]
    sums_ref[...] = jnp.zeros_like(sums_ref)
    for copy in copies:
        copy.wait()

    @pl.loop(0, D // TILE)
    def _(i):
        gentry[:, span(i, TILE)] = dot_nt(gproject_ref[...], held[span(i, TILE), :])

    @pl.loop(0, count // CHUNK)
    def _(i):
        rows = span(i, CHUNK)
        normed, inverse = norm_parts(x_ref[rows, :].astype(F32))
        grad = gentry[rows, :]
        sums_ref[0:1, :] += jnp.sum(grad * normed, axis=0, keepdims=True)
        sums_ref[1:2, :] += jnp.sum(grad, axis=0, keepdims=True)
        back = norm_back(grad * vec_ref[0:1, :], normed, inverse)
        ginputs_ref[rows, :] = gmiddle_ref[rows, :] + back


def enter(order, vec, x, gmiddle, gproject, first):
    count = x.shape[0]
    shape = jax.ShapeDtypeStruct
    return pl.pallas_call(
        enter_kernel,
        out_shape=[shape((count, D), F32), shape((8, D), F32)],
        in_specs=[SMEM] + [VMEM] * 4 + [ANY] * 2,
        out_specs=[VMEM] * 2,
        scratch_shapes=[
            pltpu.VMEM((D, 3 * D), BF),
            pltpu.VMEM((count, D), F32),
            pltpu.SemaphoreType.DMA((BLOCKS,)),
        ],
        compiler_params=params(48),
        name="enter",
    )(order, vec, x, gmiddle, gproject, *first)


def finish_kernel(order_ref, vec_ref, middle_ref, active_ref, own_ref, other_ref, out_ref, held, sems):
    copies = fetches(order_ref, own_ref, other_ref, held, sems)
    for copy in copies:
        copy.start()
    for copy in copies:
        copy.wait()

    @pl.loop(0, D // WIDE)
    def _(i):
        columns = span(i, WIDE)
        result = dot(active_ref[...], held[:, columns]) + vec_ref[7:8, columns]
        out_ref[:, columns] = (middle_ref[:, columns] + result).astype(BF)


def finish(order, vec, middle, active, mlp):
    count = middle.shape[0]
    return pl.pallas_call(
        finish_kernel,
        out_shape=jax.ShapeDtypeStruct((count, D), BF),
        in_specs=[SMEM] + [VMEM] * 3 + [ANY] * 2,
        out_specs=VMEM,
        scratch_shapes=[pltpu.VMEM((FF, D), BF), pltpu.SemaphoreType.DMA((BLOCKS,))],
        compiler_params=params(48),
        name="finish",
    )(order, vec, middle, active, *mlp)


def per_device(plan, inputs, image_ids, cotangent, gains, biases, w_qkv, w_out, w_in, w_mlp):
    me = lax.axis_index(AXES)
    order = plan.positions(me)
    gain_dev, bias_dev = gains.shape[1], biases.shape[1]
    small = jnp.concatenate([gains, biases], 1)
    rows = D // plan.devices
    first = jnp.concatenate([w_qkv.reshape(rows, 3 * D), w_out.reshape(rows, D)], 1)
    first = gather(plan, first)
    small_own, small_other = gather(plan, small)
    win = gather(plan, w_in.reshape(rows, FF))
    mlp = gather(plan, w_mlp.reshape(FF // plan.devices, D))
    placed = jnp.concatenate([small_own, small_other], 0)[:, 0]
    small_all = lax.dot_general(
        one_hot(order), placed, (((0,), (0,)), ((), ())), preferred_element_type=F32
    )
    vec = jnp.concatenate(
        [small_all[:, :gain_dev].reshape(-1), small_all[:, gain_dev:].reshape(-1)]
    ).reshape(-1, D)
    bias_in = vec[8:12].reshape(1, FF)
    vec = vec[:8]
    numbers, *first = to_blocks(order, *first)
    _, *win = to_blocks(order, *win)
    _, *mlp = to_blocks(order, *mlp)
    spot = jnp.sum(
        jnp.where(numbers[:, None] == jnp.arange(BLOCKS)[None, :], jnp.arange(BLOCKS)[:, None], 0),
        axis=0,
    ).astype(jnp.int32)
    blocks, length = image_ids.shape
    count = blocks * length
    x = inputs.reshape(count, D)
    top = jnp.where(image_ids.reshape(count, 1) >= 0, cotangent.reshape(count, D), BF(0))
    entry, project, probs, mixed, middle, second = attend(numbers, vec, x, image_ids, *first)
    active, slope, *grad_mlp = rise(numbers, spot, bias_in, second, top, *win)
    sum_mlp = scatter_sum(plan, *from_blocks(order, *grad_mlp))
    gsecond, grad_bias_in, *grad_in = fall(numbers, top, slope, second, mlp, win)
    sum_in = scatter_sum(plan, *from_blocks(order, *grad_in))
    gmiddle, gproject, sums, *grad_first = unattend(
        numbers, vec, gsecond, middle, top, mixed, entry, project, probs, first
    )
    sum_first = scatter_sum(plan, *from_blocks(order, *grad_first))
    grad_inputs, sums_one = enter(numbers, vec, x, gmiddle, gproject, first)
    output = finish(numbers, vec, middle, active, mlp)
    flat_gains = jnp.concatenate([sums_one[0], sums[0]]).reshape(-1, gain_dev)
    flat_biases = jnp.concatenate(
        [sums_one[1], sums[4], sums[6], sums[2], sums[1], sums[3], grad_bias_in[0]]
    ).reshape(-1, bias_dev)
    flat_small = jnp.concatenate([flat_gains, flat_biases], 1).astype(BF)
    moved = jnp.dot(one_hot(order), flat_small, preferred_element_type=F32).astype(BF)[:, None]
    sum_small = scatter_sum(plan, moved[: plan.half], moved[plan.half :])
    return (
        output.reshape(blocks, length, D),
        grad_inputs.reshape(blocks, length, D),
        sum_small[:, :gain_dev],
        sum_small[:, gain_dev:],
        sum_first[:, : 3 * D].reshape(1, -1),
        sum_first[:, 3 * D :].reshape(1, -1),
        sum_in.reshape(1, -1),
        sum_mlp.reshape(1, -1),
    )


def solution(mesh):
    plan = Plan(mesh)
    whole = P(AXES, None, None)
    flat = P(AXES, None)

    def body(*arrays):
        return per_device(plan, *arrays)

    return jax.shard_map(
        body,
        mesh=mesh,
        in_specs=(whole, flat, whole, flat, flat, flat, flat, flat, flat),
        out_specs=(whole, whole, flat, flat, flat, flat, flat, flat),
        check_vma=False,
    )
```

time: 2080 us -> 473 us (0.23)
  Pallas kernels: 1540 us -> 131 us
  matrix products: 117 us -> 0.46 us
  local copies, waits for them, and re-layouts: 63.4 us -> 23.7 us
  other arithmetic: 76.6 us -> 38.3 us
    pallas_call x6, Pallas kernels: 1540 us -> 131 us  [the longest x1 31.6 us: unattend(): pl.pallas_call(unattend_kernel, out_shape=[shape((count, D), F32), shape(...]
    dot_general x19 -> x1, matrix products: 117 us -> 0.2 us  [per_device(): jnp.dot(one_hot(order), flat_small, preferred_element_type=F32).astype(BF)]
    reshape x10 -> x3, local copies, waits for them, and re-layouts: 22.6 us -> 0.26 us  [the longest x1 0.1 us: per_device(): flat_biases = jnp.concatenate([sums_one[1], sums[4], sums[6], sums[2], su...]
    ppermute x16, waiting for transfers between devices: 92.7 us -> 115 us  [gather(): lax.ppermute(held, AXES, plan.pairs(stage))]
  transfers between devices with their start and end apart: 40 -> 40, of which waited for: 22 -> 25; matrix products, arithmetic and copies ran while one was open for 7% -> 11% of each run, Pallas kernels for 37% -> 28%
where the time goes in v2:
time: 473 us; the launch traced here: 469 us
  waiting for transfers between devices  210 us (44%)
  Pallas kernels  131 us (28%)
  starting transfers between devices  65.2 us (14%)
  other arithmetic  38.3 us (8%)
  local copies, waits for them, and re-layouts  23.7 us (5%)
    ppermute x16, waiting for transfers between devices, gather(): lax.ppermute(held, AXES, plan.pairs(stage))  115 us
    ppermute x16, waiting for transfers between devices, scatter_sum(): parts.append(lax.ppermute(outgoing, AXES, plan.pairs(stage)))  93.4 us
    pallas_call x1, Pallas kernels, unattend(): pl.pallas_call(unattend_kernel, out_shape=[shape((count, D), F32), shape(...  31.6 us
    ppermute x16, starting transfers between devices, scatter_sum(): parts.append(lax.ppermute(outgoing, AXES, plan.pairs(stage)))  30.4 us
    ppermute x16, starting transfers between devices, gather(): lax.ppermute(held, AXES, plan.pairs(stage))  30.3 us
    pallas_call x1, Pallas kernels, fall(): pl.pallas_call(fall_kernel, grid=(FF // TILE,), out_shape=[shape((count,...  28.9 us
    convert_element_type x16, other arithmetic, scatter_sum(): outgoing = total([part[count:2 * count] for part in parts]).astype(BF)  23.9 us
    pallas_call x1, Pallas kernels, attend(): pl.pallas_call(attend_kernel, out_shape=[shape((count, D), BF), shape((co...  22.2 us
  transfers between devices with their start and end apart: 40, of which 25 were waited for; matrix products, arithmetic and copies ran while one was open for 11% of the time, Pallas kernels for 28%

profile of v2, /device:TPU:8, one launch (start us, length us, event | category | flops | bytes accessed | tf_op | source)
XLA Modules:
  0.0 469.4 jit_solution(503635126346207034)
XLA Ops:
  17.2 12.0 %collective-permute-done.5 = bf16[1,32,4096]{2,1,0:T(8,128)(2,1)S(1)} collective-permute-done((bf16[1,32,4096]{2,1,0:T(8,128)(2,1)S(1)}, bf16[1,32,4096]{2,1,0:T(8,128)(2,1)S(1)}, u32[]{:S(2)}, u32[]{:S(2)}) %collective-permute-start.5) | collective-permute-done | bytes 262176 | tf_op jit(solution)/shard_map/ppermute | solution.py:80
  31.4 3.5 collective-permute-done.10
  37.1 3.3 collective-permute-done.15
  44.1 6.4 %collective-permute-done.6 = bf16[2,32,4096]{2,1,0:T(8,128)(2,1)S(1)} collective-permute-done((bf16[2,32,4096]{2,1,0:T(8,128)(2,1)S(1)}, bf16[2,32,4096]{2,1,0:T(8,128)(2,1)S(1)}, u32[]{:S(2)}, u32[]{:S(2)}) %collective-permute-start.6) | collective-permute-done | bytes 524320 | tf_op jit(solution)/shard_map/ppermute | solution.py:80
  52.2 9.5 %collective-permute-done.11 = bf16[2,32,4096]{2,1,0:T(8,128)(2,1)S(1)} collective-permute-done((bf16[2,32,4096]{2,1,0:T(8,128)(2,1)S(1)}, bf16[2,32,4096]{2,1,0:T(8,128)(2,1)S(1)}, u32[]{:S(2)}, u32[]{:S(2)}) %collective-permute-start.11) | collective-permute-done | bytes 524320 | tf_op jit(solution)/shard_map/ppermute | solution.py:80
  63.4 9.4 %collective-permute-done.16 = bf16[2,128,1024]{2,1,0:T(8,128)(2,1)S(1)} collective-permute-done((bf16[2,128,1024]{2,1,0:T(8,128)(2,1)S(1)}, bf16[2,128,1024]{2,1,0:T(8,128)(2,1)S(1)}, u32[]{:S(2)}, u32[]{:S(2)}) %collective-permute-start.16) | collective-permute-done | bytes 524320 | tf_op jit(solution)/shard_map/ppermute | solution.py:80
  79.4 18.4 %collective-permute-done.17 = bf16[4,128,1024]{2,1,0:T(8,128)(2,1)S(1)} collective-permute-done((bf16[4,128,1024]{2,1,0:T(8,128)(2,1)S(1)}, bf16[4,128,1024]{2,1,0:T(8,128)(2,1)S(1)}, u32[]{:S(2)}, u32[]{:S(2)}) %collective-permute-start.17) | collective-permute-done | bytes 1048608 | tf_op jit(solution)/shard_map/ppermute | solution.py:80
  98.0 2.7 collective-permute-start.18
  102.8 6.5 %collective-permute-done.8 = bf16[8,32,4096]{2,1,0:T(8,128)(2,1)S(1)} collective-permute-done((bf16[8,32,4096]{2,1,0:T(8,128)(2,1)S(1)}, bf16[8,32,4096]{2,1,0:T(8,128)(2,1)S(1)}, u32[]{:S(2)}, u32[]{:S(2)}) %collective-permute-start.8) | collective-permute-done | bytes 2097184 | tf_op jit(solution)/shard_map/ppermute | solution.py:80
  112.1 19.7 %collective-permute-done.13 = bf16[8,32,4096]{2,1,0:T(8,128)(2,1)S(1)} collective-permute-done((bf16[8,32,4096]{2,1,0:T(8,128)(2,1)S(1)}, bf16[8,32,4096]{2,1,0:T(8,128)(2,1)S(1)}, u32[]{:S(2)}, u32[]{:S(2)}) %collective-permute-start.13) | collective-permute-done | bytes 2097184 | tf_op jit(solution)/shard_map/ppermute | solution.py:80
  136.5 17.8 %collective-permute-done.18 = bf16[8,128,1024]{2,1,0:T(8,128)(2,1)S(1)} collective-permute-done((bf16[8,128,1024]{2,1,0:T(8,128)(2,1)S(1)}, bf16[8,128,1024]{2,1,0:T(8,128)(2,1)S(1)}, u32[]{:S(2)}, u32[]{:S(2)}) %collective-permute-start.18) | collective-permute-done | bytes 2097184 | tf_op jit(solution)/shard_map/ppermute | solution.py:80
  156.8 4.6 collective-permute-start
  163.9 2.7 collective-permute-done.1
  175.9 22.2 %attend.1 = (bf16[512,1024]{1,0:T(8,128)(2,1)S(1)}, bf16[512,3072]{1,0:T(8,128)(2,1)}, bf16[8,1024,256]{2,1,0:T(8,128)(2,1)}, bf16[512,1024]{1,0:T(8,128)(2,1)S(...) custom-call(s32[32]{0:T(128)S(1)} %fusion.31.order_ref, f32[8,1024]{1,0:T(8,128)S(1)} %slice.326.vec_ref, ...), custom_call_target="tpu_custom_call" | custom-call | tf_op jit(solution)/shard_map/attend/pallas_call | solution.py:273
  199.1 20.8 %rise.1 = (bf16[512,4096]{1,0:T(8,128)(2,1)}, bf16[512,4096]{1,0:T(8,128)(2,1)}, bf16[16,128,1024]{2,1,0:T(8,128)(2,1)}, bf16[16,128,1024]{2,1,0:T(8,128)(2,1)}) custom-call(s32[32]{0:T(128)S(1)} %fusion.31.order_ref, s32[32]{0:T(128)S(1)} %select_reduce_fusion.spot_ref, f32[1,4096]{1,0:T(1,128)S(1)} %bitcast.103, ...), custom_call_target="tpu_custom_call" | custom-call | tf_op jit(solution)/shard_map/rise/pallas_call | solution.py:350
  220.1 28.9 %fall.1 = (f32[512,1024]{1,0:T(8,128)}, f32[1,4096]{1,0:T(1,128)}, bf16[16,32,4096]{2,1,0:T(8,128)(2,1)}, bf16[16,32,4096]{2,1,0:T(8,128)(2,1)}) custom-call(s32[32]{0:T(128)} %copy-done.9, bf16[512,1024]{1,0:T(8,128)(2,1)} %copy-done, bf16[512,4096]{1,0:T(8,128)(2,1)} %get-tuple-element.32.slope_ref, bf16[512,1024]{1,0:T(8,128)(2,1)} %copy-done.3, ...), custom_call_target="tpu_custom_call" | custom-call | tf_op jit(solution)/shard_map/fall/pallas_call | solution.py:415
  249.0 31.6 %unattend.1 = (f32[512,1024]{1,0:T(8,128)}, bf16[512,3072]{1,0:T(8,128)(2,1)}, f32[8,1024]{1,0:T(8,128)}, bf16[16,32,4096]{2,1,0:T(8,128)(2,1)}, bf16[16,32,4096]{2,1,0:T(8,128)(2,1)}) custom-call(s32[32]{0:T(128)} %copy-done.9, f32[8,1024]{1,0:T(8,128)} %copy-done.7, f32[512,1024]{1,0:T(8,128)} %get-tuple-element.33.gsecond_ref, ...), custom_call_target="tpu_custom_call" | custom-call | tf_op jit(solution)/shard_map/unattend/pallas_call | solution.py:517
  282.8 14.8 %enter.1 = (f32[512,1024]{1,0:T(8,128)}, f32[8,1024]{1,0:T(8,128)S(1)}) custom-call(s32[32]{0:T(128)S(1)} %copy-done.10, f32[8,1024]{1,0:T(8,128)S(1)} %copy-done.8, bf16[512,1024]{1,0:T(8,128)(2,1)S(1)} %bitcast.101, f32[512,1024]{1,0:T(8,128)S(1)} %copy-done.4, bf16[512,3072]{1,0:T(8,128)(2,1)} %get-tuple-element.39.gproject_ref, ...), custom_call_target="tpu_custom_call" | custom-call | tf_op jit(solution)/shard_map/enter/pallas_call | solution.py:569
  302.3 3.3 add_convert_fusion
  310.2 3.7 add_convert_fusion.1
  318.9 2.7 collective-permute-done.23
  321.6 3.2 collective-permute-start.24
  324.8 12.3 %finish.1 = bf16[512,1024]{1,0:T(8,128)(2,1)} custom-call(s32[32]{0:T(128)S(1)} %copy-done.10, f32[8,1024]{1,0:T(8,128)S(1)} %copy-done.8, f32[512,1024]{1,0:T(8,128)S(1)} %copy-done.1, bf16[512,4096]{1,0:T(8,128)(2,1)} %get-tuple-element.31.active_ref, bf16[16,128,1024]{2,1,0:T(8,128)(2,1)} %constant_dynamic-update-slice_fusion.10.own_ref.mown_ref, ...), custom_call_target="tpu_custom_call" | custom-call | tf_op jit(solution)/shard_map/finish/pallas_call | solution.py:600
  342.1 23.4 %collective-permute-done.26 = bf16[8,32,4096]{2,1,0:T(8,128)(2,1)} collective-permute-done((bf16[8,32,4096]{2,1,0:T(8,128)(2,1)S(1)}, bf16[8,32,4096]{2,1,0:T(8,128)(2,1)}, u32[]{:S(2)}, u32[]{:S(2)}) %collective-permute-start.26) | collective-permute-done | bytes 2097184 | tf_op jit(solution)/shard_map/ppermute | solution.py:97
  369.6 29.6 %collective-permute-done.31 = bf16[8,32,4096]{2,1,0:T(8,128)(2,1)} collective-permute-done((bf16[8,32,4096]{2,1,0:T(8,128)(2,1)}, bf16[8,32,4096]{2,1,0:T(8,128)(2,1)}, u32[]{:S(2)}, u32[]{:S(2)}) %collective-permute-start.31) | collective-permute-done | bytes 2097184 | tf_op jit(solution)/shard_map/ppermute | solution.py:97
  408.0 8.1 %collective-permute-done.32 = bf16[4,32,4096]{2,1,0:T(8,128)(2,1)S(1)} collective-permute-done((bf16[4,32,4096]{2,1,0:T(8,128)(2,1)S(1)}, bf16[4,32,4096]{2,1,0:T(8,128)(2,1)S(1)}, u32[]{:S(2)}, u32[]{:S(2)}) %collective-permute-start.32) | collective-permute-done | bytes 1048608 | tf_op jit(solution)/shard_map/ppermute | solution.py:97
  420.6 3.2 collective-permute-start.39
  423.8 10.9 %collective-permute-done.28 = bf16[2,32,4096]{2,1,0:T(8,128)(2,1)S(1)} collective-permute-done((bf16[2,32,4096]{2,1,0:T(8,128)(2,1)S(1)}, bf16[2,32,4096]{2,1,0:T(8,128)(2,1)S(1)}, u32[]{:S(2)}, u32[]{:S(2)}) %collective-permute-start.28) | collective-permute-done | bytes 524320 | tf_op jit(solution)/shard_map/ppermute | solution.py:97
  435.8 4.7 %collective-permute-start.29 = (bf16[1,32,4096]{2,1,0:T(8,128)(2,1)S(1)}, bf16[1,32,4096]{2,1,0:T(8,128)(2,1)S(1)}, u32[]{:S(2)}, u32[]{:S(2)}) collective-permute-start(bf16[1,32,4096]{2,1,0:T(8,128)(2,1)S(1)} %add_convert_fusion.11), channel_id=1, source_target_pairs={{0,4},{1,5},{2,6},{3,7},{4,0},{5,1},{6,2},{7,3},{8,12},{9,13},{10,... | collective-permute-start | bytes 786440 | tf_op jit(solution)/shard_map/ppermute | solution.py:97
  440.6 6.6 %collective-permute-done.33 = bf16[2,32,4096]{2,1,0:T(8,128)(2,1)S(1)} collective-permute-done((bf16[2,32,4096]{2,1,0:T(8,128)(2,1)S(1)}, bf16[2,32,4096]{2,1,0:T(8,128)(2,1)S(1)}, u32[]{:S(2)}, u32[]{:S(2)}) %collective-permute-start.33) | collective-permute-done | bytes 524320 | tf_op jit(solution)/shard_map/ppermute | solution.py:97
  448.3 3.6 collective-permute-start.34
  451.9 9.1 %collective-permute-done.29 = bf16[1,32,4096]{2,1,0:T(8,128)(2,1)S(1)} collective-permute-done((bf16[1,32,4096]{2,1,0:T(8,128)(2,1)S(1)}, bf16[1,32,4096]{2,1,0:T(8,128)(2,1)S(1)}, u32[]{:S(2)}, u32[]{:S(2)}) %collective-permute-start.29) | collective-permute-done | bytes 262176 | tf_op jit(solution)/shard_map/ppermute | solution.py:97
  (199 shorter events, 109.0 us)
Async XLA Ops:
  4.1 25.1 %collective-permute-start.5 = (bf16[1,32,4096]{2,1,0:T(8,128)(2,1)S(1)}, bf16[1,32,4096]{2,1,0:T(8,128)(2,1)S(1)}, u32[]{:S(2)}, u32[]{:S(2)}) collective-permute-start(bf16[1,32,4096]{2,1,0:T(8,128)(2,1)S(1)} %maximum_bitcast_fusion), channel_id=1, source_target_pairs={{0,4},{1,5},{2,6},{3,7},{4,0},{5,1},{6,2},{7,3},{8,12},{9,13},{10,... | collective-permute-start | bytes 786440 | tf_op jit(solution)/shard_map/ppermute | solution.py:80
  9.4 25.4 %collective-permute-start.10 = (bf16[1,32,4096]{2,1,0:T(8,128)(2,1)S(1)}, bf16[1,32,4096]{2,1,0:T(8,128)(2,1)S(1)}, u32[]{:S(2)}, u32[]{:S(2)}) collective-permute-start(bf16[1,32,4096]{2,1,0:T(8,128)(2,1)S(1)} %broadcast_in_dim_reshape.6), channel_id=1, source_target_pairs={{0,4},{1,5},{2,6},{3,7},{4,0},{5,1},{6,2},{7,3},{8,12},{9,13},{10,... | collective-permute-start | bytes 786440 | tf_op jit(solution)/shard_map/ppermute | solution.py:80
  12.4 28.0 %collective-permute-start.15 = (bf16[1,128,1024]{2,1,0:T(8,128)(2,1)S(1)}, bf16[1,128,1024]{2,1,0:T(8,128)(2,1)S(1)}, u32[]{:S(2)}, u32[]{:S(2)}) collective-permute-start(bf16[1,128,1024]{2,1,0:T(8,128)(2,1)S(1)} %broadcast_in_dim_reshape.7), channel_id=1, source_target_pairs={{0,4},{1,5},{2,6},{3,7},{4,0},{5,1},{6,2},{7,3},{8,12},{9,13},{10,... | collective-permute-start | bytes 786440 | tf_op jit(solution)/shard_map/ppermute | solution.py:80
  29.3 21.2 %collective-permute-start.6 = (bf16[2,32,4096]{2,1,0:T(8,128)(2,1)S(1)}, bf16[2,32,4096]{2,1,0:T(8,128)(2,1)S(1)}, u32[]{:S(2)}, u32[]{:S(2)}) collective-permute-start(bf16[2,32,4096]{2,1,0:T(8,128)(2,1)S(1)} %pad_maximum_fusion.6), channel_id=1, source_target_pairs={{0,2},{1,3},{2,0},{3,1},{4,6},{5,7},{6,4},{7,5},{8,10},{9,11},{10,... | collective-permute-start | bytes 1572872 | tf_op jit(solution)/shard_map/ppermute | solution.py:80
  34.9 26.8 %collective-permute-start.11 = (bf16[2,32,4096]{2,1,0:T(8,128)(2,1)S(1)}, bf16[2,32,4096]{2,1,0:T(8,128)(2,1)S(1)}, u32[]{:S(2)}, u32[]{:S(2)}) collective-permute-start(bf16[2,32,4096]{2,1,0:T(8,128)(2,1)S(1)} %pad_maximum_fusion.7), channel_id=1, source_target_pairs={{0,2},{1,3},{2,0},{3,1},{4,6},{5,7},{6,4},{7,5},{8,10},{9,11},{10,... | collective-permute-start | bytes 1572872 | tf_op jit(solution)/shard_map/ppermute | solution.py:80
  40.4 32.4 %collective-permute-start.16 = (bf16[2,128,1024]{2,1,0:T(8,128)(2,1)S(1)}, bf16[2,128,1024]{2,1,0:T(8,128)(2,1)S(1)}, u32[]{:S(2)}, u32[]{:S(2)}) collective-permute-start(bf16[2,128,1024]{2,1,0:T(8,128)(2,1)S(1)} %pad_maximum_fusion.8), channel_id=1, source_target_pairs={{0,2},{1,3},{2,0},{3,1},{4,6},{5,7},{6,4},{7,5},{8,10},{9,11},{10,... | collective-permute-start | bytes 1572872 | tf_op jit(solution)/shard_map/ppermute | solution.py:80
  50.6 24.8 %collective-permute-start.7 = (bf16[4,32,4096]{2,1,0:T(8,128)(2,1)S(1)}, bf16[4,32,4096]{2,1,0:T(8,128)(2,1)S(1)}, u32[]{:S(2)}, u32[]{:S(2)}) collective-permute-start(bf16[4,32,4096]{2,1,0:T(8,128)(2,1)S(1)} %pad_maximum_fusion.3), channel_id=1, source_target_pairs={{0,1},{1,0},{2,3},{3,2},{4,5},{5,4},{6,7},{7,6},{8,24},{9,25},{10,... | collective-permute-start | bytes 3145736 | tf_op jit(solution)/shard_map/ppermute | solution.py:80
  61.8 15.4 %collective-permute-start.12 = (bf16[4,32,4096]{2,1,0:T(8,128)(2,1)S(1)}, bf16[4,32,4096]{2,1,0:T(8,128)(2,1)S(1)}, u32[]{:S(2)}, u32[]{:S(2)}) collective-permute-start(bf16[4,32,4096]{2,1,0:T(8,128)(2,1)S(1)} %pad_maximum_fusion.4), channel_id=1, source_target_pairs={{0,1},{1,0},{2,3},{3,2},{4,5},{5,4},{6,7},{7,6},{8,24},{9,25},{10,... | collective-permute-start | bytes 3145736 | tf_op jit(solution)/shard_map/ppermute | solution.py:80
  73.0 24.8 %collective-permute-start.17 = (bf16[4,128,1024]{2,1,0:T(8,128)(2,1)S(1)}, bf16[4,128,1024]{2,1,0:T(8,128)(2,1)S(1)}, u32[]{:S(2)}, u32[]{:S(2)}) collective-permute-start(bf16[4,128,1024]{2,1,0:T(8,128)(2,1)S(1)} %pad_maximum_fusion.5), channel_id=1, source_target_pairs={{0,1},{1,0},{2,3},{3,2},{4,5},{5,4},{6,7},{7,6},{8,24},{9,25},{10,... | collective-permute-start | bytes 3145736 | tf_op jit(solution)/shard_map/ppermute | solution.py:80
  75.6 33.7 %collective-permute-start.8 = (bf16[8,32,4096]{2,1,0:T(8,128)(2,1)S(1)}, bf16[8,32,4096]{2,1,0:T(8,128)(2,1)S(1)}, u32[]{:S(2)}, u32[]{:S(2)}) collective-permute-start(bf16[8,32,4096]{2,1,0:T(8,128)(2,1)S(1)} %pad_maximum_fusion), channel_id=1, source_target_pairs={{0,16},{1,17},{2,18},{3,19},{4,20},{5,21},{6,22},{7,23},{8,9},{9,8... | collective-permute-start | bytes 6291464 | tf_op jit(solution)/shard_map/ppermute | solution.py:80
  77.4 54.4 %collective-permute-start.13 = (bf16[8,32,4096]{2,1,0:T(8,128)(2,1)S(1)}, bf16[8,32,4096]{2,1,0:T(8,128)(2,1)S(1)}, u32[]{:S(2)}, u32[]{:S(2)}) collective-permute-start(bf16[8,32,4096]{2,1,0:T(8,128)(2,1)S(1)} %pad_maximum_fusion.1), channel_id=1, source_target_pairs={{0,16},{1,17},{2,18},{3,19},{4,20},{5,21},{6,22},{7,23},{8,9},{9,8... | collective-permute-start | bytes 6291464 | tf_op jit(solution)/shard_map/ppermute | solution.py:80
  98.0 56.3 %collective-permute-start.18 = (bf16[8,128,1024]{2,1,0:T(8,128)(2,1)S(1)}, bf16[8,128,1024]{2,1,0:T(8,128)(2,1)S(1)}, u32[]{:S(2)}, u32[]{:S(2)}) collective-permute-start(bf16[8,128,1024]{2,1,0:T(8,128)(2,1)S(1)} %pad_maximum_fusion.2), channel_id=1, source_target_pairs={{0,16},{1,17},{2,18},{3,19},{4,20},{5,21},{6,22},{7,23},{8,9},{9,8... | collective-permute-start | bytes 6291464 | tf_op jit(solution)/shard_map/ppermute | solution.py:80
  111.0 64.9 %collective-permute-start.9 = (bf16[16,32,4096]{2,1,0:T(8,128)(2,1)}, bf16[16,32,4096]{2,1,0:T(8,128)(2,1)}, u32[]{:S(2)}, u32[]{:S(2)}) collective-permute-start(bf16[16,32,4096]{2,1,0:T(8,128)(2,1)} %constant_dynamic-update-slice_fusion.own_ref), channel_id=1, source_target_pairs={{0,8},{1,9},{2,10},{3,11},{4,12},{5,13},{6,14},{7,15},{8,0},{9,1},... | collective-permute-start | bytes 12582920 | tf_op jit(solution)/shard_map/ppermute | solution.py:81
  133.4 65.7 %collective-permute-start.14 = (bf16[16,32,4096]{2,1,0:T(8,128)(2,1)}, bf16[16,32,4096]{2,1,0:T(8,128)(2,1)}, u32[]{:S(2)}, u32[]{:S(2)}) collective-permute-start(bf16[16,32,4096]{2,1,0:T(8,128)(2,1)} %constant_dynamic-update-slice_fusion.5.own_ref.iown_ref), channel_id=1, source_target_pairs={{0,8},{1,9},{2,10},{3,11},{4,12},{5,13},{6,14},{7,15},{8,0},{9,1},... | collective-permute-start | bytes 12582920 | tf_op jit(solution)/shard_map/ppermute | solution.py:81
  155.8 64.3 %collective-permute-start.19 = (bf16[16,128,1024]{2,1,0:T(8,128)(2,1)}, bf16[16,128,1024]{2,1,0:T(8,128)(2,1)}, u32[]{:S(2)}, u32[]{:S(2)}) collective-permute-start(bf16[16,128,1024]{2,1,0:T(8,128)(2,1)} %constant_dynamic-update-slice_fusion.10.own_ref.mown_ref), channel_id=1, source_target_pairs={{0,8},{1,9},{2,10},{3,11},{4,12},{5,13},{6,14},{7,15},{8,0},{9,1},... | collective-permute-start | bytes 12582920 | tf_op jit(solution)/shard_map/ppermute | solution.py:81
  219.9 82.4 %collective-permute-start.35 = (bf16[16,128,1024]{2,1,0:T(8,128)(2,1)}, bf16[16,128,1024]{2,1,0:T(8,128)(2,1)}, u32[]{:S(2)}, u32[]{:S(2)}) collective-permute-start(bf16[16,128,1024]{2,1,0:T(8,128)(2,1)} %get-tuple-element.49), channel_id=1, source_target_pairs={{0,8},{1,9},{2,10},{3,11},{4,12},{5,13},{6,14},{7,15},{8,0},{9,1},... | collective-permute-start | bytes 12582920 | tf_op jit(solution)/shard_map/ppermute | solution.py:92
  280.6 25.1 %collective-permute-start.25 = (bf16[16,32,4096]{2,1,0:T(8,128)(2,1)}, bf16[16,32,4096]{2,1,0:T(8,128)(2,1)}, u32[]{:S(2)}, u32[]{:S(2)}) collective-permute-start(bf16[16,32,4096]{2,1,0:T(8,128)(2,1)} %get-tuple-element.45), channel_id=1, source_target_pairs={{0,8},{1,9},{2,10},{3,11},{4,12},{5,13},{6,14},{7,15},{8,0},{9,1},... | collective-permute-start | bytes 12582920 | tf_op jit(solution)/shard_map/ppermute | solution.py:92
  281.0 29.1 %collective-permute-start.30 = (bf16[16,32,4096]{2,1,0:T(8,128)(2,1)}, bf16[16,32,4096]{2,1,0:T(8,128)(2,1)}, u32[]{:S(2)}, u32[]{:S(2)}) collective-permute-start(bf16[16,32,4096]{2,1,0:T(8,128)(2,1)} %get-tuple-element.47), channel_id=1, source_target_pairs={{0,8},{1,9},{2,10},{3,11},{4,12},{5,13},{6,14},{7,15},{8,0},{9,1},... | collective-permute-start | bytes 12582920 | tf_op jit(solution)/shard_map/ppermute | solution.py:92
  299.7 14.5 %collective-permute-start.21 = (bf16[8,1,384]{2,0,1:T(8,128)(2,1)S(1)}, bf16[8,1,384]{2,0,1:T(8,128)(2,1)S(1)}, u32[]{:S(2)}, u32[]{:S(2)}) collective-permute-start(bf16[8,1,384]{2,0,1:T(8,128)(2,1)S(1)} %fusion.7), channel_id=1, source_target_pairs={{0,16},{1,17},{2,18},{3,19},{4,20},{5,21},{6,22},{7,23},{8,9},{9,8... | collective-permute-start | bytes 18440 | tf_op jit(solution)/shard_map/ppermute | solution.py:97
  305.6 32.7 %collective-permute-start.36 = (bf16[8,128,1024]{2,1,0:T(8,128)(2,1)S(1)}, bf16[8,128,1024]{2,1,0:T(8,128)(2,1)}, u32[]{:S(2)}, u32[]{:S(2)}) collective-permute-start(bf16[8,128,1024]{2,1,0:T(8,128)(2,1)S(1)} %add_convert_fusion), channel_id=1, source_target_pairs={{0,16},{1,17},{2,18},{3,19},{4,20},{5,21},{6,22},{7,23},{8,9},{9,8... | collective-permute-start | bytes 6291464 | tf_op jit(solution)/shard_map/ppermute | solution.py:97
  308.3 57.3 %collective-permute-start.26 = (bf16[8,32,4096]{2,1,0:T(8,128)(2,1)S(1)}, bf16[8,32,4096]{2,1,0:T(8,128)(2,1)}, u32[]{:S(2)}, u32[]{:S(2)}) collective-permute-start(bf16[8,32,4096]{2,1,0:T(8,128)(2,1)S(1)} %add_convert_fusion.2), channel_id=1, source_target_pairs={{0,16},{1,17},{2,18},{3,19},{4,20},{5,21},{6,22},{7,23},{8,9},{9,8... | collective-permute-start | bytes 6291464 | tf_op jit(solution)/shard_map/ppermute | solution.py:97
  313.9 85.4 %collective-permute-start.31 = (bf16[8,32,4096]{2,1,0:T(8,128)(2,1)}, bf16[8,32,4096]{2,1,0:T(8,128)(2,1)}, u32[]{:S(2)}, u32[]{:S(2)}) collective-permute-start(bf16[8,32,4096]{2,1,0:T(8,128)(2,1)} %add_convert_fusion.1), channel_id=1, source_target_pairs={{0,16},{1,17},{2,18},{3,19},{4,20},{5,21},{6,22},{7,23},{8,9},{9,8... | collective-permute-start | bytes 6291464 | tf_op jit(solution)/shard_map/ppermute | solution.py:97
  321.6 15.5 %collective-permute-start.24 = (bf16[1,1,384]{2,0,1:T(2,128)(2,1)S(1)}, bf16[1,1,384]{2,0,1:T(2,128)(2,1)S(1)}, u32[]{:S(2)}, u32[]{:S(2)}) collective-permute-start(bf16[1,1,384]{2,0,1:T(2,128)(2,1)S(1)} %fusion.16), channel_id=1, source_target_pairs={{0,4},{1,5},{2,6},{3,7},{4,0},{5,1},{6,2},{7,3},{8,12},{9,13},{10,... | collective-permute-start | bytes 2312 | tf_op jit(solution)/shard_map/ppermute | solution.py:97
  340.5 62.3 %collective-permute-start.37 = (bf16[4,128,1024]{2,1,0:T(8,128)(2,1)S(1)}, bf16[4,128,1024]{2,1,0:T(8,128)(2,1)S(1)}, u32[]{:S(2)}, u32[]{:S(2)}) collective-permute-start(bf16[4,128,1024]{2,1,0:T(8,128)(2,1)S(1)} %add_convert_fusion.3), channel_id=1, source_target_pairs={{0,1},{1,0},{2,3},{3,2},{4,5},{5,4},{6,7},{7,6},{8,24},{9,25},{10,... | collective-permute-start | bytes 3145736 | tf_op jit(solution)/shard_map/ppermute | solution.py:97
  367.6 37.8 %collective-permute-start.27 = (bf16[4,32,4096]{2,1,0:T(8,128)(2,1)S(1)}, bf16[4,32,4096]{2,1,0:T(8,128)(2,1)S(1)}, u32[]{:S(2)}, u32[]{:S(2)}) collective-permute-start(bf16[4,32,4096]{2,1,0:T(8,128)(2,1)S(1)} %add_convert_fusion.5), channel_id=1, source_target_pairs={{0,1},{1,0},{2,3},{3,2},{4,5},{5,4},{6,7},{7,6},{8,24},{9,25},{10,... | collective-permute-start | bytes 3145736 | tf_op jit(solution)/shard_map/ppermute | solution.py:97
  401.3 14.9 %collective-permute-start.32 = (bf16[4,32,4096]{2,1,0:T(8,128)(2,1)S(1)}, bf16[4,32,4096]{2,1,0:T(8,128)(2,1)S(1)}, u32[]{:S(2)}, u32[]{:S(2)}) collective-permute-start(bf16[4,32,4096]{2,1,0:T(8,128)(2,1)S(1)} %add_convert_fusion.4), channel_id=1, source_target_pairs={{0,1},{1,0},{2,3},{3,2},{4,5},{5,4},{6,7},{7,6},{8,24},{9,25},{10,... | collective-permute-start | bytes 3145736 | tf_op jit(solution)/shard_map/ppermute | solution.py:97
  404.4 14.9 %collective-permute-start.38 = (bf16[2,128,1024]{2,1,0:T(8,128)(2,1)S(1)}, bf16[2,128,1024]{2,1,0:T(8,128)(2,1)S(1)}, u32[]{:S(2)}, u32[]{:S(2)}) collective-permute-start(bf16[2,128,1024]{2,1,0:T(8,128)(2,1)S(1)} %add_convert_fusion.6), channel_id=1, source_target_pairs={{0,2},{1,3},{2,0},{3,1},{4,6},{5,7},{6,4},{7,5},{8,10},{9,11},{10,... | collective-permute-start | bytes 1572872 | tf_op jit(solution)/shard_map/ppermute | solution.py:97
  406.8 27.8 %collective-permute-start.28 = (bf16[2,32,4096]{2,1,0:T(8,128)(2,1)S(1)}, bf16[2,32,4096]{2,1,0:T(8,128)(2,1)S(1)}, u32[]{:S(2)}, u32[]{:S(2)}) collective-permute-start(bf16[2,32,4096]{2,1,0:T(8,128)(2,1)S(1)} %add_convert_fusion.8), channel_id=1, source_target_pairs={{0,2},{1,3},{2,0},{3,1},{4,6},{5,7},{6,4},{7,5},{8,10},{9,11},{10,... | collective-permute-start | bytes 1572872 | tf_op jit(solution)/shard_map/ppermute | solution.py:97
  417.6 29.5 %collective-permute-start.33 = (bf16[2,32,4096]{2,1,0:T(8,128)(2,1)S(1)}, bf16[2,32,4096]{2,1,0:T(8,128)(2,1)S(1)}, u32[]{:S(2)}, u32[]{:S(2)}) collective-permute-start(bf16[2,32,4096]{2,1,0:T(8,128)(2,1)S(1)} %add_convert_fusion.7), channel_id=1, source_target_pairs={{0,2},{1,3},{2,0},{3,1},{4,6},{5,7},{6,4},{7,5},{8,10},{9,11},{10,... | collective-permute-start | bytes 1572872 | tf_op jit(solution)/shard_map/ppermute | solution.py:97
  420.6 41.7 %collective-permute-start.39 = (bf16[1,128,1024]{2,1,0:T(8,128)(2,1)S(1)}, bf16[1,128,1024]{2,1,0:T(8,128)(2,1)S(1)}, u32[]{:S(2)}, u32[]{:S(2)}) collective-permute-start(bf16[1,128,1024]{2,1,0:T(8,128)(2,1)S(1)} %add_convert_fusion.9), channel_id=1, source_target_pairs={{0,4},{1,5},{2,6},{3,7},{4,0},{5,1},{6,2},{7,3},{8,12},{9,13},{10,... | collective-permute-start | bytes 786440 | tf_op jit(solution)/shard_map/ppermute | solution.py:97
  435.8 25.2 %collective-permute-start.29 = (bf16[1,32,4096]{2,1,0:T(8,128)(2,1)S(1)}, bf16[1,32,4096]{2,1,0:T(8,128)(2,1)S(1)}, u32[]{:S(2)}, u32[]{:S(2)}) collective-permute-start(bf16[1,32,4096]{2,1,0:T(8,128)(2,1)S(1)} %add_convert_fusion.11), channel_id=1, source_target_pairs={{0,4},{1,5},{2,6},{3,7},{4,0},{5,1},{6,2},{7,3},{8,12},{9,13},{10,... | collective-permute-start | bytes 786440 | tf_op jit(solution)/shard_map/ppermute | solution.py:97
  448.3 16.6 %collective-permute-start.34 = (bf16[1,32,4096]{2,1,0:T(8,128)(2,1)S(1)}, bf16[1,32,4096]{2,1,0:T(8,128)(2,1)S(1)}, u32[]{:S(2)}, u32[]{:S(2)}) collective-permute-start(bf16[1,32,4096]{2,1,0:T(8,128)(2,1)S(1)} %add_convert_fusion.10), channel_id=1, source_target_pairs={{0,4},{1,5},{2,6},{3,7},{4,0},{5,1},{6,2},{7,3},{8,12},{9,13},{10,... | collective-permute-start | bytes 786440 | tf_op jit(solution)/shard_map/ppermute | solution.py:97
  (31 other events, 541.4 us)

commit v3 on v2

v3 whole, which is shorter than its diff:
```python
import jax
import jax.numpy as jnp
from jax import lax
from jax.experimental import pallas as pl
from jax.experimental.pallas import tpu as pltpu
from jax.sharding import PartitionSpec as P

D = 1024
FF = 4096
HEADS = 16
HEAD_DIM = 64
SEQ = 256
AXES = ("dp", "fsdp")
BLOCKS = 32
GROUP = 4
WIDE = GROUP * HEAD_DIM
TILE = 512
CHUNK = 32
BF = jnp.bfloat16
F32 = jnp.float32

eps = 1e-06
ANY = pl.BlockSpec(memory_space=pl.ANY)
VMEM = pl.BlockSpec(memory_space=pltpu.VMEM)
SMEM = pl.BlockSpec(memory_space=pltpu.SMEM)


class Plan:
    def __init__(self, mesh):
        outer, inner = mesh.shape["dp"], mesh.shape["fsdp"]
        ys = outer // 2
        xs = min(ys, inner)
        zs = inner // xs
        self.devices = outer * inner
        self.half = self.devices // 2

        def bits(size, unit):
            found = []
            while size > 1:
                size //= 2
                found.append(size * unit)
            return found

        xbits = bits(xs, 1)
        zbits = bits(zs, xs)
        self.core = inner
        ybits = bits(ys, 2 * inner)
        self.orders = (zbits + xbits + ybits, zbits + ybits + xbits)
        self.legs = [list(range(1)), list(range(1, len(zbits)))]
        for _ in range(2):
            start = self.legs[-1][-1] + 1
            self.legs.append(list(range(start, start + len(xbits))))

    def pairs(self, stage):
        return [
            (i, i ^ self.orders[1 if i & self.core else 0][stage]) for i in range(self.devices)
        ]

    def core_pairs(self):
        return [(i, i ^ self.core) for i in range(self.devices)]

    def masks(self, which):
        found = [0]
        for bit in self.orders[which]:
            found = found + [mask ^ bit for mask in found]
        return found

    def positions(self, me):
        tables = jnp.array(
            [
                self.masks(0) + [mask ^ self.core for mask in self.masks(1)],
                self.masks(1) + [mask ^ self.core for mask in self.masks(0)],
            ],
            jnp.int32,
        )
        mine = jnp.where((me & self.core) > 0, tables[1], tables[0])
        return mine ^ me


class Line:
    def __init__(self):
        self.last = []

    def tie(self, *arrays):
        if not self.last:
            return arrays
        tied = lax.optimization_barrier((arrays, tuple(self.last)))
        return tied[0]

    def run(self, step, *arrays):
        result = step(*self.tie(*arrays))
        self.last = [result[0] if isinstance(result, (list, tuple)) else result]
        return result

    def send(self, array, pairs):
        return lax.ppermute(self.tie(array)[0], AXES, pairs)

    def wait(self, *arrays):
        self.last.extend(arrays)


class Gather:
    def __init__(self, plan, line, block):
        self.plan, self.line = plan, line
        self.held = block[None]
        self.coming = None

    def take(self):
        self.line.wait(self.coming)
        self.held = self.line.run(
            lambda held, coming: jnp.concatenate([held, coming], 0), self.held, self.coming
        )

    def start(self, leg):
        for stage in self.plan.legs[leg]:
            if stage != self.plan.legs[leg][0]:
                self.take()
            self.coming = self.line.send(self.held, self.plan.pairs(stage))

    def swap_first(self):
        self.first = self.line.send(self.held, self.plan.core_pairs())

    def arrive(self):
        self.line.wait(self.coming)

    def swap_second(self):
        self.second = self.line.send(self.coming, self.plan.core_pairs())

    def parts(self):
        self.line.wait(self.first, self.second)
        return [self.held, self.coming, self.first, self.second]


def total(parts):
    result = parts[0].astype(F32)
    for part in parts[1:]:
        result = result + part.astype(F32)
    return result


class Scatter:
    def __init__(self, plan, line, parts):
        self.plan, self.line = plan, line
        keep_low, keep_high, send_low, send_high = parts
        self.high = [keep_high, line.send(send_high, plan.core_pairs())]
        self.low = [keep_low, line.send(send_low, plan.core_pairs())]
        self.count = keep_low.shape[0]

    def start(self, leg):
        for stage in reversed(self.plan.legs[leg]):
            if self.high is not None:
                parts, self.high, low = self.high, None, 0
            else:
                self.count //= 2
                parts, low = self.low, self.count
            self.line.wait(parts[-1])

            def add(*parts, low=low, high=low + self.count):
                return total([part[low:high] for part in parts]).astype(BF)

            outgoing = self.line.run(add, *parts)
            self.low.append(self.line.send(outgoing, self.plan.pairs(stage)))

    def result(self, *shape):
        self.line.wait(self.low[-1])
        return self.line.run(lambda *parts: total([part[0] for part in parts]), *self.low)


def one_hot(order):
    return (order[:, None] == jnp.arange(order.shape[0])[None, :]).astype(BF)


def to_blocks(order, parts):
    if order.shape[0] == BLOCKS:
        return parts
    width = parts[0].shape[-1]
    joined = jnp.concatenate(parts, 0).reshape(order.shape[0], -1)
    spread = lax.dot_general(
        one_hot(order), joined, (((0,), (0,)), ((), ())), preferred_element_type=BF
    ).reshape(4, BLOCKS // 4, -1, width)
    return [spread[i] for i in range(4)]


def from_blocks(order, parts):
    count = order.shape[0]
    if count == BLOCKS:
        return parts
    width = parts[0].shape[-1]
    joined = jnp.concatenate(parts, 0).reshape(count, -1)
    moved = jnp.dot(one_hot(order), joined, preferred_element_type=BF)
    moved = moved.reshape(4, count // 4, -1, width)
    return [moved[i] for i in range(4)]


def params(limit):
    return pltpu.CompilerParams(vmem_limit_bytes=limit << 20)


def rows_of(ref, number, rows):
    return ref.at[pl.ds(pl.multiple_of(number * rows, rows), rows), :]


def fetches(order_ref, part_refs, held_ref, sems, width=None):
    each, rows, _ = part_refs[0].shape
    copies = []
    for place in range(BLOCKS):
        source = part_refs[place // each].at[place % each]
        if width is not None:
            source = source.at[:, pl.ds(0, width)]
        number = order_ref[place]
        copies.append(
            pltpu.make_async_copy(source, rows_of(held_ref, number, rows), sems.at[number])
        )
    return copies


def stores(order_ref, held_ref, part_refs, sems):
    each, rows, _ = part_refs[0].shape
    copies = []
    for place in reversed(range(BLOCKS)):
        target = part_refs[place // each].at[place % each]
        copies.append(
            pltpu.make_async_copy(
                rows_of(held_ref, order_ref[place], rows), target, sems.at[place]
            )
        )
    return copies


def norm_parts(values):
    centre = values - jnp.mean(values, axis=-1, keepdims=True)
    inverse = lax.rsqrt(jnp.mean(centre * centre, axis=-1, keepdims=True) + eps)
    return centre * inverse, inverse


def norm_back(grad_norm, normed, inverse):
    return inverse * (
        grad_norm
        - jnp.mean(grad_norm, axis=-1, keepdims=True)
        - normed * jnp.mean(grad_norm * normed, axis=-1, keepdims=True)
    )


def span(index, size):
    return pl.ds(pl.multiple_of(index * size, size), size)


def dot(a, b):
    return jnp.dot(a, b, preferred_element_type=F32)


def dot_nt(a, b):
    return lax.dot_general(a, b, (((1,), (1,)), ((), ())), preferred_element_type=F32)


def dot_tn(a, b):
    return lax.dot_general(a, b, (((0,), (0,)), ((), ())), preferred_element_type=F32)


def stacked(values):
    head = lax.broadcasted_iota(jnp.int32, values.shape, 1) // HEAD_DIM
    zero = jnp.zeros_like(values)
    return jnp.concatenate([jnp.where(head == h, values, zero) for h in range(GROUP)], 0)


def unstacked(values):
    rows = values.shape[0] // GROUP
    head = lax.broadcasted_iota(jnp.int32, (rows, values.shape[1]), 1) // HEAD_DIM
    result = values[:rows]
    for h in range(1, GROUP):
        result = jnp.where(head == h, values[h * rows : (h + 1) * rows], result)
    return result


def attend_kernel(
    order_ref, vec_ref, x_ref, idr_ref, idc_ref, w0, w1, w2, w3,
    entry_ref, project_ref, probs_ref, mixed_ref, middle_ref, second_ref,
    held, project, probs, sems, out_sems,
):
    copies = fetches(order_ref, (w0, w1, w2, w3), held, sems)
    for copy in copies:
        copy.start()
    count = x_ref.shape[0]

    @pl.loop(0, count // CHUNK)
    def _(i):
        normed, _ = norm_parts(x_ref[span(i, CHUNK), :].astype(F32))
        entry_ref[span(i, CHUNK), :] = (normed * vec_ref[0:1, :] + vec_ref[2:3, :]).astype(BF)

    for copy in copies:
        copy.wait()

    @pl.loop(0, 3 * D // TILE)
    def _(i):
        third = i // (D // TILE)
        column = span(lax.rem(i, D // TILE), TILE)
        bias_row = jnp.where(third == 0, 3, 4)
        bias = jnp.where(third == 1, 0.0, vec_ref[pl.ds(bias_row, 1), column])
        project[:, span(i, TILE)] = (dot(entry_ref[...], held[:, span(i, TILE)]) + bias).astype(BF)

    project_out = pltpu.make_async_copy(project, project_ref, out_sems.at[0])
    project_out.start()
    groups = D // WIDE

    @pl.loop(0, (count // SEQ) * groups)
    def _(i):
        row, group = i // groups, lax.rem(i, groups)
        rows = span(row, SEQ)
        queries = project[rows, span(group, WIDE)] * BF(HEAD_DIM**-0.5)
        keys = project[rows, span(groups + group, WIDE)]
        values = project[rows, span(2 * groups + group, WIDE)]
        scores = dot_nt(stacked(queries), keys)
        same = idc_ref[rows, :] == idr_ref[pl.ds(row, 1), :]
        scores = jnp.where(same[None], scores.reshape(GROUP, SEQ, SEQ), -1e9)
        expo = jnp.exp(scores - jnp.max(scores, axis=-1, keepdims=True))
        low = (expo / jnp.sum(expo, axis=-1, keepdims=True)).astype(BF)
        low = low.reshape(GROUP * SEQ, SEQ)
        probs[i] = low
        pltpu.make_async_copy(probs.at[i], probs_ref.at[i], out_sems.at[1 + i]).start()
        mixed_ref[rows, span(group, WIDE)] = unstacked(dot(low, values)).astype(BF)

    @pl.loop(0, D // TILE)
    def _(i):
        columns = span(i, TILE)
        branch = dot(mixed_ref[...], held[:, span(3 * D // TILE + i, TILE)])
        middle_ref[:, columns] = x_ref[:, columns].astype(F32) + (branch + vec_ref[5:6, columns])

    @pl.loop(0, count // CHUNK)
    def _(i):
        normed, _ = norm_parts(middle_ref[span(i, CHUNK), :])
        second_ref[span(i, CHUNK), :] = (normed * vec_ref[1:2, :] + vec_ref[6:7, :]).astype(BF)

    project_out.wait()
    for i in range((count // SEQ) * groups):
        pltpu.make_async_copy(probs.at[i], probs_ref.at[i], out_sems.at[1 + i]).wait()


def attend(order, vec, x, ids, *first):
    count = x.shape[0]
    steps = (count // SEQ) * (D // WIDE)
    shape = jax.ShapeDtypeStruct
    return pl.pallas_call(
        attend_kernel,
        out_shape=[
            shape((count, D), BF),
            shape((count, 3 * D), BF),
            shape((steps, GROUP * SEQ, SEQ), BF),
            shape((count, D), BF),
            shape((count, D), F32),
            shape((count, D), BF),
        ],
        in_specs=[SMEM] + [VMEM] * 4 + [ANY] * 4,
        out_specs=[VMEM, ANY, ANY, VMEM, VMEM, VMEM],
        scratch_shapes=[
            pltpu.VMEM((D, 4 * D), BF),
            pltpu.VMEM((count, 3 * D), BF),
            pltpu.VMEM((steps, GROUP * SEQ, SEQ), BF),
            pltpu.SemaphoreType.DMA((BLOCKS,)),
            pltpu.SemaphoreType.DMA((1 + steps,)),
        ],
        compiler_params=params(48),
        name="attend",
    )(order, vec, x, ids, ids.reshape(count, 1), *first)


def rise_kernel(
    order_ref, spot_ref, bias_ref, second_ref, top_ref, w0, w1, w2, w3,
    active_ref, slope_ref, g0, g1, g2, g3,
    held, grads, sems, out_sems,
):
    step = pl.program_id(0)
    each, rows, _ = g0.shape

    @pl.when(step == 0)
    def _():
        copies = fetches(order_ref, (w0, w1, w2, w3), held, sems)
        for copy in copies:
            copy.start()
        for copy in copies:
            copy.wait()

    hidden = dot(second_ref[...], held[:, span(step, TILE)]) + bias_ref[...]
    cdf = 0.5 + 0.5 * lax.erf(hidden * (0.5**0.5))
    slope = cdf + hidden * jnp.exp(-0.5 * hidden * hidden) * 0.3989422804014327
    active = (hidden * cdf).astype(BF)
    active_ref[...] = active
    slope_ref[...] = slope.astype(BF)
    grads[span(step, TILE), :] = dot_tn(active, top_ref[...]).astype(BF)
    for block in range(TILE // rows):
        number = step * (TILE // rows) + block
        place = spot_ref[number]

        for part, target in enumerate((g0, g1, g2, g3)):

            @pl.when(place // each == part)
            def _(part=part, target=target):
                pltpu.make_async_copy(
                    rows_of(grads, number, rows),
                    target.at[place - part * each],
                    out_sems.at[number],
                ).start()

    @pl.when(step == FF // TILE - 1)
    def _():
        for number in range(BLOCKS):
            pltpu.make_async_copy(
                rows_of(grads, number, rows), g0.at[0], out_sems.at[number]
            ).wait()


def rise(order, spot, bias, second, top, *win):
    count = second.shape[0]
    shape = jax.ShapeDtypeStruct
    whole = pl.BlockSpec((count, D), lambda t: (0, 0))
    columns = pl.BlockSpec((count, TILE), lambda t: (0, t))
    grad = shape((BLOCKS // 4, FF // BLOCKS, D), BF)
    return pl.pallas_call(
        rise_kernel,
        grid=(FF // TILE,),
        out_shape=[shape((count, FF), BF)] * 2 + [grad] * 4,
        in_specs=[SMEM, SMEM, pl.BlockSpec((1, TILE), lambda t: (0, t)), whole, whole] + [ANY] * 4,
        out_specs=[columns] * 2 + [ANY] * 4,
        scratch_shapes=[
            pltpu.VMEM((D, FF), BF),
            pltpu.VMEM((FF, D), BF),
            pltpu.SemaphoreType.DMA((BLOCKS,)),
            pltpu.SemaphoreType.DMA((BLOCKS,)),
        ],
        compiler_params=params(48),
        name="rise",
    )(order, spot, bias, second, top, *win)


def fall_kernel(
    order_ref, top_ref, slope_ref, second_ref, w0, w1, w2, w3,
    ghidden_ref, bias_ref, g0, g1, g2, g3,
    held, turned, grads, sems, out_sems,
):
    step = pl.program_id(0)
    rows = w0.shape[1]

    @pl.when(step == 0)
    def _():
        for copy in fetches(order_ref, (w0, w1, w2, w3), held, sems):
            copy.start()
        turned[...] = second_ref[...].T

    for block in range(TILE // rows):
        number = step * (TILE // rows) + block
        pltpu.make_async_copy(w0.at[0], rows_of(held, number, rows), sems.at[number]).wait()
    grad_active = dot_nt(top_ref[...], held[span(step, TILE), :])
    grad_hidden = (grad_active * slope_ref[...].astype(F32)).astype(BF)
    ghidden_ref[...] = grad_hidden
    bias_ref[...] = jnp.sum(grad_hidden.astype(F32), axis=0, keepdims=True)
    grads[:, span(step, TILE)] = dot(turned[...], grad_hidden).astype(BF)

    @pl.when(step == FF // TILE - 1)
    def _():
        copies = stores(order_ref, grads, (g0, g1, g2, g3), out_sems)
        for copy in copies:
            copy.start()
        for copy in copies:
            copy.wait()


def fall(order, top, slope, second, *mlp):
    count = second.shape[0]
    shape = jax.ShapeDtypeStruct
    whole = pl.BlockSpec((count, D), lambda t: (0, 0))
    columns = pl.BlockSpec((count, TILE), lambda t: (0, t))
    grad = shape((BLOCKS // 4, D // BLOCKS, FF), BF)
    return pl.pallas_call(
        fall_kernel,
        grid=(FF // TILE,),
        out_shape=[shape((count, FF), BF), shape((1, FF), F32)] + [grad] * 4,
        in_specs=[SMEM, whole, columns, whole] + [ANY] * 4,
        out_specs=[columns, pl.BlockSpec((1, TILE), lambda t: (0, t))] + [ANY] * 4,
        scratch_shapes=[
            pltpu.VMEM((FF, D), BF),
            pltpu.VMEM((D, count), BF),
            pltpu.VMEM((D, FF), BF),
            pltpu.SemaphoreType.DMA((BLOCKS,)),
            pltpu.SemaphoreType.DMA((BLOCKS,)),
        ],
        compiler_params=params(48),
        name="fall",
    )(order, top, slope, second, *mlp)


def back_kernel(
    order_ref, vec_ref, ghidden_ref, middle_ref, top_ref, w0, w1, w2, w3,
    gmiddle_ref, sums_ref,
    held, gsecond, sems,
):
    copies = fetches(order_ref, (w0, w1, w2, w3), held, sems)
    for copy in copies:
        copy.start()
    count = middle_ref.shape[0]
    sums_ref[...] = jnp.zeros_like(sums_ref)
    for copy in copies:
        copy.wait()

    @pl.loop(0, D // WIDE)
    def _(i):
        gsecond[:, span(i, WIDE)] = dot_nt(ghidden_ref[...], held[span(i, WIDE), :])

    @pl.loop(0, count // CHUNK)
    def _(i):
        rows = span(i, CHUNK)
        normed, inverse = norm_parts(middle_ref[rows, :])
        grad = gsecond[rows, :]
        sums_ref[0:1, :] += jnp.sum(grad * normed, axis=0, keepdims=True)
        sums_ref[1:2, :] += jnp.sum(grad, axis=0, keepdims=True)
        top = top_ref[rows, :].astype(F32)
        sums_ref[3:4, :] += jnp.sum(top, axis=0, keepdims=True)
        gmiddle = top + norm_back(grad * vec_ref[1:2, :], normed, inverse)
        gmiddle_ref[rows, :] = gmiddle
        low = gmiddle.astype(BF)
        sums_ref[2:3, :] += jnp.sum(low.astype(F32), axis=0, keepdims=True)


def back(order, vec, ghidden, middle, top, *win):
    count = middle.shape[0]
    shape = jax.ShapeDtypeStruct
    return pl.pallas_call(
        back_kernel,
        out_shape=[shape((count, D), F32), shape((8, D), F32)],
        in_specs=[SMEM] + [VMEM] * 4 + [ANY] * 4,
        out_specs=[VMEM] * 2,
        scratch_shapes=[
            pltpu.VMEM((D, FF), BF),
            pltpu.VMEM((count, D), F32),
            pltpu.SemaphoreType.DMA((BLOCKS,)),
        ],
        compiler_params=params(48),
        name="back",
    )(order, vec, ghidden, middle, top, *win)


def unattend_kernel(
    order_ref, gmiddle_ref, mixed_ref, entry_ref, project_ref,
    probs_ref, w0, w1, w2, w3,
    gproject_ref, sums_ref, g0, g1, g2, g3,
    held, branch, gmixed, turned, grads, sems, out_sems,
):
    rows = w0.shape[1]
    copies = []
    for place in range(BLOCKS):
        source = (w0, w1, w2, w3)[place // w0.shape[0]].at[place % w0.shape[0]]
        copies.append(
            pltpu.make_async_copy(
                source.at[:, pl.ds(3 * D, D)],
                rows_of(held, order_ref[place], rows),
                sems.at[place],
            )
        )
    for copy in copies:
        copy.start()
    count = gmiddle_ref.shape[0]
    branch[...] = gmiddle_ref[...].astype(BF)
    turned[...] = mixed_ref[...].T
    for copy in copies:
        copy.wait()

    @pl.loop(0, D // TILE)
    def _(i):
        columns = span(i, TILE)
        grads[:, span(3 * D // TILE + i, TILE)] = dot(turned[...], branch[:, columns]).astype(BF)
        gmixed[:, columns] = dot_nt(branch[...], held[columns, :]).astype(BF)

    turned[...] = entry_ref[...].T
    groups = D // WIDE

    @pl.loop(0, (count // SEQ) * groups)
    def _(i):
        row, group = i // groups, lax.rem(i, groups)
        rows = span(row, SEQ)
        scale = HEAD_DIM**-0.5
        queries = stacked(project_ref[rows, span(group, WIDE)] * BF(scale))
        keys = project_ref[rows, span(groups + group, WIDE)]
        values = project_ref[rows, span(2 * groups + group, WIDE)]
        gmix = stacked(gmixed[rows, span(group, WIDE)])
        low = probs_ref[i]
        gprobs = dot_nt(gmix, values)
        gvalues = dot_tn(low, gmix)
        weight = low.astype(F32)
        inner = jnp.sum(weight * gprobs, axis=-1, keepdims=True)
        gscores = (weight * (gprobs - inner)).astype(BF)
        gqueries = unstacked(dot(gscores, keys)) * scale
        gkeys = dot_tn(gscores, queries)
        gproject_ref[rows, span(group, WIDE)] = gqueries.astype(BF)
        gproject_ref[rows, span(groups + group, WIDE)] = gkeys.astype(BF)
        gproject_ref[rows, span(2 * groups + group, WIDE)] = gvalues.astype(BF)

    @pl.loop(0, 3 * D // TILE)
    def _(i):
        gpart = gproject_ref[:, span(i, TILE)]
        grads[:, span(i, TILE)] = dot(turned[...], gpart).astype(BF)
        third = i // (D // TILE)
        column = span(lax.rem(i, D // TILE), TILE)
        sums_ref[pl.ds(third, 1), column] = jnp.sum(gpart.astype(F32), axis=0, keepdims=True)

    copies = stores(order_ref, grads, (g0, g1, g2, g3), out_sems)
    for copy in copies:
        copy.start()
    for copy in copies:
        copy.wait()


def unattend(order, gmiddle, mixed, entry, project, probs, *first):
    count = gmiddle.shape[0]
    shape = jax.ShapeDtypeStruct
    grad = shape((BLOCKS // 4, D // BLOCKS, 4 * D), BF)
    return pl.pallas_call(
        unattend_kernel,
        out_shape=[
            shape((count, 3 * D), BF), shape((8, D), F32), grad, grad, grad, grad,
        ],
        in_specs=[SMEM] + [VMEM] * 5 + [ANY] * 4,
        out_specs=[VMEM] * 2 + [ANY] * 4,
        scratch_shapes=[
            pltpu.VMEM((D, D), BF),
            pltpu.VMEM((count, D), BF),
            pltpu.VMEM((count, D), BF),
            pltpu.VMEM((D, count), BF),
            pltpu.VMEM((D, 4 * D), BF),
            pltpu.SemaphoreType.DMA((BLOCKS,)),
            pltpu.SemaphoreType.DMA((BLOCKS,)),
        ],
        compiler_params=params(56),
        name="unattend",
    )(order, gmiddle, mixed, entry, project, probs, *first)


def enter_kernel(
    order_ref, vec_ref, x_ref, gmiddle_ref, gproject_ref, w0, w1, w2, w3,
    ginputs_ref, sums_ref,
    held, gentry, sems,
):
    copies = fetches(order_ref, (w0, w1, w2, w3), held, sems, 3 * D)
    for copy in copies:
        copy.start()
    count = x_ref.shape[0]
    sums_ref[...] = jnp.zeros_like(sums_ref)
    for copy in copies:
        copy.wait()

    @pl.loop(0, D // TILE)
    def _(i):
        gentry[:, span(i, TILE)] = dot_nt(gproject_ref[...], held[span(i, TILE), :])

    @pl.loop(0, count // CHUNK)
    def _(i):
        rows = span(i, CHUNK)
        normed, inverse = norm_parts(x_ref[rows, :].astype(F32))
        grad = gentry[rows, :]
        sums_ref[0:1, :] += jnp.sum(grad * normed, axis=0, keepdims=True)
        sums_ref[1:2, :] += jnp.sum(grad, axis=0, keepdims=True)
        back = norm_back(grad * vec_ref[0:1, :], normed, inverse)
        ginputs_ref[rows, :] = gmiddle_ref[rows, :] + back


def enter(order, vec, x, gmiddle, gproject, *first):
    count = x.shape[0]
    shape = jax.ShapeDtypeStruct
    return pl.pallas_call(
        enter_kernel,
        out_shape=[shape((count, D), F32), shape((8, D), F32)],
        in_specs=[SMEM] + [VMEM] * 4 + [ANY] * 4,
        out_specs=[VMEM] * 2,
        scratch_shapes=[
            pltpu.VMEM((D, 3 * D), BF),
            pltpu.VMEM((count, D), F32),
            pltpu.SemaphoreType.DMA((BLOCKS,)),
        ],
        compiler_params=params(48),
        name="enter",
    )(order, vec, x, gmiddle, gproject, *first)


def finish_kernel(
    order_ref, vec_ref, middle_ref, active_ref, w0, w1, w2, w3, out_ref, held, sems
):
    copies = fetches(order_ref, (w0, w1, w2, w3), held, sems)
    for copy in copies:
        copy.start()
    for copy in copies:
        copy.wait()

    @pl.loop(0, D // WIDE)
    def _(i):
        columns = span(i, WIDE)
        result = dot(active_ref[...], held[:, columns]) + vec_ref[7:8, columns]
        out_ref[:, columns] = (middle_ref[:, columns] + result).astype(BF)


def finish(order, vec, middle, active, *mlp):
    count = middle.shape[0]
    return pl.pallas_call(
        finish_kernel,
        out_shape=jax.ShapeDtypeStruct((count, D), BF),
        in_specs=[SMEM] + [VMEM] * 3 + [ANY] * 4,
        out_specs=VMEM,
        scratch_shapes=[pltpu.VMEM((FF, D), BF), pltpu.SemaphoreType.DMA((BLOCKS,))],
        compiler_params=params(48),
        name="finish",
    )(order, vec, middle, active, *mlp)


def per_device(plan, inputs, image_ids, cotangent, gains, biases, w_qkv, w_out, w_in, w_mlp):
    me = lax.axis_index(AXES)
    order = plan.positions(me)
    gain_dev, bias_dev = gains.shape[1], biases.shape[1]
    rows = D // plan.devices
    blocks, length = image_ids.shape
    count = blocks * length
    x = inputs.reshape(count, D)
    numbers = order if plan.devices == BLOCKS else jnp.arange(BLOCKS, dtype=jnp.int32)
    spot = jnp.sum(
        jnp.where(numbers[:, None] == jnp.arange(BLOCKS)[None, :], jnp.arange(BLOCKS)[:, None], 0),
        axis=0,
    ).astype(jnp.int32)
    line = Line()

    first = Gather(
        plan, line, jnp.concatenate([w_qkv.reshape(rows, 3 * D), w_out.reshape(rows, D)], 1)
    )
    first.start(0)
    small = Gather(plan, line, jnp.concatenate([gains, biases], 1))
    small.start(0)
    win = Gather(plan, line, w_in.reshape(rows, FF))
    mlp = Gather(plan, line, w_mlp.reshape(FF // plan.devices, D))
    top = jnp.where(image_ids.reshape(count, 1) >= 0, cotangent.reshape(count, D), BF(0))
    first.take()
    first.start(1)
    win.start(0)
    small.take()
    small.start(1)
    first.take()
    first.start(2)
    win.take()
    win.start(1)
    mlp.start(0)
    small.take()
    small.start(2)
    first.take()
    first.start(3)
    first.swap_first()
    win.take()
    mlp.take()
    mlp.start(1)
    small.take()
    small.start(3)
    small.swap_first()
    small.arrive()
    small.swap_second()
    first.arrive()
    win.start(2)
    first.swap_second()
    mlp.take()
    placed = jnp.concatenate(small.parts(), 0)[:, 0]

    def unpack(placed):
        spread = lax.dot_general(
            one_hot(order), placed, (((0,), (0,)), ((), ())), preferred_element_type=F32
        )
        return jnp.concatenate(
            [spread[:, :gain_dev].reshape(-1), spread[:, gain_dev:].reshape(-1)]
        ).reshape(-1, D)

    vec = line.run(unpack, placed)
    bias_in = vec[8:12].reshape(1, FF)
    vec = vec[:8]
    first_parts = to_blocks(order, first.parts())
    win.take()
    win.start(3)
    win.swap_first()
    entry, project, probs, mixed, middle, second = line.run(
        attend, numbers, vec, x, image_ids, *first_parts
    )
    win.arrive()
    mlp.start(2)
    win.swap_second()
    win_parts = to_blocks(order, win.parts())
    mlp.take()
    mlp.start(3)
    mlp.swap_first()
    active, slope, *grads = line.run(rise, numbers, spot, bias_in, second, top, *win_parts)
    sum_mlp = Scatter(plan, line, from_blocks(order, grads))
    mlp.arrive()
    mlp.swap_second()
    sum_mlp.start(3)
    mlp_parts = to_blocks(order, mlp.parts())
    ghidden, grad_bias_in, *grads = line.run(fall, numbers, top, slope, second, *mlp_parts)
    sum_in = Scatter(plan, line, from_blocks(order, grads))
    gmiddle, sums = line.run(back, numbers, vec, ghidden, middle, top, *win_parts)
    sum_mlp.start(2)
    sum_in.start(3)
    gproject, sums_qkv, *grads = line.run(
        unattend, numbers, gmiddle, mixed, entry, project, probs, *first_parts
    )
    sum_first = Scatter(plan, line, from_blocks(order, grads))
    sum_mlp.start(1)
    sum_in.start(2)
    sum_first.start(3)
    grad_inputs, sums_one = line.run(enter, numbers, vec, x, gmiddle, gproject, *first_parts)
    flat_gains = jnp.concatenate([sums_one[0], sums[0]]).reshape(-1, gain_dev)
    flat_biases = jnp.concatenate(
        [sums_one[1], sums_qkv[0], sums_qkv[2], sums[2], sums[1], sums[3], grad_bias_in[0]]
    ).reshape(-1, bias_dev)
    flat_small = jnp.concatenate([flat_gains, flat_biases], 1).astype(BF)
    moved = jnp.dot(one_hot(order), flat_small, preferred_element_type=F32).astype(BF)
    moved = moved.reshape(4, plan.devices // 4, 1, -1)
    sum_small = Scatter(plan, line, [moved[i] for i in range(4)])
    sum_mlp.start(0)
    sum_in.start(1)
    sum_small.start(3)
    sum_small.start(2)
    sum_first.start(2)
    output = line.run(finish, numbers, vec, middle, active, *mlp_parts)
    sum_small.start(1)
    grad_mlp = sum_mlp.result()
    sum_in.start(0)
    sum_small.start(0)
    sum_first.start(1)
    grad_small = sum_small.result()
    grad_in = sum_in.result()
    sum_first.start(0)
    grad_first = sum_first.result()
    return (
        output.reshape(blocks, length, D),
        grad_inputs.reshape(blocks, length, D),
        grad_small[:, :gain_dev],
        grad_small[:, gain_dev:],
        grad_first[:, : 3 * D].reshape(1, -1),
        grad_first[:, 3 * D :].reshape(1, -1),
        grad_in.reshape(1, -1),
        grad_mlp.reshape(1, -1),
    )


def solution(mesh):
    plan = Plan(mesh)
    whole = P(AXES, None, None)
    flat = P(AXES, None)

    def body(*arrays):
        return per_device(plan, *arrays)

    return jax.shard_map(
        body,
        mesh=mesh,
        in_specs=(whole, flat, whole, flat, flat, flat, flat, flat, flat),
        out_specs=(whole, whole, flat, flat, flat, flat, flat, flat),
        check_vma=False,
    )
```

time: 473 us -> 388 us (0.82)
  waiting for transfers between devices: 210 us -> 147 us
  starting transfers between devices: 65.2 us -> 44.8 us
  local copies, waits for them, and re-layouts: 23.7 us -> 18.1 us
    ppermute x40 -> x48, waiting for transfers between devices: 210 us -> 147 us  [send(): return lax.ppermute(self.tie(array)[0], AXES, pairs)]
    ppermute x40 -> x48, starting transfers between devices: 65.2 us -> 44.8 us  [send(): return lax.ppermute(self.tie(array)[0], AXES, pairs)]
    pallas_call x1, Pallas kernels: 28.9 us -> 18.1 us  [fall(): pl.pallas_call(fall_kernel, grid=(FF // TILE,), out_shape=[shape((count,...]
    pallas_call x1 -> x2, Pallas kernels: 31.6 us -> 42.2 us  [the longest x1 26.2 us: unattend(): pl.pallas_call(unattend_kernel, out_shape=[shape((count, 3 * D), BF), sha...]
    unnamed x71 -> x89, local copies, waits for them, and re-layouts: 16.8 us -> 12.4 us
    unnamed x7 -> x6, other arithmetic: 11.5 us -> 9.35 us
  transfers between devices with their start and end apart: 40 -> 48, of which waited for: 25 -> 23; matrix products, arithmetic and copies ran while one was open for 11% -> 11% of each run, Pallas kernels for 28% -> 34%
where the time goes in v3:
time: 388 us; the launch traced here: 383 us
  waiting for transfers between devices  147 us (38%)
  Pallas kernels  130 us (34%)
  starting transfers between devices  44.8 us (12%)
  other arithmetic  41.4 us (11%)
  local copies, waits for them, and re-layouts  18.1 us (5%)
    ppermute x48, waiting for transfers between devices, send(): return lax.ppermute(self.tie(array)[0], AXES, pairs)  147 us
    ppermute x48, starting transfers between devices, send(): return lax.ppermute(self.tie(array)[0], AXES, pairs)  44.8 us
    convert_element_type x16, other arithmetic, add(): return total([part[low:high] for part in parts]).astype(BF)  28.3 us
    pallas_call x1, Pallas kernels, unattend(): pl.pallas_call(unattend_kernel, out_shape=[shape((count, 3 * D), BF), sha...  26.2 us
    pallas_call x1, Pallas kernels, attend(): pl.pallas_call(attend_kernel, out_shape=[shape((count, D), BF), shape((co...  22.2 us
    pallas_call x1, Pallas kernels, rise(): pl.pallas_call(rise_kernel, grid=(FF // TILE,), out_shape=[shape((count,...  21.2 us
    pallas_call x1, Pallas kernels, fall(): pl.pallas_call(fall_kernel, grid=(FF // TILE,), out_shape=[shape((count,...  18.1 us
    pallas_call x1, Pallas kernels, back(): pl.pallas_call(back_kernel, out_shape=[shape((count, D), F32), shape((8,...  16 us
  transfers between devices with their start and end apart: 48, of which 23 were waited for; matrix products, arithmetic and copies ran while one was open for 11% of the time, Pallas kernels for 34%

profile of v3, /device:TPU:8, one launch (start us, length us, event | category | flops | bytes accessed | tf_op | source)
XLA Modules:
  0.0 383.0 jit_solution(11613546371739008418)
XLA Ops:
  4.2 2.7 collective-permute-start.1
  6.9 11.1 %collective-permute-done.1 = bf16[1,32,4096]{2,1,0:T(8,128)(2,1)S(1)} collective-permute-done((bf16[1,32,4096]{2,1,0:T(8,128)(2,1)S(1)}, bf16[1,32,4096]{2,1,0:T(8,128)(2,1)S(1)}, u32[]{:S(2)}, u32[]{:S(2)}) %collective-permute-start.1) | collective-permute-done | bytes 262176 | tf_op jit(solution)/shard_map/ppermute | solution.py:96
  19.5 2.1 collective-permute-start
  23.3 10.4 %collective-permute-done = bf16[1,1,384]{2,0,1:T(2,128)(2,1)S(1)} collective-permute-done((bf16[1,1,384]{2,0,1:T(2,128)(2,1)S(1)}, bf16[1,1,384]{2,0,1:T(2,128)(2,1)S(1)}, u32[]{:S(2)}, u32[]{:S(2)}) %collective-permute-start) | collective-permute-done | bytes 800 | tf_op jit(solution)/shard_map/ppermute | solution.py:96
  36.5 7.9 %collective-permute-done.3 = bf16[1,32,4096]{2,1,0:T(8,128)(2,1)S(1)} collective-permute-done((bf16[1,32,4096]{2,1,0:T(8,128)(2,1)S(1)}, bf16[1,32,4096]{2,1,0:T(8,128)(2,1)S(1)}, u32[]{:S(2)}, u32[]{:S(2)}) %collective-permute-start.3) | collective-permute-done | bytes 262176 | tf_op jit(solution)/shard_map/ppermute | solution.py:96
  44.5 4.2 %collective-permute-done.8 = bf16[4,32,4096]{2,1,0:T(8,128)(2,1)S(1)} collective-permute-done((bf16[4,32,4096]{2,1,0:T(8,128)(2,1)S(1)}, bf16[4,32,4096]{2,1,0:T(8,128)(2,1)S(1)}, u32[]{:S(2)}, u32[]{:S(2)}) %collective-permute-start.8) | collective-permute-done | bytes 1048608 | tf_op jit(solution)/shard_map/ppermute | solution.py:96
  56.6 9.4 %collective-permute-done.7 = bf16[2,32,4096]{2,1,0:T(8,128)(2,1)} collective-permute-done((bf16[2,32,4096]{2,1,0:T(8,128)(2,1)S(1)}, bf16[2,32,4096]{2,1,0:T(8,128)(2,1)}, u32[]{:S(2)}, u32[]{:S(2)}) %collective-permute-start.7) | collective-permute-done | bytes 524320 | tf_op jit(solution)/shard_map/ppermute | solution.py:96
  70.4 4.7 %collective-permute-done.9 = bf16[8,1,384]{2,0,1:T(8,128)(2,1)S(1)} collective-permute-done((bf16[8,1,384]{2,0,1:T(8,128)(2,1)S(1)}, bf16[8,1,384]{2,0,1:T(8,128)(2,1)S(1)}, u32[]{:S(2)}, u32[]{:S(2)}) %collective-permute-start.9) | collective-permute-done | bytes 6176 | tf_op jit(solution)/shard_map/ppermute | solution.py:96
  77.9 12.0 %collective-permute-done.16 = bf16[4,32,4096]{2,1,0:T(8,128)(2,1)S(1)} collective-permute-done((bf16[4,32,4096]{2,1,0:T(8,128)(2,1)S(1)}, bf16[4,32,4096]{2,1,0:T(8,128)(2,1)S(1)}, u32[]{:S(2)}, u32[]{:S(2)}) %collective-permute-start.16) | collective-permute-done | bytes 1048608 | tf_op jit(solution)/shard_map/ppermute | solution.py:96
  96.1 10.7 %collective-permute-done.12 = bf16[2,128,1024]{2,1,0:T(8,128)(2,1)} collective-permute-done((bf16[2,128,1024]{2,1,0:T(8,128)(2,1)S(1)}, bf16[2,128,1024]{2,1,0:T(8,128)(2,1)}, u32[]{:S(2)}, u32[]{:S(2)}) %collective-permute-start.12) | collective-permute-done | bytes 524320 | tf_op jit(solution)/shard_map/ppermute | solution.py:96
  108.7 22.2 %attend.1 = (bf16[512,1024]{1,0:T(8,128)(2,1)S(1)}, bf16[512,3072]{1,0:T(8,128)(2,1)}, bf16[8,1024,256]{2,1,0:T(8,128)(2,1)}, bf16[512,1024]{1,0:T(8,128)(2,1)S(...) custom-call(s32[32]{0:T(128)S(1)} %fusion.9.order_ref, f32[8,1024]{1,0:T(8,128)S(1)} %slice.300.vec_ref, ...), custom_call_target="tpu_custom_call" | custom-call | tf_op jit(solution)/shard_map/attend/pallas_call | solution.py:342
  132.1 14.2 %collective-permute-done.20 = bf16[4,128,1024]{2,1,0:T(8,128)(2,1)S(1)} collective-permute-done((bf16[4,128,1024]{2,1,0:T(8,128)(2,1)S(1)}, bf16[4,128,1024]{2,1,0:T(8,128)(2,1)S(1)}, u32[]{:S(2)}, u32[]{:S(2)}) %collective-permute-start.20) | collective-permute-done | bytes 1048608 | tf_op jit(solution)/shard_map/ppermute | solution.py:96
  150.9 21.2 %rise.1 = (bf16[512,4096]{1,0:T(8,128)(2,1)}, bf16[512,4096]{1,0:T(8,128)(2,1)}, bf16[8,128,1024]{2,1,0:T(8,128)(2,1)S(1)}, bf16[8,128,1024]{2,1,0:T(8,128)(2,1)...) custom-call(s32[32]{0:T(128)S(1)} %fusion.9.order_ref, s32[32]{0:T(128)S(1)} %select_reduce_fusion.spot_ref, ...), custom_call_target="tpu_custom_call" | custom-call | tf_op jit(solution)/shard_map/rise/pallas_call | solution.py:417
  174.5 4.2 %collective-permute-done.24 = bf16[8,128,1024]{2,1,0:T(8,128)(2,1)S(1)} collective-permute-done((bf16[8,128,1024]{2,1,0:T(8,128)(2,1)}, bf16[8,128,1024]{2,1,0:T(8,128)(2,1)S(1)}, u32[]{:S(2)}, u32[]{:S(2)}) %collective-permute-start.24) | collective-permute-done | bytes 2097184 | tf_op jit(solution)/shard_map/ppermute | solution.py:96
  178.7 2.6 add_convert_fusion.2
  182.1 3.0 collective-permute-done.22.w2
  186.9 18.1 %fall.1 = (bf16[512,4096]{1,0:T(8,128)(2,1)}, f32[1,4096]{1,0:T(1,128)S(1)}, bf16[8,32,4096]{2,1,0:T(8,128)(2,1)S(1)}, bf16[8,32,4096]{2,1,0:T(8,128)(2,1)}, bf1...) custom-call(s32[32]{0:T(128)S(1)} %fusion.9.order_ref, bf16[512,1024]{1,0:T(8,128)(2,1)S(1)} %bitcast_select_fusion.top_ref, ...), custom_call_target="tpu_custom_call" | custom-call | tf_op jit(solution)/shard_map/fall/pallas_call | solution.py:472
  208.0 16.0 %back.1 = (f32[512,1024]{1,0:T(8,128)S(1)}, f32[8,1024]{1,0:T(8,128)S(1)}) custom-call(s32[32]{0:T(128)S(1)} %fusion.9.order_ref, f32[8,1024]{1,0:T(8,128)S(1)} %slice.300.vec_ref, bf16[512,4096]{1,0:T(8,128)(2,1)} %get-tuple-element.325.ghidden_ref, f32[512,1024]{1,0:T(8,128)S(1)} %copy-done.4, bf16[512,1024]{1,0:T(8,128)(2,1)S(1)} %bitcast_select_fusion.top_ref, ...), custom_call_target="tpu_custom_call" | custom-call | tf_op jit(solution)/shard_map/back/pallas_call | solution.py:525
  224.2 4.0 %add_convert_fusion.5 = bf16[4,128,1024]{2,1,0:T(8,128)(2,1)} fusion(bf16[8,128,1024]{2,1,0:T(8,128)(2,1)} %collective-permute-done.27, bf16[8,128,1024]{2,1,0:T(8,128)(2,1)} %collective-permute-done.26, bf16[8,128,1024]{2,1,0:T(8,128)(2,1)S(1)} %get-tuple-element.474), kind=kLoop, calls=%fused_computation.5 | loop fusion | flops 3145728 | bytes 4194304 | tf_op jit(solution)/shard_map/convert_element_type | solution.py:159
  228.1 3.7 add_convert_fusion.1
  233.3 26.2 %unattend.1 = (bf16[512,3072]{1,0:T(8,128)(2,1)}, f32[8,1024]{1,0:T(8,128)}, bf16[8,32,4096]{2,1,0:T(8,128)(2,1)}, bf16[8,32,4096]{2,1,0:T(8,128)(2,1)}, bf16[8,...) custom-call(s32[32]{0:T(128)} %copy-done.15, f32[512,1024]{1,0:T(8,128)} %copy-done.5, bf16[512,1024]{1,0:T(8,128)(2,1)} %copy-done.14, ...), custom_call_target="tpu_custom_call" | custom-call | tf_op jit(solution)/shard_map/unattend/pallas_call | solution.py:614
  264.1 5.2 %collective-permute-done.31 = bf16[8,32,4096]{2,1,0:T(8,128)(2,1)} collective-permute-done((bf16[8,32,4096]{2,1,0:T(8,128)(2,1)}, bf16[8,32,4096]{2,1,0:T(8,128)(2,1)}, u32[]{:S(2)}, u32[]{:S(2)}) %collective-permute-start.31) | collective-permute-done | bytes 2097184 | tf_op jit(solution)/shard_map/ppermute | solution.py:96
  269.2 3.1 add_convert_fusion.4
  273.2 3.9 %add_convert_fusion = bf16[8,32,4096]{2,1,0:T(8,128)(2,1)} fusion(bf16[8,32,4096]{2,1,0:T(8,128)(2,1)} %collective-permute-done.29, bf16[8,32,4096]{2,1,0:T(8,128)(2,1)S(1)} %copy-done.22), kind=kLoop, calls=%fused_computation | loop fusion | flops 4194304 | bytes 6291456 | tf_op jit(solution)/shard_map/convert_element_type | solution.py:159
  277.0 14.7 %enter.1 = (f32[512,1024]{1,0:T(8,128)}, f32[8,1024]{1,0:T(8,128)S(1)}) custom-call(s32[32]{0:T(128)S(1)} %copy-done.16, f32[8,1024]{1,0:T(8,128)S(1)} %slice.300.vec_ref, bf16[512,1024]{1,0:T(8,128)(2,1)S(1)} %bitcast.45, f32[512,1024]{1,0:T(8,128)S(1)} %copy-done.6, bf16[512,3072]{1,0:T(8,128)(2,1)} %get-tuple-element.384.gproject_ref, ...), custom_call_target="tpu_custom_call" | custom-call | tf_op jit(solution)/shard_map/enter/pallas_call | solution.py:666
  301.0 2.1 collective-permute-start.47
  303.1 16.1 %collective-permute-done.38 = bf16[8,1,384]{2,0,1:T(8,128)(2,1)S(1)} collective-permute-done((bf16[8,1,384]{2,0,1:T(8,128)(2,1)S(1)}, bf16[8,1,384]{2,0,1:T(8,128)(2,1)S(1)}, u32[]{:S(2)}, u32[]{:S(2)}) %collective-permute-start.38) | collective-permute-done | bytes 6176 | tf_op jit(solution)/shard_map/ppermute | solution.py:96
  322.5 11.8 %finish.1 = bf16[512,1024]{1,0:T(8,128)(2,1)} custom-call(s32[32]{0:T(128)S(1)} %copy-done.16, f32[8,1024]{1,0:T(8,128)S(1)} %slice.300.vec_ref, f32[512,1024]{1,0:T(8,128)S(1)} %copy-done.4, bf16[512,4096]{1,0:T(8,128)(2,1)} %get-tuple-element.419.active_ref, bf16[8,128,1024]{2,1,0:T(8,128)(2,1)S(1)} %copy-done.3, ...), custom_call_target="tpu_custom_call" | custom-call | tf_op jit(solution)/shard_map/finish/pallas_call | solution.py:699
  338.0 12.3 %collective-permute-done.43 = bf16[4,32,4096]{2,1,0:T(8,128)(2,1)S(1)} collective-permute-done((bf16[4,32,4096]{2,1,0:T(8,128)(2,1)S(1)}, bf16[4,32,4096]{2,1,0:T(8,128)(2,1)S(1)}, u32[]{:S(2)}, u32[]{:S(2)}) %collective-permute-start.43) | collective-permute-done | bytes 1048608 | tf_op jit(solution)/shard_map/ppermute | solution.py:96
  352.6 3.0 collective-permute-start.46
  358.5 11.9 %collective-permute-done.42 = bf16[1,1,384]{2,0,1:T(2,128)(2,1)S(1)} collective-permute-done((bf16[1,1,384]{2,0,1:T(2,128)(2,1)S(1)}, bf16[1,1,384]{2,0,1:T(2,128)(2,1)S(1)}, u32[]{:S(2)}, u32[]{:S(2)}) %collective-permute-start.42) | collective-permute-done | bytes 800 | tf_op jit(solution)/shard_map/ppermute | solution.py:96
  375.7 4.1 %collective-permute-done.45 = bf16[1,32,4096]{2,1,0:T(8,128)(2,1)S(1)} collective-permute-done((bf16[1,32,4096]{2,1,0:T(8,128)(2,1)S(1)}, bf16[1,32,4096]{2,1,0:T(8,128)(2,1)S(1)}, u32[]{:S(2)}, u32[]{:S(2)}) %collective-permute-start.45) | collective-permute-done | bytes 262176 | tf_op jit(solution)/shard_map/ppermute | solution.py:96
  (231 shorter events, 82.7 us)
Async XLA Ops:
  18.0 15.7 %collective-permute-start.4 = (bf16[2,32,4096]{2,1,0:T(8,128)(2,1)S(1)}, bf16[2,32,4096]{2,1,0:T(8,128)(2,1)S(1)}, u32[]{:S(2)}, u32[]{:S(2)}) collective-permute-start(bf16[2,32,4096]{2,1,0:T(8,128)(2,1)S(1)} %constant_dynamic-update-slice_fusion), channel_id=1, source_target_pairs={{0,2},{1,3},{2,0},{3,1},{4,6},{5,7},{6,4},{7,5},{8,10},{9,11},{10,... | collective-permute-start | bytes 1572872 | tf_op jit(solution)/shard_map/ppermute | solution.py:96
  19.5 14.2 %collective-permute-start = (bf16[1,1,384]{2,0,1:T(2,128)(2,1)S(1)}, bf16[1,1,384]{2,0,1:T(2,128)(2,1)S(1)}, u32[]{:S(2)}, u32[]{:S(2)}) collective-permute-start(bf16[1,1,384]{2,0,1:T(2,128)(2,1)S(1)} %maximum_bitcast_fusion.1), channel_id=1, source_target_pairs={{0,4},{1,5},{2,6},{3,7},{4,0},{5,1},{6,2},{7,3},{8,12},{9,13},{10,... | collective-permute-start | bytes 2312 | tf_op jit(solution)/shard_map/ppermute | solution.py:96
  33.8 14.9 %collective-permute-start.8 = (bf16[4,32,4096]{2,1,0:T(8,128)(2,1)S(1)}, bf16[4,32,4096]{2,1,0:T(8,128)(2,1)S(1)}, u32[]{:S(2)}, u32[]{:S(2)}) collective-permute-start(bf16[4,32,4096]{2,1,0:T(8,128)(2,1)S(1)} %constant_dynamic-update-slice_fusion.2), channel_id=1, source_target_pairs={{0,1},{1,0},{2,3},{3,2},{4,5},{5,4},{6,7},{7,6},{8,24},{9,25},{10,... | collective-permute-start | bytes 3145736 | tf_op jit(solution)/shard_map/ppermute | solution.py:96
  48.9 26.2 %collective-permute-start.13 = (bf16[8,32,4096]{2,1,0:T(8,128)(2,1)S(1)}, bf16[8,32,4096]{2,1,0:T(8,128)(2,1)}, u32[]{:S(2)}, u32[]{:S(2)}) collective-permute-start(bf16[8,32,4096]{2,1,0:T(8,128)(2,1)S(1)} %constant_dynamic-update-slice_fusion.6.w0), channel_id=1, source_target_pairs={{0,16},{1,17},{2,18},{3,19},{4,20},{5,21},{6,22},{7,23},{8,9},{9,8... | collective-permute-start | bytes 6291464 | tf_op jit(solution)/shard_map/ppermute | solution.py:96
  50.5 15.6 %collective-permute-start.7 = (bf16[2,32,4096]{2,1,0:T(8,128)(2,1)S(1)}, bf16[2,32,4096]{2,1,0:T(8,128)(2,1)}, u32[]{:S(2)}, u32[]{:S(2)}) collective-permute-start(bf16[2,32,4096]{2,1,0:T(8,128)(2,1)S(1)} %constant_dynamic-update-slice_fusion.4), channel_id=1, source_target_pairs={{0,2},{1,3},{2,0},{3,1},{4,6},{5,7},{6,4},{7,5},{8,10},{9,11},{10,... | collective-permute-start | bytes 1572872 | tf_op jit(solution)/shard_map/ppermute | solution.py:96
  53.3 15.5 %collective-permute-start.5 = (bf16[4,1,384]{2,0,1:T(4,128)(2,1)S(1)}, bf16[4,1,384]{2,0,1:T(4,128)(2,1)S(1)}, u32[]{:S(2)}, u32[]{:S(2)}) collective-permute-start(bf16[4,1,384]{2,0,1:T(4,128)(2,1)S(1)} %pad_maximum_fusion.2), channel_id=1, source_target_pairs={{0,1},{1,0},{2,3},{3,2},{4,5},{5,4},{6,7},{7,6},{8,24},{9,25},{10,... | collective-permute-start | bytes 9224 | tf_op jit(solution)/shard_map/ppermute | solution.py:96
  54.9 13.8 %collective-permute-start.6 = (bf16[1,128,1024]{2,1,0:T(8,128)(2,1)S(1)}, bf16[1,128,1024]{2,1,0:T(8,128)(2,1)S(1)}, u32[]{:S(2)}, u32[]{:S(2)}) collective-permute-start(bf16[1,128,1024]{2,1,0:T(8,128)(2,1)S(1)} %broadcast_in_dim_reshape.7), channel_id=1, source_target_pairs={{0,4},{1,5},{2,6},{3,7},{4,0},{5,1},{6,2},{7,3},{8,12},{9,13},{10,... | collective-permute-start | bytes 786440 | tf_op jit(solution)/shard_map/ppermute | solution.py:96
  75.1 14.8 %collective-permute-start.15 = (bf16[8,32,4096]{2,1,0:T(8,128)(2,1)}, bf16[8,32,4096]{2,1,0:T(8,128)(2,1)}, u32[]{:S(2)}, u32[]{:S(2)}) collective-permute-start(bf16[8,32,4096]{2,1,0:T(8,128)(2,1)} %collective-permute-done.13.w1), channel_id=1, source_target_pairs={{0,8},{1,9},{2,10},{3,11},{4,12},{5,13},{6,14},{7,15},{8,0},{9,1},... | collective-permute-start | bytes 6291464 | tf_op jit(solution)/shard_map/ppermute | solution.py:96
  75.1 14.8 %collective-permute-start.16 = (bf16[4,32,4096]{2,1,0:T(8,128)(2,1)S(1)}, bf16[4,32,4096]{2,1,0:T(8,128)(2,1)S(1)}, u32[]{:S(2)}, u32[]{:S(2)}) collective-permute-start(bf16[4,32,4096]{2,1,0:T(8,128)(2,1)S(1)} %constant_dynamic-update-slice_fusion.8), channel_id=1, source_target_pairs={{0,1},{1,0},{2,3},{3,2},{4,5},{5,4},{6,7},{7,6},{8,24},{9,25},{10,... | collective-permute-start | bytes 3145736 | tf_op jit(solution)/shard_map/ppermute | solution.py:96
  92.0 39.0 %collective-permute-start.17 = (bf16[8,32,4096]{2,1,0:T(8,128)(2,1)}, bf16[8,32,4096]{2,1,0:T(8,128)(2,1)}, u32[]{:S(2)}, u32[]{:S(2)}) collective-permute-start(bf16[8,32,4096]{2,1,0:T(8,128)(2,1)} %constant_dynamic-update-slice_fusion.14.w0), channel_id=1, source_target_pairs={{0,16},{1,17},{2,18},{3,19},{4,20},{5,21},{6,22},{7,23},{8,9},{9,8... | collective-permute-start | bytes 6291464 | tf_op jit(solution)/shard_map/ppermute | solution.py:96
  108.5 23.6 %collective-permute-start.18 = (bf16[8,32,4096]{2,1,0:T(8,128)(2,1)}, bf16[8,32,4096]{2,1,0:T(8,128)(2,1)}, u32[]{:S(2)}, u32[]{:S(2)}) collective-permute-start(bf16[8,32,4096]{2,1,0:T(8,128)(2,1)} %constant_dynamic-update-slice_fusion.14.w0), channel_id=1, source_target_pairs={{0,8},{1,9},{2,10},{3,11},{4,12},{5,13},{6,14},{7,15},{8,0},{9,1},... | collective-permute-start | bytes 6291464 | tf_op jit(solution)/shard_map/ppermute | solution.py:96
  131.0 15.4 %collective-permute-start.19 = (bf16[8,32,4096]{2,1,0:T(8,128)(2,1)}, bf16[8,32,4096]{2,1,0:T(8,128)(2,1)}, u32[]{:S(2)}, u32[]{:S(2)}) collective-permute-start(bf16[8,32,4096]{2,1,0:T(8,128)(2,1)} %collective-permute-done.17.w1), channel_id=1, source_target_pairs={{0,8},{1,9},{2,10},{3,11},{4,12},{5,13},{6,14},{7,15},{8,0},{9,1},... | collective-permute-start | bytes 6291464 | tf_op jit(solution)/shard_map/ppermute | solution.py:96
  131.5 14.8 %collective-permute-start.20 = (bf16[4,128,1024]{2,1,0:T(8,128)(2,1)S(1)}, bf16[4,128,1024]{2,1,0:T(8,128)(2,1)S(1)}, u32[]{:S(2)}, u32[]{:S(2)}) collective-permute-start(bf16[4,128,1024]{2,1,0:T(8,128)(2,1)S(1)} %constant_dynamic-update-slice_fusion.12), channel_id=1, source_target_pairs={{0,1},{1,0},{2,3},{3,2},{4,5},{5,4},{6,7},{7,6},{8,24},{9,25},{10,... | collective-permute-start | bytes 3145736 | tf_op jit(solution)/shard_map/ppermute | solution.py:96
  147.8 26.2 %collective-permute-start.21 = (bf16[8,128,1024]{2,1,0:T(8,128)(2,1)S(1)}, bf16[8,128,1024]{2,1,0:T(8,128)(2,1)}, u32[]{:S(2)}, u32[]{:S(2)}) collective-permute-start(bf16[8,128,1024]{2,1,0:T(8,128)(2,1)S(1)} %constant_dynamic-update-slice_fusion.16.w0), channel_id=1, source_target_pairs={{0,16},{1,17},{2,18},{3,19},{4,20},{5,21},{6,22},{7,23},{8,9},{9,8... | collective-permute-start | bytes 6291464 | tf_op jit(solution)/shard_map/ppermute | solution.py:96
  174.0 50.1 %collective-permute-start.26 = (bf16[8,128,1024]{2,1,0:T(8,128)(2,1)}, bf16[8,128,1024]{2,1,0:T(8,128)(2,1)}, u32[]{:S(2)}, u32[]{:S(2)}) collective-permute-start(bf16[8,128,1024]{2,1,0:T(8,128)(2,1)} %get-tuple-element.341), channel_id=1, source_target_pairs={{0,8},{1,9},{2,10},{3,11},{4,12},{5,13},{6,14},{7,15},{8,0},{9,1},... | collective-permute-start | bytes 6291464 | tf_op jit(solution)/shard_map/ppermute | solution.py:96
  181.4 42.7 %collective-permute-start.27 = (bf16[8,128,1024]{2,1,0:T(8,128)(2,1)S(1)}, bf16[8,128,1024]{2,1,0:T(8,128)(2,1)}, u32[]{:S(2)}, u32[]{:S(2)}) collective-permute-start(bf16[8,128,1024]{2,1,0:T(8,128)(2,1)S(1)} %add_convert_fusion.2), channel_id=1, source_target_pairs={{0,16},{1,17},{2,18},{3,19},{4,20},{5,21},{6,22},{7,23},{8,9},{9,8... | collective-permute-start | bytes 6291464 | tf_op jit(solution)/shard_map/ppermute | solution.py:96
  206.4 21.8 %collective-permute-start.25 = (bf16[8,32,4096]{2,1,0:T(8,128)(2,1)}, bf16[8,32,4096]{2,1,0:T(8,128)(2,1)}, u32[]{:S(2)}, u32[]{:S(2)}) collective-permute-start(bf16[8,32,4096]{2,1,0:T(8,128)(2,1)} %get-tuple-element.338), channel_id=1, source_target_pairs={{0,8},{1,9},{2,10},{3,11},{4,12},{5,13},{6,14},{7,15},{8,0},{9,1},... | collective-permute-start | bytes 6291464 | tf_op jit(solution)/shard_map/ppermute | solution.py:96
  224.1 40.0 %collective-permute-start.30 = (bf16[8,32,4096]{2,1,0:T(8,128)(2,1)}, bf16[8,32,4096]{2,1,0:T(8,128)(2,1)}, u32[]{:S(2)}, u32[]{:S(2)}) collective-permute-start(bf16[8,32,4096]{2,1,0:T(8,128)(2,1)} %get-tuple-element.367), channel_id=1, source_target_pairs={{0,8},{1,9},{2,10},{3,11},{4,12},{5,13},{6,14},{7,15},{8,0},{9,1},... | collective-permute-start | bytes 6291464 | tf_op jit(solution)/shard_map/ppermute | solution.py:96
  231.8 37.4 %collective-permute-start.31 = (bf16[8,32,4096]{2,1,0:T(8,128)(2,1)}, bf16[8,32,4096]{2,1,0:T(8,128)(2,1)}, u32[]{:S(2)}, u32[]{:S(2)}) collective-permute-start(bf16[8,32,4096]{2,1,0:T(8,128)(2,1)} %add_convert_fusion.1), channel_id=1, source_target_pairs={{0,16},{1,17},{2,18},{3,19},{4,20},{5,21},{6,22},{7,23},{8,9},{9,8... | collective-permute-start | bytes 6291464 | tf_op jit(solution)/shard_map/ppermute | solution.py:96
  232.7 27.1 %collective-permute-start.32 = (bf16[4,128,1024]{2,1,0:T(8,128)(2,1)}, bf16[4,128,1024]{2,1,0:T(8,128)(2,1)}, u32[]{:S(2)}, u32[]{:S(2)}) collective-permute-start(bf16[4,128,1024]{2,1,0:T(8,128)(2,1)} %add_convert_fusion.5), channel_id=1, source_target_pairs={{0,1},{1,0},{2,3},{3,2},{4,5},{5,4},{6,7},{7,6},{8,24},{9,25},{10,... | collective-permute-start | bytes 3145736 | tf_op jit(solution)/shard_map/ppermute | solution.py:96
  262.6 29.2 %collective-permute-start.37 = (bf16[2,128,1024]{2,1,0:T(8,128)(2,1)S(1)}, bf16[2,128,1024]{2,1,0:T(8,128)(2,1)S(1)}, u32[]{:S(2)}, u32[]{:S(2)}) collective-permute-start(bf16[2,128,1024]{2,1,0:T(8,128)(2,1)S(1)} %add_convert_fusion.8), channel_id=1, source_target_pairs={{0,2},{1,3},{2,0},{3,1},{4,6},{5,7},{6,4},{7,5},{8,10},{9,11},{10,... | collective-permute-start | bytes 1572872 | tf_op jit(solution)/shard_map/ppermute | solution.py:96
  263.8 56.7 %collective-permute-start.28 = (bf16[8,32,4096]{2,1,0:T(8,128)(2,1)}, bf16[8,32,4096]{2,1,0:T(8,128)(2,1)}, u32[]{:S(2)}, u32[]{:S(2)}) collective-permute-start(bf16[8,32,4096]{2,1,0:T(8,128)(2,1)} %get-tuple-element.361), channel_id=1, source_target_pairs={{0,8},{1,9},{2,10},{3,11},{4,12},{5,13},{6,14},{7,15},{8,0},{9,1},... | collective-permute-start | bytes 6291464 | tf_op jit(solution)/shard_map/ppermute | solution.py:96
  272.4 23.3 %collective-permute-start.36 = (bf16[4,32,4096]{2,1,0:T(8,128)(2,1)}, bf16[4,32,4096]{2,1,0:T(8,128)(2,1)}, u32[]{:S(2)}, u32[]{:S(2)}) collective-permute-start(bf16[4,32,4096]{2,1,0:T(8,128)(2,1)} %add_convert_fusion.4), channel_id=1, source_target_pairs={{0,1},{1,0},{2,3},{3,2},{4,5},{5,4},{6,7},{7,6},{8,24},{9,25},{10,... | collective-permute-start | bytes 3145736 | tf_op jit(solution)/shard_map/ppermute | solution.py:96
  292.8 27.7 %collective-permute-start.33 = (bf16[8,32,4096]{2,1,0:T(8,128)(2,1)}, bf16[8,32,4096]{2,1,0:T(8,128)(2,1)S(1)}, u32[]{:S(2)}, u32[]{:S(2)}) collective-permute-start(bf16[8,32,4096]{2,1,0:T(8,128)(2,1)} %add_convert_fusion), channel_id=1, source_target_pairs={{0,16},{1,17},{2,18},{3,19},{4,20},{5,21},{6,22},{7,23},{8,9},{9,8... | collective-permute-start | bytes 6291464 | tf_op jit(solution)/shard_map/ppermute | solution.py:96
  297.4 23.1 %collective-permute-start.41 = (bf16[2,32,4096]{2,1,0:T(8,128)(2,1)S(1)}, bf16[2,32,4096]{2,1,0:T(8,128)(2,1)S(1)}, u32[]{:S(2)}, u32[]{:S(2)}) collective-permute-start(bf16[2,32,4096]{2,1,0:T(8,128)(2,1)S(1)} %add_convert_fusion.7), channel_id=1, source_target_pairs={{0,2},{1,3},{2,0},{3,1},{4,6},{5,7},{6,4},{7,5},{8,10},{9,11},{10,... | collective-permute-start | bytes 1572872 | tf_op jit(solution)/shard_map/ppermute | solution.py:96
  299.8 19.4 %collective-permute-start.38 = (bf16[8,1,384]{2,0,1:T(8,128)(2,1)S(1)}, bf16[8,1,384]{2,0,1:T(8,128)(2,1)S(1)}, u32[]{:S(2)}, u32[]{:S(2)}) collective-permute-start(bf16[8,1,384]{2,0,1:T(8,128)(2,1)S(1)} %add_convert_fusion.12), channel_id=1, source_target_pairs={{0,16},{1,17},{2,18},{3,19},{4,20},{5,21},{6,22},{7,23},{8,9},{9,8... | collective-permute-start | bytes 18440 | tf_op jit(solution)/shard_map/ppermute | solution.py:96
  301.0 54.7 %collective-permute-start.47 = (bf16[1,128,1024]{2,1,0:T(8,128)(2,1)S(1)}, bf16[1,128,1024]{2,1,0:T(8,128)(2,1)S(1)}, u32[]{:S(2)}, u32[]{:S(2)}) collective-permute-start(bf16[1,128,1024]{2,1,0:T(8,128)(2,1)S(1)} %add_convert_fusion.11), channel_id=1, source_target_pairs={{0,4},{1,5},{2,6},{3,7},{4,0},{5,1},{6,2},{7,3},{8,12},{9,13},{10,... | collective-permute-start | bytes 786440 | tf_op jit(solution)/shard_map/ppermute | solution.py:96
  319.2 15.1 %collective-permute-start.39 = (bf16[4,1,384]{2,0,1:T(4,128)(2,1)S(1)}, bf16[4,1,384]{2,0,1:T(4,128)(2,1)S(1)}, u32[]{:S(2)}, u32[]{:S(2)}) collective-permute-start(bf16[4,1,384]{2,0,1:T(4,128)(2,1)S(1)} %add_convert_fusion.13), channel_id=1, source_target_pairs={{0,1},{1,0},{2,3},{3,2},{4,5},{5,4},{6,7},{7,6},{8,24},{9,25},{10,... | collective-permute-start | bytes 9224 | tf_op jit(solution)/shard_map/ppermute | solution.py:96
  335.6 14.8 %collective-permute-start.43 = (bf16[4,32,4096]{2,1,0:T(8,128)(2,1)S(1)}, bf16[4,32,4096]{2,1,0:T(8,128)(2,1)S(1)}, u32[]{:S(2)}, u32[]{:S(2)}) collective-permute-start(bf16[4,32,4096]{2,1,0:T(8,128)(2,1)S(1)} %add_convert_fusion.3), channel_id=1, source_target_pairs={{0,1},{1,0},{2,3},{3,2},{4,5},{5,4},{6,7},{7,6},{8,24},{9,25},{10,... | collective-permute-start | bytes 3145736 | tf_op jit(solution)/shard_map/ppermute | solution.py:96
  351.7 18.7 %collective-permute-start.44 = (bf16[2,32,4096]{2,1,0:T(8,128)(2,1)S(1)}, bf16[2,32,4096]{2,1,0:T(8,128)(2,1)S(1)}, u32[]{:S(2)}, u32[]{:S(2)}) collective-permute-start(bf16[2,32,4096]{2,1,0:T(8,128)(2,1)S(1)} %add_convert_fusion.6), channel_id=1, source_target_pairs={{0,2},{1,3},{2,0},{3,1},{4,6},{5,7},{6,4},{7,5},{8,10},{9,11},{10,... | collective-permute-start | bytes 1572872 | tf_op jit(solution)/shard_map/ppermute | solution.py:96
  352.6 17.8 %collective-permute-start.46 = (bf16[1,32,4096]{2,1,0:T(8,128)(2,1)S(1)}, bf16[1,32,4096]{2,1,0:T(8,128)(2,1)S(1)}, u32[]{:S(2)}, u32[]{:S(2)}) collective-permute-start(bf16[1,32,4096]{2,1,0:T(8,128)(2,1)S(1)} %add_convert_fusion.10), channel_id=1, source_target_pairs={{0,4},{1,5},{2,6},{3,7},{4,0},{5,1},{6,2},{7,3},{8,12},{9,13},{10,... | collective-permute-start | bytes 786440 | tf_op jit(solution)/shard_map/ppermute | solution.py:96
  355.7 14.7 %collective-permute-start.42 = (bf16[1,1,384]{2,0,1:T(2,128)(2,1)S(1)}, bf16[1,1,384]{2,0,1:T(2,128)(2,1)S(1)}, u32[]{:S(2)}, u32[]{:S(2)}) collective-permute-start(bf16[1,1,384]{2,0,1:T(2,128)(2,1)S(1)} %add_convert_fusion.15), channel_id=1, source_target_pairs={{0,4},{1,5},{2,6},{3,7},{4,0},{5,1},{6,2},{7,3},{8,12},{9,13},{10,... | collective-permute-start | bytes 2312 | tf_op jit(solution)/shard_map/ppermute | solution.py:96
  (49 other events, 686.9 us)

commit v4 on v3

v4 whole, which is shorter than its diff:
```python
import jax
import jax.numpy as jnp
from jax import lax
from jax.experimental import pallas as pl
from jax.experimental.pallas import tpu as pltpu
from jax.sharding import PartitionSpec as P

D = 1024
FF = 4096
HEADS = 16
HEAD_DIM = 64
SEQ = 256
AXES = ("dp", "fsdp")
BLOCKS = 32
GROUP = 4
WIDE = GROUP * HEAD_DIM
TILE = 512
CHUNK = 128
PIECE = FF // BLOCKS
BF = jnp.bfloat16
F32 = jnp.float32

eps = 1e-06
ANY = pl.BlockSpec(memory_space=pl.ANY)
VMEM = pl.BlockSpec(memory_space=pltpu.VMEM)
SMEM = pl.BlockSpec(memory_space=pltpu.SMEM)


class Plan:
    def __init__(self, mesh):
        outer, inner = mesh.shape["dp"], mesh.shape["fsdp"]
        ys = outer // 2
        xs = min(ys, inner)
        zs = inner // xs
        self.devices = outer * inner
        self.half = self.devices // 2

        def bits(size, unit):
            found = []
            while size > 1:
                size //= 2
                found.append(size * unit)
            return found

        xbits = bits(xs, 1)
        zbits = bits(zs, xs)
        self.core = inner
        ybits = bits(ys, 2 * inner)
        self.orders = (zbits + xbits + ybits, zbits + ybits + xbits)
        self.legs = [list(range(1)), list(range(1, len(zbits)))]
        for _ in range(2):
            start = self.legs[-1][-1] + 1
            self.legs.append(list(range(start, start + len(xbits))))

    def pairs(self, stage):
        return [
            (i, i ^ self.orders[1 if i & self.core else 0][stage]) for i in range(self.devices)
        ]

    def core_pairs(self):
        return [(i, i ^ self.core) for i in range(self.devices)]

    def masks(self, which):
        found = [0]
        for bit in self.orders[which]:
            found = found + [mask ^ bit for mask in found]
        return found

    def positions(self, me):
        tables = jnp.array(
            [
                self.masks(0) + [mask ^ self.core for mask in self.masks(1)],
                self.masks(1) + [mask ^ self.core for mask in self.masks(0)],
            ],
            jnp.int32,
        )
        mine = jnp.where((me & self.core) > 0, tables[1], tables[0])
        return mine ^ me


class Line:
    def __init__(self):
        self.last = []

    def tie(self, *arrays):
        if not self.last:
            return arrays
        tied = lax.optimization_barrier((arrays, tuple(self.last)))
        return tied[0]

    def run(self, step, *arrays):
        result = step(*self.tie(*arrays))
        self.last = [result[0] if isinstance(result, (list, tuple)) else result]
        return result

    def send(self, array, pairs, name="swap"):
        with jax.named_scope(name):
            return lax.ppermute(self.tie(array)[0], AXES, pairs)

    def wait(self, *arrays):
        self.last.extend(arrays)


class Gather:
    def __init__(self, plan, line, name, block):
        self.plan, self.line, self.name = plan, line, name
        self.held = block[None]
        self.coming = None

    def take(self):
        self.line.wait(self.coming)
        self.held = self.line.run(
            lambda held, coming: jnp.concatenate([held, coming], 0), self.held, self.coming
        )

    def start(self, leg):
        for stage in self.plan.legs[leg]:
            if stage != self.plan.legs[leg][0]:
                self.take()
            self.coming = self.line.send(
                self.held, self.plan.pairs(stage), f"gather_{self.name}_{stage}"
            )

    def swap_first(self):
        self.first = self.line.send(
            self.held, self.plan.core_pairs(), f"gather_{self.name}_swap_first"
        )

    def arrive(self):
        self.line.wait(self.coming)

    def swap_second(self):
        self.second = self.line.send(
            self.coming, self.plan.core_pairs(), f"gather_{self.name}_swap_second"
        )

    def parts(self):
        self.line.wait(self.first, self.second)
        return [self.held, self.coming, self.first, self.second]


def total(parts):
    if len(parts) == 2:
        return parts[0] + parts[1]
    result = parts[0].astype(F32)
    for part in parts[1:]:
        result = result + part.astype(F32)
    return result


class Scatter:
    def __init__(self, plan, line, name, parts):
        self.plan, self.line, self.name = plan, line, name
        keep_low, keep_high, send_low, send_high = parts
        self.high = [keep_high, line.send(send_high, plan.core_pairs(), f"sum_{name}_swap_high")]
        self.low = [keep_low, line.send(send_low, plan.core_pairs(), f"sum_{name}_swap_low")]
        self.side = []
        self.count = keep_low.shape[0]
        self.width = keep_low.shape[-1]

    def join(self, parts):
        half = self.plan.half
        self.side = [
            parts[:half],
            self.line.send(parts[half:], self.plan.core_pairs(), f"sum_{self.name}_swap_side"),
        ]

    def sum(self, low, high, parts):
        wide = total([part[low:high, :, : self.width] for part in parts])
        if not self.side:
            return wide
        offset = low if self.high is None else low + self.count
        narrow = [part[low:high, :, self.width :] for part in parts[2:]]
        narrow += [part[offset : offset + high - low] for part in self.side]
        return jnp.concatenate([wide, total(narrow)], -1)

    def start(self, leg):
        for stage in reversed(self.plan.legs[leg]):
            if self.high is not None:
                parts, low = self.high, 0
            else:
                self.count //= 2
                parts, low = self.low, self.count
            self.line.wait(parts[-1], *self.side)
            outgoing = self.line.run(
                lambda *parts: self.sum(low, low + self.count, parts).astype(BF), *parts
            )
            self.high = None
            self.low.append(
                self.line.send(outgoing, self.plan.pairs(stage), f"sum_{self.name}_{stage}")
            )

    def arrive(self):
        self.line.wait(self.low[-1])

    def result(self):
        self.arrive()
        return self.line.run(lambda *parts: self.sum(0, 1, parts)[0].astype(F32), *self.low)


def one_hot(order):
    return (order[:, None] == jnp.arange(order.shape[0])[None, :]).astype(BF)


def to_blocks(order, parts):
    if order.shape[0] == BLOCKS:
        return parts
    width = parts[0].shape[-1]
    joined = jnp.concatenate(parts, 0).reshape(order.shape[0], -1)
    spread = lax.dot_general(
        one_hot(order), joined, (((0,), (0,)), ((), ())), preferred_element_type=BF
    ).reshape(4, BLOCKS // 4, -1, width)
    return [spread[i] for i in range(4)]


def from_blocks(order, parts):
    count = order.shape[0]
    if count == BLOCKS:
        return parts
    width = parts[0].shape[-1]
    joined = jnp.concatenate(parts, 0).reshape(count, -1)
    moved = jnp.dot(one_hot(order), joined, preferred_element_type=BF)
    moved = moved.reshape(4, count // 4, -1, width)
    return [moved[i] for i in range(4)]


def params(limit):
    return pltpu.CompilerParams(vmem_limit_bytes=limit << 20)


def rows_of(ref, number, rows):
    return ref.at[pl.ds(pl.multiple_of(number * rows, rows), rows), :]


def fetches(order_ref, part_refs, held_ref, sems, start=0, width=None):
    each, rows, _ = part_refs[0].shape
    width = held_ref.shape[1] if width is None else width
    copies = []
    for place in range(BLOCKS):
        source = part_refs[place // each].at[place % each, :, pl.ds(start, width)]
        number = order_ref[place]
        copies.append(
            pltpu.make_async_copy(source, rows_of(held_ref, number, rows), sems.at[number])
        )
    return copies


def norm_parts(values):
    centre = values - jnp.mean(values, axis=-1, keepdims=True)
    inverse = lax.rsqrt(jnp.mean(centre * centre, axis=-1, keepdims=True) + eps)
    return centre * inverse, inverse


def norm_back(grad_norm, normed, inverse):
    return inverse * (
        grad_norm
        - jnp.mean(grad_norm, axis=-1, keepdims=True)
        - normed * jnp.mean(grad_norm * normed, axis=-1, keepdims=True)
    )


def span(index, size):
    if isinstance(index, int):
        return pl.ds(index * size, size)
    return pl.ds(pl.multiple_of(index * size, size), size)


def each(count):
    def run(body):
        for index in range(count):
            body(index)

    return run


def dot(a, b):
    return jnp.dot(a, b, preferred_element_type=F32)


def dot_nt(a, b):
    return lax.dot_general(a, b, (((1,), (1,)), ((), ())), preferred_element_type=F32)


def dot_tn(a, b):
    return lax.dot_general(a, b, (((0,), (0,)), ((), ())), preferred_element_type=F32)


def stacked(values):
    head = lax.broadcasted_iota(jnp.int32, values.shape, 1) // HEAD_DIM
    zero = jnp.zeros_like(values)
    return jnp.concatenate([jnp.where(head == h, values, zero) for h in range(GROUP)], 0)


def unstacked(values):
    rows = values.shape[0] // GROUP
    head = lax.broadcasted_iota(jnp.int32, (rows, values.shape[1]), 1) // HEAD_DIM
    result = values[:rows]
    for h in range(1, GROUP):
        result = jnp.where(head == h, values[h * rows : (h + 1) * rows], result)
    return result


def project_kernel(
    order_ref, vec_ref, x_ref, w0, w1, w2, w3, entry_ref, project_ref, held, sems
):
    copies = fetches(order_ref, (w0, w1, w2, w3), held, sems)
    for copy in copies:
        copy.start()

    @each(x_ref.shape[0] // CHUNK)
    def _(i):
        normed, _ = norm_parts(x_ref[span(i, CHUNK), :].astype(F32))
        entry_ref[span(i, CHUNK), :] = (normed * vec_ref[0:1, :] + vec_ref[2:3, :]).astype(BF)

    for copy in copies:
        copy.wait()

    @each(3 * D // TILE)
    def _(i):
        third = i // (D // TILE)
        column = span(i % (D // TILE), TILE)
        part = dot(entry_ref[...], held[:, span(i, TILE)])
        if third != 1:
            part = part + vec_ref[pl.ds(3 if third == 0 else 4, 1), column]
        project_ref[:, span(i, TILE)] = part.astype(BF)


def project_all(order, vec, x, *first):
    count = x.shape[0]
    shape = jax.ShapeDtypeStruct
    return pl.pallas_call(
        project_kernel,
        out_shape=[shape((count, D), BF), shape((count, 3 * D), BF)],
        in_specs=[SMEM] + [VMEM] * 2 + [ANY] * 4,
        out_specs=[VMEM] * 2,
        scratch_shapes=[pltpu.VMEM((D, 3 * D), BF), pltpu.SemaphoreType.DMA((BLOCKS,))],
        compiler_params=params(32),
        name="project",
    )(order, vec, x, *first)


def attend_kernel(project_ref, idr_ref, idc_ref, probs_ref, mixed_ref, probs, out_sems):
    groups = D // WIDE
    copies = []

    @each((mixed_ref.shape[0] // SEQ) * groups)
    def _(i):
        row, group = i // groups, i % groups
        rows = span(row, SEQ)
        queries = project_ref[rows, span(group, WIDE)] * BF(HEAD_DIM**-0.5)
        keys = project_ref[rows, span(groups + group, WIDE)]
        values = project_ref[rows, span(2 * groups + group, WIDE)]
        scores = dot_nt(stacked(queries), keys)
        same = idc_ref[rows, :] == idr_ref[pl.ds(row, 1), :]
        scores = jnp.where(same[None], scores.reshape(GROUP, SEQ, SEQ), -1e9)
        expo = jnp.exp(scores - jnp.max(scores, axis=-1, keepdims=True))
        low = (expo / jnp.sum(expo, axis=-1, keepdims=True)).astype(BF)
        low = low.reshape(GROUP * SEQ, SEQ)
        probs[i] = low
        copy = pltpu.make_async_copy(probs.at[i], probs_ref.at[i], out_sems.at[i])
        copy.start()
        copies.append(copy)
        mixed_ref[rows, span(group, WIDE)] = unstacked(dot(low, values)).astype(BF)

    for copy in copies:
        copy.wait()


def attend(project, ids):
    count = project.shape[0]
    steps = (count // SEQ) * (D // WIDE)
    shape = jax.ShapeDtypeStruct
    return pl.pallas_call(
        attend_kernel,
        out_shape=[shape((steps, GROUP * SEQ, SEQ), BF), shape((count, D), BF)],
        in_specs=[VMEM] * 3,
        out_specs=[ANY, VMEM],
        scratch_shapes=[
            pltpu.VMEM((steps, GROUP * SEQ, SEQ), BF),
            pltpu.SemaphoreType.DMA((steps,)),
        ],
        compiler_params=params(32),
        name="attend",
    )(project, ids, ids.reshape(count, 1))


def piece(number):
    return pl.ds(pl.multiple_of(number * PIECE, PIECE), PIECE)


def settle_kernel(
    order_ref, vec_ref, x_ref, mixed_ref, w0, w1, w2, w3, middle_ref, second_ref, held, sems
):
    copies = fetches(order_ref, (w0, w1, w2, w3), held, sems, FF)
    for copy in copies:
        copy.start()
    for copy in copies:
        copy.wait()

    @each(D // TILE)
    def _(i):
        columns = span(i, TILE)
        branch = dot(mixed_ref[...], held[:, columns]) + vec_ref[5:6, columns]
        middle_ref[:, columns] = x_ref[:, columns].astype(F32) + branch

    @pl.loop(0, x_ref.shape[0] // CHUNK)
    def _(i):
        normed, _ = norm_parts(middle_ref[span(i, CHUNK), :])
        second_ref[span(i, CHUNK), :] = (normed * vec_ref[1:2, :] + vec_ref[6:7, :]).astype(BF)


def settle(order, vec, x, mixed, *win):
    count = x.shape[0]
    shape = jax.ShapeDtypeStruct
    return pl.pallas_call(
        settle_kernel,
        out_shape=[shape((count, D), F32), shape((count, D), BF)],
        in_specs=[SMEM] + [VMEM] * 3 + [ANY] * 4,
        out_specs=[VMEM] * 2,
        scratch_shapes=[pltpu.VMEM((D, D), BF), pltpu.SemaphoreType.DMA((BLOCKS,))],
        compiler_params=params(32),
        name="settle",
    )(order, vec, x, mixed, *win)


def rise_kernel(
    order_ref, bias_ref, second_ref, top_ref, w0, w1, w2, w3,
    active_ref, slope_ref, g0, g1, g2, g3,
    held, active, slope, grads, sems, tile_sems,
):
    copies = fetches(order_ref, (w0, w1, w2, w3), held, sems)
    for copy in copies:
        copy.start()
    for copy in copies:
        copy.wait()
    outs = []
    places = TILE // PIECE

    @each(FF // TILE)
    def _(step):
        columns = span(step, TILE)
        numbers = [order_ref[step * places + j] for j in range(places)]
        weight = jnp.concatenate([held[:, piece(number)] for number in numbers], 1)
        bias = jnp.concatenate([bias_ref[:, piece(number)] for number in numbers], 1)
        hidden = dot(second_ref[...], weight) + bias
        cdf = 0.5 + 0.5 * lax.erf(hidden * (0.5**0.5))
        grow = cdf + hidden * jnp.exp(-0.5 * hidden * hidden) * 0.3989422804014327
        low = (hidden * cdf).astype(BF)
        active[:, columns] = low
        slope[:, columns] = grow.astype(BF)
        grad = dot_tn(low, top_ref[...]).astype(BF)
        block = pl.ds(step * places, places)
        grads[block] = grad.reshape(places, PIECE, D)
        apiece = g0.shape[0]
        target = (g0, g1, g2, g3)[step * places // apiece]
        target = target.at[pl.ds(step * places % apiece, places)]
        for number, (source, target) in enumerate(
            (
                (active.at[:, columns], active_ref.at[:, columns]),
                (slope.at[:, columns], slope_ref.at[:, columns]),
                (grads.at[block], target),
            )
        ):
            copy = pltpu.make_async_copy(source, target, tile_sems.at[step, number])
            copy.start()
            outs.append(copy)

    for copy in outs:
        copy.wait()


def rise(order, bias, second, top, *win):
    count = second.shape[0]
    shape = jax.ShapeDtypeStruct
    grad = shape((BLOCKS // 4, PIECE, D), BF)
    return pl.pallas_call(
        rise_kernel,
        out_shape=[shape((count, FF), BF)] * 2 + [grad] * 4,
        in_specs=[SMEM] + [VMEM] * 3 + [ANY] * 4,
        out_specs=[ANY] * 6,
        scratch_shapes=[
            pltpu.VMEM((D, FF), BF),
            pltpu.VMEM((count, FF), BF),
            pltpu.VMEM((count, FF), BF),
            pltpu.VMEM((BLOCKS, PIECE, D), BF),
            pltpu.SemaphoreType.DMA((BLOCKS,)),
            pltpu.SemaphoreType.DMA((FF // TILE, 3)),
        ],
        compiler_params=params(48),
        name="rise",
    )(order, bias, second, top, *win)


def part_fetches(part_refs, held_ref, sems):
    apiece = part_refs[0].shape[0]
    return [
        pltpu.make_async_copy(part, held_ref.at[pl.ds(i * apiece, apiece)], sems.at[i])
        for i, part in enumerate(part_refs)
    ]


def block_rows(order_ref, ref, part, apiece, rows):
    return jnp.concatenate(
        [ref[span(order_ref[part * apiece + j], rows), :] for j in range(apiece)], 0
    )


def fall_kernel(
    order_ref, vec_ref, top_ref, slope_ref, second_ref, middle_ref,
    m0, m1, m2, m3, w0, w1, w2, w3,
    gmiddle_ref, sums_ref, bias_ref, g0, g1, g2, g3,
    mheld, held, slope, ghidden, turned, middle, gsecond, grads,
    msems, sems, tile_sems, out_sems,
):
    copies = part_fetches((m0, m1, m2, m3), mheld, msems)
    apiece, rows, _ = g0.shape
    places = TILE // PIECE
    slopes = [
        pltpu.make_async_copy(
            slope_ref.at[:, span(i, FF // 4)], slope.at[:, span(i, FF // 4)], tile_sems.at[i]
        )
        for i in range(4)
    ]
    for i in range(4):
        copies[i].start()
        slopes[i].start()
    later = fetches(order_ref, (w0, w1, w2, w3), held, sems)
    later.append(pltpu.make_async_copy(middle_ref, middle, tile_sems.at[4]))
    for copy in later:
        copy.start()
    turned[...] = second_ref[...].T
    sums_ref[...] = jnp.zeros_like(sums_ref)

    @each(FF // TILE)
    def _(step):
        part = step * places // apiece
        if step * places % apiece == 0:
            copies[part].wait()
            slopes[part].wait()
        weight = mheld[pl.ds(step * places, places)].reshape(TILE, D)
        grad_active = dot_nt(top_ref[...], weight)
        grad = grad_active * slope[:, span(step, TILE)].astype(F32)
        low = grad.astype(BF)
        sums = jnp.sum(low.astype(F32), axis=0, keepdims=True)
        for j in range(places):
            number = order_ref[step * places + j]
            ghidden[:, piece(number)] = low[:, j * PIECE : (j + 1) * PIECE]
            bias_ref[:, piece(number)] = sums[:, j * PIECE : (j + 1) * PIECE]

    for copy in later:
        copy.wait()
    for i in range(D // WIDE):
        gsecond[:, span(i, WIDE)] = dot_nt(ghidden[...], held[span(i, WIDE), :])
    outs = []
    chunk = middle_ref.shape[0] // 4
    for part in (3, 2, 1, 0):
        left = block_rows(order_ref, turned, part, apiece, rows)
        for i in range(FF // TILE):
            grad = dot(left, ghidden[:, span(i, TILE)]).astype(BF)
            grads[part, :, :, span(i, TILE)] = grad.reshape(apiece, rows, TILE)
        copy = pltpu.make_async_copy(grads.at[part], (g0, g1, g2, g3)[part], out_sems.at[part])
        copy.start()
        outs.append(copy)
        places_of = span(part, chunk)
        normed, inverse = norm_parts(middle[places_of, :])
        grad = gsecond[places_of, :]
        top = top_ref[places_of, :].astype(F32)
        gmiddle = top + norm_back(grad * vec_ref[1:2, :], normed, inverse)
        gmiddle_ref[places_of, :] = gmiddle
        low = gmiddle.astype(BF).astype(F32)
        for row, value in enumerate((grad * normed, grad, low, top)):
            sums_ref[row : row + 1, :] += jnp.sum(value, axis=0, keepdims=True)
    for copy in outs:
        copy.wait()


def fall(order, vec, top, slope, second, middle, mlp, win):
    count = second.shape[0]
    shape = jax.ShapeDtypeStruct
    grad = shape((BLOCKS // 4, D // BLOCKS, FF), BF)
    return pl.pallas_call(
        fall_kernel,
        out_shape=[shape((count, D), F32), shape((8, D), F32), shape((1, FF), F32)] + [grad] * 4,
        in_specs=[SMEM, VMEM, VMEM, ANY, VMEM, ANY] + [ANY] * 8,
        out_specs=[VMEM] * 3 + [ANY] * 4,
        scratch_shapes=[
            pltpu.VMEM((BLOCKS, PIECE, D), BF),
            pltpu.VMEM((D, FF), BF),
            pltpu.VMEM((count, FF), BF),
            pltpu.VMEM((count, FF), BF),
            pltpu.VMEM((D, count), BF),
            pltpu.VMEM((count, D), F32),
            pltpu.VMEM((count, D), F32),
            pltpu.VMEM((4, *grad.shape), BF),
            pltpu.SemaphoreType.DMA((4,)),
            pltpu.SemaphoreType.DMA((BLOCKS,)),
            pltpu.SemaphoreType.DMA((5,)),
            pltpu.SemaphoreType.DMA((4,)),
        ],
        compiler_params=params(56),
        name="fall",
    )(order, vec, top, slope, second, middle, *mlp, *win)


def unattend_kernel(
    order_ref, vec_ref, x_ref, gmiddle_ref, project_ref, probs_ref, entry_ref, mixed_ref,
    w0, w1, w2, w3, f0, f1, f2, f3,
    ginputs_ref, sums_ref, g0, g1, g2, g3,
    oheld, held, project, probs, both, turned, branch, gmixed, gproject, gentry, grads,
    osems, sems, in_sems, probs_sems, out_sems,
):
    count = gmiddle_ref.shape[0]
    groups = D // WIDE
    ocopies = fetches(order_ref, (w0, w1, w2, w3), oheld, osems, FF)
    load = [
        pltpu.make_async_copy(project_ref, project, in_sems.at[0]),
        pltpu.make_async_copy(entry_ref, both.at[0], in_sems.at[1]),
        pltpu.make_async_copy(mixed_ref, both.at[1], in_sems.at[2]),
    ]
    pieces = [
        pltpu.make_async_copy(probs_ref.at[i], probs.at[i], probs_sems.at[i])
        for i in range((count // SEQ) * groups)
    ]
    copies = fetches(order_ref, (f0, f1, f2, f3), held, sems)
    for copy in ocopies + load + pieces + copies:
        copy.start()
    branch[...] = gmiddle_ref[...].astype(BF)
    sums_ref[...] = jnp.zeros_like(sums_ref)
    for copy in ocopies:
        copy.wait()

    @each(D // TILE)
    def _(i):
        gmixed[:, span(i, TILE)] = dot_nt(branch[...], oheld[span(i, TILE), :]).astype(BF)

    for copy in load:
        copy.wait()
    for i in range(2):
        turned[i] = both[i].T
    apiece, rows, _ = g0.shape

    @each((count // SEQ) * groups)
    def _(i):
        row, group = i // groups, i % groups
        where = span(row, SEQ)
        scale = HEAD_DIM**-0.5
        pieces[i].wait()
        queries = stacked(project[where, span(group, WIDE)] * BF(scale))
        keys = project[where, span(groups + group, WIDE)]
        values = project[where, span(2 * groups + group, WIDE)]
        gmix = stacked(gmixed[where, span(group, WIDE)])
        low = probs[i]
        gprobs = dot_nt(gmix, values)
        gvalues = dot_tn(low, gmix)
        weight = low.astype(F32)
        inner = jnp.sum(weight * gprobs, axis=-1, keepdims=True)
        gscores = (weight * (gprobs - inner)).astype(BF)
        gqueries = unstacked(dot(gscores, keys)) * scale
        gkeys = dot_tn(gscores, queries)
        for third, grad in enumerate((gqueries, gkeys, gvalues)):
            low = grad.astype(BF)
            gproject[where, span(third * groups + group, WIDE)] = low
            sums_ref[third : third + 1, span(group, WIDE)] += jnp.sum(
                low.astype(F32), axis=0, keepdims=True
            )

    for copy in copies:
        copy.wait()
    for i in range(D // WIDE):
        gentry[:, span(i, WIDE)] = dot_nt(gproject[...], held[span(i, WIDE), :])
    outs = []
    chunk = count // 4
    for part in (3, 2, 1, 0):
        left = block_rows(order_ref, turned.at[0], part, apiece, rows)
        for i in range(3 * D // TILE):
            grad = dot(left, gproject[:, span(i, TILE)]).astype(BF)
            grads[part, :, :, span(i, TILE)] = grad.reshape(apiece, rows, TILE)
        left = block_rows(order_ref, turned.at[1], part, apiece, rows)
        for i in range(D // TILE):
            grad = dot(left, branch[:, span(i, TILE)]).astype(BF)
            grads[part, :, :, span(3 * D // TILE + i, TILE)] = grad.reshape(apiece, rows, TILE)
        copy = pltpu.make_async_copy(grads.at[part], (g0, g1, g2, g3)[part], out_sems.at[part])
        copy.start()
        outs.append(copy)
        where = span(part, chunk)
        normed, inverse = norm_parts(x_ref[where, :].astype(F32))
        grad = gentry[where, :]
        back = norm_back(grad * vec_ref[0:1, :], normed, inverse)
        ginputs_ref[where, :] = gmiddle_ref[where, :] + back
        sums_ref[3:4, :] += jnp.sum(grad * normed, axis=0, keepdims=True)
        sums_ref[4:5, :] += jnp.sum(grad, axis=0, keepdims=True)
    for copy in outs:
        copy.wait()


def unattend(order, vec, x, gmiddle, project, probs, entry, mixed, win, first):
    count = gmiddle.shape[0]
    shape = jax.ShapeDtypeStruct
    grad = shape((BLOCKS // 4, D // BLOCKS, 4 * D), BF)
    return pl.pallas_call(
        unattend_kernel,
        out_shape=[shape((count, D), F32), shape((8, D), F32)] + [grad] * 4,
        in_specs=[SMEM] + [VMEM] * 3 + [ANY] * 12,
        out_specs=[VMEM] * 2 + [ANY] * 4,
        scratch_shapes=[
            pltpu.VMEM((D, D), BF),
            pltpu.VMEM((D, 3 * D), BF),
            pltpu.VMEM((count, 3 * D), BF),
            pltpu.VMEM(probs.shape, BF),
            pltpu.VMEM((2, count, D), BF),
            pltpu.VMEM((2, D, count), BF),
            pltpu.VMEM((count, D), BF),
            pltpu.VMEM((count, D), BF),
            pltpu.VMEM((count, 3 * D), BF),
            pltpu.VMEM((count, D), F32),
            pltpu.VMEM((4, *grad.shape), BF),
            pltpu.SemaphoreType.DMA((BLOCKS,)),
            pltpu.SemaphoreType.DMA((BLOCKS,)),
            pltpu.SemaphoreType.DMA((3,)),
            pltpu.SemaphoreType.DMA((probs.shape[0],)),
            pltpu.SemaphoreType.DMA((4,)),
        ],
        compiler_params=params(56),
        name="unattend",
    )(order, vec, x, gmiddle, project, probs, entry, mixed, *win, *first)


def finish_kernel(
    vec_ref, middle_ref, active_ref, w0, w1, w2, w3,
    out_ref, held, active, sems, tile_sems,
):
    copies = [
        pltpu.make_async_copy(
            active_ref.at[:, span(half, FF // 2)], active.at[half], tile_sems.at[half]
        )
        for half in range(2)
    ]
    fetch = part_fetches((w0, w1, w2, w3), held, sems)
    for copy in fetch + copies:
        copy.start()
    for copy in fetch + copies:
        copy.wait()

    @each(D // WIDE)
    def _(i):
        columns = span(i, WIDE)
        weight = held[:, :, columns].reshape(FF, WIDE)
        result = dot(active[0], weight[: FF // 2])
        result = result + dot(active[1], weight[FF // 2 :]) + vec_ref[7:8, columns]
        out_ref[:, columns] = (middle_ref[:, columns] + result).astype(BF)


def finish(vec, middle, active, *mlp):
    count = middle.shape[0]
    return pl.pallas_call(
        finish_kernel,
        out_shape=jax.ShapeDtypeStruct((count, D), BF),
        in_specs=[VMEM, VMEM, ANY] + [ANY] * 4,
        out_specs=VMEM,
        scratch_shapes=[
            pltpu.VMEM((BLOCKS, PIECE, D), BF),
            pltpu.VMEM((2, count, FF // 2), BF),
            pltpu.SemaphoreType.DMA((4,)),
            pltpu.SemaphoreType.DMA((2,)),
        ],
        compiler_params=params(32),
        name="finish",
    )(vec, middle, active, *mlp)


def per_device(plan, inputs, image_ids, cotangent, gains, biases, w_qkv, w_out, w_in, w_mlp):
    me = lax.axis_index(AXES)
    order = plan.positions(me)
    gain_dev, bias_dev = gains.shape[1], biases.shape[1]
    small_dev = gain_dev + bias_dev
    rows = D // plan.devices
    blocks, length = image_ids.shape
    count = blocks * length
    x = inputs.reshape(count, D)
    numbers = order if plan.devices == BLOCKS else jnp.arange(BLOCKS, dtype=jnp.int32)
    line = Line()
    side = 128

    small = jnp.concatenate([gains, biases], 1)
    small = jnp.pad(small, ((0, 0), (0, rows * side - small_dev))).reshape(rows, side)
    first = Gather(plan, line, "qkv", jnp.concatenate([w_qkv.reshape(rows, 3 * D), small], 1))
    first.start(0)
    win = Gather(
        plan, line, "in", jnp.concatenate([w_in.reshape(rows, FF), w_out.reshape(rows, D)], 1)
    )
    mlp = Gather(plan, line, "mlp", w_mlp.reshape(FF // plan.devices, D))
    top = jnp.where(image_ids.reshape(count, 1) >= 0, cotangent.reshape(count, D), BF(0))
    first.take()
    first.start(1)
    win.start(0)
    first.take()
    win.take()
    first.start(2)
    win.start(1)
    first.take()
    win.take()
    first.start(3)
    first.swap_first()
    mlp.start(0)
    first.arrive()
    mlp.take()
    first.swap_second()
    win.start(2)
    mlp.start(1)
    first_parts = first.parts()

    def unpack(*parts):
        placed = jnp.concatenate([part[:, :, 3 * D :] for part in parts], 0)
        placed = placed.reshape(-1, rows * side)[:, :small_dev]
        spread = lax.dot_general(
            one_hot(order), placed, (((0,), (0,)), ((), ())), preferred_element_type=F32
        )
        return jnp.concatenate(
            [spread[:, :gain_dev].reshape(-1), spread[:, gain_dev:].reshape(-1)]
        ).reshape(-1, D)

    vec = line.run(unpack, *first_parts)
    line.wait(*first_parts)
    bias_in = vec[8:12].reshape(1, FF)
    vec = vec[:8]
    if plan.devices != BLOCKS:
        first_parts = [part[:, :, : 3 * D] for part in first_parts]
    first_parts = to_blocks(order, first_parts)
    entry, project = line.run(project_all, numbers, vec, x, *first_parts)
    win.take()
    mlp.take()
    win.start(3)
    win.swap_first()
    probs, mixed = line.run(attend, project, image_ids)
    win.arrive()
    line.wait(win.first)
    win.swap_second()
    mlp.start(2)
    win_parts = to_blocks(order, win.parts())
    middle, second = line.run(settle, numbers, vec, x, mixed, *win_parts)
    mlp.take()
    mlp.start(3)
    mlp.swap_first()
    active, slope, *grads = line.run(rise, numbers, bias_in, second, top, *win_parts)
    line.wait(mlp.first)
    mlp.arrive()
    sum_mlp = Scatter(plan, line, "mlp", from_blocks(order, grads))
    mlp.swap_second()
    sum_mlp.start(3)
    mlp_parts = to_blocks(order, mlp.parts())
    gmiddle, sums, grad_bias_in, *grads = line.run(
        fall, numbers, vec, top, slope, second, middle, mlp_parts, win_parts
    )
    sum_mlp.arrive()
    sum_in = Scatter(plan, line, "in", from_blocks(order, grads))
    sum_mlp.start(2)
    sum_in.start(3)
    grad_inputs, sums_one, *grads = line.run(
        unattend, numbers, vec, x, gmiddle, project, probs, entry, mixed, win_parts, first_parts
    )
    sum_mlp.arrive()
    sum_in.arrive()
    sum_first = Scatter(plan, line, "first", from_blocks(order, grads))
    sum_in.start(2)
    sum_mlp.start(1)

    def pack(sums_one, sums, grad_bias_in):
        flat_gains = jnp.concatenate([sums_one[3], sums[0]]).reshape(-1, gain_dev)
        flat_biases = jnp.concatenate(
            [sums_one[4], sums_one[0], sums_one[2], sums[2], sums[1], sums[3], grad_bias_in[0]]
        ).reshape(-1, bias_dev)
        flat_small = jnp.concatenate([flat_gains, flat_biases], 1).astype(BF)
        moved = jnp.dot(one_hot(order), flat_small, preferred_element_type=F32).astype(BF)
        moved = jnp.pad(moved, ((0, 0), (0, rows * side - small_dev)))
        return moved.reshape(plan.devices, rows, side)

    sum_first.join(pack(sums_one, sums, grad_bias_in))
    sum_in.arrive()
    sum_first.start(3)
    sum_in.start(1)
    output = line.run(finish, vec, middle, active, *mlp_parts)
    sum_mlp.start(0)
    sum_in.start(0)
    sum_first.start(2)
    grad_mlp = sum_mlp.result()
    grad_in = sum_in.result()
    sum_first.start(1)
    sum_first.start(0)
    grad_first = sum_first.result()
    grad_small = grad_first[:, 4 * D :].reshape(1, -1)[:, :small_dev]
    return (
        output.reshape(blocks, length, D),
        grad_inputs.reshape(blocks, length, D),
        grad_small[:, :gain_dev],
        grad_small[:, gain_dev:],
        grad_first[:, : 3 * D].reshape(1, -1),
        grad_first[:, 3 * D : 4 * D].reshape(1, -1),
        grad_in.reshape(1, -1),
        grad_mlp.reshape(1, -1),
    )


def solution(mesh):
    plan = Plan(mesh)
    whole = P(AXES, None, None)
    flat = P(AXES, None)

    def body(*arrays):
        return per_device(plan, *arrays)

    return jax.shard_map(
        body,
        mesh=mesh,
        in_specs=(whole, flat, whole, flat, flat, flat, flat, flat, flat),
        out_specs=(whole, whole, flat, flat, flat, flat, flat, flat),
        check_vma=False,
    )
```

time: 388 us -> 363 us (0.936)
  the two profiles are of different devices: /device:TPU:8 before, /device:TPU:0 now
where the time goes in v4:
time: 363 us; the launch traced here: 357 us
  waiting for transfers between devices  159 us (44%)
  Pallas kernels  101 us (28%)
  other arithmetic  36.3 us (10%)
  starting transfers between devices  35.2 us (10%)
  local copies, waits for them, and re-layouts  23.3 us (6%)
    ppermute x37, waiting for transfers between devices, send(): return lax.ppermute(self.tie(array)[0], AXES, pairs)  159 us
    ppermute x37, starting transfers between devices, send(): return lax.ppermute(self.tie(array)[0], AXES, pairs)  35.2 us
    pallas_call x1, Pallas kernels, unattend(): pl.pallas_call(unattend_kernel, out_shape=[shape((count, D), F32), shape(...  29.7 us
    pallas_call x1, Pallas kernels, fall(): pl.pallas_call(fall_kernel, out_shape=[shape((count, D), F32), shape((8,...  25.5 us
    pallas_call x1, Pallas kernels, rise(): pl.pallas_call(rise_kernel, out_shape=[shape((count, FF), BF)] * 2 + [gra...  18.8 us
    unnamed x105, local copies, waits for them, and re-layouts  15.3 us
    convert_element_type x6, other arithmetic, start(): self.sum(low, low + self.count, parts).astype(BF)  12.9 us
    unnamed x8, other arithmetic  10.9 us
  transfers between devices with their start and end apart: 37, of which 22 were waited for; matrix products, arithmetic and copies ran while one was open for 12% of the time, Pallas kernels for 28%

profile of v4, /device:TPU:0, one launch (start us, length us, event | category | flops | bytes accessed | tf_op | source)
XLA Modules:
  0.0 357.1 jit_solution(5771686079720325777)
XLA Ops:
  3.6 4.1 %collective-permute-start = (bf16[1,32,3200]{2,1,0:T(8,128)(2,1)S(1)}, bf16[1,32,3200]{2,1,0:T(8,128)(2,1)S(1)}, u32[]{:S(2)}, u32[]{:S(2)}) collective-permute-start(bf16[1,32,3200]{2,1,0:T(8,128)(2,1)S(1)} %maximum_bitcast_fusion.2), channel_id=1, source_target_pairs={{0,4},{1,5},{2,6},{3,7},{4,0},{5,1},{6,2},{7,3},{8,12},{9,13},{10,... | collective-permute-start | bytes 614408 | tf_op jit(solution)/shard_map/gather_qkv_0/ppermute | solution.py:98
  11.6 5.5 %collective-permute-done = bf16[1,32,3200]{2,1,0:T(8,128)(2,1)S(1)} collective-permute-done((bf16[1,32,3200]{2,1,0:T(8,128)(2,1)S(1)}, bf16[1,32,3200]{2,1,0:T(8,128)(2,1)S(1)}, u32[]{:S(2)}, u32[]{:S(2)}) %collective-permute-start) | collective-permute-done | bytes 204832 | tf_op jit(solution)/shard_map/gather_qkv_0/ppermute | solution.py:98
  18.0 3.4 collective-permute-start.2
  21.5 13.5 %collective-permute-done.1 = bf16[2,32,3200]{2,1,0:T(8,128)(2,1)S(1)} collective-permute-done((bf16[2,32,3200]{2,1,0:T(8,128)(2,1)S(1)}, bf16[2,32,3200]{2,1,0:T(8,128)(2,1)S(1)}, u32[]{:S(2)}, u32[]{:S(2)}) %collective-permute-start.1) | collective-permute-done | bytes 409632 | tf_op jit(solution)/shard_map/gather_qkv_1/ppermute | solution.py:98
  36.4 3.3 collective-permute-start.4
  39.7 7.8 %collective-permute-done.3 = bf16[4,32,3200]{2,1,0:T(8,128)(2,1)S(1)} collective-permute-done((bf16[4,32,3200]{2,1,0:T(8,128)(2,1)S(1)}, bf16[4,32,3200]{2,1,0:T(8,128)(2,1)S(1)}, u32[]{:S(2)}, u32[]{:S(2)}) %collective-permute-start.3) | collective-permute-done | bytes 819232 | tf_op jit(solution)/shard_map/gather_qkv_2/ppermute | solution.py:98
  47.7 6.1 %collective-permute-done.4 = bf16[2,32,5120]{2,1,0:T(8,128)(2,1)S(1)} collective-permute-done((bf16[2,32,5120]{2,1,0:T(8,128)(2,1)S(1)}, bf16[2,32,5120]{2,1,0:T(8,128)(2,1)S(1)}, u32[]{:S(2)}, u32[]{:S(2)}) %collective-permute-start.4) | collective-permute-done | bytes 655392 | tf_op jit(solution)/shard_map/gather_in_1/ppermute | solution.py:98
  60.1 13.8 %collective-permute-done.7 = bf16[1,128,1024]{2,1,0:T(8,128)(2,1)S(1)} collective-permute-done((bf16[1,128,1024]{2,1,0:T(8,128)(2,1)S(1)}, bf16[1,128,1024]{2,1,0:T(8,128)(2,1)S(1)}, u32[]{:S(2)}, u32[]{:S(2)}) %collective-permute-start.7) | collective-permute-done | bytes 262176 | tf_op jit(solution)/shard_map/gather_mlp_0/ppermute | solution.py:98
  73.9 2.9 collective-permute-done.5.w1.f1
  85.4 8.0 %project.1 = (bf16[512,1024]{1,0:T(8,128)(2,1)S(1)}, bf16[512,3072]{1,0:T(8,128)(2,1)S(1)}) custom-call(s32[32]{0:T(128)S(1)} %fusion.21.order_ref, f32[8,1024]{1,0:T(8,128)S(1)} %slice.346.vec_ref, bf16[512,1024]{1,0:T(8,128)(2,1)S(1)} %bitcast.67, bf16[8,32,3200]{2,1,0:T(8,128)(2,1)S(1)} %constant_dynamic-update-slice_fusion.6.w0.f0, ...), custom_call_target="tpu_custom_call" | custom-call | tf_op jit(solution)/shard_map/project/pallas_call | solution.py:331
  93.4 2.8 collective-permute-done.10
  103.6 6.3 %attend.1 = (bf16[8,1024,256]{2,1,0:T(8,128)(2,1)S(1)}, bf16[512,1024]{1,0:T(8,128)(2,1)S(1)}) custom-call(bf16[512,3072]{1,0:T(8,128)(2,1)S(1)} %copy-done.5, s32[2,256]{1,0:T(2,128)S(1)} %copy-done.26, s32[512,1]{1,0:T(8,128)S(1)} %bitcast.69), custom_call_target="tpu_custom_call" | custom-call | tf_op jit(solution)/shard_map/attend/pallas_call | solution.py:373
  111.9 20.5 %collective-permute-done.11.w1 = bf16[8,32,5120]{2,1,0:T(8,128)(2,1)} collective-permute-done((bf16[8,32,5120]{2,1,0:T(8,128)(2,1)S(1)}, bf16[8,32,5120]{2,1,0:T(8,128)(2,1)}, u32[]{:S(2)}, u32[]{:S(2)}) %collective-permute-start.11) | collective-permute-done | bytes 2621472 | tf_op jit(solution)/shard_map/gather_in_3/ppermute | solution.py:98
  134.0 3.6 %collective-permute-done.13.w3 = bf16[8,32,5120]{2,1,0:T(8,128)(2,1)S(1)} collective-permute-done((bf16[8,32,5120]{2,1,0:T(8,128)(2,1)}, bf16[8,32,5120]{2,1,0:T(8,128)(2,1)S(1)}, u32[]{:S(2)}, u32[]{:S(2)}) %collective-permute-start.13) | collective-permute-done | bytes 2621472 | tf_op jit(solution)/shard_map/gather_in_swap_second/ppermute | solution.py:98
  137.6 4.7 %settle.1 = (f32[512,1024]{1,0:T(8,128)S(1)}, bf16[512,1024]{1,0:T(8,128)(2,1)S(1)}) custom-call(s32[32]{0:T(128)S(1)} %fusion.21.order_ref, f32[8,1024]{1,0:T(8,128)S(1)} %slice.346.vec_ref, bf16[512,1024]{1,0:T(8,128)(2,1)S(1)} %bitcast.68, bf16[512,1024]{1,0:T(8,128)(2,1)S(1)} %get-tuple-element.322.mixed_ref, ...), custom_call_target="tpu_custom_call" | custom-call | tf_op jit(solution)/shard_map/settle/pallas_call | solution.py:415
  142.3 4.9 %collective-permute-done.14 = bf16[4,128,1024]{2,1,0:T(8,128)(2,1)S(1)} collective-permute-done((bf16[4,128,1024]{2,1,0:T(8,128)(2,1)S(1)}, bf16[4,128,1024]{2,1,0:T(8,128)(2,1)S(1)}, u32[]{:S(2)}, u32[]{:S(2)}) %collective-permute-start.14) | collective-permute-done | bytes 1048608 | tf_op jit(solution)/shard_map/gather_mlp_2/ppermute | solution.py:98
  150.0 18.8 %rise.1 = (bf16[512,4096]{1,0:T(8,128)(2,1)}, bf16[512,4096]{1,0:T(8,128)(2,1)}, bf16[8,128,1024]{2,1,0:T(8,128)(2,1)S(1)}, bf16[8,128,1024]{2,1,0:T(8,128)(2,1)...) custom-call(s32[32]{0:T(128)S(1)} %fusion.21.order_ref, f32[1,4096]{1,0:T(1,128)S(1)} %bitcast.70, ...), custom_call_target="tpu_custom_call" | custom-call | tf_op jit(solution)/shard_map/rise/pallas_call | solution.py:476
  168.8 5.0 %collective-permute-done.15.m1.w1 = bf16[8,128,1024]{2,1,0:T(8,128)(2,1)} collective-permute-done((bf16[8,128,1024]{2,1,0:T(8,128)(2,1)S(1)}, bf16[8,128,1024]{2,1,0:T(8,128)(2,1)}, u32[]{:S(2)}, u32[]{:S(2)}) %collective-permute-start.15) | collective-permute-done | bytes 2097184 | tf_op jit(solution)/shard_map/gather_mlp_3/ppermute | solution.py:98
  174.3 3.9 %collective-permute-done.18 = bf16[8,128,1024]{2,1,0:T(8,128)(2,1)S(1)} collective-permute-done((bf16[8,128,1024]{2,1,0:T(8,128)(2,1)}, bf16[8,128,1024]{2,1,0:T(8,128)(2,1)S(1)}, u32[]{:S(2)}, u32[]{:S(2)}) %collective-permute-start.18) | collective-permute-done | bytes 2097184 | tf_op jit(solution)/shard_map/sum_mlp_swap_high/ppermute | solution.py:98
  178.1 4.0 %add.188 = bf16[8,128,1024]{2,1,0:T(8,128)(2,1)} add(bf16[8,128,1024]{2,1,0:T(8,128)(2,1)} %get-tuple-element.282, bf16[8,128,1024]{2,1,0:T(8,128)(2,1)S(1)} %collective-permute-done.18) | non-fusion elementwise | flops 1048576 | bytes 6291456 | tf_op jit(solution)/shard_map/add | solution.py:144
  184.8 25.5 %fall.1 = (f32[512,1024]{1,0:T(8,128)}, f32[8,1024]{1,0:T(8,128)}, f32[1,4096]{1,0:T(1,128)}, bf16[8,32,4096]{2,1,0:T(8,128)(2,1)}, bf16[8,32,4096]{2,1,0:T(8,12...) custom-call(s32[32]{0:T(128)} %copy-done.24, f32[8,1024]{1,0:T(8,128)} %copy-done.21, ...), custom_call_target="tpu_custom_call" | custom-call | tf_op jit(solution)/shard_map/fall/pallas_call | solution.py:581
  210.4 3.3 add_convert_fusion.2
  218.3 29.7 %unattend.1 = (f32[512,1024]{1,0:T(8,128)}, f32[8,1024]{1,0:T(8,128)}, bf16[8,32,4096]{2,1,0:T(8,128)(2,1)}, bf16[8,32,4096]{2,1,0:T(8,128)(2,1)}, bf16[8,32,409...) custom-call(s32[32]{0:T(128)} %copy-done.24, f32[8,1024]{1,0:T(8,128)} %copy-done.21, bf16[512,1024]{1,0:T(8,128)(2,1)} %bitcast.66, ...), custom_call_target="tpu_custom_call" | custom-call | tf_op jit(solution)/shard_map/unattend/pallas_call | solution.py:700
  249.0 4.2 %collective-permute-done.23 = bf16[8,32,4096]{2,1,0:T(8,128)(2,1)} collective-permute-done((bf16[8,32,4096]{2,1,0:T(8,128)(2,1)S(1)}, bf16[8,32,4096]{2,1,0:T(8,128)(2,1)}, u32[]{:S(2)}, u32[]{:S(2)}) %collective-permute-start.23) | collective-permute-done | bytes 2097184 | tf_op jit(solution)/shard_map/sum_in_3/ppermute | solution.py:98
  253.2 3.1 add_convert_fusion.1
  261.7 9.8 %collective-permute-done.25 = bf16[4,32,4096]{2,1,0:T(8,128)(2,1)} collective-permute-done((bf16[4,32,4096]{2,1,0:T(8,128)(2,1)}, bf16[4,32,4096]{2,1,0:T(8,128)(2,1)}, u32[]{:S(2)}, u32[]{:S(2)}) %collective-permute-start.25) | collective-permute-done | bytes 1048608 | tf_op jit(solution)/shard_map/sum_in_2/ppermute | solution.py:98
  271.5 2.5 add.197
  279.1 7.9 %finish.1 = bf16[512,1024]{1,0:T(8,128)(2,1)} custom-call(f32[8,1024]{1,0:T(8,128)S(1)} %copy-done.22, f32[512,1024]{1,0:T(8,128)S(1)} %copy-done.11, bf16[512,4096]{1,0:T(8,128)(2,1)S(1)} %copy-done.18, bf16[8,128,1024]{2,1,0:T(8,128)(2,1)S(1)} %copy-done.3, bf16[8,128,1024]{2,1,0:T(8,128)(2,1)} %collective-permute-done.15.m1.w1, ...), custom_call_target="tpu_custom_call" | custom-call | tf_op jit(solution)/shard_map/finish/pallas_call | solution.py:755
  291.6 9.5 %collective-permute-done.29 = bf16[8,32,4224]{2,1,0:T(8,128)(2,1)S(1)} collective-permute-done((bf16[8,32,4224]{2,1,0:T(8,128)(2,1)S(1)}, bf16[8,32,4224]{2,1,0:T(8,128)(2,1)S(1)}, u32[]{:S(2)}, u32[]{:S(2)}) %collective-permute-start.29) | collective-permute-done | bytes 2162720 | tf_op jit(solution)/shard_map/sum_first_3/ppermute | solution.py:98
  305.5 17.2 %collective-permute-done.35 = bf16[1,32,4096]{2,1,0:T(8,128)(2,1)S(1)} collective-permute-done((bf16[1,32,4096]{2,1,0:T(8,128)(2,1)S(1)}, bf16[1,32,4096]{2,1,0:T(8,128)(2,1)S(1)}, u32[]{:S(2)}, u32[]{:S(2)}) %collective-permute-start.35) | collective-permute-done | bytes 262176 | tf_op jit(solution)/shard_map/sum_in_0/ppermute | solution.py:98
  327.0 11.5 %collective-permute-done.33 = bf16[2,32,4224]{2,1,0:T(8,128)(2,1)S(1)} collective-permute-done((bf16[2,32,4224]{2,1,0:T(8,128)(2,1)S(1)}, bf16[2,32,4224]{2,1,0:T(8,128)(2,1)S(1)}, u32[]{:S(2)}, u32[]{:S(2)}) %collective-permute-start.33) | collective-permute-done | bytes 540704 | tf_op jit(solution)/shard_map/sum_first_1/ppermute | solution.py:98
  341.7 11.8 %collective-permute-done.34 = bf16[1,32,4224]{2,1,0:T(8,128)(2,1)S(1)} collective-permute-done((bf16[1,32,4224]{2,1,0:T(8,128)(2,1)S(1)}, bf16[1,32,4224]{2,1,0:T(8,128)(2,1)S(1)}, u32[]{:S(2)}, u32[]{:S(2)}) %collective-permute-start.34) | collective-permute-done | bytes 270368 | tf_op jit(solution)/shard_map/sum_first_0/ppermute | solution.py:98
  (232 shorter events, 76.3 us)
Async XLA Ops:
  3.6 13.6 %collective-permute-start = (bf16[1,32,3200]{2,1,0:T(8,128)(2,1)S(1)}, bf16[1,32,3200]{2,1,0:T(8,128)(2,1)S(1)}, u32[]{:S(2)}, u32[]{:S(2)}) collective-permute-start(bf16[1,32,3200]{2,1,0:T(8,128)(2,1)S(1)} %maximum_bitcast_fusion.2), channel_id=1, source_target_pairs={{0,4},{1,5},{2,6},{3,7},{4,0},{5,1},{6,2},{7,3},{8,12},{9,13},{10,... | collective-permute-start | bytes 614408 | tf_op jit(solution)/shard_map/gather_qkv_0/ppermute | solution.py:98
  17.2 17.7 %collective-permute-start.1 = (bf16[2,32,3200]{2,1,0:T(8,128)(2,1)S(1)}, bf16[2,32,3200]{2,1,0:T(8,128)(2,1)S(1)}, u32[]{:S(2)}, u32[]{:S(2)}) collective-permute-start(bf16[2,32,3200]{2,1,0:T(8,128)(2,1)S(1)} %constant_dynamic-update-slice_fusion), channel_id=1, source_target_pairs={{0,2},{1,3},{2,0},{3,1},{4,6},{5,7},{6,4},{7,5},{8,10},{9,11},{10,... | collective-permute-start | bytes 1228808 | tf_op jit(solution)/shard_map/gather_qkv_1/ppermute | solution.py:98
  18.0 17.0 %collective-permute-start.2 = (bf16[1,32,5120]{2,1,0:T(8,128)(2,1)S(1)}, bf16[1,32,5120]{2,1,0:T(8,128)(2,1)S(1)}, u32[]{:S(2)}, u32[]{:S(2)}) collective-permute-start(bf16[1,32,5120]{2,1,0:T(8,128)(2,1)S(1)} %maximum_bitcast_fusion.1), channel_id=1, source_target_pairs={{0,4},{1,5},{2,6},{3,7},{4,0},{5,1},{6,2},{7,3},{8,12},{9,13},{10,... | collective-permute-start | bytes 983048 | tf_op jit(solution)/shard_map/gather_in_0/ppermute | solution.py:98
  35.1 12.4 %collective-permute-start.3 = (bf16[4,32,3200]{2,1,0:T(8,128)(2,1)S(1)}, bf16[4,32,3200]{2,1,0:T(8,128)(2,1)S(1)}, u32[]{:S(2)}, u32[]{:S(2)}) collective-permute-start(bf16[4,32,3200]{2,1,0:T(8,128)(2,1)S(1)} %constant_dynamic-update-slice_fusion.2), channel_id=1, source_target_pairs={{0,1},{1,0},{2,3},{3,2},{4,5},{5,4},{6,7},{7,6},{8,24},{9,25},{10,... | collective-permute-start | bytes 2457608 | tf_op jit(solution)/shard_map/gather_qkv_2/ppermute | solution.py:98
  36.4 17.4 %collective-permute-start.4 = (bf16[2,32,5120]{2,1,0:T(8,128)(2,1)S(1)}, bf16[2,32,5120]{2,1,0:T(8,128)(2,1)S(1)}, u32[]{:S(2)}, u32[]{:S(2)}) collective-permute-start(bf16[2,32,5120]{2,1,0:T(8,128)(2,1)S(1)} %constant_dynamic-update-slice_fusion.4), channel_id=1, source_target_pairs={{0,2},{1,3},{2,0},{3,1},{4,6},{5,7},{6,4},{7,5},{8,10},{9,11},{10,... | collective-permute-start | bytes 1966088 | tf_op jit(solution)/shard_map/gather_in_1/ppermute | solution.py:98
  55.6 21.2 %collective-permute-start.5 = (bf16[8,32,3200]{2,1,0:T(8,128)(2,1)S(1)}, bf16[8,32,3200]{2,1,0:T(8,128)(2,1)}, u32[]{:S(2)}, u32[]{:S(2)}) collective-permute-start(bf16[8,32,3200]{2,1,0:T(8,128)(2,1)S(1)} %constant_dynamic-update-slice_fusion.6.w0.f0), channel_id=1, source_target_pairs={{0,16},{1,17},{2,18},{3,19},{4,20},{5,21},{6,22},{7,23},{8,9},{9,8... | collective-permute-start | bytes 4915208 | tf_op jit(solution)/shard_map/gather_qkv_3/ppermute | solution.py:98
  58.7 15.2 %collective-permute-start.7 = (bf16[1,128,1024]{2,1,0:T(8,128)(2,1)S(1)}, bf16[1,128,1024]{2,1,0:T(8,128)(2,1)S(1)}, u32[]{:S(2)}, u32[]{:S(2)}) collective-permute-start(bf16[1,128,1024]{2,1,0:T(8,128)(2,1)S(1)} %broadcast_in_dim_reshape.3), channel_id=1, source_target_pairs={{0,4},{1,5},{2,6},{3,7},{4,0},{5,1},{6,2},{7,3},{8,12},{9,13},{10,... | collective-permute-start | bytes 786440 | tf_op jit(solution)/shard_map/gather_mlp_0/ppermute | solution.py:98
  60.1 21.5 %collective-permute-start.6 = (bf16[8,32,3200]{2,1,0:T(8,128)(2,1)S(1)}, bf16[8,32,3200]{2,1,0:T(8,128)(2,1)}, u32[]{:S(2)}, u32[]{:S(2)}) collective-permute-start(bf16[8,32,3200]{2,1,0:T(8,128)(2,1)S(1)} %constant_dynamic-update-slice_fusion.6.w0.f0), channel_id=1, source_target_pairs={{0,8},{1,9},{2,10},{3,11},{4,12},{5,13},{6,14},{7,15},{8,0},{9,1},... | collective-permute-start | bytes 4915208 | tf_op jit(solution)/shard_map/gather_qkv_swap_first/ppermute | solution.py:98
  78.2 17.9 %collective-permute-start.10 = (bf16[4,32,5120]{2,1,0:T(8,128)(2,1)}, bf16[4,32,5120]{2,1,0:T(8,128)(2,1)}, u32[]{:S(2)}, u32[]{:S(2)}) collective-permute-start(bf16[4,32,5120]{2,1,0:T(8,128)(2,1)} %constant_dynamic-update-slice_fusion.8), channel_id=1, source_target_pairs={{0,1},{1,0},{2,3},{3,2},{4,5},{5,4},{6,7},{7,6},{8,24},{9,25},{10,... | collective-permute-start | bytes 3932168 | tf_op jit(solution)/shard_map/gather_in_2/ppermute | solution.py:98
  79.8 19.3 %collective-permute-start.9 = (bf16[2,128,1024]{2,1,0:T(8,128)(2,1)}, bf16[2,128,1024]{2,1,0:T(8,128)(2,1)S(1)}, u32[]{:S(2)}, u32[]{:S(2)}) collective-permute-start(bf16[2,128,1024]{2,1,0:T(8,128)(2,1)} %constant_dynamic-update-slice_fusion.10), channel_id=1, source_target_pairs={{0,2},{1,3},{2,0},{3,1},{4,6},{5,7},{6,4},{7,5},{8,10},{9,11},{10,... | collective-permute-start | bytes 1572872 | tf_op jit(solution)/shard_map/gather_mlp_1/ppermute | solution.py:98
  100.6 11.4 %collective-permute-start.12 = (bf16[8,32,5120]{2,1,0:T(8,128)(2,1)S(1)}, bf16[8,32,5120]{2,1,0:T(8,128)(2,1)}, u32[]{:S(2)}, u32[]{:S(2)}) collective-permute-start(bf16[8,32,5120]{2,1,0:T(8,128)(2,1)S(1)} %constant_dynamic-update-slice_fusion.12.w0), channel_id=1, source_target_pairs={{0,8},{1,9},{2,10},{3,11},{4,12},{5,13},{6,14},{7,15},{8,0},{9,1},... | collective-permute-start | bytes 7864328 | tf_op jit(solution)/shard_map/gather_in_swap_first/ppermute | solution.py:98
  100.7 31.8 %collective-permute-start.11 = (bf16[8,32,5120]{2,1,0:T(8,128)(2,1)S(1)}, bf16[8,32,5120]{2,1,0:T(8,128)(2,1)}, u32[]{:S(2)}, u32[]{:S(2)}) collective-permute-start(bf16[8,32,5120]{2,1,0:T(8,128)(2,1)S(1)} %constant_dynamic-update-slice_fusion.12.w0), channel_id=1, source_target_pairs={{0,16},{1,17},{2,18},{3,19},{4,20},{5,21},{6,22},{7,23},{8,9},{9,8... | collective-permute-start | bytes 7864328 | tf_op jit(solution)/shard_map/gather_in_3/ppermute | solution.py:98
  132.5 14.8 %collective-permute-start.14 = (bf16[4,128,1024]{2,1,0:T(8,128)(2,1)S(1)}, bf16[4,128,1024]{2,1,0:T(8,128)(2,1)S(1)}, u32[]{:S(2)}, u32[]{:S(2)}) collective-permute-start(bf16[4,128,1024]{2,1,0:T(8,128)(2,1)S(1)} %copy-done.28), channel_id=1, source_target_pairs={{0,1},{1,0},{2,3},{3,2},{4,5},{5,4},{6,7},{7,6},{8,24},{9,25},{10,... | collective-permute-start | bytes 3145736 | tf_op jit(solution)/shard_map/gather_mlp_2/ppermute | solution.py:98
  147.5 21.3 %collective-permute-start.16 = (bf16[8,128,1024]{2,1,0:T(8,128)(2,1)S(1)}, bf16[8,128,1024]{2,1,0:T(8,128)(2,1)}, u32[]{:S(2)}, u32[]{:S(2)}) collective-permute-start(bf16[8,128,1024]{2,1,0:T(8,128)(2,1)S(1)} %constant_dynamic-update-slice_fusion.16.m0.w0), channel_id=1, source_target_pairs={{0,8},{1,9},{2,10},{3,11},{4,12},{5,13},{6,14},{7,15},{8,0},{9,1},... | collective-permute-start | bytes 6291464 | tf_op jit(solution)/shard_map/gather_mlp_swap_first/ppermute | solution.py:98
  147.6 26.2 %collective-permute-start.15 = (bf16[8,128,1024]{2,1,0:T(8,128)(2,1)S(1)}, bf16[8,128,1024]{2,1,0:T(8,128)(2,1)}, u32[]{:S(2)}, u32[]{:S(2)}) collective-permute-start(bf16[8,128,1024]{2,1,0:T(8,128)(2,1)S(1)} %constant_dynamic-update-slice_fusion.16.m0.w0), channel_id=1, source_target_pairs={{0,16},{1,17},{2,18},{3,19},{4,20},{5,21},{6,22},{7,23},{8,9},{9,8... | collective-permute-start | bytes 6291464 | tf_op jit(solution)/shard_map/gather_mlp_3/ppermute | solution.py:98
  173.8 9.8 %collective-permute-start.17 = (bf16[8,128,1024]{2,1,0:T(8,128)(2,1)}, bf16[8,128,1024]{2,1,0:T(8,128)(2,1)S(1)}, u32[]{:S(2)}, u32[]{:S(2)}) collective-permute-start(bf16[8,128,1024]{2,1,0:T(8,128)(2,1)} %collective-permute-done.15.m1.w1), channel_id=1, source_target_pairs={{0,8},{1,9},{2,10},{3,11},{4,12},{5,13},{6,14},{7,15},{8,0},{9,1},... | collective-permute-start | bytes 6291464 | tf_op jit(solution)/shard_map/gather_mlp_swap_second/ppermute | solution.py:98
  182.2 28.1 %collective-permute-start.19 = (bf16[8,128,1024]{2,1,0:T(8,128)(2,1)}, bf16[8,128,1024]{2,1,0:T(8,128)(2,1)}, u32[]{:S(2)}, u32[]{:S(2)}) collective-permute-start(bf16[8,128,1024]{2,1,0:T(8,128)(2,1)} %add.188), channel_id=1, source_target_pairs={{0,16},{1,17},{2,18},{3,19},{4,20},{5,21},{6,22},{7,23},{8,9},{9,8... | collective-permute-start | bytes 6291464 | tf_op jit(solution)/shard_map/sum_mlp_3/ppermute | solution.py:98
  182.7 27.7 %collective-permute-start.22 = (bf16[8,128,1024]{2,1,0:T(8,128)(2,1)S(1)}, bf16[8,128,1024]{2,1,0:T(8,128)(2,1)}, u32[]{:S(2)}, u32[]{:S(2)}) collective-permute-start(bf16[8,128,1024]{2,1,0:T(8,128)(2,1)S(1)} %copy-done.38), channel_id=1, source_target_pairs={{0,8},{1,9},{2,10},{3,11},{4,12},{5,13},{6,14},{7,15},{8,0},{9,1},... | collective-permute-start | bytes 6291464 | tf_op jit(solution)/shard_map/sum_mlp_swap_low/ppermute | solution.py:98
  215.8 37.4 %collective-permute-start.23 = (bf16[8,32,4096]{2,1,0:T(8,128)(2,1)S(1)}, bf16[8,32,4096]{2,1,0:T(8,128)(2,1)}, u32[]{:S(2)}, u32[]{:S(2)}) collective-permute-start(bf16[8,32,4096]{2,1,0:T(8,128)(2,1)S(1)} %add.191), channel_id=1, source_target_pairs={{0,16},{1,17},{2,18},{3,19},{4,20},{5,21},{6,22},{7,23},{8,9},{9,8... | collective-permute-start | bytes 6291464 | tf_op jit(solution)/shard_map/sum_in_3/ppermute | solution.py:98
  216.6 36.6 %collective-permute-start.20 = (bf16[8,32,4096]{2,1,0:T(8,128)(2,1)}, bf16[8,32,4096]{2,1,0:T(8,128)(2,1)}, u32[]{:S(2)}, u32[]{:S(2)}) collective-permute-start(bf16[8,32,4096]{2,1,0:T(8,128)(2,1)} %get-tuple-element.302), channel_id=1, source_target_pairs={{0,8},{1,9},{2,10},{3,11},{4,12},{5,13},{6,14},{7,15},{8,0},{9,1},... | collective-permute-start | bytes 6291464 | tf_op jit(solution)/shard_map/sum_in_swap_low/ppermute | solution.py:98
  216.7 32.3 %collective-permute-start.24 = (bf16[4,128,1024]{2,1,0:T(8,128)(2,1)}, bf16[4,128,1024]{2,1,0:T(8,128)(2,1)S(1)}, u32[]{:S(2)}, u32[]{:S(2)}) collective-permute-start(bf16[4,128,1024]{2,1,0:T(8,128)(2,1)} %add_convert_fusion.2), channel_id=1, source_target_pairs={{0,1},{1,0},{2,3},{3,2},{4,5},{5,4},{6,7},{7,6},{8,24},{9,25},{10,... | collective-permute-start | bytes 3145736 | tf_op jit(solution)/shard_map/sum_mlp_2/ppermute | solution.py:98
  253.2 18.3 %collective-permute-start.26 = (bf16[8,32,4096]{2,1,0:T(8,128)(2,1)}, bf16[8,32,4096]{2,1,0:T(8,128)(2,1)}, u32[]{:S(2)}, u32[]{:S(2)}) collective-permute-start(bf16[8,32,4096]{2,1,0:T(8,128)(2,1)} %get-tuple-element.339), channel_id=1, source_target_pairs={{0,8},{1,9},{2,10},{3,11},{4,12},{5,13},{6,14},{7,15},{8,0},{9,1},... | collective-permute-start | bytes 6291464 | tf_op jit(solution)/shard_map/sum_first_swap_high/ppermute | solution.py:98
  256.4 15.1 %collective-permute-start.25 = (bf16[4,32,4096]{2,1,0:T(8,128)(2,1)}, bf16[4,32,4096]{2,1,0:T(8,128)(2,1)}, u32[]{:S(2)}, u32[]{:S(2)}) collective-permute-start(bf16[4,32,4096]{2,1,0:T(8,128)(2,1)} %add_convert_fusion.1), channel_id=1, source_target_pairs={{0,1},{1,0},{2,3},{3,2},{4,5},{5,4},{6,7},{7,6},{8,24},{9,25},{10,... | collective-permute-start | bytes 3145736 | tf_op jit(solution)/shard_map/sum_in_2/ppermute | solution.py:98
  259.6 32.0 %collective-permute-start.28 = (bf16[8,32,4096]{2,1,0:T(8,128)(2,1)}, bf16[8,32,4096]{2,1,0:T(8,128)(2,1)S(1)}, u32[]{:S(2)}, u32[]{:S(2)}) collective-permute-start(bf16[8,32,4096]{2,1,0:T(8,128)(2,1)} %get-tuple-element.363), channel_id=1, source_target_pairs={{0,8},{1,9},{2,10},{3,11},{4,12},{5,13},{6,14},{7,15},{8,0},{9,1},... | collective-permute-start | bytes 6291464 | tf_op jit(solution)/shard_map/sum_first_swap_low/ppermute | solution.py:98
  259.9 27.1 %collective-permute-start.31 = (bf16[2,128,1024]{2,1,0:T(8,128)(2,1)S(1)}, bf16[2,128,1024]{2,1,0:T(8,128)(2,1)S(1)}, u32[]{:S(2)}, u32[]{:S(2)}) collective-permute-start(bf16[2,128,1024]{2,1,0:T(8,128)(2,1)S(1)} %add_convert_fusion.5), channel_id=1, source_target_pairs={{0,2},{1,3},{2,0},{3,1},{4,6},{5,7},{6,4},{7,5},{8,10},{9,11},{10,... | collective-permute-start | bytes 1572872 | tf_op jit(solution)/shard_map/sum_mlp_1/ppermute | solution.py:98
  274.3 26.8 %collective-permute-start.29 = (bf16[8,32,4224]{2,1,0:T(8,128)(2,1)S(1)}, bf16[8,32,4224]{2,1,0:T(8,128)(2,1)S(1)}, u32[]{:S(2)}, u32[]{:S(2)}) collective-permute-start(bf16[8,32,4224]{2,1,0:T(8,128)(2,1)S(1)} %pad_maximum_fusion), channel_id=1, source_target_pairs={{0,16},{1,17},{2,18},{3,19},{4,20},{5,21},{6,22},{7,23},{8,9},{9,8... | collective-permute-start | bytes 6488072 | tf_op jit(solution)/shard_map/sum_first_3/ppermute | solution.py:98
  277.2 13.1 %collective-permute-start.30 = (bf16[2,32,4096]{2,1,0:T(8,128)(2,1)S(1)}, bf16[2,32,4096]{2,1,0:T(8,128)(2,1)S(1)}, u32[]{:S(2)}, u32[]{:S(2)}) collective-permute-start(bf16[2,32,4096]{2,1,0:T(8,128)(2,1)S(1)} %add_convert_fusion.4), channel_id=1, source_target_pairs={{0,2},{1,3},{2,0},{3,1},{4,6},{5,7},{6,4},{7,5},{8,10},{9,11},{10,... | collective-permute-start | bytes 1572872 | tf_op jit(solution)/shard_map/sum_in_1/ppermute | solution.py:98
  301.6 21.1 %collective-permute-start.32 = (bf16[4,32,4224]{2,1,0:T(8,128)(2,1)S(1)}, bf16[4,32,4224]{2,1,0:T(8,128)(2,1)S(1)}, u32[]{:S(2)}, u32[]{:S(2)}) collective-permute-start(bf16[4,32,4224]{2,1,0:T(8,128)(2,1)S(1)} %pad_maximum_fusion.1), channel_id=1, source_target_pairs={{0,1},{1,0},{2,3},{3,2},{4,5},{5,4},{6,7},{7,6},{8,24},{9,25},{10,... | collective-permute-start | bytes 3244040 | tf_op jit(solution)/shard_map/sum_first_2/ppermute | solution.py:98
  302.4 20.2 %collective-permute-start.35 = (bf16[1,32,4096]{2,1,0:T(8,128)(2,1)S(1)}, bf16[1,32,4096]{2,1,0:T(8,128)(2,1)S(1)}, u32[]{:S(2)}, u32[]{:S(2)}) collective-permute-start(bf16[1,32,4096]{2,1,0:T(8,128)(2,1)S(1)} %add_convert_fusion.7), channel_id=1, source_target_pairs={{0,4},{1,5},{2,6},{3,7},{4,0},{5,1},{6,2},{7,3},{8,12},{9,13},{10,... | collective-permute-start | bytes 786440 | tf_op jit(solution)/shard_map/sum_in_0/ppermute | solution.py:98
  303.8 23.3 %collective-permute-start.36 = (bf16[1,128,1024]{2,1,0:T(8,128)(2,1)S(1)}, bf16[1,128,1024]{2,1,0:T(8,128)(2,1)S(1)}, u32[]{:S(2)}, u32[]{:S(2)}) collective-permute-start(bf16[1,128,1024]{2,1,0:T(8,128)(2,1)S(1)} %add_convert_fusion.8), channel_id=1, source_target_pairs={{0,4},{1,5},{2,6},{3,7},{4,0},{5,1},{6,2},{7,3},{8,12},{9,13},{10,... | collective-permute-start | bytes 786440 | tf_op jit(solution)/shard_map/sum_mlp_0/ppermute | solution.py:98
  323.0 15.5 %collective-permute-start.33 = (bf16[2,32,4224]{2,1,0:T(8,128)(2,1)S(1)}, bf16[2,32,4224]{2,1,0:T(8,128)(2,1)S(1)}, u32[]{:S(2)}, u32[]{:S(2)}) collective-permute-start(bf16[2,32,4224]{2,1,0:T(8,128)(2,1)S(1)} %pad_maximum_fusion.2), channel_id=1, source_target_pairs={{0,2},{1,3},{2,0},{3,1},{4,6},{5,7},{6,4},{7,5},{8,10},{9,11},{10,... | collective-permute-start | bytes 1622024 | tf_op jit(solution)/shard_map/sum_first_1/ppermute | solution.py:98
  338.8 14.7 %collective-permute-start.34 = (bf16[1,32,4224]{2,1,0:T(8,128)(2,1)S(1)}, bf16[1,32,4224]{2,1,0:T(8,128)(2,1)S(1)}, u32[]{:S(2)}, u32[]{:S(2)}) collective-permute-start(bf16[1,32,4224]{2,1,0:T(8,128)(2,1)S(1)} %pad_maximum_fusion.3), channel_id=1, source_target_pairs={{0,4},{1,5},{2,6},{3,7},{4,0},{5,1},{6,2},{7,3},{8,12},{9,13},{10,... | collective-permute-start | bytes 811016 | tf_op jit(solution)/shard_map/sum_first_0/ppermute | solution.py:98
  (44 other events, 630.5 us)

commit v5 on v4

--- a/solution.py
+++ b/solution.py
@@ -27,7 +27,7 @@
 
 
 class Plan:
-    def __init__(self, mesh):
+    def __init__(self, mesh, late=False):
         outer, inner = mesh.shape["dp"], mesh.shape["fsdp"]
         ys = outer // 2
         xs = min(ys, inner)
@@ -46,11 +46,18 @@
         zbits = bits(zs, xs)
         self.core = inner
         ybits = bits(ys, 2 * inner)
-        self.orders = (zbits + xbits + ybits, zbits + ybits + xbits)
-        self.legs = [list(range(1)), list(range(1, len(zbits)))]
-        for _ in range(2):
-            start = self.legs[-1][-1] + 1
-            self.legs.append(list(range(start, start + len(xbits))))
+        self.late = late
+        z_legs, xy_legs = [1, len(zbits) - 1], [len(xbits)] * 2
+        if late:
+            self.orders = (xbits + ybits + zbits, ybits + xbits + zbits)
+            lengths = xy_legs + z_legs
+        else:
+            self.orders = (zbits + xbits + ybits, zbits + ybits + xbits)
+            lengths = z_legs + xy_legs
+        self.legs = []
+        for length in lengths:
+            start = self.legs[-1][-1] + 1 if self.legs else 0
+            self.legs.append(list(range(start, start + length)))
 
     def pairs(self, stage):
         return [
@@ -491,12 +498,33 @@
     )(order, bias, second, top, *win)
 
 
-def part_fetches(part_refs, held_ref, sems):
-    apiece = part_refs[0].shape[0]
-    return [
-        pltpu.make_async_copy(part, held_ref.at[pl.ds(i * apiece, apiece)], sems.at[i])
-        for i, part in enumerate(part_refs)
+def mlp_fetches(spot_ref, early_refs, late_refs, held_ref, sems):
+    apiece, _, width = early_refs[0].shape
+    early = [
+        pltpu.make_async_copy(
+            part, held_ref.at[pl.ds(i * apiece, apiece), :, pl.ds(0, width)], sems.at[BLOCKS + i]
+        )
+        for i, part in enumerate(early_refs)
     ]
+    late = [
+        pltpu.make_async_copy(
+            late_refs[place // apiece].at[place % apiece],
+            held_ref.at[spot_ref[place], :, pl.ds(width, width)],
+            sems.at[spot_ref[place]],
+        )
+        for place in range(BLOCKS)
+    ]
+    return early, late
+
+
+def start(copies):
+    for copy in copies:
+        copy.start()
+
+
+def wait(copies):
+    for copy in copies:
+        copy.wait()
 
 
 def block_rows(order_ref, ref, part, apiece, rows):
@@ -506,13 +534,12 @@
 
 
 def fall_kernel(
-    order_ref, vec_ref, top_ref, slope_ref, second_ref, middle_ref,
-    m0, m1, m2, m3, w0, w1, w2, w3,
-    gmiddle_ref, sums_ref, bias_ref, g0, g1, g2, g3,
-    mheld, held, slope, ghidden, turned, middle, gsecond, grads,
-    msems, sems, tile_sems, out_sems,
+    order_ref, spot_ref, top_ref, slope_ref, second_ref,
+    m0, m1, m2, m3, l0, l1, l2, l3,
+    ghidden_ref, bias_ref, g0, g1, g2, g3,
+    mheld, slope, ghidden, turned, grads, msems, tile_sems, out_sems,
 ):
-    copies = part_fetches((m0, m1, m2, m3), mheld, msems)
+    copies, late = mlp_fetches(spot_ref, (m0, m1, m2, m3), (l0, l1, l2, l3), mheld, msems)
     apiece, rows, _ = g0.shape
     places = TILE // PIECE
     slopes = [
@@ -524,12 +551,10 @@
     for i in range(4):
         copies[i].start()
         slopes[i].start()
-    later = fetches(order_ref, (w0, w1, w2, w3), held, sems)
-    later.append(pltpu.make_async_copy(middle_ref, middle, tile_sems.at[4]))
-    for copy in later:
-        copy.start()
+        if i == 0:
+            for copy in late:
+                copy.start()
     turned[...] = second_ref[...].T
-    sums_ref[...] = jnp.zeros_like(sums_ref)
 
     @each(FF // TILE)
     def _(step):
@@ -537,6 +562,10 @@
         if step * places % apiece == 0:
             copies[part].wait()
             slopes[part].wait()
+        for place in range(step * places, (step + 1) * places):
+            pltpu.make_async_copy(
+                l0.at[0], mheld.at[place, :, pl.ds(D // 2, D // 2)], msems.at[place]
+            ).wait()
         weight = mheld[pl.ds(step * places, places)].reshape(TILE, D)
         grad_active = dot_nt(top_ref[...], weight)
         grad = grad_active * slope[:, span(step, TILE)].astype(F32)
@@ -547,12 +576,8 @@
             ghidden[:, piece(number)] = low[:, j * PIECE : (j + 1) * PIECE]
             bias_ref[:, piece(number)] = sums[:, j * PIECE : (j + 1) * PIECE]
 
-    for copy in later:
-        copy.wait()
-    for i in range(D // WIDE):
-        gsecond[:, span(i, WIDE)] = dot_nt(ghidden[...], held[span(i, WIDE), :])
-    outs = []
-    chunk = middle_ref.shape[0] // 4
+    outs = [pltpu.make_async_copy(ghidden, ghidden_ref, out_sems.at[4])]
+    start(outs)
     for part in (3, 2, 1, 0):
         left = block_rows(order_ref, turned, part, apiece, rows)
         for i in range(FF // TILE):
@@ -561,52 +586,98 @@
         copy = pltpu.make_async_copy(grads.at[part], (g0, g1, g2, g3)[part], out_sems.at[part])
         copy.start()
         outs.append(copy)
-        places_of = span(part, chunk)
-        normed, inverse = norm_parts(middle[places_of, :])
-        grad = gsecond[places_of, :]
-        top = top_ref[places_of, :].astype(F32)
-        gmiddle = top + norm_back(grad * vec_ref[1:2, :], normed, inverse)
-        gmiddle_ref[places_of, :] = gmiddle
-        low = gmiddle.astype(BF).astype(F32)
-        for row, value in enumerate((grad * normed, grad, low, top)):
-            sums_ref[row : row + 1, :] += jnp.sum(value, axis=0, keepdims=True)
     for copy in outs:
         copy.wait()
 
 
-def fall(order, vec, top, slope, second, middle, mlp, win):
+def fall(order, spot, top, slope, second, *mlp):
     count = second.shape[0]
     shape = jax.ShapeDtypeStruct
     grad = shape((BLOCKS // 4, D // BLOCKS, FF), BF)
     return pl.pallas_call(
         fall_kernel,
-        out_shape=[shape((count, D), F32), shape((8, D), F32), shape((1, FF), F32)] + [grad] * 4,
-        in_specs=[SMEM, VMEM, VMEM, ANY, VMEM, ANY] + [ANY] * 8,
-        out_specs=[VMEM] * 3 + [ANY] * 4,
+        out_shape=[shape((count, FF), BF), shape((1, FF), F32)] + [grad] * 4,
+        in_specs=[SMEM, SMEM, VMEM, ANY, VMEM] + [ANY] * 8,
+        out_specs=[ANY, VMEM] + [ANY] * 4,
         scratch_shapes=[
             pltpu.VMEM((BLOCKS, PIECE, D), BF),
-            pltpu.VMEM((D, FF), BF),
             pltpu.VMEM((count, FF), BF),
             pltpu.VMEM((count, FF), BF),
             pltpu.VMEM((D, count), BF),
+            pltpu.VMEM((4, *grad.shape), BF),
+            pltpu.SemaphoreType.DMA((BLOCKS + 4,)),
+            pltpu.SemaphoreType.DMA((4,)),
+            pltpu.SemaphoreType.DMA((5,)),
+        ],
+        compiler_params=params(40),
+        name="fall",
+    )(order, spot, top, slope, second, *mlp)
+
+
+def back_kernel(
+    order_ref, vec_ref, ghidden_ref, top_ref, middle_ref, w0, w1, w2, w3,
+    gmiddle_ref, sums_ref,
+    held, ghidden, middle, gsecond, gmiddle, sems, in_sems, out_sems,
+):
+    later = [
+        pltpu.make_async_copy(ghidden_ref, ghidden, in_sems.at[0]),
+        *fetches(order_ref, (w0, w1, w2, w3), held, sems),
+        pltpu.make_async_copy(middle_ref, middle, in_sems.at[1]),
+    ]
+    start(later)
+    sums_ref[...] = jnp.zeros_like(sums_ref)
+    outs = []
+    for copy in later:
+        copy.wait()
+    chunk = middle_ref.shape[0] // 2
+    for half in range(2):
+        where = span(half, chunk)
+        for i in range(D // TILE):
+            gsecond[where, span(i, TILE)] = dot_nt(ghidden[where, :], held[span(i, TILE), :])
+        normed, inverse = norm_parts(middle[where, :])
+        grad = gsecond[where, :]
+        top = top_ref[where, :].astype(F32)
+        total_grad = top + norm_back(grad * vec_ref[1:2, :], normed, inverse)
+        gmiddle[where, :] = total_grad
+        copy = pltpu.make_async_copy(
+            gmiddle.at[where, :], gmiddle_ref.at[where, :], out_sems.at[half]
+        )
+        copy.start()
+        outs.append(copy)
+        low = total_grad.astype(BF).astype(F32)
+        for row, value in enumerate((grad * normed, grad, low, top)):
+            sums_ref[row : row + 1, :] += jnp.sum(value, axis=0, keepdims=True)
+    wait(outs)
+
+
+def back(order, vec, ghidden, top, middle, *win):
+    count = middle.shape[0]
+    shape = jax.ShapeDtypeStruct
+    return pl.pallas_call(
+        back_kernel,
+        out_shape=[shape((count, D), F32), shape((8, D), F32)],
+        in_specs=[SMEM, VMEM, ANY, VMEM, ANY] + [ANY] * 4,
+        out_specs=[ANY, VMEM],
+        scratch_shapes=[
+            pltpu.VMEM((D, FF), BF),
+            pltpu.VMEM((count, FF), BF),
             pltpu.VMEM((count, D), F32),
             pltpu.VMEM((count, D), F32),
-            pltpu.VMEM((4, *grad.shape), BF),
-            pltpu.SemaphoreType.DMA((4,)),
+            pltpu.VMEM((count, D), F32),
             pltpu.SemaphoreType.DMA((BLOCKS,)),
-            pltpu.SemaphoreType.DMA((5,)),
-            pltpu.SemaphoreType.DMA((4,)),
+            pltpu.SemaphoreType.DMA((2,)),
+            pltpu.SemaphoreType.DMA((2,)),
         ],
-        compiler_params=params(56),
-        name="fall",
-    )(order, vec, top, slope, second, middle, *mlp, *win)
+        compiler_params=params(32),
+        name="back",
+    )(order, vec, ghidden, top, middle, *win)
 
 
 def unattend_kernel(
     order_ref, vec_ref, x_ref, gmiddle_ref, project_ref, probs_ref, entry_ref, mixed_ref,
     w0, w1, w2, w3, f0, f1, f2, f3,
     ginputs_ref, sums_ref, g0, g1, g2, g3,
-    oheld, held, project, probs, both, turned, branch, gmixed, gproject, gentry, grads,
+    oheld, held, project, probs, both, turned, branch, gmixed, gproject, gentry, ginputs, grads,
     osems, sems, in_sems, probs_sems, out_sems,
 ):
     count = gmiddle_ref.shape[0]
@@ -622,22 +693,26 @@
         for i in range((count // SEQ) * groups)
     ]
     copies = fetches(order_ref, (f0, f1, f2, f3), held, sems)
-    for copy in ocopies + load + pieces + copies:
-        copy.start()
+    start([load[2], *ocopies])
     branch[...] = gmiddle_ref[...].astype(BF)
     sums_ref[...] = jnp.zeros_like(sums_ref)
-    for copy in ocopies:
-        copy.wait()
+    apiece, rows, _ = g0.shape
+    load[2].wait()
+    start([load[0]])
+    turned[1] = both[1].T
+    for part in (3, 2, 1, 0):
+        left = block_rows(order_ref, turned.at[1], part, apiece, rows)
+        for i in range(D // TILE):
+            grad = dot(left, branch[:, span(i, TILE)]).astype(BF)
+            grads[part, :, :, span(3 * D // TILE + i, TILE)] = grad.reshape(apiece, rows, TILE)
+    wait(ocopies)
+    start(pieces[:2])
 
     @each(D // TILE)
     def _(i):
         gmixed[:, span(i, TILE)] = dot_nt(branch[...], oheld[span(i, TILE), :]).astype(BF)
 
-    for copy in load:
-        copy.wait()
-    for i in range(2):
-        turned[i] = both[i].T
-    apiece, rows, _ = g0.shape
+    load[0].wait()
 
     @each((count // SEQ) * groups)
     def _(i):
@@ -645,6 +720,8 @@
         where = span(row, SEQ)
         scale = HEAD_DIM**-0.5
         pieces[i].wait()
+        if i % 2 == 0:
+            start(pieces[i + 2 : i + 4] if i + 2 < len(pieces) else [load[1], *copies])
         queries = stacked(project[where, span(group, WIDE)] * BF(scale))
         keys = project[where, span(groups + group, WIDE)]
         values = project[where, span(2 * groups + group, WIDE)]
@@ -664,29 +741,33 @@
                 low.astype(F32), axis=0, keepdims=True
             )
 
-    for copy in copies:
-        copy.wait()
-    for i in range(D // WIDE):
-        gentry[:, span(i, WIDE)] = dot_nt(gproject[...], held[span(i, WIDE), :])
+    load[1].wait()
+    turned[0] = both[0].T
     outs = []
-    chunk = count // 4
     for part in (3, 2, 1, 0):
         left = block_rows(order_ref, turned.at[0], part, apiece, rows)
         for i in range(3 * D // TILE):
             grad = dot(left, gproject[:, span(i, TILE)]).astype(BF)
             grads[part, :, :, span(i, TILE)] = grad.reshape(apiece, rows, TILE)
-        left = block_rows(order_ref, turned.at[1], part, apiece, rows)
-        for i in range(D // TILE):
-            grad = dot(left, branch[:, span(i, TILE)]).astype(BF)
-            grads[part, :, :, span(3 * D // TILE + i, TILE)] = grad.reshape(apiece, rows, TILE)
         copy = pltpu.make_async_copy(grads.at[part], (g0, g1, g2, g3)[part], out_sems.at[part])
         copy.start()
         outs.append(copy)
-        where = span(part, chunk)
+    for copy in copies:
+        copy.wait()
+    chunk = count // 2
+    for half in range(2):
+        where = span(half, chunk)
+        for i in range(D // TILE):
+            gentry[where, span(i, TILE)] = dot_nt(gproject[where, :], held[span(i, TILE), :])
         normed, inverse = norm_parts(x_ref[where, :].astype(F32))
         grad = gentry[where, :]
         back = norm_back(grad * vec_ref[0:1, :], normed, inverse)
-        ginputs_ref[where, :] = gmiddle_ref[where, :] + back
+        ginputs[where, :] = gmiddle_ref[where, :] + back
+        copy = pltpu.make_async_copy(
+            ginputs.at[where, :], ginputs_ref.at[where, :], out_sems.at[4 + half]
+        )
+        copy.start()
+        outs.append(copy)
         sums_ref[3:4, :] += jnp.sum(grad * normed, axis=0, keepdims=True)
         sums_ref[4:5, :] += jnp.sum(grad, axis=0, keepdims=True)
     for copy in outs:
@@ -701,7 +782,7 @@
         unattend_kernel,
         out_shape=[shape((count, D), F32), shape((8, D), F32)] + [grad] * 4,
         in_specs=[SMEM] + [VMEM] * 3 + [ANY] * 12,
-        out_specs=[VMEM] * 2 + [ANY] * 4,
+        out_specs=[ANY, VMEM] + [ANY] * 4,
         scratch_shapes=[
             pltpu.VMEM((D, D), BF),
             pltpu.VMEM((D, 3 * D), BF),
@@ -713,12 +794,13 @@
             pltpu.VMEM((count, D), BF),
             pltpu.VMEM((count, 3 * D), BF),
             pltpu.VMEM((count, D), F32),
+            pltpu.VMEM((count, D), F32),
             pltpu.VMEM((4, *grad.shape), BF),
             pltpu.SemaphoreType.DMA((BLOCKS,)),
             pltpu.SemaphoreType.DMA((BLOCKS,)),
             pltpu.SemaphoreType.DMA((3,)),
             pltpu.SemaphoreType.DMA((probs.shape[0],)),
-            pltpu.SemaphoreType.DMA((4,)),
+            pltpu.SemaphoreType.DMA((6,)),
         ],
         compiler_params=params(56),
         name="unattend",
@@ -726,7 +808,7 @@
 
 
 def finish_kernel(
-    vec_ref, middle_ref, active_ref, w0, w1, w2, w3,
+    spot_ref, vec_ref, middle_ref, active_ref, m0, m1, m2, m3, l0, l1, l2, l3,
     out_ref, held, active, sems, tile_sems,
 ):
     copies = [
@@ -735,7 +817,8 @@
         )
         for half in range(2)
     ]
-    fetch = part_fetches((w0, w1, w2, w3), held, sems)
+    early, late = mlp_fetches(spot_ref, (m0, m1, m2, m3), (l0, l1, l2, l3), held, sems)
+    fetch = early + late
     for copy in fetch + copies:
         copy.start()
     for copy in fetch + copies:
@@ -750,25 +833,25 @@
         out_ref[:, columns] = (middle_ref[:, columns] + result).astype(BF)
 
 
-def finish(vec, middle, active, *mlp):
+def finish(spot, vec, middle, active, *mlp):
     count = middle.shape[0]
     return pl.pallas_call(
         finish_kernel,
         out_shape=jax.ShapeDtypeStruct((count, D), BF),
-        in_specs=[VMEM, VMEM, ANY] + [ANY] * 4,
+        in_specs=[SMEM, VMEM, VMEM, ANY] + [ANY] * 8,
         out_specs=VMEM,
         scratch_shapes=[
             pltpu.VMEM((BLOCKS, PIECE, D), BF),
             pltpu.VMEM((2, count, FF // 2), BF),
-            pltpu.SemaphoreType.DMA((4,)),
+            pltpu.SemaphoreType.DMA((BLOCKS + 4,)),
             pltpu.SemaphoreType.DMA((2,)),
         ],
         compiler_params=params(32),
         name="finish",
-    )(vec, middle, active, *mlp)
-
-
-def per_device(plan, inputs, image_ids, cotangent, gains, biases, w_qkv, w_out, w_in, w_mlp):
+    )(spot, vec, middle, active, *mlp)
+
+
+def per_device(plan, late_plan, inputs, image_ids, cotangent, gains, biases, w_qkv, w_out, w_in, w_mlp):
     me = lax.axis_index(AXES)
     order = plan.positions(me)
     gain_dev, bias_dev = gains.shape[1], biases.shape[1]
@@ -778,35 +861,43 @@
     count = blocks * length
     x = inputs.reshape(count, D)
     numbers = order if plan.devices == BLOCKS else jnp.arange(BLOCKS, dtype=jnp.int32)
+    late_order = late_plan.positions(me)
+    spot = jnp.arange(BLOCKS, dtype=jnp.int32)
+    if plan.devices == BLOCKS:
+        spot = jnp.sum(jnp.where(late_order[:, None] == order[None], spot[None], 0), axis=1)
     line = Line()
     side = 128
 
     small = jnp.concatenate([gains, biases], 1)
     small = jnp.pad(small, ((0, 0), (0, rows * side - small_dev))).reshape(rows, side)
     first = Gather(plan, line, "qkv", jnp.concatenate([w_qkv.reshape(rows, 3 * D), small], 1))
-    first.start(0)
     win = Gather(
         plan, line, "in", jnp.concatenate([w_in.reshape(rows, FF), w_out.reshape(rows, D)], 1)
     )
-    mlp = Gather(plan, line, "mlp", w_mlp.reshape(FF // plan.devices, D))
+    mlp_block = w_mlp.reshape(FF // plan.devices, D)
+    mlp = Gather(plan, line, "mlp", mlp_block[:, : D // 2])
+    late = Gather(late_plan, line, "late", mlp_block[:, D // 2 :])
     top = jnp.where(image_ids.reshape(count, 1) >= 0, cotangent.reshape(count, D), BF(0))
+    first.start(0)
+    late.start(0)
     first.take()
+    late.take()
     first.start(1)
     win.start(0)
+    late.start(1)
     first.take()
     win.take()
+    late.take()
     first.start(2)
-    win.start(1)
     first.take()
-    win.take()
     first.start(3)
     first.swap_first()
-    mlp.start(0)
+    win.start(1)
     first.arrive()
-    mlp.take()
+    win.take()
     first.swap_second()
     win.start(2)
-    mlp.start(1)
+    mlp.start(0)
     first_parts = first.parts()
 
     def unpack(*parts):
@@ -827,42 +918,50 @@
         first_parts = [part[:, :, : 3 * D] for part in first_parts]
     first_parts = to_blocks(order, first_parts)
     entry, project = line.run(project_all, numbers, vec, x, *first_parts)
+    line.wait(mlp.coming)
     win.take()
-    mlp.take()
     win.start(3)
     win.swap_first()
+    mlp.take()
+    mlp.start(1)
+    late.start(2)
     probs, mixed = line.run(attend, project, image_ids)
+    line.wait(mlp.coming, late.coming)
     win.arrive()
     line.wait(win.first)
     win.swap_second()
+    mlp.take()
     mlp.start(2)
     win_parts = to_blocks(order, win.parts())
     middle, second = line.run(settle, numbers, vec, x, mixed, *win_parts)
+    line.wait(mlp.coming)
+    late.take()
+    late.start(3)
+    late.swap_first()
     mlp.take()
     mlp.start(3)
     mlp.swap_first()
     active, slope, *grads = line.run(rise, numbers, bias_in, second, top, *win_parts)
-    line.wait(mlp.first)
+    line.wait(mlp.first, late.first)
     mlp.arrive()
+    late.arrive()
     sum_mlp = Scatter(plan, line, "mlp", from_blocks(order, grads))
     mlp.swap_second()
+    late.swap_second()
     sum_mlp.start(3)
-    mlp_parts = to_blocks(order, mlp.parts())
-    gmiddle, sums, grad_bias_in, *grads = line.run(
-        fall, numbers, vec, top, slope, second, middle, mlp_parts, win_parts
-    )
+    mlp_parts = to_blocks(order, mlp.parts()) + to_blocks(late_order, late.parts())
+    ghidden, grad_bias_in, *grads = line.run(fall, numbers, spot, top, slope, second, *mlp_parts)
     sum_mlp.arrive()
     sum_in = Scatter(plan, line, "in", from_blocks(order, grads))
     sum_mlp.start(2)
     sum_in.start(3)
+    gmiddle, sums = line.run(back, numbers, vec, ghidden, top, middle, *win_parts)
     grad_inputs, sums_one, *grads = line.run(
         unattend, numbers, vec, x, gmiddle, project, probs, entry, mixed, win_parts, first_parts
     )
     sum_mlp.arrive()
     sum_in.arrive()
     sum_first = Scatter(plan, line, "first", from_blocks(order, grads))
-    sum_in.start(2)
-    sum_mlp.start(1)
 
     def pack(sums_one, sums, grad_bias_in):
         flat_gains = jnp.concatenate([sums_one[3], sums[0]]).reshape(-1, gain_dev)
@@ -875,16 +974,21 @@
         return moved.reshape(plan.devices, rows, side)
 
     sum_first.join(pack(sums_one, sums, grad_bias_in))
+    sum_in.start(2)
+    sum_first.start(3)
+    sum_mlp.start(1)
+    output = line.run(finish, spot, vec, middle, active, *mlp_parts)
+    sum_mlp.arrive()
+    sum_in.start(1)
+    sum_mlp.start(0)
     sum_in.arrive()
-    sum_first.start(3)
-    sum_in.start(1)
-    output = line.run(finish, vec, middle, active, *mlp_parts)
-    sum_mlp.start(0)
+    sum_mlp.arrive()
+    sum_first.start(2)
     sum_in.start(0)
-    sum_first.start(2)
     grad_mlp = sum_mlp.result()
+    sum_in.arrive()
+    sum_first.start(1)
     grad_in = sum_in.result()
-    sum_first.start(1)
     sum_first.start(0)
     grad_first = sum_first.result()
     grad_small = grad_first[:, 4 * D :].reshape(1, -1)[:, :small_dev]
@@ -901,12 +1005,12 @@
 
 
 def solution(mesh):
-    plan = Plan(mesh)
+    plan, late_plan = Plan(mesh), Plan(mesh, late=True)
     whole = P(AXES, None, None)
     flat = P(AXES, None)
 
     def body(*arrays):
-        return per_device(plan, *arrays)
+        return per_device(plan, late_plan, *arrays)
 
     return jax.shard_map(
         body,

time: 363 us -> 348 us (0.959)
  waiting for transfers between devices: 159 us -> 131 us
  starting transfers between devices: 35.2 us -> 53.9 us
  other arithmetic: 36.3 us -> 30.6 us
    ppermute x37 -> x43, waiting for transfers between devices: 159 us -> 131 us  [send(): return lax.ppermute(self.tie(array)[0], AXES, pairs)]
    ppermute x37 -> x43, starting transfers between devices: 35.2 us -> 53.9 us  [send(): return lax.ppermute(self.tie(array)[0], AXES, pairs)]
    unnamed x105 -> x134, local copies, waits for them, and re-layouts: 15.3 us -> 17.3 us
    pallas_call x1 -> x2, Pallas kernels: 25.5 us -> 24.9 us  [the longest x1 14.6 us: fall(): pl.pallas_call(fall_kernel, out_shape=[shape((count, FF), BF), shape((1,...]
  transfers between devices with their start and end apart: 37 -> 43, of which waited for: 22 -> 22; matrix products, arithmetic and copies ran while one was open for 12% -> 9% of each run, Pallas kernels for 28% -> 29%
where the time goes in v5:
time: 348 us; the launch traced here: 342 us
  waiting for transfers between devices  131 us (38%)
  Pallas kernels  97.6 us (28%)
  starting transfers between devices  53.9 us (15%)
  other arithmetic  30.6 us (9%)
  local copies, waits for them, and re-layouts  26.3 us (8%)
    ppermute x43, waiting for transfers between devices, send(): return lax.ppermute(self.tie(array)[0], AXES, pairs)  131 us
    ppermute x43, starting transfers between devices, send(): return lax.ppermute(self.tie(array)[0], AXES, pairs)  53.9 us
    pallas_call x1, Pallas kernels, unattend(): pl.pallas_call(unattend_kernel, out_shape=[shape((count, D), F32), shape(...  26.4 us
    pallas_call x1, Pallas kernels, rise(): pl.pallas_call(rise_kernel, out_shape=[shape((count, FF), BF)] * 2 + [gra...  18.4 us
    unnamed x134, local copies, waits for them, and re-layouts  17.3 us
    pallas_call x1, Pallas kernels, fall(): pl.pallas_call(fall_kernel, out_shape=[shape((count, FF), BF), shape((1,...  14.6 us
    pallas_call x1, Pallas kernels, back(): pl.pallas_call(back_kernel, out_shape=[shape((count, D), F32), shape((8,...  10.3 us
    convert_element_type x6, other arithmetic, start(): self.sum(low, low + self.count, parts).astype(BF)  9.27 us
  transfers between devices with their start and end apart: 43, of which 22 were waited for; matrix products, arithmetic and copies ran while one was open for 9% of the time, Pallas kernels for 29%

profile of v5, /device:TPU:0, one launch (start us, length us, event | category | flops | bytes accessed | tf_op | source)
XLA Modules:
  0.0 341.6 jit_solution(15612748133073087267)
XLA Ops:
  3.7 4.1 %collective-permute-start = (bf16[1,32,3200]{2,1,0:T(8,128)(2,1)S(1)}, bf16[1,32,3200]{2,1,0:T(8,128)(2,1)S(1)}, u32[]{:S(2)}, u32[]{:S(2)}) collective-permute-start(bf16[1,32,3200]{2,1,0:T(8,128)(2,1)S(1)} %maximum_bitcast_fusion.2), channel_id=1, source_target_pairs={{0,4},{1,5},{2,6},{3,7},{4,0},{5,1},{6,2},{7,3},{8,12},{9,13},{10,... | collective-permute-start | bytes 614408 | tf_op jit(solution)/shard_map/gather_qkv_0/ppermute | solution.py:105
  14.2 3.1 collective-permute-done
  19.7 3.4 collective-permute-start.4
  23.1 12.0 %collective-permute-done.2 = bf16[2,32,3200]{2,1,0:T(8,128)(2,1)S(1)} collective-permute-done((bf16[2,32,3200]{2,1,0:T(8,128)(2,1)S(1)}, bf16[2,32,3200]{2,1,0:T(8,128)(2,1)S(1)}, u32[]{:S(2)}, u32[]{:S(2)}) %collective-permute-start.2) | collective-permute-done | bytes 409632 | tf_op jit(solution)/shard_map/gather_qkv_1/ppermute | solution.py:105
  37.9 11.1 %collective-permute-done.5 = bf16[4,32,3200]{2,1,0:T(8,128)(2,1)S(1)} collective-permute-done((bf16[4,32,3200]{2,1,0:T(8,128)(2,1)S(1)}, bf16[4,32,3200]{2,1,0:T(8,128)(2,1)S(1)}, u32[]{:S(2)}, u32[]{:S(2)}) %collective-permute-start.5) | collective-permute-done | bytes 819232 | tf_op jit(solution)/shard_map/gather_qkv_2/ppermute | solution.py:105
  50.6 3.3 collective-permute-start.8
  53.8 13.2 %collective-permute-done.8 = bf16[2,32,5120]{2,1,0:T(8,128)(2,1)S(1)} collective-permute-done((bf16[2,32,5120]{2,1,0:T(8,128)(2,1)S(1)}, bf16[2,32,5120]{2,1,0:T(8,128)(2,1)S(1)}, u32[]{:S(2)}, u32[]{:S(2)}) %collective-permute-start.8) | collective-permute-done | bytes 655392 | tf_op jit(solution)/shard_map/gather_in_1/ppermute | solution.py:105
  67.1 3.5 %collective-permute-done.6.w1.f1 = bf16[8,32,3200]{2,1,0:T(8,128)(2,1)} collective-permute-done((bf16[8,32,3200]{2,1,0:T(8,128)(2,1)S(1)}, bf16[8,32,3200]{2,1,0:T(8,128)(2,1)}, u32[]{:S(2)}, u32[]{:S(2)}) %collective-permute-start.6) | collective-permute-done | bytes 1638432 | tf_op jit(solution)/shard_map/gather_qkv_3/ppermute | solution.py:105
  79.5 8.0 %project.1 = (bf16[512,1024]{1,0:T(8,128)(2,1)S(1)}, bf16[512,3072]{1,0:T(8,128)(2,1)S(1)}) custom-call(s32[32]{0:T(128)S(1)} %fusion.23.order_ref, f32[8,1024]{1,0:T(8,128)S(1)} %slice.361.vec_ref, bf16[512,1024]{1,0:T(8,128)(2,1)S(1)} %bitcast.73, bf16[8,32,3200]{2,1,0:T(8,128)(2,1)S(1)} %constant_dynamic-update-slice_fusion.10.w0.f0, ...), custom_call_target="tpu_custom_call" | custom-call | tf_op jit(solution)/shard_map/project/pallas_call | solution.py:338
  97.2 2.9 collective-permute-start.14
  102.2 6.3 %attend.1 = (bf16[8,1024,256]{2,1,0:T(8,128)(2,1)S(1)}, bf16[512,1024]{1,0:T(8,128)(2,1)S(1)}) custom-call(bf16[512,3072]{1,0:T(8,128)(2,1)S(1)} %copy-done.5, s32[2,256]{1,0:T(2,128)S(1)} %copy-done.37, s32[512,1]{1,0:T(8,128)S(1)} %bitcast.75), custom_call_target="tpu_custom_call" | custom-call | tf_op jit(solution)/shard_map/attend/pallas_call | solution.py:380
  110.5 4.1 %collective-permute-done.14 = bf16[2,128,512]{2,1,0:T(8,128)(2,1)S(1)} collective-permute-done((bf16[2,128,512]{2,1,0:T(8,128)(2,1)S(1)}, bf16[2,128,512]{2,1,0:T(8,128)(2,1)S(1)}, u32[]{:S(2)}, u32[]{:S(2)}) %collective-permute-start.14) | collective-permute-done | bytes 262176 | tf_op jit(solution)/shard_map/gather_mlp_1/ppermute | solution.py:105
  114.6 6.4 %collective-permute-done.15 = bf16[4,128,512]{2,1,0:T(8,128)(2,1)} collective-permute-done((bf16[4,128,512]{2,1,0:T(8,128)(2,1)}, bf16[4,128,512]{2,1,0:T(8,128)(2,1)}, u32[]{:S(2)}, u32[]{:S(2)}) %collective-permute-start.15) | collective-permute-done | bytes 524320 | tf_op jit(solution)/shard_map/gather_late_2/ppermute | solution.py:105
  121.0 4.0 %collective-permute-done.12.w1 = bf16[8,32,5120]{2,1,0:T(8,128)(2,1)} collective-permute-done((bf16[8,32,5120]{2,1,0:T(8,128)(2,1)S(1)}, bf16[8,32,5120]{2,1,0:T(8,128)(2,1)}, u32[]{:S(2)}, u32[]{:S(2)}) %collective-permute-start.12) | collective-permute-done | bytes 2621472 | tf_op jit(solution)/shard_map/gather_in_3/ppermute | solution.py:105
  126.3 3.8 %collective-permute-done.16.w3 = bf16[8,32,5120]{2,1,0:T(8,128)(2,1)S(1)} collective-permute-done((bf16[8,32,5120]{2,1,0:T(8,128)(2,1)}, bf16[8,32,5120]{2,1,0:T(8,128)(2,1)S(1)}, u32[]{:S(2)}, u32[]{:S(2)}) %collective-permute-start.16) | collective-permute-done | bytes 2621472 | tf_op jit(solution)/shard_map/gather_in_swap_second/ppermute | solution.py:105
  130.1 5.1 %settle.1 = (f32[512,1024]{1,0:T(8,128)S(1)}, bf16[512,1024]{1,0:T(8,128)(2,1)S(1)}) custom-call(s32[32]{0:T(128)S(1)} %fusion.23.order_ref, f32[8,1024]{1,0:T(8,128)S(1)} %slice.361.vec_ref, bf16[512,1024]{1,0:T(8,128)(2,1)S(1)} %bitcast.74, bf16[512,1024]{1,0:T(8,128)(2,1)S(1)} %get-tuple-element.362.mixed_ref, ...), custom_call_target="tpu_custom_call" | custom-call | tf_op jit(solution)/shard_map/settle/pallas_call | solution.py:422
  139.4 3.3 collective-permute-start.21
  144.2 18.4 %rise.1 = (bf16[512,4096]{1,0:T(8,128)(2,1)}, bf16[512,4096]{1,0:T(8,128)(2,1)}, bf16[8,128,1024]{2,1,0:T(8,128)(2,1)S(1)}, bf16[8,128,1024]{2,1,0:T(8,128)(2,1)...) custom-call(s32[32]{0:T(128)S(1)} %fusion.23.order_ref, f32[1,4096]{1,0:T(1,128)S(1)} %bitcast.76, ...), custom_call_target="tpu_custom_call" | custom-call | tf_op jit(solution)/shard_map/rise/pallas_call | solution.py:483
  162.7 3.5 %collective-permute-done.21.l1 = bf16[8,128,512]{2,1,0:T(8,128)(2,1)} collective-permute-done((bf16[8,128,512]{2,1,0:T(8,128)(2,1)S(1)}, bf16[8,128,512]{2,1,0:T(8,128)(2,1)}, u32[]{:S(2)}, u32[]{:S(2)}) %collective-permute-start.21) | collective-permute-done | bytes 1048608 | tf_op jit(solution)/shard_map/gather_late_3/ppermute | solution.py:105
  166.2 4.4 %collective-permute-done.25 = bf16[8,128,1024]{2,1,0:T(8,128)(2,1)S(1)} collective-permute-done((bf16[8,128,1024]{2,1,0:T(8,128)(2,1)}, bf16[8,128,1024]{2,1,0:T(8,128)(2,1)S(1)}, u32[]{:S(2)}, u32[]{:S(2)}) %collective-permute-start.25) | collective-permute-done | bytes 2097184 | tf_op jit(solution)/shard_map/sum_mlp_swap_high/ppermute | solution.py:105
  177.1 3.0 collective-permute-done.23.l3
  180.1 14.6 %fall.1 = (bf16[512,4096]{1,0:T(8,128)(2,1)}, f32[1,4096]{1,0:T(1,128)S(1)}, bf16[8,32,4096]{2,1,0:T(8,128)(2,1)S(1)}, bf16[8,32,4096]{2,1,0:T(8,128)(2,1)}, bf1...) custom-call(s32[32]{0:T(128)S(1)} %fusion.23.order_ref, s32[32]{0:T(128)S(1)} %select_reduce_fusion.spot_ref, ...), custom_call_target="tpu_custom_call" | custom-call | tf_op jit(solution)/shard_map/fall/pallas_call | solution.py:597
  194.7 4.7 %collective-permute-done.26 = bf16[8,128,1024]{2,1,0:T(8,128)(2,1)S(1)} collective-permute-done((bf16[8,128,1024]{2,1,0:T(8,128)(2,1)S(1)}, bf16[8,128,1024]{2,1,0:T(8,128)(2,1)S(1)}, u32[]{:S(2)}, u32[]{:S(2)}) %collective-permute-start.26) | collective-permute-done | bytes 2097184 | tf_op jit(solution)/shard_map/sum_mlp_3/ppermute | solution.py:105
  210.3 10.3 %back.1 = (f32[512,1024]{1,0:T(8,128)S(1)}, f32[8,1024]{1,0:T(8,128)S(1)}) custom-call(s32[32]{0:T(128)S(1)} %fusion.23.order_ref, f32[8,1024]{1,0:T(8,128)S(1)} %slice.361.vec_ref, bf16[512,4096]{1,0:T(8,128)(2,1)S(1)} %copy-done.17, bf16[512,1024]{1,0:T(8,128)(2,1)S(1)} %bitcast_select_fusion.top_ref, f32[512,1024]{1,0:T(8,128)S(1)} %copy-done.10, ...), custom_call_target="tpu_custom_call" | custom-call | tf_op jit(solution)/shard_map/back/pallas_call | solution.py:656
  221.9 26.4 %unattend.1 = (f32[512,1024]{1,0:T(8,128)}, f32[8,1024]{1,0:T(8,128)}, bf16[8,32,4096]{2,1,0:T(8,128)(2,1)}, bf16[8,32,4096]{2,1,0:T(8,128)(2,1)}, bf16[8,32,409...) custom-call(s32[32]{0:T(128)} %copy-done.35, f32[8,1024]{1,0:T(8,128)} %copy-done.32, bf16[512,1024]{1,0:T(8,128)(2,1)} %bitcast.72, ...), custom_call_target="tpu_custom_call" | custom-call | tf_op jit(solution)/shard_map/unattend/pallas_call | solution.py:781
  260.9 8.6 %finish.1 = bf16[512,1024]{1,0:T(8,128)(2,1)} custom-call(s32[32]{0:T(128)S(1)} %select_reduce_fusion.spot_ref, f32[8,1024]{1,0:T(8,128)S(1)} %copy-done.33, f32[512,1024]{1,0:T(8,128)S(1)} %copy-done.10, bf16[512,4096]{1,0:T(8,128)(2,1)S(1)} %copy-done.15, bf16[8,128,512]{2,1,0:T(8,128)(2,1)S(1)} %copy-done.14, ...), custom_call_target="tpu_custom_call" | custom-call | tf_op jit(solution)/shard_map/finish/pallas_call | solution.py:838
  269.5 6.5 %collective-permute-done.36 = bf16[4,32,4096]{2,1,0:T(8,128)(2,1)S(1)} collective-permute-done((bf16[4,32,4096]{2,1,0:T(8,128)(2,1)S(1)}, bf16[4,32,4096]{2,1,0:T(8,128)(2,1)S(1)}, u32[]{:S(2)}, u32[]{:S(2)}) %collective-permute-start.36) | collective-permute-done | bytes 1048608 | tf_op jit(solution)/shard_map/sum_in_2/ppermute | solution.py:105
  282.2 11.5 %collective-permute-done.38 = bf16[1,128,1024]{2,1,0:T(8,128)(2,1)S(1)} collective-permute-done((bf16[1,128,1024]{2,1,0:T(8,128)(2,1)S(1)}, bf16[1,128,1024]{2,1,0:T(8,128)(2,1)S(1)}, u32[]{:S(2)}, u32[]{:S(2)}) %collective-permute-start.38) | collective-permute-done | bytes 262176 | tf_op jit(solution)/shard_map/sum_mlp_0/ppermute | solution.py:105
  300.3 10.3 %collective-permute-done.40 = bf16[1,32,4096]{2,1,0:T(8,128)(2,1)S(1)} collective-permute-done((bf16[1,32,4096]{2,1,0:T(8,128)(2,1)S(1)}, bf16[1,32,4096]{2,1,0:T(8,128)(2,1)S(1)}, u32[]{:S(2)}, u32[]{:S(2)}) %collective-permute-start.40) | collective-permute-done | bytes 262176 | tf_op jit(solution)/shard_map/sum_in_0/ppermute | solution.py:105
  315.2 8.8 %collective-permute-done.41 = bf16[2,32,4224]{2,1,0:T(8,128)(2,1)S(1)} collective-permute-done((bf16[2,32,4224]{2,1,0:T(8,128)(2,1)S(1)}, bf16[2,32,4224]{2,1,0:T(8,128)(2,1)S(1)}, u32[]{:S(2)}, u32[]{:S(2)}) %collective-permute-start.41) | collective-permute-done | bytes 540704 | tf_op jit(solution)/shard_map/sum_first_1/ppermute | solution.py:105
  324.2 2.9 collective-permute-start.42
  329.7 8.3 %collective-permute-done.42 = bf16[1,32,4224]{2,1,0:T(8,128)(2,1)S(1)} collective-permute-done((bf16[1,32,4224]{2,1,0:T(8,128)(2,1)S(1)}, bf16[1,32,4224]{2,1,0:T(8,128)(2,1)S(1)}, u32[]{:S(2)}, u32[]{:S(2)}) %collective-permute-start.42) | collective-permute-done | bytes 270368 | tf_op jit(solution)/shard_map/sum_first_0/ppermute | solution.py:105
  (280 shorter events, 100.3 us)
Async XLA Ops:
  3.7 13.6 %collective-permute-start = (bf16[1,32,3200]{2,1,0:T(8,128)(2,1)S(1)}, bf16[1,32,3200]{2,1,0:T(8,128)(2,1)S(1)}, u32[]{:S(2)}, u32[]{:S(2)}) collective-permute-start(bf16[1,32,3200]{2,1,0:T(8,128)(2,1)S(1)} %maximum_bitcast_fusion.2), channel_id=1, source_target_pairs={{0,4},{1,5},{2,6},{3,7},{4,0},{5,1},{6,2},{7,3},{8,12},{9,13},{10,... | collective-permute-start | bytes 614408 | tf_op jit(solution)/shard_map/gather_qkv_0/ppermute | solution.py:105
  17.4 17.7 %collective-permute-start.2 = (bf16[2,32,3200]{2,1,0:T(8,128)(2,1)S(1)}, bf16[2,32,3200]{2,1,0:T(8,128)(2,1)S(1)}, u32[]{:S(2)}, u32[]{:S(2)}) collective-permute-start(bf16[2,32,3200]{2,1,0:T(8,128)(2,1)S(1)} %constant_dynamic-update-slice_fusion), channel_id=1, source_target_pairs={{0,2},{1,3},{2,0},{3,1},{4,6},{5,7},{6,4},{7,5},{8,10},{9,11},{10,... | collective-permute-start | bytes 1228808 | tf_op jit(solution)/shard_map/gather_qkv_1/ppermute | solution.py:105
  18.2 17.1 %collective-permute-start.3 = (bf16[2,128,512]{2,1,0:T(8,128)(2,1)S(1)}, bf16[2,128,512]{2,1,0:T(8,128)(2,1)S(1)}, u32[]{:S(2)}, u32[]{:S(2)}) collective-permute-start(bf16[2,128,512]{2,1,0:T(8,128)(2,1)S(1)} %constant_dynamic-update-slice_fusion.2), channel_id=1, source_target_pairs={{0,16},{1,17},{2,18},{3,19},{4,20},{5,21},{6,22},{7,23},{8,9},{9,8... | collective-permute-start | bytes 786440 | tf_op jit(solution)/shard_map/gather_late_1/ppermute | solution.py:105
  19.7 15.4 %collective-permute-start.4 = (bf16[1,32,5120]{2,1,0:T(8,128)(2,1)S(1)}, bf16[1,32,5120]{2,1,0:T(8,128)(2,1)S(1)}, u32[]{:S(2)}, u32[]{:S(2)}) collective-permute-start(bf16[1,32,5120]{2,1,0:T(8,128)(2,1)S(1)} %maximum_bitcast_fusion.1), channel_id=1, source_target_pairs={{0,4},{1,5},{2,6},{3,7},{4,0},{5,1},{6,2},{7,3},{8,12},{9,13},{10,... | collective-permute-start | bytes 983048 | tf_op jit(solution)/shard_map/gather_in_0/ppermute | solution.py:105
  49.2 21.3 %collective-permute-start.6 = (bf16[8,32,3200]{2,1,0:T(8,128)(2,1)S(1)}, bf16[8,32,3200]{2,1,0:T(8,128)(2,1)}, u32[]{:S(2)}, u32[]{:S(2)}) collective-permute-start(bf16[8,32,3200]{2,1,0:T(8,128)(2,1)S(1)} %constant_dynamic-update-slice_fusion.10.w0.f0), channel_id=1, source_target_pairs={{0,16},{1,17},{2,18},{3,19},{4,20},{5,21},{6,22},{7,23},{8,9},{9,8... | collective-permute-start | bytes 4915208 | tf_op jit(solution)/shard_map/gather_qkv_3/ppermute | solution.py:105
  50.6 16.5 %collective-permute-start.8 = (bf16[2,32,5120]{2,1,0:T(8,128)(2,1)S(1)}, bf16[2,32,5120]{2,1,0:T(8,128)(2,1)S(1)}, u32[]{:S(2)}, u32[]{:S(2)}) collective-permute-start(bf16[2,32,5120]{2,1,0:T(8,128)(2,1)S(1)} %constant_dynamic-update-slice_fusion.6), channel_id=1, source_target_pairs={{0,2},{1,3},{2,0},{3,1},{4,6},{5,7},{6,4},{7,5},{8,10},{9,11},{10,... | collective-permute-start | bytes 1966088 | tf_op jit(solution)/shard_map/gather_in_1/ppermute | solution.py:105
  53.8 22.4 %collective-permute-start.7 = (bf16[8,32,3200]{2,1,0:T(8,128)(2,1)S(1)}, bf16[8,32,3200]{2,1,0:T(8,128)(2,1)}, u32[]{:S(2)}, u32[]{:S(2)}) collective-permute-start(bf16[8,32,3200]{2,1,0:T(8,128)(2,1)S(1)} %constant_dynamic-update-slice_fusion.10.w0.f0), channel_id=1, source_target_pairs={{0,8},{1,9},{2,10},{3,11},{4,12},{5,13},{6,14},{7,15},{8,0},{9,1},... | collective-permute-start | bytes 4915208 | tf_op jit(solution)/shard_map/gather_qkv_swap_first/ppermute | solution.py:105
  72.3 17.9 %collective-permute-start.11 = (bf16[4,32,5120]{2,1,0:T(8,128)(2,1)}, bf16[4,32,5120]{2,1,0:T(8,128)(2,1)}, u32[]{:S(2)}, u32[]{:S(2)}) collective-permute-start(bf16[4,32,5120]{2,1,0:T(8,128)(2,1)} %constant_dynamic-update-slice_fusion.12), channel_id=1, source_target_pairs={{0,1},{1,0},{2,3},{3,2},{4,5},{5,4},{6,7},{7,6},{8,24},{9,25},{10,... | collective-permute-start | bytes 3932168 | tf_op jit(solution)/shard_map/gather_in_2/ppermute | solution.py:105
  73.6 14.0 %collective-permute-start.10 = (bf16[1,128,512]{2,1,0:T(8,128)(2,1)S(1)}, bf16[1,128,512]{2,1,0:T(8,128)(2,1)S(1)}, u32[]{:S(2)}, u32[]{:S(2)}) collective-permute-start(bf16[1,128,512]{2,1,0:T(8,128)(2,1)S(1)} %get-tuple-element.272), channel_id=1, source_target_pairs={{0,4},{1,5},{2,6},{3,7},{4,0},{5,1},{6,2},{7,3},{8,12},{9,13},{10,... | collective-permute-start | bytes 393224 | tf_op jit(solution)/shard_map/gather_mlp_0/ppermute | solution.py:105
  93.1 27.9 %collective-permute-start.13 = (bf16[8,32,5120]{2,1,0:T(8,128)(2,1)S(1)}, bf16[8,32,5120]{2,1,0:T(8,128)(2,1)}, u32[]{:S(2)}, u32[]{:S(2)}) collective-permute-start(bf16[8,32,5120]{2,1,0:T(8,128)(2,1)S(1)} %constant_dynamic-update-slice_fusion.14.w0), channel_id=1, source_target_pairs={{0,8},{1,9},{2,10},{3,11},{4,12},{5,13},{6,14},{7,15},{8,0},{9,1},... | collective-permute-start | bytes 7864328 | tf_op jit(solution)/shard_map/gather_in_swap_first/ppermute | solution.py:105
  93.2 31.8 %collective-permute-start.12 = (bf16[8,32,5120]{2,1,0:T(8,128)(2,1)S(1)}, bf16[8,32,5120]{2,1,0:T(8,128)(2,1)}, u32[]{:S(2)}, u32[]{:S(2)}) collective-permute-start(bf16[8,32,5120]{2,1,0:T(8,128)(2,1)S(1)} %constant_dynamic-update-slice_fusion.14.w0), channel_id=1, source_target_pairs={{0,16},{1,17},{2,18},{3,19},{4,20},{5,21},{6,22},{7,23},{8,9},{9,8... | collective-permute-start | bytes 7864328 | tf_op jit(solution)/shard_map/gather_in_3/ppermute | solution.py:105
  94.5 26.5 %collective-permute-start.15 = (bf16[4,128,512]{2,1,0:T(8,128)(2,1)}, bf16[4,128,512]{2,1,0:T(8,128)(2,1)}, u32[]{:S(2)}, u32[]{:S(2)}) collective-permute-start(bf16[4,128,512]{2,1,0:T(8,128)(2,1)} %constant_dynamic-update-slice_fusion.8), channel_id=1, source_target_pairs={{0,4},{1,5},{2,6},{3,7},{4,0},{5,1},{6,2},{7,3},{8,12},{9,13},{10,... | collective-permute-start | bytes 1572872 | tf_op jit(solution)/shard_map/gather_late_2/ppermute | solution.py:105
  97.2 17.4 %collective-permute-start.14 = (bf16[2,128,512]{2,1,0:T(8,128)(2,1)S(1)}, bf16[2,128,512]{2,1,0:T(8,128)(2,1)S(1)}, u32[]{:S(2)}, u32[]{:S(2)}) collective-permute-start(bf16[2,128,512]{2,1,0:T(8,128)(2,1)S(1)} %constant_dynamic-update-slice_fusion.16), channel_id=1, source_target_pairs={{0,2},{1,3},{2,0},{3,1},{4,6},{5,7},{6,4},{7,5},{8,10},{9,11},{10,... | collective-permute-start | bytes 786440 | tf_op jit(solution)/shard_map/gather_mlp_1/ppermute | solution.py:105
  137.9 24.7 %collective-permute-start.19 = (bf16[8,128,512]{2,1,0:T(8,128)(2,1)S(1)}, bf16[8,128,512]{2,1,0:T(8,128)(2,1)S(1)}, u32[]{:S(2)}, u32[]{:S(2)}) collective-permute-start(bf16[8,128,512]{2,1,0:T(8,128)(2,1)S(1)} %constant_dynamic-update-slice_fusion.22.m0), channel_id=1, source_target_pairs={{0,8},{1,9},{2,10},{3,11},{4,12},{5,13},{6,14},{7,15},{8,0},{9,1},... | collective-permute-start | bytes 3145736 | tf_op jit(solution)/shard_map/gather_mlp_swap_first/ppermute | solution.py:105
  138.1 24.5 %collective-permute-start.18 = (bf16[8,128,512]{2,1,0:T(8,128)(2,1)S(1)}, bf16[8,128,512]{2,1,0:T(8,128)(2,1)}, u32[]{:S(2)}, u32[]{:S(2)}) collective-permute-start(bf16[8,128,512]{2,1,0:T(8,128)(2,1)S(1)} %constant_dynamic-update-slice_fusion.22.m0), channel_id=1, source_target_pairs={{0,16},{1,17},{2,18},{3,19},{4,20},{5,21},{6,22},{7,23},{8,9},{9,8... | collective-permute-start | bytes 3145736 | tf_op jit(solution)/shard_map/gather_mlp_3/ppermute | solution.py:105
  139.4 26.7 %collective-permute-start.21 = (bf16[8,128,512]{2,1,0:T(8,128)(2,1)S(1)}, bf16[8,128,512]{2,1,0:T(8,128)(2,1)}, u32[]{:S(2)}, u32[]{:S(2)}) collective-permute-start(bf16[8,128,512]{2,1,0:T(8,128)(2,1)S(1)} %constant_dynamic-update-slice_fusion.20.l0), channel_id=1, source_target_pairs={{0,2},{1,3},{2,0},{3,1},{4,6},{5,7},{6,4},{7,5},{8,10},{9,11},{10,... | collective-permute-start | bytes 3145736 | tf_op jit(solution)/shard_map/gather_late_3/ppermute | solution.py:105
  142.7 23.5 %collective-permute-start.20 = (bf16[8,128,512]{2,1,0:T(8,128)(2,1)S(1)}, bf16[8,128,512]{2,1,0:T(8,128)(2,1)}, u32[]{:S(2)}, u32[]{:S(2)}) collective-permute-start(bf16[8,128,512]{2,1,0:T(8,128)(2,1)S(1)} %constant_dynamic-update-slice_fusion.20.l0), channel_id=1, source_target_pairs={{0,8},{1,9},{2,10},{3,11},{4,12},{5,13},{6,14},{7,15},{8,0},{9,1},... | collective-permute-start | bytes 3145736 | tf_op jit(solution)/shard_map/gather_late_swap_first/ppermute | solution.py:105
  173.3 26.1 %collective-permute-start.26 = (bf16[8,128,1024]{2,1,0:T(8,128)(2,1)S(1)}, bf16[8,128,1024]{2,1,0:T(8,128)(2,1)S(1)}, u32[]{:S(2)}, u32[]{:S(2)}) collective-permute-start(bf16[8,128,1024]{2,1,0:T(8,128)(2,1)S(1)} %add.188), channel_id=1, source_target_pairs={{0,16},{1,17},{2,18},{3,19},{4,20},{5,21},{6,22},{7,23},{8,9},{9,8... | collective-permute-start | bytes 6291464 | tf_op jit(solution)/shard_map/sum_mlp_3/ppermute | solution.py:105
  174.7 24.7 %collective-permute-start.24 = (bf16[8,128,1024]{2,1,0:T(8,128)(2,1)S(1)}, bf16[8,128,1024]{2,1,0:T(8,128)(2,1)S(1)}, u32[]{:S(2)}, u32[]{:S(2)}) collective-permute-start(bf16[8,128,1024]{2,1,0:T(8,128)(2,1)S(1)} %copy-done.51), channel_id=1, source_target_pairs={{0,8},{1,9},{2,10},{3,11},{4,12},{5,13},{6,14},{7,15},{8,0},{9,1},... | collective-permute-start | bytes 6291464 | tf_op jit(solution)/shard_map/sum_mlp_swap_low/ppermute | solution.py:105
  205.9 43.4 %collective-permute-start.29 = (bf16[8,32,4096]{2,1,0:T(8,128)(2,1)}, bf16[8,32,4096]{2,1,0:T(8,128)(2,1)}, u32[]{:S(2)}, u32[]{:S(2)}) collective-permute-start(bf16[8,32,4096]{2,1,0:T(8,128)(2,1)} %add.191), channel_id=1, source_target_pairs={{0,16},{1,17},{2,18},{3,19},{4,20},{5,21},{6,22},{7,23},{8,9},{9,8... | collective-permute-start | bytes 6291464 | tf_op jit(solution)/shard_map/sum_in_3/ppermute | solution.py:105
  206.8 43.2 %collective-permute-start.31 = (bf16[8,32,4096]{2,1,0:T(8,128)(2,1)}, bf16[8,32,4096]{2,1,0:T(8,128)(2,1)}, u32[]{:S(2)}, u32[]{:S(2)}) collective-permute-start(bf16[8,32,4096]{2,1,0:T(8,128)(2,1)} %get-tuple-element.378), channel_id=1, source_target_pairs={{0,8},{1,9},{2,10},{3,11},{4,12},{5,13},{6,14},{7,15},{8,0},{9,1},... | collective-permute-start | bytes 6291464 | tf_op jit(solution)/shard_map/sum_in_swap_low/ppermute | solution.py:105
  206.8 42.5 %collective-permute-start.27 = (bf16[4,128,1024]{2,1,0:T(8,128)(2,1)}, bf16[4,128,1024]{2,1,0:T(8,128)(2,1)S(1)}, u32[]{:S(2)}, u32[]{:S(2)}) collective-permute-start(bf16[4,128,1024]{2,1,0:T(8,128)(2,1)} %add_convert_fusion.2), channel_id=1, source_target_pairs={{0,1},{1,0},{2,3},{3,2},{4,5},{5,4},{6,7},{7,6},{8,24},{9,25},{10,... | collective-permute-start | bytes 3145736 | tf_op jit(solution)/shard_map/sum_mlp_2/ppermute | solution.py:105
  253.1 22.9 %collective-permute-start.36 = (bf16[4,32,4096]{2,1,0:T(8,128)(2,1)S(1)}, bf16[4,32,4096]{2,1,0:T(8,128)(2,1)S(1)}, u32[]{:S(2)}, u32[]{:S(2)}) collective-permute-start(bf16[4,32,4096]{2,1,0:T(8,128)(2,1)S(1)} %add_convert_fusion.1), channel_id=1, source_target_pairs={{0,1},{1,0},{2,3},{3,2},{4,5},{5,4},{6,7},{7,6},{8,24},{9,25},{10,... | collective-permute-start | bytes 3145736 | tf_op jit(solution)/shard_map/sum_in_2/ppermute | solution.py:105
  253.8 28.4 %collective-permute-start.33 = (bf16[8,32,4096]{2,1,0:T(8,128)(2,1)}, bf16[8,32,4096]{2,1,0:T(8,128)(2,1)S(1)}, u32[]{:S(2)}, u32[]{:S(2)}) collective-permute-start(bf16[8,32,4096]{2,1,0:T(8,128)(2,1)} %get-tuple-element.406), channel_id=1, source_target_pairs={{0,8},{1,9},{2,10},{3,11},{4,12},{5,13},{6,14},{7,15},{8,0},{9,1},... | collective-permute-start | bytes 6291464 | tf_op jit(solution)/shard_map/sum_first_swap_low/ppermute | solution.py:105
  256.7 38.3 %collective-permute-start.34 = (bf16[8,32,4224]{2,1,0:T(8,128)(2,1)S(1)}, bf16[8,32,4224]{2,1,0:T(8,128)(2,1)S(1)}, u32[]{:S(2)}, u32[]{:S(2)}) collective-permute-start(bf16[8,32,4224]{2,1,0:T(8,128)(2,1)S(1)} %pad_maximum_fusion), channel_id=1, source_target_pairs={{0,16},{1,17},{2,18},{3,19},{4,20},{5,21},{6,22},{7,23},{8,9},{9,8... | collective-permute-start | bytes 6488072 | tf_op jit(solution)/shard_map/sum_first_3/ppermute | solution.py:105
  259.1 16.8 %collective-permute-start.35 = (bf16[2,128,1024]{2,1,0:T(8,128)(2,1)}, bf16[2,128,1024]{2,1,0:T(8,128)(2,1)}, u32[]{:S(2)}, u32[]{:S(2)}) collective-permute-start(bf16[2,128,1024]{2,1,0:T(8,128)(2,1)} %add_convert_fusion.5), channel_id=1, source_target_pairs={{0,2},{1,3},{2,0},{3,1},{4,6},{5,7},{6,4},{7,5},{8,10},{9,11},{10,... | collective-permute-start | bytes 1572872 | tf_op jit(solution)/shard_map/sum_mlp_1/ppermute | solution.py:105
  277.4 17.5 %collective-permute-start.37 = (bf16[2,32,4096]{2,1,0:T(8,128)(2,1)S(1)}, bf16[2,32,4096]{2,1,0:T(8,128)(2,1)S(1)}, u32[]{:S(2)}, u32[]{:S(2)}) collective-permute-start(bf16[2,32,4096]{2,1,0:T(8,128)(2,1)S(1)} %add_convert_fusion.4), channel_id=1, source_target_pairs={{0,2},{1,3},{2,0},{3,1},{4,6},{5,7},{6,4},{7,5},{8,10},{9,11},{10,... | collective-permute-start | bytes 1572872 | tf_op jit(solution)/shard_map/sum_in_1/ppermute | solution.py:105
  279.9 13.8 %collective-permute-start.38 = (bf16[1,128,1024]{2,1,0:T(8,128)(2,1)S(1)}, bf16[1,128,1024]{2,1,0:T(8,128)(2,1)S(1)}, u32[]{:S(2)}, u32[]{:S(2)}) collective-permute-start(bf16[1,128,1024]{2,1,0:T(8,128)(2,1)S(1)} %add_convert_fusion.8), channel_id=1, source_target_pairs={{0,4},{1,5},{2,6},{3,7},{4,0},{5,1},{6,2},{7,3},{8,12},{9,13},{10,... | collective-permute-start | bytes 786440 | tf_op jit(solution)/shard_map/sum_mlp_0/ppermute | solution.py:105
  295.4 15.2 %collective-permute-start.39 = (bf16[4,32,4224]{2,1,0:T(8,128)(2,1)S(1)}, bf16[4,32,4224]{2,1,0:T(8,128)(2,1)S(1)}, u32[]{:S(2)}, u32[]{:S(2)}) collective-permute-start(bf16[4,32,4224]{2,1,0:T(8,128)(2,1)S(1)} %pad_maximum_fusion.1), channel_id=1, source_target_pairs={{0,1},{1,0},{2,3},{3,2},{4,5},{5,4},{6,7},{7,6},{8,24},{9,25},{10,... | collective-permute-start | bytes 3244040 | tf_op jit(solution)/shard_map/sum_first_2/ppermute | solution.py:105
  297.6 13.1 %collective-permute-start.40 = (bf16[1,32,4096]{2,1,0:T(8,128)(2,1)S(1)}, bf16[1,32,4096]{2,1,0:T(8,128)(2,1)S(1)}, u32[]{:S(2)}, u32[]{:S(2)}) collective-permute-start(bf16[1,32,4096]{2,1,0:T(8,128)(2,1)S(1)} %add_convert_fusion.7), channel_id=1, source_target_pairs={{0,4},{1,5},{2,6},{3,7},{4,0},{5,1},{6,2},{7,3},{8,12},{9,13},{10,... | collective-permute-start | bytes 786440 | tf_op jit(solution)/shard_map/sum_in_0/ppermute | solution.py:105
  311.0 13.0 %collective-permute-start.41 = (bf16[2,32,4224]{2,1,0:T(8,128)(2,1)S(1)}, bf16[2,32,4224]{2,1,0:T(8,128)(2,1)S(1)}, u32[]{:S(2)}, u32[]{:S(2)}) collective-permute-start(bf16[2,32,4224]{2,1,0:T(8,128)(2,1)S(1)} %pad_maximum_fusion.2), channel_id=1, source_target_pairs={{0,2},{1,3},{2,0},{3,1},{4,6},{5,7},{6,4},{7,5},{8,10},{9,11},{10,... | collective-permute-start | bytes 1622024 | tf_op jit(solution)/shard_map/sum_first_1/ppermute | solution.py:105
  324.2 13.8 %collective-permute-start.42 = (bf16[1,32,4224]{2,1,0:T(8,128)(2,1)S(1)}, bf16[1,32,4224]{2,1,0:T(8,128)(2,1)S(1)}, u32[]{:S(2)}, u32[]{:S(2)}) collective-permute-start(bf16[1,32,4224]{2,1,0:T(8,128)(2,1)S(1)} %pad_maximum_fusion.3), channel_id=1, source_target_pairs={{0,4},{1,5},{2,6},{3,7},{4,0},{5,1},{6,2},{7,3},{8,12},{9,13},{10,... | collective-permute-start | bytes 811016 | tf_op jit(solution)/shard_map/sum_first_0/ppermute | solution.py:105
  (63 other events, 942.2 us)

commit v6 on v5

--- a/solution.py
+++ b/solution.py
@@ -22,6 +22,7 @@
 
 eps = 1e-06
 ANY = pl.BlockSpec(memory_space=pl.ANY)
+HBM = pl.BlockSpec(memory_space=pltpu.HBM)
 VMEM = pl.BlockSpec(memory_space=pltpu.VMEM)
 SMEM = pl.BlockSpec(memory_space=pltpu.SMEM)
 
@@ -164,6 +165,7 @@
         self.side = []
         self.count = keep_low.shape[0]
         self.width = keep_low.shape[-1]
+        self.owned = []
 
     def join(self, parts):
         half = self.plan.half
@@ -197,12 +199,42 @@
                 self.line.send(outgoing, self.plan.pairs(stage), f"sum_{self.name}_{stage}")
             )
 
+    def last(self):
+        self.line.wait(self.low[-1])
+        stages = self.plan.legs[0] + self.plan.legs[1]
+        outgoing = self.line.run(
+            lambda *parts: [
+                self.sum(index, index + 1, parts).astype(BF) for index in range(1, self.count)
+            ],
+            *self.low,
+        )
+        for index in range(1, self.count):
+            masks = [0, 0]
+            for bit, stage in enumerate(stages):
+                if index >> bit & 1:
+                    masks = [mask ^ order[stage] for mask, order in zip(masks, self.plan.orders)]
+            pairs = [(i, i ^ masks[1 if i & self.plan.core else 0]) for i in range(self.plan.devices)]
+            self.owned.append(
+                self.line.send(outgoing[index - 1], pairs, f"sum_{self.name}_last_{index}")
+            )
+
     def arrive(self):
-        self.line.wait(self.low[-1])
+        self.line.wait(self.low[-1], *self.owned)
 
     def result(self):
+        before = self.line.last
         self.arrive()
-        return self.line.run(lambda *parts: self.sum(0, 1, parts)[0].astype(F32), *self.low)
+        count = len(self.low)
+
+        def add(*parts):
+            summed = self.sum(0, 1, parts[:count]).astype(F32)
+            for part in parts[count:]:
+                summed = summed + part.astype(F32)
+            return summed[0]
+
+        result = self.line.run(add, *self.low, *self.owned)
+        self.line.last = before
+        return result
 
 
 def one_hot(order):
@@ -598,7 +630,7 @@
         fall_kernel,
         out_shape=[shape((count, FF), BF), shape((1, FF), F32)] + [grad] * 4,
         in_specs=[SMEM, SMEM, VMEM, ANY, VMEM] + [ANY] * 8,
-        out_specs=[ANY, VMEM] + [ANY] * 4,
+        out_specs=[HBM, VMEM] + [ANY] * 4,
         scratch_shapes=[
             pltpu.VMEM((BLOCKS, PIECE, D), BF),
             pltpu.VMEM((count, FF), BF),
@@ -616,8 +648,8 @@
 
 def back_kernel(
     order_ref, vec_ref, ghidden_ref, top_ref, middle_ref, w0, w1, w2, w3,
-    gmiddle_ref, sums_ref,
-    held, ghidden, middle, gsecond, gmiddle, sems, in_sems, out_sems,
+    gmiddle_ref, branch_ref, sums_ref,
+    held, ghidden, middle, gsecond, gmiddle, branch, sems, in_sems, out_sems,
 ):
     later = [
         pltpu.make_async_copy(ghidden_ref, ghidden, in_sems.at[0]),
@@ -644,9 +676,12 @@
         )
         copy.start()
         outs.append(copy)
+        branch[where, :] = total_grad.astype(BF)
         low = total_grad.astype(BF).astype(F32)
         for row, value in enumerate((grad * normed, grad, low, top)):
             sums_ref[row : row + 1, :] += jnp.sum(value, axis=0, keepdims=True)
+    outs.append(pltpu.make_async_copy(branch, branch_ref, out_sems.at[2]))
+    outs[-1].start()
     wait(outs)
 
 
@@ -655,18 +690,19 @@
     shape = jax.ShapeDtypeStruct
     return pl.pallas_call(
         back_kernel,
-        out_shape=[shape((count, D), F32), shape((8, D), F32)],
-        in_specs=[SMEM, VMEM, ANY, VMEM, ANY] + [ANY] * 4,
-        out_specs=[ANY, VMEM],
+        out_shape=[shape((count, D), F32), shape((count, D), BF), shape((8, D), F32)],
+        in_specs=[SMEM, VMEM, HBM, VMEM, HBM] + [ANY] * 4,
+        out_specs=[HBM, HBM, VMEM],
         scratch_shapes=[
             pltpu.VMEM((D, FF), BF),
             pltpu.VMEM((count, FF), BF),
             pltpu.VMEM((count, D), F32),
             pltpu.VMEM((count, D), F32),
             pltpu.VMEM((count, D), F32),
+            pltpu.VMEM((count, D), BF),
             pltpu.SemaphoreType.DMA((BLOCKS,)),
             pltpu.SemaphoreType.DMA((2,)),
-            pltpu.SemaphoreType.DMA((2,)),
+            pltpu.SemaphoreType.DMA((3,)),
         ],
         compiler_params=params(32),
         name="back",
@@ -674,32 +710,34 @@
 
 
 def unattend_kernel(
-    order_ref, vec_ref, x_ref, gmiddle_ref, project_ref, probs_ref, entry_ref, mixed_ref,
+    order_ref, vec_ref, x_ref, gmiddle_ref, branch_ref, project_ref, probs_ref, entry_ref, mixed_ref,
     w0, w1, w2, w3, f0, f1, f2, f3,
     ginputs_ref, sums_ref, g0, g1, g2, g3,
-    oheld, held, project, probs, both, turned, branch, gmixed, gproject, gentry, ginputs, grads,
+    oheld, held, project, probs, both, turned, gmiddle, branch, gmixed, gproject, gentry, ginputs, grads,
     osems, sems, in_sems, probs_sems, out_sems,
 ):
-    count = gmiddle_ref.shape[0]
+    count = x_ref.shape[0]
     groups = D // WIDE
     ocopies = fetches(order_ref, (w0, w1, w2, w3), oheld, osems, FF)
     load = [
         pltpu.make_async_copy(project_ref, project, in_sems.at[0]),
         pltpu.make_async_copy(entry_ref, both.at[0], in_sems.at[1]),
         pltpu.make_async_copy(mixed_ref, both.at[1], in_sems.at[2]),
+        pltpu.make_async_copy(branch_ref, branch, in_sems.at[3]),
+        pltpu.make_async_copy(gmiddle_ref, gmiddle, in_sems.at[4]),
     ]
     pieces = [
         pltpu.make_async_copy(probs_ref.at[i], probs.at[i], probs_sems.at[i])
         for i in range((count // SEQ) * groups)
     ]
     copies = fetches(order_ref, (f0, f1, f2, f3), held, sems)
-    start([load[2], *ocopies])
-    branch[...] = gmiddle_ref[...].astype(BF)
+    start([load[2], load[3], *ocopies])
     sums_ref[...] = jnp.zeros_like(sums_ref)
     apiece, rows, _ = g0.shape
     load[2].wait()
     start([load[0]])
     turned[1] = both[1].T
+    load[3].wait()
     for part in (3, 2, 1, 0):
         left = block_rows(order_ref, turned.at[1], part, apiece, rows)
         for i in range(D // TILE):
@@ -721,7 +759,7 @@
         scale = HEAD_DIM**-0.5
         pieces[i].wait()
         if i % 2 == 0:
-            start(pieces[i + 2 : i + 4] if i + 2 < len(pieces) else [load[1], *copies])
+            start(pieces[i + 2 : i + 4] if i + 2 < len(pieces) else [load[1], load[4], *copies])
         queries = stacked(project[where, span(group, WIDE)] * BF(scale))
         keys = project[where, span(groups + group, WIDE)]
         values = project[where, span(2 * groups + group, WIDE)]
@@ -752,8 +790,8 @@
         copy = pltpu.make_async_copy(grads.at[part], (g0, g1, g2, g3)[part], out_sems.at[part])
         copy.start()
         outs.append(copy)
-    for copy in copies:
-        copy.wait()
+    wait(copies)
+    load[4].wait()
     chunk = count // 2
     for half in range(2):
         where = span(half, chunk)
@@ -762,7 +800,7 @@
         normed, inverse = norm_parts(x_ref[where, :].astype(F32))
         grad = gentry[where, :]
         back = norm_back(grad * vec_ref[0:1, :], normed, inverse)
-        ginputs[where, :] = gmiddle_ref[where, :] + back
+        ginputs[where, :] = gmiddle[where, :] + back
         copy = pltpu.make_async_copy(
             ginputs.at[where, :], ginputs_ref.at[where, :], out_sems.at[4 + half]
         )
@@ -774,14 +812,14 @@
         copy.wait()
 
 
-def unattend(order, vec, x, gmiddle, project, probs, entry, mixed, win, first):
+def unattend(order, vec, x, gmiddle, branch, project, probs, entry, mixed, win, first):
     count = gmiddle.shape[0]
     shape = jax.ShapeDtypeStruct
     grad = shape((BLOCKS // 4, D // BLOCKS, 4 * D), BF)
     return pl.pallas_call(
         unattend_kernel,
         out_shape=[shape((count, D), F32), shape((8, D), F32)] + [grad] * 4,
-        in_specs=[SMEM] + [VMEM] * 3 + [ANY] * 12,
+        in_specs=[SMEM] + [VMEM] * 2 + [HBM] * 6 + [ANY] * 8,
         out_specs=[ANY, VMEM] + [ANY] * 4,
         scratch_shapes=[
             pltpu.VMEM((D, D), BF),
@@ -790,6 +828,7 @@
             pltpu.VMEM(probs.shape, BF),
             pltpu.VMEM((2, count, D), BF),
             pltpu.VMEM((2, D, count), BF),
+            pltpu.VMEM((count, D), F32),
             pltpu.VMEM((count, D), BF),
             pltpu.VMEM((count, D), BF),
             pltpu.VMEM((count, 3 * D), BF),
@@ -798,13 +837,13 @@
             pltpu.VMEM((4, *grad.shape), BF),
             pltpu.SemaphoreType.DMA((BLOCKS,)),
             pltpu.SemaphoreType.DMA((BLOCKS,)),
-            pltpu.SemaphoreType.DMA((3,)),
+            pltpu.SemaphoreType.DMA((5,)),
             pltpu.SemaphoreType.DMA((probs.shape[0],)),
             pltpu.SemaphoreType.DMA((6,)),
         ],
         compiler_params=params(56),
         name="unattend",
-    )(order, vec, x, gmiddle, project, probs, entry, mixed, *win, *first)
+    )(order, vec, x, gmiddle, branch, project, probs, entry, mixed, *win, *first)
 
 
 def finish_kernel(
@@ -951,13 +990,12 @@
     sum_mlp.start(3)
     mlp_parts = to_blocks(order, mlp.parts()) + to_blocks(late_order, late.parts())
     ghidden, grad_bias_in, *grads = line.run(fall, numbers, spot, top, slope, second, *mlp_parts)
-    sum_mlp.arrive()
     sum_in = Scatter(plan, line, "in", from_blocks(order, grads))
     sum_mlp.start(2)
     sum_in.start(3)
-    gmiddle, sums = line.run(back, numbers, vec, ghidden, top, middle, *win_parts)
+    gmiddle, branch, sums = line.run(back, numbers, vec, ghidden, top, middle, *win_parts)
     grad_inputs, sums_one, *grads = line.run(
-        unattend, numbers, vec, x, gmiddle, project, probs, entry, mixed, win_parts, first_parts
+        unattend, numbers, vec, x, gmiddle, branch, project, probs, entry, mixed, win_parts, first_parts
     )
     sum_mlp.arrive()
     sum_in.arrive()
@@ -987,9 +1025,8 @@
     sum_in.start(0)
     grad_mlp = sum_mlp.result()
     sum_in.arrive()
-    sum_first.start(1)
+    sum_first.last()
     grad_in = sum_in.result()
-    sum_first.start(0)
     grad_first = sum_first.result()
     grad_small = grad_first[:, 4 * D :].reshape(1, -1)[:, :small_dev]
     return (

time: 348 us -> 342 us (0.983)
  the two profiles are of different devices: /device:TPU:0 before, /device:TPU:8 now
where the time goes in v6:
time: 342 us; the launch traced here: 336 us
  waiting for transfers between devices  135 us (39%)
  Pallas kernels  97 us (28%)
  starting transfers between devices  42.2 us (12%)
  other arithmetic  30.4 us (9%)
  local copies, waits for them, and re-layouts  28.9 us (8%)
    ppermute x44, waiting for transfers between devices, send(): return lax.ppermute(self.tie(array)[0], AXES, pairs)  135 us
    ppermute x44, starting transfers between devices, send(): return lax.ppermute(self.tie(array)[0], AXES, pairs)  42.2 us
    pallas_call x1, Pallas kernels, unattend(): pl.pallas_call(unattend_kernel, out_shape=[shape((count, D), F32), shape(...  25.5 us
    unnamed x134, local copies, waits for them, and re-layouts  19.8 us
    pallas_call x1, Pallas kernels, rise(): pl.pallas_call(rise_kernel, out_shape=[shape((count, FF), BF)] * 2 + [gra...  18.4 us
    pallas_call x1, Pallas kernels, fall(): pl.pallas_call(fall_kernel, out_shape=[shape((count, FF), BF), shape((1,...  14.7 us
    pallas_call x1, Pallas kernels, back(): pl.pallas_call(back_kernel, out_shape=[shape((count, D), F32), shape((cou...  10.4 us
    convert_element_type x6, other arithmetic, start(): self.sum(low, low + self.count, parts).astype(BF)  9.25 us
  transfers between devices with their start and end apart: 44, of which 22 were waited for; matrix products, arithmetic and copies ran while one was open for 10% of the time, Pallas kernels for 29%

profile of v6, /device:TPU:8, one launch (start us, length us, event | category | flops | bytes accessed | tf_op | source)
XLA Modules:
  0.0 335.9 jit_solution(17038023350054995049)
XLA Ops:
  3.7 2.7 collective-permute-start
  20.1 11.5 %collective-permute-done.2 = bf16[2,32,3200]{2,1,0:T(8,128)(2,1)S(1)} collective-permute-done((bf16[2,32,3200]{2,1,0:T(8,128)(2,1)S(1)}, bf16[2,32,3200]{2,1,0:T(8,128)(2,1)S(1)}, u32[]{:S(2)}, u32[]{:S(2)}) %collective-permute-start.2) | collective-permute-done | bytes 409632 | tf_op jit(solution)/shard_map/gather_qkv_1/ppermute | solution.py:106
  31.7 3.5 %collective-permute-done.4 = bf16[1,32,5120]{2,1,0:T(8,128)(2,1)S(1)} collective-permute-done((bf16[1,32,5120]{2,1,0:T(8,128)(2,1)S(1)}, bf16[1,32,5120]{2,1,0:T(8,128)(2,1)S(1)}, u32[]{:S(2)}, u32[]{:S(2)}) %collective-permute-start.4) | collective-permute-done | bytes 327712 | tf_op jit(solution)/shard_map/gather_in_0/ppermute | solution.py:106
  38.2 10.8 %collective-permute-done.5 = bf16[4,32,3200]{2,1,0:T(8,128)(2,1)S(1)} collective-permute-done((bf16[4,32,3200]{2,1,0:T(8,128)(2,1)S(1)}, bf16[4,32,3200]{2,1,0:T(8,128)(2,1)S(1)}, u32[]{:S(2)}, u32[]{:S(2)}) %collective-permute-start.5) | collective-permute-done | bytes 819232 | tf_op jit(solution)/shard_map/gather_qkv_2/ppermute | solution.py:106
  50.8 15.0 %collective-permute-done.8 = bf16[2,32,5120]{2,1,0:T(8,128)(2,1)S(1)} collective-permute-done((bf16[2,32,5120]{2,1,0:T(8,128)(2,1)S(1)}, bf16[2,32,5120]{2,1,0:T(8,128)(2,1)S(1)}, u32[]{:S(2)}, u32[]{:S(2)}) %collective-permute-start.8) | collective-permute-done | bytes 655392 | tf_op jit(solution)/shard_map/gather_in_1/ppermute | solution.py:106
  65.8 4.7 %collective-permute-done.6.w1.f1 = bf16[8,32,3200]{2,1,0:T(8,128)(2,1)} collective-permute-done((bf16[8,32,3200]{2,1,0:T(8,128)(2,1)S(1)}, bf16[8,32,3200]{2,1,0:T(8,128)(2,1)}, u32[]{:S(2)}, u32[]{:S(2)}) %collective-permute-start.6) | collective-permute-done | bytes 1638432 | tf_op jit(solution)/shard_map/gather_qkv_3/ppermute | solution.py:106
  79.4 8.0 %project.1 = (bf16[512,1024]{1,0:T(8,128)(2,1)S(1)}, bf16[512,3072]{1,0:T(8,128)(2,1)S(1)}) custom-call(s32[32]{0:T(128)S(1)} %fusion.26.order_ref, f32[8,1024]{1,0:T(8,128)S(1)} %slice.369.vec_ref, bf16[512,1024]{1,0:T(8,128)(2,1)S(1)} %bitcast.67, bf16[8,32,3200]{2,1,0:T(8,128)(2,1)S(1)} %constant_dynamic-update-slice_fusion.10.w0.f0, ...), custom_call_target="tpu_custom_call" | custom-call | tf_op jit(solution)/shard_map/project/pallas_call | solution.py:370
  87.4 2.8 collective-permute-done.11
  99.1 6.3 %attend.1 = (bf16[8,1024,256]{2,1,0:T(8,128)(2,1)S(1)}, bf16[512,1024]{1,0:T(8,128)(2,1)S(1)}) custom-call(bf16[512,3072]{1,0:T(8,128)(2,1)S(1)} %copy-done.5, s32[2,256]{1,0:T(2,128)S(1)} %copy-done.38, s32[512,1]{1,0:T(8,128)S(1)} %bitcast.69), custom_call_target="tpu_custom_call" | custom-call | tf_op jit(solution)/shard_map/attend/pallas_call | solution.py:412
  107.5 6.6 %collective-permute-done.14 = bf16[2,128,512]{2,1,0:T(8,128)(2,1)S(1)} collective-permute-done((bf16[2,128,512]{2,1,0:T(8,128)(2,1)S(1)}, bf16[2,128,512]{2,1,0:T(8,128)(2,1)S(1)}, u32[]{:S(2)}, u32[]{:S(2)}) %collective-permute-start.14) | collective-permute-done | bytes 262176 | tf_op jit(solution)/shard_map/gather_mlp_1/ppermute | solution.py:106
  114.0 4.7 %collective-permute-done.15 = bf16[4,128,512]{2,1,0:T(8,128)(2,1)} collective-permute-done((bf16[4,128,512]{2,1,0:T(8,128)(2,1)}, bf16[4,128,512]{2,1,0:T(8,128)(2,1)}, u32[]{:S(2)}, u32[]{:S(2)}) %collective-permute-start.15) | collective-permute-done | bytes 524320 | tf_op jit(solution)/shard_map/gather_late_2/ppermute | solution.py:106
  118.7 6.3 %collective-permute-done.12.w1 = bf16[8,32,5120]{2,1,0:T(8,128)(2,1)} collective-permute-done((bf16[8,32,5120]{2,1,0:T(8,128)(2,1)S(1)}, bf16[8,32,5120]{2,1,0:T(8,128)(2,1)}, u32[]{:S(2)}, u32[]{:S(2)}) %collective-permute-start.12) | collective-permute-done | bytes 2621472 | tf_op jit(solution)/shard_map/gather_in_3/ppermute | solution.py:106
  126.6 3.5 %collective-permute-done.16.w3 = bf16[8,32,5120]{2,1,0:T(8,128)(2,1)S(1)} collective-permute-done((bf16[8,32,5120]{2,1,0:T(8,128)(2,1)}, bf16[8,32,5120]{2,1,0:T(8,128)(2,1)S(1)}, u32[]{:S(2)}, u32[]{:S(2)}) %collective-permute-start.16) | collective-permute-done | bytes 2621472 | tf_op jit(solution)/shard_map/gather_in_swap_second/ppermute | solution.py:106
  130.1 5.1 %settle.1 = (f32[512,1024]{1,0:T(8,128)S(1)}, bf16[512,1024]{1,0:T(8,128)(2,1)S(1)}) custom-call(s32[32]{0:T(128)S(1)} %fusion.26.order_ref, f32[8,1024]{1,0:T(8,128)S(1)} %slice.369.vec_ref, bf16[512,1024]{1,0:T(8,128)(2,1)S(1)} %bitcast.68, bf16[512,1024]{1,0:T(8,128)(2,1)S(1)} %get-tuple-element.363.mixed_ref, ...), custom_call_target="tpu_custom_call" | custom-call | tf_op jit(solution)/shard_map/settle/pallas_call | solution.py:454
  141.3 18.4 %rise.1 = (bf16[512,4096]{1,0:T(8,128)(2,1)}, bf16[512,4096]{1,0:T(8,128)(2,1)}, bf16[8,128,1024]{2,1,0:T(8,128)(2,1)S(1)}, bf16[8,128,1024]{2,1,0:T(8,128)(2,1)...) custom-call(s32[32]{0:T(128)S(1)} %fusion.26.order_ref, f32[1,4096]{1,0:T(1,128)S(1)} %bitcast.70, ...), custom_call_target="tpu_custom_call" | custom-call | tf_op jit(solution)/shard_map/rise/pallas_call | solution.py:515
  159.8 5.1 %collective-permute-done.21.l1 = bf16[8,128,512]{2,1,0:T(8,128)(2,1)} collective-permute-done((bf16[8,128,512]{2,1,0:T(8,128)(2,1)S(1)}, bf16[8,128,512]{2,1,0:T(8,128)(2,1)}, u32[]{:S(2)}, u32[]{:S(2)}) %collective-permute-start.21) | collective-permute-done | bytes 1048608 | tf_op jit(solution)/shard_map/gather_late_3/ppermute | solution.py:106
  165.9 3.3 collective-permute-done.25
  169.3 2.7 add.197
  173.6 14.7 %fall.1 = (bf16[512,4096]{1,0:T(8,128)(2,1)}, f32[1,4096]{1,0:T(1,128)S(1)}, bf16[8,32,4096]{2,1,0:T(8,128)(2,1)S(1)}, bf16[8,32,4096]{2,1,0:T(8,128)(2,1)}, bf1...) custom-call(s32[32]{0:T(128)S(1)} %fusion.26.order_ref, s32[32]{0:T(128)S(1)} %select_reduce_fusion.spot_ref, ...), custom_call_target="tpu_custom_call" | custom-call | tf_op jit(solution)/shard_map/fall/pallas_call | solution.py:629
  188.4 9.6 %collective-permute-done.26 = bf16[8,128,1024]{2,1,0:T(8,128)(2,1)S(1)} collective-permute-done((bf16[8,128,1024]{2,1,0:T(8,128)(2,1)S(1)}, bf16[8,128,1024]{2,1,0:T(8,128)(2,1)S(1)}, u32[]{:S(2)}, u32[]{:S(2)}) %collective-permute-start.26) | collective-permute-done | bytes 2097184 | tf_op jit(solution)/shard_map/sum_mlp_3/ppermute | solution.py:106
  207.2 10.4 %back.1 = (f32[512,1024]{1,0:T(8,128)S(1)}, bf16[512,1024]{1,0:T(8,128)(2,1)S(1)}, f32[8,1024]{1,0:T(8,128)S(1)}) custom-call(s32[32]{0:T(128)S(1)} %fusion.26.order_ref, f32[8,1024]{1,0:T(8,128)S(1)} %slice.369.vec_ref, bf16[512,4096]{1,0:T(8,128)(2,1)S(1)} %copy-done.17, bf16[512,1024]{1,0:T(8,128)(2,1)S(1)} %bitcast_select_fusion.top_ref, ...), custom_call_target="tpu_custom_call" | custom-call | tf_op jit(solution)/shard_map/back/pallas_call | solution.py:691
  220.0 25.5 %unattend.1 = (f32[512,1024]{1,0:T(8,128)}, f32[8,1024]{1,0:T(8,128)}, bf16[8,32,4096]{2,1,0:T(8,128)(2,1)}, bf16[8,32,4096]{2,1,0:T(8,128)(2,1)}, bf16[8,32,409...) custom-call(s32[32]{0:T(128)} %copy-done.36, f32[8,1024]{1,0:T(8,128)} %copy-done.32, bf16[512,1024]{1,0:T(8,128)(2,1)} %bitcast.66, ...), custom_call_target="tpu_custom_call" | custom-call | tf_op jit(solution)/shard_map/unattend/pallas_call | solution.py:819
  247.6 2.6 add_convert_fusion.1
  257.2 8.6 %finish.1 = bf16[512,1024]{1,0:T(8,128)(2,1)} custom-call(s32[32]{0:T(128)S(1)} %select_reduce_fusion.spot_ref, f32[8,1024]{1,0:T(8,128)S(1)} %copy-done.33, f32[512,1024]{1,0:T(8,128)S(1)} %copy-done.10, bf16[512,4096]{1,0:T(8,128)(2,1)S(1)} %copy-done.15, bf16[8,128,512]{2,1,0:T(8,128)(2,1)S(1)} %copy-done.14, ...), custom_call_target="tpu_custom_call" | custom-call | tf_op jit(solution)/shard_map/finish/pallas_call | solution.py:877
  265.7 6.4 %collective-permute-done.36 = bf16[4,32,4096]{2,1,0:T(8,128)(2,1)S(1)} collective-permute-done((bf16[4,32,4096]{2,1,0:T(8,128)(2,1)S(1)}, bf16[4,32,4096]{2,1,0:T(8,128)(2,1)S(1)}, u32[]{:S(2)}, u32[]{:S(2)}) %collective-permute-start.36) | collective-permute-done | bytes 1048608 | tf_op jit(solution)/shard_map/sum_in_2/ppermute | solution.py:106
  277.2 7.8 %collective-permute-done.38 = bf16[1,128,1024]{2,1,0:T(8,128)(2,1)S(1)} collective-permute-done((bf16[1,128,1024]{2,1,0:T(8,128)(2,1)S(1)}, bf16[1,128,1024]{2,1,0:T(8,128)(2,1)S(1)}, u32[]{:S(2)}, u32[]{:S(2)}) %collective-permute-start.38) | collective-permute-done | bytes 262176 | tf_op jit(solution)/shard_map/sum_mlp_0/ppermute | solution.py:106
  285.0 6.2 %collective-permute-done.37 = bf16[2,32,4096]{2,1,0:T(8,128)(2,1)S(1)} collective-permute-done((bf16[2,32,4096]{2,1,0:T(8,128)(2,1)S(1)}, bf16[2,32,4096]{2,1,0:T(8,128)(2,1)S(1)}, u32[]{:S(2)}, u32[]{:S(2)}) %collective-permute-start.37) | collective-permute-done | bytes 524320 | tf_op jit(solution)/shard_map/sum_in_1/ppermute | solution.py:106
  294.1 3.2 collective-permute-start.40
  299.9 6.0 %collective-permute-done.40 = bf16[1,32,4096]{2,1,0:T(8,128)(2,1)S(1)} collective-permute-done((bf16[1,32,4096]{2,1,0:T(8,128)(2,1)S(1)}, bf16[1,32,4096]{2,1,0:T(8,128)(2,1)S(1)}, u32[]{:S(2)}, u32[]{:S(2)}) %collective-permute-start.40) | collective-permute-done | bytes 262176 | tf_op jit(solution)/shard_map/sum_in_0/ppermute | solution.py:106
  307.5 3.4 %collective-permute-start.41 = (bf16[1,32,4224]{2,1,0:T(8,128)(2,1)S(1)}, bf16[1,32,4224]{2,1,0:T(8,128)(2,1)S(1)}, u32[]{:S(2)}, u32[]{:S(2)}) collective-permute-start(bf16[1,32,4224]{2,1,0:T(8,128)(2,1)S(1)} %get-tuple-element.436), channel_id=1, source_target_pairs={{0,4},{1,5},{2,6},{3,7},{4,0},{5,1},{6,2},{7,3},{8,12},{9,13},{10,... | collective-permute-start | bytes 811016 | tf_op jit(solution)/shard_map/sum_first_last_1/ppermute | solution.py:106
  315.0 9.6 %collective-permute-done.41 = bf16[1,32,4224]{2,1,0:T(8,128)(2,1)S(1)} collective-permute-done((bf16[1,32,4224]{2,1,0:T(8,128)(2,1)S(1)}, bf16[1,32,4224]{2,1,0:T(8,128)(2,1)S(1)}, u32[]{:S(2)}, u32[]{:S(2)}) %collective-permute-start.41) | collective-permute-done | bytes 270368 | tf_op jit(solution)/shard_map/sum_first_last_1/ppermute | solution.py:106
  324.6 7.7 %collective-permute-done.43 = bf16[1,32,4224]{2,1,0:T(8,128)(2,1)S(1)} collective-permute-done((bf16[1,32,4224]{2,1,0:T(8,128)(2,1)S(1)}, bf16[1,32,4224]{2,1,0:T(8,128)(2,1)S(1)}, u32[]{:S(2)}, u32[]{:S(2)}) %collective-permute-start.43) | collective-permute-done | bytes 270368 | tf_op jit(solution)/shard_map/sum_first_last_3/ppermute | solution.py:106
  (279 shorter events, 91.3 us)
Async XLA Ops:
  15.0 16.6 %collective-permute-start.2 = (bf16[2,32,3200]{2,1,0:T(8,128)(2,1)S(1)}, bf16[2,32,3200]{2,1,0:T(8,128)(2,1)S(1)}, u32[]{:S(2)}, u32[]{:S(2)}) collective-permute-start(bf16[2,32,3200]{2,1,0:T(8,128)(2,1)S(1)} %constant_dynamic-update-slice_fusion), channel_id=1, source_target_pairs={{0,2},{1,3},{2,0},{3,1},{4,6},{5,7},{6,4},{7,5},{8,10},{9,11},{10,... | collective-permute-start | bytes 1228808 | tf_op jit(solution)/shard_map/gather_qkv_1/ppermute | solution.py:106
  16.4 18.8 %collective-permute-start.3 = (bf16[2,128,512]{2,1,0:T(8,128)(2,1)S(1)}, bf16[2,128,512]{2,1,0:T(8,128)(2,1)S(1)}, u32[]{:S(2)}, u32[]{:S(2)}) collective-permute-start(bf16[2,128,512]{2,1,0:T(8,128)(2,1)S(1)} %constant_dynamic-update-slice_fusion.2), channel_id=1, source_target_pairs={{0,16},{1,17},{2,18},{3,19},{4,20},{5,21},{6,22},{7,23},{8,9},{9,8... | collective-permute-start | bytes 786440 | tf_op jit(solution)/shard_map/gather_late_1/ppermute | solution.py:106
  18.1 17.1 %collective-permute-start.4 = (bf16[1,32,5120]{2,1,0:T(8,128)(2,1)S(1)}, bf16[1,32,5120]{2,1,0:T(8,128)(2,1)S(1)}, u32[]{:S(2)}, u32[]{:S(2)}) collective-permute-start(bf16[1,32,5120]{2,1,0:T(8,128)(2,1)S(1)} %maximum_bitcast_fusion), channel_id=1, source_target_pairs={{0,4},{1,5},{2,6},{3,7},{4,0},{5,1},{6,2},{7,3},{8,12},{9,13},{10,... | collective-permute-start | bytes 983048 | tf_op jit(solution)/shard_map/gather_in_0/ppermute | solution.py:106
  36.7 12.3 %collective-permute-start.5 = (bf16[4,32,3200]{2,1,0:T(8,128)(2,1)S(1)}, bf16[4,32,3200]{2,1,0:T(8,128)(2,1)S(1)}, u32[]{:S(2)}, u32[]{:S(2)}) collective-permute-start(bf16[4,32,3200]{2,1,0:T(8,128)(2,1)S(1)} %constant_dynamic-update-slice_fusion.4), channel_id=1, source_target_pairs={{0,1},{1,0},{2,3},{3,2},{4,5},{5,4},{6,7},{7,6},{8,24},{9,25},{10,... | collective-permute-start | bytes 2457608 | tf_op jit(solution)/shard_map/gather_qkv_2/ppermute | solution.py:106
  49.2 21.3 %collective-permute-start.6 = (bf16[8,32,3200]{2,1,0:T(8,128)(2,1)S(1)}, bf16[8,32,3200]{2,1,0:T(8,128)(2,1)}, u32[]{:S(2)}, u32[]{:S(2)}) collective-permute-start(bf16[8,32,3200]{2,1,0:T(8,128)(2,1)S(1)} %constant_dynamic-update-slice_fusion.10.w0.f0), channel_id=1, source_target_pairs={{0,16},{1,17},{2,18},{3,19},{4,20},{5,21},{6,22},{7,23},{8,9},{9,8... | collective-permute-start | bytes 4915208 | tf_op jit(solution)/shard_map/gather_qkv_3/ppermute | solution.py:106
  50.8 15.0 %collective-permute-start.8 = (bf16[2,32,5120]{2,1,0:T(8,128)(2,1)S(1)}, bf16[2,32,5120]{2,1,0:T(8,128)(2,1)S(1)}, u32[]{:S(2)}, u32[]{:S(2)}) collective-permute-start(bf16[2,32,5120]{2,1,0:T(8,128)(2,1)S(1)} %constant_dynamic-update-slice_fusion.6), channel_id=1, source_target_pairs={{0,2},{1,3},{2,0},{3,1},{4,6},{5,7},{6,4},{7,5},{8,10},{9,11},{10,... | collective-permute-start | bytes 1966088 | tf_op jit(solution)/shard_map/gather_in_1/ppermute | solution.py:106
  50.8 24.9 %collective-permute-start.7 = (bf16[8,32,3200]{2,1,0:T(8,128)(2,1)S(1)}, bf16[8,32,3200]{2,1,0:T(8,128)(2,1)}, u32[]{:S(2)}, u32[]{:S(2)}) collective-permute-start(bf16[8,32,3200]{2,1,0:T(8,128)(2,1)S(1)} %constant_dynamic-update-slice_fusion.10.w0.f0), channel_id=1, source_target_pairs={{0,8},{1,9},{2,10},{3,11},{4,12},{5,13},{6,14},{7,15},{8,0},{9,1},... | collective-permute-start | bytes 4915208 | tf_op jit(solution)/shard_map/gather_qkv_swap_first/ppermute | solution.py:106
  72.3 17.9 %collective-permute-start.11 = (bf16[4,32,5120]{2,1,0:T(8,128)(2,1)}, bf16[4,32,5120]{2,1,0:T(8,128)(2,1)}, u32[]{:S(2)}, u32[]{:S(2)}) collective-permute-start(bf16[4,32,5120]{2,1,0:T(8,128)(2,1)} %constant_dynamic-update-slice_fusion.12), channel_id=1, source_target_pairs={{0,1},{1,0},{2,3},{3,2},{4,5},{5,4},{6,7},{7,6},{8,24},{9,25},{10,... | collective-permute-start | bytes 3932168 | tf_op jit(solution)/shard_map/gather_in_2/ppermute | solution.py:106
  73.8 13.6 %collective-permute-start.10 = (bf16[1,128,512]{2,1,0:T(8,128)(2,1)S(1)}, bf16[1,128,512]{2,1,0:T(8,128)(2,1)S(1)}, u32[]{:S(2)}, u32[]{:S(2)}) collective-permute-start(bf16[1,128,512]{2,1,0:T(8,128)(2,1)S(1)} %get-tuple-element.271), channel_id=1, source_target_pairs={{0,4},{1,5},{2,6},{3,7},{4,0},{5,1},{6,2},{7,3},{8,12},{9,13},{10,... | collective-permute-start | bytes 393224 | tf_op jit(solution)/shard_map/gather_mlp_0/ppermute | solution.py:106
  93.1 25.6 %collective-permute-start.13 = (bf16[8,32,5120]{2,1,0:T(8,128)(2,1)S(1)}, bf16[8,32,5120]{2,1,0:T(8,128)(2,1)}, u32[]{:S(2)}, u32[]{:S(2)}) collective-permute-start(bf16[8,32,5120]{2,1,0:T(8,128)(2,1)S(1)} %constant_dynamic-update-slice_fusion.14.w0), channel_id=1, source_target_pairs={{0,8},{1,9},{2,10},{3,11},{4,12},{5,13},{6,14},{7,15},{8,0},{9,1},... | collective-permute-start | bytes 7864328 | tf_op jit(solution)/shard_map/gather_in_swap_first/ppermute | solution.py:106
  93.1 31.8 %collective-permute-start.12 = (bf16[8,32,5120]{2,1,0:T(8,128)(2,1)S(1)}, bf16[8,32,5120]{2,1,0:T(8,128)(2,1)}, u32[]{:S(2)}, u32[]{:S(2)}) collective-permute-start(bf16[8,32,5120]{2,1,0:T(8,128)(2,1)S(1)} %constant_dynamic-update-slice_fusion.14.w0), channel_id=1, source_target_pairs={{0,16},{1,17},{2,18},{3,19},{4,20},{5,21},{6,22},{7,23},{8,9},{9,8... | collective-permute-start | bytes 7864328 | tf_op jit(solution)/shard_map/gather_in_3/ppermute | solution.py:106
  94.8 23.9 %collective-permute-start.15 = (bf16[4,128,512]{2,1,0:T(8,128)(2,1)}, bf16[4,128,512]{2,1,0:T(8,128)(2,1)}, u32[]{:S(2)}, u32[]{:S(2)}) collective-permute-start(bf16[4,128,512]{2,1,0:T(8,128)(2,1)} %constant_dynamic-update-slice_fusion.8), channel_id=1, source_target_pairs={{0,4},{1,5},{2,6},{3,7},{4,0},{5,1},{6,2},{7,3},{8,12},{9,13},{10,... | collective-permute-start | bytes 1572872 | tf_op jit(solution)/shard_map/gather_late_2/ppermute | solution.py:106
  97.1 17.0 %collective-permute-start.14 = (bf16[2,128,512]{2,1,0:T(8,128)(2,1)S(1)}, bf16[2,128,512]{2,1,0:T(8,128)(2,1)S(1)}, u32[]{:S(2)}, u32[]{:S(2)}) collective-permute-start(bf16[2,128,512]{2,1,0:T(8,128)(2,1)S(1)} %constant_dynamic-update-slice_fusion.16), channel_id=1, source_target_pairs={{0,2},{1,3},{2,0},{3,1},{4,6},{5,7},{6,4},{7,5},{8,10},{9,11},{10,... | collective-permute-start | bytes 786440 | tf_op jit(solution)/shard_map/gather_mlp_1/ppermute | solution.py:106
  137.9 21.8 %collective-permute-start.19 = (bf16[8,128,512]{2,1,0:T(8,128)(2,1)S(1)}, bf16[8,128,512]{2,1,0:T(8,128)(2,1)S(1)}, u32[]{:S(2)}, u32[]{:S(2)}) collective-permute-start(bf16[8,128,512]{2,1,0:T(8,128)(2,1)S(1)} %constant_dynamic-update-slice_fusion.22.m0), channel_id=1, source_target_pairs={{0,8},{1,9},{2,10},{3,11},{4,12},{5,13},{6,14},{7,15},{8,0},{9,1},... | collective-permute-start | bytes 3145736 | tf_op jit(solution)/shard_map/gather_mlp_swap_first/ppermute | solution.py:106
  138.1 21.6 %collective-permute-start.18 = (bf16[8,128,512]{2,1,0:T(8,128)(2,1)S(1)}, bf16[8,128,512]{2,1,0:T(8,128)(2,1)}, u32[]{:S(2)}, u32[]{:S(2)}) collective-permute-start(bf16[8,128,512]{2,1,0:T(8,128)(2,1)S(1)} %constant_dynamic-update-slice_fusion.22.m0), channel_id=1, source_target_pairs={{0,16},{1,17},{2,18},{3,19},{4,20},{5,21},{6,22},{7,23},{8,9},{9,8... | collective-permute-start | bytes 3145736 | tf_op jit(solution)/shard_map/gather_mlp_3/ppermute | solution.py:106
  139.6 25.2 %collective-permute-start.21 = (bf16[8,128,512]{2,1,0:T(8,128)(2,1)S(1)}, bf16[8,128,512]{2,1,0:T(8,128)(2,1)}, u32[]{:S(2)}, u32[]{:S(2)}) collective-permute-start(bf16[8,128,512]{2,1,0:T(8,128)(2,1)S(1)} %constant_dynamic-update-slice_fusion.20.l0), channel_id=1, source_target_pairs={{0,2},{1,3},{2,0},{3,1},{4,6},{5,7},{6,4},{7,5},{8,10},{9,11},{10,... | collective-permute-start | bytes 3145736 | tf_op jit(solution)/shard_map/gather_late_3/ppermute | solution.py:106
  139.6 25.2 %collective-permute-start.20 = (bf16[8,128,512]{2,1,0:T(8,128)(2,1)S(1)}, bf16[8,128,512]{2,1,0:T(8,128)(2,1)}, u32[]{:S(2)}, u32[]{:S(2)}) collective-permute-start(bf16[8,128,512]{2,1,0:T(8,128)(2,1)S(1)} %constant_dynamic-update-slice_fusion.20.l0), channel_id=1, source_target_pairs={{0,8},{1,9},{2,10},{3,11},{4,12},{5,13},{6,14},{7,15},{8,0},{9,1},... | collective-permute-start | bytes 3145736 | tf_op jit(solution)/shard_map/gather_late_swap_first/ppermute | solution.py:106
  165.4 23.0 %collective-permute-start.24 = (bf16[8,128,1024]{2,1,0:T(8,128)(2,1)}, bf16[8,128,1024]{2,1,0:T(8,128)(2,1)S(1)}, u32[]{:S(2)}, u32[]{:S(2)}) collective-permute-start(bf16[8,128,1024]{2,1,0:T(8,128)(2,1)} %get-tuple-element.313), channel_id=1, source_target_pairs={{0,8},{1,9},{2,10},{3,11},{4,12},{5,13},{6,14},{7,15},{8,0},{9,1},... | collective-permute-start | bytes 6291464 | tf_op jit(solution)/shard_map/sum_mlp_swap_low/ppermute | solution.py:106
  171.9 26.1 %collective-permute-start.26 = (bf16[8,128,1024]{2,1,0:T(8,128)(2,1)S(1)}, bf16[8,128,1024]{2,1,0:T(8,128)(2,1)S(1)}, u32[]{:S(2)}, u32[]{:S(2)}) collective-permute-start(bf16[8,128,1024]{2,1,0:T(8,128)(2,1)S(1)} %add.197), channel_id=1, source_target_pairs={{0,16},{1,17},{2,18},{3,19},{4,20},{5,21},{6,22},{7,23},{8,9},{9,8... | collective-permute-start | bytes 6291464 | tf_op jit(solution)/shard_map/sum_mlp_3/ppermute | solution.py:106
  202.9 43.7 %collective-permute-start.29 = (bf16[8,32,4096]{2,1,0:T(8,128)(2,1)}, bf16[8,32,4096]{2,1,0:T(8,128)(2,1)}, u32[]{:S(2)}, u32[]{:S(2)}) collective-permute-start(bf16[8,32,4096]{2,1,0:T(8,128)(2,1)} %add.200), channel_id=1, source_target_pairs={{0,16},{1,17},{2,18},{3,19},{4,20},{5,21},{6,22},{7,23},{8,9},{9,8... | collective-permute-start | bytes 6291464 | tf_op jit(solution)/shard_map/sum_in_3/ppermute | solution.py:106
  204.2 43.1 %collective-permute-start.31 = (bf16[8,32,4096]{2,1,0:T(8,128)(2,1)}, bf16[8,32,4096]{2,1,0:T(8,128)(2,1)}, u32[]{:S(2)}, u32[]{:S(2)}) collective-permute-start(bf16[8,32,4096]{2,1,0:T(8,128)(2,1)} %get-tuple-element.379), channel_id=1, source_target_pairs={{0,8},{1,9},{2,10},{3,11},{4,12},{5,13},{6,14},{7,15},{8,0},{9,1},... | collective-permute-start | bytes 6291464 | tf_op jit(solution)/shard_map/sum_in_swap_low/ppermute | solution.py:106
  204.2 42.4 %collective-permute-start.27 = (bf16[4,128,1024]{2,1,0:T(8,128)(2,1)}, bf16[4,128,1024]{2,1,0:T(8,128)(2,1)S(1)}, u32[]{:S(2)}, u32[]{:S(2)}) collective-permute-start(bf16[4,128,1024]{2,1,0:T(8,128)(2,1)} %add_convert_fusion.2), channel_id=1, source_target_pairs={{0,1},{1,0},{2,3},{3,2},{4,5},{5,4},{6,7},{7,6},{8,24},{9,25},{10,... | collective-permute-start | bytes 3145736 | tf_op jit(solution)/shard_map/sum_mlp_2/ppermute | solution.py:106
  250.3 21.9 %collective-permute-start.36 = (bf16[4,32,4096]{2,1,0:T(8,128)(2,1)S(1)}, bf16[4,32,4096]{2,1,0:T(8,128)(2,1)S(1)}, u32[]{:S(2)}, u32[]{:S(2)}) collective-permute-start(bf16[4,32,4096]{2,1,0:T(8,128)(2,1)S(1)} %add_convert_fusion.1), channel_id=1, source_target_pairs={{0,1},{1,0},{2,3},{3,2},{4,5},{5,4},{6,7},{7,6},{8,24},{9,25},{10,... | collective-permute-start | bytes 3145736 | tf_op jit(solution)/shard_map/sum_in_2/ppermute | solution.py:106
  255.5 16.6 %collective-permute-start.35 = (bf16[2,128,1024]{2,1,0:T(8,128)(2,1)}, bf16[2,128,1024]{2,1,0:T(8,128)(2,1)}, u32[]{:S(2)}, u32[]{:S(2)}) collective-permute-start(bf16[2,128,1024]{2,1,0:T(8,128)(2,1)} %add_convert_fusion.4), channel_id=1, source_target_pairs={{0,2},{1,3},{2,0},{3,1},{4,6},{5,7},{6,4},{7,5},{8,10},{9,11},{10,... | collective-permute-start | bytes 1572872 | tf_op jit(solution)/shard_map/sum_mlp_1/ppermute | solution.py:106
  255.5 35.7 %collective-permute-start.34 = (bf16[8,32,4224]{2,1,0:T(8,128)(2,1)S(1)}, bf16[8,32,4224]{2,1,0:T(8,128)(2,1)S(1)}, u32[]{:S(2)}, u32[]{:S(2)}) collective-permute-start(bf16[8,32,4224]{2,1,0:T(8,128)(2,1)S(1)} %pad_maximum_fusion), channel_id=1, source_target_pairs={{0,16},{1,17},{2,18},{3,19},{4,20},{5,21},{6,22},{7,23},{8,9},{9,8... | collective-permute-start | bytes 6488072 | tf_op jit(solution)/shard_map/sum_first_3/ppermute | solution.py:106
  256.7 20.6 %collective-permute-start.33 = (bf16[8,32,4096]{2,1,0:T(8,128)(2,1)}, bf16[8,32,4096]{2,1,0:T(8,128)(2,1)S(1)}, u32[]{:S(2)}, u32[]{:S(2)}) collective-permute-start(bf16[8,32,4096]{2,1,0:T(8,128)(2,1)} %get-tuple-element.407), channel_id=1, source_target_pairs={{0,8},{1,9},{2,10},{3,11},{4,12},{5,13},{6,14},{7,15},{8,0},{9,1},... | collective-permute-start | bytes 6291464 | tf_op jit(solution)/shard_map/sum_first_swap_low/ppermute | solution.py:106
  277.1 14.1 %collective-permute-start.37 = (bf16[2,32,4096]{2,1,0:T(8,128)(2,1)S(1)}, bf16[2,32,4096]{2,1,0:T(8,128)(2,1)S(1)}, u32[]{:S(2)}, u32[]{:S(2)}) collective-permute-start(bf16[2,32,4096]{2,1,0:T(8,128)(2,1)S(1)} %add_convert_fusion.3), channel_id=1, source_target_pairs={{0,2},{1,3},{2,0},{3,1},{4,6},{5,7},{6,4},{7,5},{8,10},{9,11},{10,... | collective-permute-start | bytes 1572872 | tf_op jit(solution)/shard_map/sum_in_1/ppermute | solution.py:106
  291.8 15.2 %collective-permute-start.39 = (bf16[4,32,4224]{2,1,0:T(8,128)(2,1)S(1)}, bf16[4,32,4224]{2,1,0:T(8,128)(2,1)S(1)}, u32[]{:S(2)}, u32[]{:S(2)}) collective-permute-start(bf16[4,32,4224]{2,1,0:T(8,128)(2,1)S(1)} %pad_maximum_fusion.1), channel_id=1, source_target_pairs={{0,1},{1,0},{2,3},{3,2},{4,5},{5,4},{6,7},{7,6},{8,24},{9,25},{10,... | collective-permute-start | bytes 3244040 | tf_op jit(solution)/shard_map/sum_first_2/ppermute | solution.py:106
  294.1 11.7 %collective-permute-start.40 = (bf16[1,32,4096]{2,1,0:T(8,128)(2,1)S(1)}, bf16[1,32,4096]{2,1,0:T(8,128)(2,1)S(1)}, u32[]{:S(2)}, u32[]{:S(2)}) collective-permute-start(bf16[1,32,4096]{2,1,0:T(8,128)(2,1)S(1)} %add_convert_fusion.8), channel_id=1, source_target_pairs={{0,4},{1,5},{2,6},{3,7},{4,0},{5,1},{6,2},{7,3},{8,12},{9,13},{10,... | collective-permute-start | bytes 786440 | tf_op jit(solution)/shard_map/sum_in_0/ppermute | solution.py:106
  307.5 17.1 %collective-permute-start.41 = (bf16[1,32,4224]{2,1,0:T(8,128)(2,1)S(1)}, bf16[1,32,4224]{2,1,0:T(8,128)(2,1)S(1)}, u32[]{:S(2)}, u32[]{:S(2)}) collective-permute-start(bf16[1,32,4224]{2,1,0:T(8,128)(2,1)S(1)} %get-tuple-element.436), channel_id=1, source_target_pairs={{0,4},{1,5},{2,6},{3,7},{4,0},{5,1},{6,2},{7,3},{8,12},{9,13},{10,... | collective-permute-start | bytes 811016 | tf_op jit(solution)/shard_map/sum_first_last_1/ppermute | solution.py:106
  310.9 21.4 %collective-permute-start.43 = (bf16[1,32,4224]{2,1,0:T(8,128)(2,1)S(1)}, bf16[1,32,4224]{2,1,0:T(8,128)(2,1)S(1)}, u32[]{:S(2)}, u32[]{:S(2)}) collective-permute-start(bf16[1,32,4224]{2,1,0:T(8,128)(2,1)S(1)} %pad_maximum_fusion.4), channel_id=1, source_target_pairs={{0,6},{1,7},{2,4},{3,5},{4,2},{5,3},{6,0},{7,1},{8,14},{9,15},{10,... | collective-permute-start | bytes 811016 | tf_op jit(solution)/shard_map/sum_first_last_3/ppermute | solution.py:106
  310.9 21.4 %collective-permute-start.42 = (bf16[1,32,4224]{2,1,0:T(8,128)(2,1)S(1)}, bf16[1,32,4224]{2,1,0:T(8,128)(2,1)S(1)}, u32[]{:S(2)}, u32[]{:S(2)}) collective-permute-start(bf16[1,32,4224]{2,1,0:T(8,128)(2,1)S(1)} %get-tuple-element.437), channel_id=1, source_target_pairs={{0,2},{1,3},{2,0},{3,1},{4,6},{5,7},{6,4},{7,5},{8,10},{9,11},{10,... | collective-permute-start | bytes 811016 | tf_op jit(solution)/shard_map/sum_first_last_2/ppermute | solution.py:106
  (64 other events, 931.8 us)

commit v7 on v6

--- a/solution.py
+++ b/solution.py
@@ -651,21 +651,30 @@
     gmiddle_ref, branch_ref, sums_ref,
     held, ghidden, middle, gsecond, gmiddle, branch, sems, in_sems, out_sems,
 ):
-    later = [
-        pltpu.make_async_copy(ghidden_ref, ghidden, in_sems.at[0]),
-        *fetches(order_ref, (w0, w1, w2, w3), held, sems),
-        pltpu.make_async_copy(middle_ref, middle, in_sems.at[1]),
+    wide = FF // 2
+    loads = [
+        [
+            pltpu.make_async_copy(
+                ghidden_ref.at[:, span(k, wide)], ghidden.at[k], in_sems.at[k]
+            ),
+            *fetches(order_ref, (w0, w1, w2, w3), held.at[k], sems.at[k], k * wide, wide),
+        ]
+        for k in range(2)
     ]
-    start(later)
+    loads[1].append(pltpu.make_async_copy(middle_ref, middle, in_sems.at[2]))
+    start(loads[0])
+    start(loads[1])
     sums_ref[...] = jnp.zeros_like(sums_ref)
     outs = []
-    for copy in later:
-        copy.wait()
+    wait(loads[0])
+    for i in range(D // TILE):
+        gsecond[:, span(i, TILE)] = dot_nt(ghidden[0], held[0, span(i, TILE), :])
+    wait(loads[1])
     chunk = middle_ref.shape[0] // 2
     for half in range(2):
         where = span(half, chunk)
         for i in range(D // TILE):
-            gsecond[where, span(i, TILE)] = dot_nt(ghidden[where, :], held[span(i, TILE), :])
+            gsecond[where, span(i, TILE)] += dot_nt(ghidden[1, where, :], held[1, span(i, TILE), :])
         normed, inverse = norm_parts(middle[where, :])
         grad = gsecond[where, :]
         top = top_ref[where, :].astype(F32)
@@ -694,17 +703,17 @@
         in_specs=[SMEM, VMEM, HBM, VMEM, HBM] + [ANY] * 4,
         out_specs=[HBM, HBM, VMEM],
         scratch_shapes=[
-            pltpu.VMEM((D, FF), BF),
-            pltpu.VMEM((count, FF), BF),
+            pltpu.VMEM((2, D, FF // 2), BF),
+            pltpu.VMEM((2, count, FF // 2), BF),
             pltpu.VMEM((count, D), F32),
             pltpu.VMEM((count, D), F32),
             pltpu.VMEM((count, D), F32),
             pltpu.VMEM((count, D), BF),
-            pltpu.SemaphoreType.DMA((BLOCKS,)),
-            pltpu.SemaphoreType.DMA((2,)),
+            pltpu.SemaphoreType.DMA((2, BLOCKS)),
+            pltpu.SemaphoreType.DMA((3,)),
             pltpu.SemaphoreType.DMA((3,)),
         ],
-        compiler_params=params(32),
+        compiler_params=params(52),
         name="back",
     )(order, vec, ghidden, top, middle, *win)
 
@@ -991,9 +1000,11 @@
     mlp_parts = to_blocks(order, mlp.parts()) + to_blocks(late_order, late.parts())
     ghidden, grad_bias_in, *grads = line.run(fall, numbers, spot, top, slope, second, *mlp_parts)
     sum_in = Scatter(plan, line, "in", from_blocks(order, grads))
+    gmiddle, branch, sums = line.run(back, numbers, vec, ghidden, top, middle, *win_parts)
+    line.wait(sum_in.high[-1])
+    sum_mlp.arrive()
+    sum_in.start(3)
     sum_mlp.start(2)
-    sum_in.start(3)
-    gmiddle, branch, sums = line.run(back, numbers, vec, ghidden, top, middle, *win_parts)
     grad_inputs, sums_one, *grads = line.run(
         unattend, numbers, vec, x, gmiddle, branch, project, probs, entry, mixed, win_parts, first_parts
     )

time: 342 us -> 340 us (level)
  other arithmetic: 30.4 us -> 33.9 us
  local copies, waits for them, and re-layouts: 28.9 us -> 25.4 us
    unnamed x134 -> x110, local copies, waits for them, and re-layouts: 19.8 us -> 15.4 us
  transfers between devices with their start and end apart: 44 -> 44, of which waited for: 22 -> 24; matrix products, arithmetic and copies ran while one was open for 10% -> 12% of each run, Pallas kernels for 29% -> 30%
where the time goes in v7:
time: 340 us; the launch traced here: 333 us
  waiting for transfers between devices  132 us (39%)
  Pallas kernels  100 us (29%)
  starting transfers between devices  39.1 us (12%)
  other arithmetic  33.9 us (10%)
  local copies, waits for them, and re-layouts  25.4 us (7%)
    ppermute x44, waiting for transfers between devices, send(): return lax.ppermute(self.tie(array)[0], AXES, pairs)  132 us
    ppermute x44, starting transfers between devices, send(): return lax.ppermute(self.tie(array)[0], AXES, pairs)  39.1 us
    pallas_call x1, Pallas kernels, unattend(): pl.pallas_call(unattend_kernel, out_shape=[shape((count, D), F32), shape(...  25.8 us
    pallas_call x1, Pallas kernels, rise(): pl.pallas_call(rise_kernel, out_shape=[shape((count, FF), BF)] * 2 + [gra...  18.4 us
    unnamed x110, local copies, waits for them, and re-layouts  15.4 us
    pallas_call x1, Pallas kernels, fall(): pl.pallas_call(fall_kernel, out_shape=[shape((count, FF), BF), shape((1,...  14.7 us
    pallas_call x1, Pallas kernels, back(): pl.pallas_call(back_kernel, out_shape=[shape((count, D), F32), shape((cou...  13.1 us
    convert_element_type x6, other arithmetic, start(): self.sum(low, low + self.count, parts).astype(BF)  11.4 us
  transfers between devices with their start and end apart: 44, of which 24 were waited for; matrix products, arithmetic and copies ran while one was open for 12% of the time, Pallas kernels for 30%

profile of v7, /device:TPU:8, one launch (start us, length us, event | category | flops | bytes accessed | tf_op | source)
XLA Modules:
  0.0 333.0 jit_solution(617837775573218562)
XLA Ops:
  3.7 2.7 collective-permute-start
  20.1 11.5 %collective-permute-done.2 = bf16[2,32,3200]{2,1,0:T(8,128)(2,1)S(1)} collective-permute-done((bf16[2,32,3200]{2,1,0:T(8,128)(2,1)S(1)}, bf16[2,32,3200]{2,1,0:T(8,128)(2,1)S(1)}, u32[]{:S(2)}, u32[]{:S(2)}) %collective-permute-start.2) | collective-permute-done | bytes 409632 | tf_op jit(solution)/shard_map/gather_qkv_1/ppermute | solution.py:106
  31.7 3.5 %collective-permute-done.4 = bf16[1,32,5120]{2,1,0:T(8,128)(2,1)S(1)} collective-permute-done((bf16[1,32,5120]{2,1,0:T(8,128)(2,1)S(1)}, bf16[1,32,5120]{2,1,0:T(8,128)(2,1)S(1)}, u32[]{:S(2)}, u32[]{:S(2)}) %collective-permute-start.4) | collective-permute-done | bytes 327712 | tf_op jit(solution)/shard_map/gather_in_0/ppermute | solution.py:106
  38.2 10.8 %collective-permute-done.5 = bf16[4,32,3200]{2,1,0:T(8,128)(2,1)S(1)} collective-permute-done((bf16[4,32,3200]{2,1,0:T(8,128)(2,1)S(1)}, bf16[4,32,3200]{2,1,0:T(8,128)(2,1)S(1)}, u32[]{:S(2)}, u32[]{:S(2)}) %collective-permute-start.5) | collective-permute-done | bytes 819232 | tf_op jit(solution)/shard_map/gather_qkv_2/ppermute | solution.py:106
  50.8 15.0 %collective-permute-done.8 = bf16[2,32,5120]{2,1,0:T(8,128)(2,1)S(1)} collective-permute-done((bf16[2,32,5120]{2,1,0:T(8,128)(2,1)S(1)}, bf16[2,32,5120]{2,1,0:T(8,128)(2,1)S(1)}, u32[]{:S(2)}, u32[]{:S(2)}) %collective-permute-start.8) | collective-permute-done | bytes 655392 | tf_op jit(solution)/shard_map/gather_in_1/ppermute | solution.py:106
  65.8 4.7 %collective-permute-done.6.w1.f1 = bf16[8,32,3200]{2,1,0:T(8,128)(2,1)} collective-permute-done((bf16[8,32,3200]{2,1,0:T(8,128)(2,1)S(1)}, bf16[8,32,3200]{2,1,0:T(8,128)(2,1)}, u32[]{:S(2)}, u32[]{:S(2)}) %collective-permute-start.6) | collective-permute-done | bytes 1638432 | tf_op jit(solution)/shard_map/gather_qkv_3/ppermute | solution.py:106
  79.4 8.0 %project.1 = (bf16[512,1024]{1,0:T(8,128)(2,1)S(1)}, bf16[512,3072]{1,0:T(8,128)(2,1)S(1)}) custom-call(s32[32]{0:T(128)S(1)} %fusion.26.order_ref, f32[8,1024]{1,0:T(8,128)S(1)} %slice.369.vec_ref, bf16[512,1024]{1,0:T(8,128)(2,1)S(1)} %bitcast.67, bf16[8,32,3200]{2,1,0:T(8,128)(2,1)S(1)} %constant_dynamic-update-slice_fusion.10.w0.f0, ...), custom_call_target="tpu_custom_call" | custom-call | tf_op jit(solution)/shard_map/project/pallas_call | solution.py:370
  87.4 2.8 collective-permute-done.11
  99.1 6.3 %attend.1 = (bf16[8,1024,256]{2,1,0:T(8,128)(2,1)S(1)}, bf16[512,1024]{1,0:T(8,128)(2,1)S(1)}) custom-call(bf16[512,3072]{1,0:T(8,128)(2,1)S(1)} %copy-done.4, s32[2,256]{1,0:T(2,128)S(1)} %copy-done.29, s32[512,1]{1,0:T(8,128)S(1)} %bitcast.69), custom_call_target="tpu_custom_call" | custom-call | tf_op jit(solution)/shard_map/attend/pallas_call | solution.py:412
  107.5 6.7 %collective-permute-done.14 = bf16[2,128,512]{2,1,0:T(8,128)(2,1)} collective-permute-done((bf16[2,128,512]{2,1,0:T(8,128)(2,1)S(1)}, bf16[2,128,512]{2,1,0:T(8,128)(2,1)}, u32[]{:S(2)}, u32[]{:S(2)}) %collective-permute-start.14) | collective-permute-done | bytes 262176 | tf_op jit(solution)/shard_map/gather_mlp_1/ppermute | solution.py:106
  114.1 4.6 %collective-permute-done.15 = bf16[4,128,512]{2,1,0:T(8,128)(2,1)} collective-permute-done((bf16[4,128,512]{2,1,0:T(8,128)(2,1)}, bf16[4,128,512]{2,1,0:T(8,128)(2,1)}, u32[]{:S(2)}, u32[]{:S(2)}) %collective-permute-start.15) | collective-permute-done | bytes 524320 | tf_op jit(solution)/shard_map/gather_late_2/ppermute | solution.py:106
  118.7 6.3 %collective-permute-done.12.w1 = bf16[8,32,5120]{2,1,0:T(8,128)(2,1)} collective-permute-done((bf16[8,32,5120]{2,1,0:T(8,128)(2,1)S(1)}, bf16[8,32,5120]{2,1,0:T(8,128)(2,1)}, u32[]{:S(2)}, u32[]{:S(2)}) %collective-permute-start.12) | collective-permute-done | bytes 2621472 | tf_op jit(solution)/shard_map/gather_in_3/ppermute | solution.py:106
  127.5 2.6 collective-permute-done.16.w3
  130.1 5.2 %settle.1 = (f32[512,1024]{1,0:T(8,128)S(1)}, bf16[512,1024]{1,0:T(8,128)(2,1)S(1)}) custom-call(s32[32]{0:T(128)S(1)} %fusion.26.order_ref, f32[8,1024]{1,0:T(8,128)S(1)} %slice.369.vec_ref, bf16[512,1024]{1,0:T(8,128)(2,1)S(1)} %bitcast.68, bf16[512,1024]{1,0:T(8,128)(2,1)S(1)} %get-tuple-element.363.mixed_ref, ...), custom_call_target="tpu_custom_call" | custom-call | tf_op jit(solution)/shard_map/settle/pallas_call | solution.py:454
  141.3 18.4 %rise.1 = (bf16[512,4096]{1,0:T(8,128)(2,1)}, bf16[512,4096]{1,0:T(8,128)(2,1)}, bf16[8,128,1024]{2,1,0:T(8,128)(2,1)S(1)}, bf16[8,128,1024]{2,1,0:T(8,128)(2,1)...) custom-call(s32[32]{0:T(128)S(1)} %fusion.26.order_ref, f32[1,4096]{1,0:T(1,128)S(1)} %bitcast.70, ...), custom_call_target="tpu_custom_call" | custom-call | tf_op jit(solution)/shard_map/rise/pallas_call | solution.py:515
  159.7 5.2 %collective-permute-done.21.l1 = bf16[8,128,512]{2,1,0:T(8,128)(2,1)} collective-permute-done((bf16[8,128,512]{2,1,0:T(8,128)(2,1)S(1)}, bf16[8,128,512]{2,1,0:T(8,128)(2,1)}, u32[]{:S(2)}, u32[]{:S(2)}) %collective-permute-start.21) | collective-permute-done | bytes 1048608 | tf_op jit(solution)/shard_map/gather_late_3/ppermute | solution.py:106
  165.6 3.7 %collective-permute-done.25 = bf16[8,128,1024]{2,1,0:T(8,128)(2,1)S(1)} collective-permute-done((bf16[8,128,1024]{2,1,0:T(8,128)(2,1)}, bf16[8,128,1024]{2,1,0:T(8,128)(2,1)S(1)}, u32[]{:S(2)}, u32[]{:S(2)}) %collective-permute-start.25) | collective-permute-done | bytes 2097184 | tf_op jit(solution)/shard_map/sum_mlp_swap_high/ppermute | solution.py:106
  169.3 3.9 %add.197 = bf16[8,128,1024]{2,1,0:T(8,128)(2,1)} add(bf16[8,128,1024]{2,1,0:T(8,128)(2,1)} %get-tuple-element.317, bf16[8,128,1024]{2,1,0:T(8,128)(2,1)S(1)} %collective-permute-done.25) | non-fusion elementwise | flops 1048576 | bytes 6291456 | tf_op jit(solution)/shard_map/add | solution.py:152
  174.6 14.7 %fall.1 = (bf16[512,4096]{1,0:T(8,128)(2,1)}, f32[1,4096]{1,0:T(1,128)S(1)}, bf16[8,32,4096]{2,1,0:T(8,128)(2,1)S(1)}, bf16[8,32,4096]{2,1,0:T(8,128)(2,1)}, bf1...) custom-call(s32[32]{0:T(128)S(1)} %fusion.26.order_ref, s32[32]{0:T(128)S(1)} %select_reduce_fusion.spot_ref, ...), custom_call_target="tpu_custom_call" | custom-call | tf_op jit(solution)/shard_map/fall/pallas_call | solution.py:629
  191.3 13.1 %back.1 = (f32[512,1024]{1,0:T(8,128)}, bf16[512,1024]{1,0:T(8,128)(2,1)S(1)}, f32[8,1024]{1,0:T(8,128)S(1)}) custom-call(s32[32]{0:T(128)S(1)} %fusion.26.order_ref, f32[8,1024]{1,0:T(8,128)S(1)} %slice.369.vec_ref, bf16[512,4096]{1,0:T(8,128)(2,1)} %get-tuple-element.340.ghidden_ref, bf16[512,1024]{1,0:T(8,128)(2,1)} %copy-done.2, f32[512,1024]{1,0:T(8,128)} %copy-done.8, ...), custom_call_target="tpu_custom_call" | custom-call | tf_op jit(solution)/shard_map/back/pallas_call | solution.py:700
  207.2 3.2 add_convert_fusion.2
  211.7 25.8 %unattend.1 = (f32[512,1024]{1,0:T(8,128)}, f32[8,1024]{1,0:T(8,128)}, bf16[8,32,4096]{2,1,0:T(8,128)(2,1)}, bf16[8,32,4096]{2,1,0:T(8,128)(2,1)}, bf16[8,32,409...) custom-call(s32[32]{0:T(128)} %copy-done.27, f32[8,1024]{1,0:T(8,128)} %copy-done.23, bf16[512,1024]{1,0:T(8,128)(2,1)} %bitcast.66, ...), custom_call_target="tpu_custom_call" | custom-call | tf_op jit(solution)/shard_map/unattend/pallas_call | solution.py:828
  238.4 5.7 %collective-permute-done.29 = bf16[8,32,4096]{2,1,0:T(8,128)(2,1)} collective-permute-done((bf16[8,32,4096]{2,1,0:T(8,128)(2,1)}, bf16[8,32,4096]{2,1,0:T(8,128)(2,1)}, u32[]{:S(2)}, u32[]{:S(2)}) %collective-permute-start.29) | collective-permute-done | bytes 2097184 | tf_op jit(solution)/shard_map/sum_in_3/ppermute | solution.py:106
  248.6 2.5 add.203
  254.6 8.6 %finish.1 = bf16[512,1024]{1,0:T(8,128)(2,1)} custom-call(s32[32]{0:T(128)S(1)} %select_reduce_fusion.spot_ref, f32[8,1024]{1,0:T(8,128)S(1)} %copy-done.24, f32[512,1024]{1,0:T(8,128)S(1)} %copy-done.9, bf16[512,4096]{1,0:T(8,128)(2,1)S(1)} %copy-done.10, bf16[8,128,512]{2,1,0:T(8,128)(2,1)S(1)} %constant_dynamic-update-slice_fusion.22.m0, ...), custom_call_target="tpu_custom_call" | custom-call | tf_op jit(solution)/shard_map/finish/pallas_call | solution.py:886
  263.2 5.3 %collective-permute-done.36 = bf16[4,32,4096]{2,1,0:T(8,128)(2,1)S(1)} collective-permute-done((bf16[4,32,4096]{2,1,0:T(8,128)(2,1)S(1)}, bf16[4,32,4096]{2,1,0:T(8,128)(2,1)S(1)}, u32[]{:S(2)}, u32[]{:S(2)}) %collective-permute-start.36) | collective-permute-done | bytes 1048608 | tf_op jit(solution)/shard_map/sum_in_2/ppermute | solution.py:106
  273.5 9.1 %collective-permute-done.38 = bf16[1,128,1024]{2,1,0:T(8,128)(2,1)S(1)} collective-permute-done((bf16[1,128,1024]{2,1,0:T(8,128)(2,1)S(1)}, bf16[1,128,1024]{2,1,0:T(8,128)(2,1)S(1)}, u32[]{:S(2)}, u32[]{:S(2)}) %collective-permute-start.38) | collective-permute-done | bytes 262176 | tf_op jit(solution)/shard_map/sum_mlp_0/ppermute | solution.py:106
  282.6 6.6 %collective-permute-done.37 = bf16[2,32,4096]{2,1,0:T(8,128)(2,1)S(1)} collective-permute-done((bf16[2,32,4096]{2,1,0:T(8,128)(2,1)S(1)}, bf16[2,32,4096]{2,1,0:T(8,128)(2,1)S(1)}, u32[]{:S(2)}, u32[]{:S(2)}) %collective-permute-start.37) | collective-permute-done | bytes 524320 | tf_op jit(solution)/shard_map/sum_in_1/ppermute | solution.py:106
  296.5 5.6 %collective-permute-done.40 = bf16[1,32,4096]{2,1,0:T(8,128)(2,1)S(1)} collective-permute-done((bf16[1,32,4096]{2,1,0:T(8,128)(2,1)S(1)}, bf16[1,32,4096]{2,1,0:T(8,128)(2,1)S(1)}, u32[]{:S(2)}, u32[]{:S(2)}) %collective-permute-start.40) | collective-permute-done | bytes 262176 | tf_op jit(solution)/shard_map/sum_in_0/ppermute | solution.py:106
  302.1 2.8 collective-permute-done.39
  312.5 9.1 %collective-permute-done.41 = bf16[1,32,4224]{2,1,0:T(8,128)(2,1)S(1)} collective-permute-done((bf16[1,32,4224]{2,1,0:T(8,128)(2,1)S(1)}, bf16[1,32,4224]{2,1,0:T(8,128)(2,1)S(1)}, u32[]{:S(2)}, u32[]{:S(2)}) %collective-permute-start.41) | collective-permute-done | bytes 270368 | tf_op jit(solution)/shard_map/sum_first_last_1/ppermute | solution.py:106
  321.6 7.8 %collective-permute-done.43 = bf16[1,32,4224]{2,1,0:T(8,128)(2,1)S(1)} collective-permute-done((bf16[1,32,4224]{2,1,0:T(8,128)(2,1)S(1)}, bf16[1,32,4224]{2,1,0:T(8,128)(2,1)S(1)}, u32[]{:S(2)}, u32[]{:S(2)}) %collective-permute-start.43) | collective-permute-done | bytes 270368 | tf_op jit(solution)/shard_map/sum_first_last_3/ppermute | solution.py:106
  (255 shorter events, 89.7 us)
Async XLA Ops:
  15.0 16.6 %collective-permute-start.2 = (bf16[2,32,3200]{2,1,0:T(8,128)(2,1)S(1)}, bf16[2,32,3200]{2,1,0:T(8,128)(2,1)S(1)}, u32[]{:S(2)}, u32[]{:S(2)}) collective-permute-start(bf16[2,32,3200]{2,1,0:T(8,128)(2,1)S(1)} %constant_dynamic-update-slice_fusion), channel_id=1, source_target_pairs={{0,2},{1,3},{2,0},{3,1},{4,6},{5,7},{6,4},{7,5},{8,10},{9,11},{10,... | collective-permute-start | bytes 1228808 | tf_op jit(solution)/shard_map/gather_qkv_1/ppermute | solution.py:106
  16.4 18.8 %collective-permute-start.3 = (bf16[2,128,512]{2,1,0:T(8,128)(2,1)S(1)}, bf16[2,128,512]{2,1,0:T(8,128)(2,1)S(1)}, u32[]{:S(2)}, u32[]{:S(2)}) collective-permute-start(bf16[2,128,512]{2,1,0:T(8,128)(2,1)S(1)} %constant_dynamic-update-slice_fusion.2), channel_id=1, source_target_pairs={{0,16},{1,17},{2,18},{3,19},{4,20},{5,21},{6,22},{7,23},{8,9},{9,8... | collective-permute-start | bytes 786440 | tf_op jit(solution)/shard_map/gather_late_1/ppermute | solution.py:106
  18.1 17.1 %collective-permute-start.4 = (bf16[1,32,5120]{2,1,0:T(8,128)(2,1)S(1)}, bf16[1,32,5120]{2,1,0:T(8,128)(2,1)S(1)}, u32[]{:S(2)}, u32[]{:S(2)}) collective-permute-start(bf16[1,32,5120]{2,1,0:T(8,128)(2,1)S(1)} %maximum_bitcast_fusion), channel_id=1, source_target_pairs={{0,4},{1,5},{2,6},{3,7},{4,0},{5,1},{6,2},{7,3},{8,12},{9,13},{10,... | collective-permute-start | bytes 983048 | tf_op jit(solution)/shard_map/gather_in_0/ppermute | solution.py:106
  36.7 12.3 %collective-permute-start.5 = (bf16[4,32,3200]{2,1,0:T(8,128)(2,1)S(1)}, bf16[4,32,3200]{2,1,0:T(8,128)(2,1)S(1)}, u32[]{:S(2)}, u32[]{:S(2)}) collective-permute-start(bf16[4,32,3200]{2,1,0:T(8,128)(2,1)S(1)} %constant_dynamic-update-slice_fusion.4), channel_id=1, source_target_pairs={{0,1},{1,0},{2,3},{3,2},{4,5},{5,4},{6,7},{7,6},{8,24},{9,25},{10,... | collective-permute-start | bytes 2457608 | tf_op jit(solution)/shard_map/gather_qkv_2/ppermute | solution.py:106
  49.2 21.3 %collective-permute-start.6 = (bf16[8,32,3200]{2,1,0:T(8,128)(2,1)S(1)}, bf16[8,32,3200]{2,1,0:T(8,128)(2,1)}, u32[]{:S(2)}, u32[]{:S(2)}) collective-permute-start(bf16[8,32,3200]{2,1,0:T(8,128)(2,1)S(1)} %constant_dynamic-update-slice_fusion.10.w0.f0), channel_id=1, source_target_pairs={{0,16},{1,17},{2,18},{3,19},{4,20},{5,21},{6,22},{7,23},{8,9},{9,8... | collective-permute-start | bytes 4915208 | tf_op jit(solution)/shard_map/gather_qkv_3/ppermute | solution.py:106
  50.8 15.0 %collective-permute-start.8 = (bf16[2,32,5120]{2,1,0:T(8,128)(2,1)S(1)}, bf16[2,32,5120]{2,1,0:T(8,128)(2,1)S(1)}, u32[]{:S(2)}, u32[]{:S(2)}) collective-permute-start(bf16[2,32,5120]{2,1,0:T(8,128)(2,1)S(1)} %constant_dynamic-update-slice_fusion.6), channel_id=1, source_target_pairs={{0,2},{1,3},{2,0},{3,1},{4,6},{5,7},{6,4},{7,5},{8,10},{9,11},{10,... | collective-permute-start | bytes 1966088 | tf_op jit(solution)/shard_map/gather_in_1/ppermute | solution.py:106
  50.8 24.9 %collective-permute-start.7 = (bf16[8,32,3200]{2,1,0:T(8,128)(2,1)S(1)}, bf16[8,32,3200]{2,1,0:T(8,128)(2,1)}, u32[]{:S(2)}, u32[]{:S(2)}) collective-permute-start(bf16[8,32,3200]{2,1,0:T(8,128)(2,1)S(1)} %constant_dynamic-update-slice_fusion.10.w0.f0), channel_id=1, source_target_pairs={{0,8},{1,9},{2,10},{3,11},{4,12},{5,13},{6,14},{7,15},{8,0},{9,1},... | collective-permute-start | bytes 4915208 | tf_op jit(solution)/shard_map/gather_qkv_swap_first/ppermute | solution.py:106
  72.3 17.9 %collective-permute-start.11 = (bf16[4,32,5120]{2,1,0:T(8,128)(2,1)}, bf16[4,32,5120]{2,1,0:T(8,128)(2,1)}, u32[]{:S(2)}, u32[]{:S(2)}) collective-permute-start(bf16[4,32,5120]{2,1,0:T(8,128)(2,1)} %constant_dynamic-update-slice_fusion.12), channel_id=1, source_target_pairs={{0,1},{1,0},{2,3},{3,2},{4,5},{5,4},{6,7},{7,6},{8,24},{9,25},{10,... | collective-permute-start | bytes 3932168 | tf_op jit(solution)/shard_map/gather_in_2/ppermute | solution.py:106
  73.8 13.6 %collective-permute-start.10 = (bf16[1,128,512]{2,1,0:T(8,128)(2,1)S(1)}, bf16[1,128,512]{2,1,0:T(8,128)(2,1)S(1)}, u32[]{:S(2)}, u32[]{:S(2)}) collective-permute-start(bf16[1,128,512]{2,1,0:T(8,128)(2,1)S(1)} %get-tuple-element.271), channel_id=1, source_target_pairs={{0,4},{1,5},{2,6},{3,7},{4,0},{5,1},{6,2},{7,3},{8,12},{9,13},{10,... | collective-permute-start | bytes 393224 | tf_op jit(solution)/shard_map/gather_mlp_0/ppermute | solution.py:106
  93.1 25.6 %collective-permute-start.13 = (bf16[8,32,5120]{2,1,0:T(8,128)(2,1)S(1)}, bf16[8,32,5120]{2,1,0:T(8,128)(2,1)}, u32[]{:S(2)}, u32[]{:S(2)}) collective-permute-start(bf16[8,32,5120]{2,1,0:T(8,128)(2,1)S(1)} %constant_dynamic-update-slice_fusion.14.w0), channel_id=1, source_target_pairs={{0,8},{1,9},{2,10},{3,11},{4,12},{5,13},{6,14},{7,15},{8,0},{9,1},... | collective-permute-start | bytes 7864328 | tf_op jit(solution)/shard_map/gather_in_swap_first/ppermute | solution.py:106
  93.1 31.8 %collective-permute-start.12 = (bf16[8,32,5120]{2,1,0:T(8,128)(2,1)S(1)}, bf16[8,32,5120]{2,1,0:T(8,128)(2,1)}, u32[]{:S(2)}, u32[]{:S(2)}) collective-permute-start(bf16[8,32,5120]{2,1,0:T(8,128)(2,1)S(1)} %constant_dynamic-update-slice_fusion.14.w0), channel_id=1, source_target_pairs={{0,16},{1,17},{2,18},{3,19},{4,20},{5,21},{6,22},{7,23},{8,9},{9,8... | collective-permute-start | bytes 7864328 | tf_op jit(solution)/shard_map/gather_in_3/ppermute | solution.py:106
  94.8 23.9 %collective-permute-start.15 = (bf16[4,128,512]{2,1,0:T(8,128)(2,1)}, bf16[4,128,512]{2,1,0:T(8,128)(2,1)}, u32[]{:S(2)}, u32[]{:S(2)}) collective-permute-start(bf16[4,128,512]{2,1,0:T(8,128)(2,1)} %constant_dynamic-update-slice_fusion.8), channel_id=1, source_target_pairs={{0,4},{1,5},{2,6},{3,7},{4,0},{5,1},{6,2},{7,3},{8,12},{9,13},{10,... | collective-permute-start | bytes 1572872 | tf_op jit(solution)/shard_map/gather_late_2/ppermute | solution.py:106
  97.1 17.1 %collective-permute-start.14 = (bf16[2,128,512]{2,1,0:T(8,128)(2,1)S(1)}, bf16[2,128,512]{2,1,0:T(8,128)(2,1)}, u32[]{:S(2)}, u32[]{:S(2)}) collective-permute-start(bf16[2,128,512]{2,1,0:T(8,128)(2,1)S(1)} %constant_dynamic-update-slice_fusion.16), channel_id=1, source_target_pairs={{0,2},{1,3},{2,0},{3,1},{4,6},{5,7},{6,4},{7,5},{8,10},{9,11},{10,... | collective-permute-start | bytes 786440 | tf_op jit(solution)/shard_map/gather_mlp_1/ppermute | solution.py:106
  138.0 21.7 %collective-permute-start.19 = (bf16[8,128,512]{2,1,0:T(8,128)(2,1)S(1)}, bf16[8,128,512]{2,1,0:T(8,128)(2,1)S(1)}, u32[]{:S(2)}, u32[]{:S(2)}) collective-permute-start(bf16[8,128,512]{2,1,0:T(8,128)(2,1)S(1)} %constant_dynamic-update-slice_fusion.22.m0), channel_id=1, source_target_pairs={{0,8},{1,9},{2,10},{3,11},{4,12},{5,13},{6,14},{7,15},{8,0},{9,1},... | collective-permute-start | bytes 3145736 | tf_op jit(solution)/shard_map/gather_mlp_swap_first/ppermute | solution.py:106
  138.2 21.6 %collective-permute-start.18 = (bf16[8,128,512]{2,1,0:T(8,128)(2,1)S(1)}, bf16[8,128,512]{2,1,0:T(8,128)(2,1)}, u32[]{:S(2)}, u32[]{:S(2)}) collective-permute-start(bf16[8,128,512]{2,1,0:T(8,128)(2,1)S(1)} %constant_dynamic-update-slice_fusion.22.m0), channel_id=1, source_target_pairs={{0,16},{1,17},{2,18},{3,19},{4,20},{5,21},{6,22},{7,23},{8,9},{9,8... | collective-permute-start | bytes 3145736 | tf_op jit(solution)/shard_map/gather_mlp_3/ppermute | solution.py:106
  139.7 25.2 %collective-permute-start.21 = (bf16[8,128,512]{2,1,0:T(8,128)(2,1)S(1)}, bf16[8,128,512]{2,1,0:T(8,128)(2,1)}, u32[]{:S(2)}, u32[]{:S(2)}) collective-permute-start(bf16[8,128,512]{2,1,0:T(8,128)(2,1)S(1)} %constant_dynamic-update-slice_fusion.20.l0), channel_id=1, source_target_pairs={{0,2},{1,3},{2,0},{3,1},{4,6},{5,7},{6,4},{7,5},{8,10},{9,11},{10,... | collective-permute-start | bytes 3145736 | tf_op jit(solution)/shard_map/gather_late_3/ppermute | solution.py:106
  139.7 25.2 %collective-permute-start.20 = (bf16[8,128,512]{2,1,0:T(8,128)(2,1)S(1)}, bf16[8,128,512]{2,1,0:T(8,128)(2,1)}, u32[]{:S(2)}, u32[]{:S(2)}) collective-permute-start(bf16[8,128,512]{2,1,0:T(8,128)(2,1)S(1)} %constant_dynamic-update-slice_fusion.20.l0), channel_id=1, source_target_pairs={{0,8},{1,9},{2,10},{3,11},{4,12},{5,13},{6,14},{7,15},{8,0},{9,1},... | collective-permute-start | bytes 3145736 | tf_op jit(solution)/shard_map/gather_late_swap_first/ppermute | solution.py:106
  173.2 31.2 %collective-permute-start.26 = (bf16[8,128,1024]{2,1,0:T(8,128)(2,1)}, bf16[8,128,1024]{2,1,0:T(8,128)(2,1)}, u32[]{:S(2)}, u32[]{:S(2)}) collective-permute-start(bf16[8,128,1024]{2,1,0:T(8,128)(2,1)} %add.197), channel_id=1, source_target_pairs={{0,16},{1,17},{2,18},{3,19},{4,20},{5,21},{6,22},{7,23},{8,9},{9,8... | collective-permute-start | bytes 6291464 | tf_op jit(solution)/shard_map/sum_mlp_3/ppermute | solution.py:106
  190.7 13.7 %collective-permute-start.27 = (bf16[8,32,4096]{2,1,0:T(8,128)(2,1)}, bf16[8,32,4096]{2,1,0:T(8,128)(2,1)S(1)}, u32[]{:S(2)}, u32[]{:S(2)}) collective-permute-start(bf16[8,32,4096]{2,1,0:T(8,128)(2,1)} %get-tuple-element.337), channel_id=1, source_target_pairs={{0,8},{1,9},{2,10},{3,11},{4,12},{5,13},{6,14},{7,15},{8,0},{9,1},... | collective-permute-start | bytes 6291464 | tf_op jit(solution)/shard_map/sum_in_swap_high/ppermute | solution.py:106
  190.8 16.5 %collective-permute-start.24 = (bf16[8,128,1024]{2,1,0:T(8,128)(2,1)}, bf16[8,128,1024]{2,1,0:T(8,128)(2,1)}, u32[]{:S(2)}, u32[]{:S(2)}) collective-permute-start(bf16[8,128,1024]{2,1,0:T(8,128)(2,1)} %get-tuple-element.313), channel_id=1, source_target_pairs={{0,8},{1,9},{2,10},{3,11},{4,12},{5,13},{6,14},{7,15},{8,0},{9,1},... | collective-permute-start | bytes 6291464 | tf_op jit(solution)/shard_map/sum_mlp_swap_low/ppermute | solution.py:106
  206.5 37.6 %collective-permute-start.29 = (bf16[8,32,4096]{2,1,0:T(8,128)(2,1)}, bf16[8,32,4096]{2,1,0:T(8,128)(2,1)}, u32[]{:S(2)}, u32[]{:S(2)}) collective-permute-start(bf16[8,32,4096]{2,1,0:T(8,128)(2,1)} %add.198), channel_id=1, source_target_pairs={{0,16},{1,17},{2,18},{3,19},{4,20},{5,21},{6,22},{7,23},{8,9},{9,8... | collective-permute-start | bytes 6291464 | tf_op jit(solution)/shard_map/sum_in_3/ppermute | solution.py:106
  207.2 37.3 %collective-permute-start.31 = (bf16[8,32,4096]{2,1,0:T(8,128)(2,1)}, bf16[8,32,4096]{2,1,0:T(8,128)(2,1)}, u32[]{:S(2)}, u32[]{:S(2)}) collective-permute-start(bf16[8,32,4096]{2,1,0:T(8,128)(2,1)} %get-tuple-element.379), channel_id=1, source_target_pairs={{0,8},{1,9},{2,10},{3,11},{4,12},{5,13},{6,14},{7,15},{8,0},{9,1},... | collective-permute-start | bytes 6291464 | tf_op jit(solution)/shard_map/sum_in_swap_low/ppermute | solution.py:106
  210.4 28.0 %collective-permute-start.28 = (bf16[4,128,1024]{2,1,0:T(8,128)(2,1)}, bf16[4,128,1024]{2,1,0:T(8,128)(2,1)}, u32[]{:S(2)}, u32[]{:S(2)}) collective-permute-start(bf16[4,128,1024]{2,1,0:T(8,128)(2,1)} %add_convert_fusion.2), channel_id=1, source_target_pairs={{0,1},{1,0},{2,3},{3,2},{4,5},{5,4},{6,7},{7,6},{8,24},{9,25},{10,... | collective-permute-start | bytes 3145736 | tf_op jit(solution)/shard_map/sum_mlp_2/ppermute | solution.py:106
  247.5 21.0 %collective-permute-start.36 = (bf16[4,32,4096]{2,1,0:T(8,128)(2,1)S(1)}, bf16[4,32,4096]{2,1,0:T(8,128)(2,1)S(1)}, u32[]{:S(2)}, u32[]{:S(2)}) collective-permute-start(bf16[4,32,4096]{2,1,0:T(8,128)(2,1)S(1)} %add_convert_fusion.1), channel_id=1, source_target_pairs={{0,1},{1,0},{2,3},{3,2},{4,5},{5,4},{6,7},{7,6},{8,24},{9,25},{10,... | collective-permute-start | bytes 3145736 | tf_op jit(solution)/shard_map/sum_in_2/ppermute | solution.py:106
  253.2 15.3 %collective-permute-start.35 = (bf16[2,128,1024]{2,1,0:T(8,128)(2,1)S(1)}, bf16[2,128,1024]{2,1,0:T(8,128)(2,1)S(1)}, u32[]{:S(2)}, u32[]{:S(2)}) collective-permute-start(bf16[2,128,1024]{2,1,0:T(8,128)(2,1)S(1)} %add_convert_fusion.4), channel_id=1, source_target_pairs={{0,2},{1,3},{2,0},{3,1},{4,6},{5,7},{6,4},{7,5},{8,10},{9,11},{10,... | collective-permute-start | bytes 1572872 | tf_op jit(solution)/shard_map/sum_mlp_1/ppermute | solution.py:106
  253.3 35.9 %collective-permute-start.34 = (bf16[8,32,4224]{2,1,0:T(8,128)(2,1)S(1)}, bf16[8,32,4224]{2,1,0:T(8,128)(2,1)S(1)}, u32[]{:S(2)}, u32[]{:S(2)}) collective-permute-start(bf16[8,32,4224]{2,1,0:T(8,128)(2,1)S(1)} %pad_maximum_fusion), channel_id=1, source_target_pairs={{0,16},{1,17},{2,18},{3,19},{4,20},{5,21},{6,22},{7,23},{8,9},{9,8... | collective-permute-start | bytes 6488072 | tf_op jit(solution)/shard_map/sum_first_3/ppermute | solution.py:106
  254.3 19.1 %collective-permute-start.33 = (bf16[8,32,4096]{2,1,0:T(8,128)(2,1)S(1)}, bf16[8,32,4096]{2,1,0:T(8,128)(2,1)S(1)}, u32[]{:S(2)}, u32[]{:S(2)}) collective-permute-start(bf16[8,32,4096]{2,1,0:T(8,128)(2,1)S(1)} %copy-done.39), channel_id=1, source_target_pairs={{0,8},{1,9},{2,10},{3,11},{4,12},{5,13},{6,14},{7,15},{8,0},{9,1},... | collective-permute-start | bytes 6291464 | tf_op jit(solution)/shard_map/sum_first_swap_low/ppermute | solution.py:106
  273.4 15.8 %collective-permute-start.37 = (bf16[2,32,4096]{2,1,0:T(8,128)(2,1)S(1)}, bf16[2,32,4096]{2,1,0:T(8,128)(2,1)S(1)}, u32[]{:S(2)}, u32[]{:S(2)}) collective-permute-start(bf16[2,32,4096]{2,1,0:T(8,128)(2,1)S(1)} %add_convert_fusion.3), channel_id=1, source_target_pairs={{0,2},{1,3},{2,0},{3,1},{4,6},{5,7},{6,4},{7,5},{8,10},{9,11},{10,... | collective-permute-start | bytes 1572872 | tf_op jit(solution)/shard_map/sum_in_1/ppermute | solution.py:106
  289.8 15.2 %collective-permute-start.39 = (bf16[4,32,4224]{2,1,0:T(8,128)(2,1)S(1)}, bf16[4,32,4224]{2,1,0:T(8,128)(2,1)S(1)}, u32[]{:S(2)}, u32[]{:S(2)}) collective-permute-start(bf16[4,32,4224]{2,1,0:T(8,128)(2,1)S(1)} %pad_maximum_fusion.1), channel_id=1, source_target_pairs={{0,1},{1,0},{2,3},{3,2},{4,5},{5,4},{6,7},{7,6},{8,24},{9,25},{10,... | collective-permute-start | bytes 3244040 | tf_op jit(solution)/shard_map/sum_first_2/ppermute | solution.py:106
  305.5 16.1 %collective-permute-start.41 = (bf16[1,32,4224]{2,1,0:T(8,128)(2,1)S(1)}, bf16[1,32,4224]{2,1,0:T(8,128)(2,1)S(1)}, u32[]{:S(2)}, u32[]{:S(2)}) collective-permute-start(bf16[1,32,4224]{2,1,0:T(8,128)(2,1)S(1)} %get-tuple-element.436), channel_id=1, source_target_pairs={{0,4},{1,5},{2,6},{3,7},{4,0},{5,1},{6,2},{7,3},{8,12},{9,13},{10,... | collective-permute-start | bytes 811016 | tf_op jit(solution)/shard_map/sum_first_last_1/ppermute | solution.py:106
  307.9 21.5 %collective-permute-start.43 = (bf16[1,32,4224]{2,1,0:T(8,128)(2,1)S(1)}, bf16[1,32,4224]{2,1,0:T(8,128)(2,1)S(1)}, u32[]{:S(2)}, u32[]{:S(2)}) collective-permute-start(bf16[1,32,4224]{2,1,0:T(8,128)(2,1)S(1)} %pad_maximum_fusion.4), channel_id=1, source_target_pairs={{0,6},{1,7},{2,4},{3,5},{4,2},{5,3},{6,0},{7,1},{8,14},{9,15},{10,... | collective-permute-start | bytes 811016 | tf_op jit(solution)/shard_map/sum_first_last_3/ppermute | solution.py:106
  308.2 21.2 %collective-permute-start.42 = (bf16[1,32,4224]{2,1,0:T(8,128)(2,1)S(1)}, bf16[1,32,4224]{2,1,0:T(8,128)(2,1)S(1)}, u32[]{:S(2)}, u32[]{:S(2)}) collective-permute-start(bf16[1,32,4224]{2,1,0:T(8,128)(2,1)S(1)} %get-tuple-element.437), channel_id=1, source_target_pairs={{0,2},{1,3},{2,0},{3,1},{4,6},{5,7},{6,4},{7,5},{8,10},{9,11},{10,... | collective-permute-start | bytes 811016 | tf_op jit(solution)/shard_map/sum_first_last_2/ppermute | solution.py:106
  (52 other events, 858.8 us)

commit v8 on v7

--- a/solution.py
+++ b/solution.py
@@ -1008,7 +1008,7 @@
     grad_inputs, sums_one, *grads = line.run(
         unattend, numbers, vec, x, gmiddle, branch, project, probs, entry, mixed, win_parts, first_parts
     )
-    sum_mlp.arrive()
+    sum_mlp.start(1)
     sum_in.arrive()
     sum_first = Scatter(plan, line, "first", from_blocks(order, grads))
 
@@ -1025,13 +1025,11 @@
     sum_first.join(pack(sums_one, sums, grad_bias_in))
     sum_in.start(2)
     sum_first.start(3)
-    sum_mlp.start(1)
+    sum_mlp.start(0)
     output = line.run(finish, spot, vec, middle, active, *mlp_parts)
     sum_mlp.arrive()
     sum_in.start(1)
-    sum_mlp.start(0)
     sum_in.arrive()
-    sum_mlp.arrive()
     sum_first.start(2)
     sum_in.start(0)
     grad_mlp = sum_mlp.result()

time: 340 us -> 341 us (level)
  starting transfers between devices: 39.1 us -> 43 us
    ppermute x44, starting transfers between devices: 39.1 us -> 43 us  [send(): return lax.ppermute(self.tie(array)[0], AXES, pairs)]
    unnamed x110 -> x108, local copies, waits for them, and re-layouts: 15.4 us -> 15.2 us
  transfers between devices with their start and end apart: 44 -> 44, of which waited for: 24 -> 22; matrix products, arithmetic and copies ran while one was open for 12% -> 12% of each run, Pallas kernels for 30% -> 30%
where the time goes in v8:
time: 341 us; the launch traced here: 335 us
  waiting for transfers between devices  130 us (38%)
  Pallas kernels  100 us (29%)
  starting transfers between devices  43 us (13%)
  other arithmetic  34.9 us (10%)
  local copies, waits for them, and re-layouts  24.2 us (7%)
    ppermute x44, waiting for transfers between devices, send(): return lax.ppermute(self.tie(array)[0], AXES, pairs)  130 us
    ppermute x44, starting transfers between devices, send(): return lax.ppermute(self.tie(array)[0], AXES, pairs)  43 us
    pallas_call x1, Pallas kernels, unattend(): pl.pallas_call(unattend_kernel, out_shape=[shape((count, D), F32), shape(...  25.8 us
    pallas_call x1, Pallas kernels, rise(): pl.pallas_call(rise_kernel, out_shape=[shape((count, FF), BF)] * 2 + [gra...  18.4 us
    unnamed x108, local copies, waits for them, and re-layouts  15.2 us
    pallas_call x1, Pallas kernels, fall(): pl.pallas_call(fall_kernel, out_shape=[shape((count, FF), BF), shape((1,...  14.7 us
    pallas_call x1, Pallas kernels, back(): pl.pallas_call(back_kernel, out_shape=[shape((count, D), F32), shape((cou...  13.1 us
    convert_element_type x6, other arithmetic, start(): self.sum(low, low + self.count, parts).astype(BF)  12.3 us
  transfers between devices with their start and end apart: 44, of which 22 were waited for; matrix products, arithmetic and copies ran while one was open for 12% of the time, Pallas kernels for 30%

profile of v8, /device:TPU:8, one launch (start us, length us, event | category | flops | bytes accessed | tf_op | source)
XLA Modules:
  0.0 334.7 jit_solution(5526302455484612308)
XLA Ops:
  3.7 2.7 collective-permute-start
  20.1 11.5 %collective-permute-done.2 = bf16[2,32,3200]{2,1,0:T(8,128)(2,1)S(1)} collective-permute-done((bf16[2,32,3200]{2,1,0:T(8,128)(2,1)S(1)}, bf16[2,32,3200]{2,1,0:T(8,128)(2,1)S(1)}, u32[]{:S(2)}, u32[]{:S(2)}) %collective-permute-start.2) | collective-permute-done | bytes 409632 | tf_op jit(solution)/shard_map/gather_qkv_1/ppermute | solution.py:106
  31.7 3.5 %collective-permute-done.4 = bf16[1,32,5120]{2,1,0:T(8,128)(2,1)S(1)} collective-permute-done((bf16[1,32,5120]{2,1,0:T(8,128)(2,1)S(1)}, bf16[1,32,5120]{2,1,0:T(8,128)(2,1)S(1)}, u32[]{:S(2)}, u32[]{:S(2)}) %collective-permute-start.4) | collective-permute-done | bytes 327712 | tf_op jit(solution)/shard_map/gather_in_0/ppermute | solution.py:106
  38.2 10.8 %collective-permute-done.5 = bf16[4,32,3200]{2,1,0:T(8,128)(2,1)S(1)} collective-permute-done((bf16[4,32,3200]{2,1,0:T(8,128)(2,1)S(1)}, bf16[4,32,3200]{2,1,0:T(8,128)(2,1)S(1)}, u32[]{:S(2)}, u32[]{:S(2)}) %collective-permute-start.5) | collective-permute-done | bytes 819232 | tf_op jit(solution)/shard_map/gather_qkv_2/ppermute | solution.py:106
  50.8 15.0 %collective-permute-done.8 = bf16[2,32,5120]{2,1,0:T(8,128)(2,1)S(1)} collective-permute-done((bf16[2,32,5120]{2,1,0:T(8,128)(2,1)S(1)}, bf16[2,32,5120]{2,1,0:T(8,128)(2,1)S(1)}, u32[]{:S(2)}, u32[]{:S(2)}) %collective-permute-start.8) | collective-permute-done | bytes 655392 | tf_op jit(solution)/shard_map/gather_in_1/ppermute | solution.py:106
  65.8 4.7 %collective-permute-done.6.w1.f1 = bf16[8,32,3200]{2,1,0:T(8,128)(2,1)} collective-permute-done((bf16[8,32,3200]{2,1,0:T(8,128)(2,1)S(1)}, bf16[8,32,3200]{2,1,0:T(8,128)(2,1)}, u32[]{:S(2)}, u32[]{:S(2)}) %collective-permute-start.6) | collective-permute-done | bytes 1638432 | tf_op jit(solution)/shard_map/gather_qkv_3/ppermute | solution.py:106
  79.4 8.0 %project.1 = (bf16[512,1024]{1,0:T(8,128)(2,1)S(1)}, bf16[512,3072]{1,0:T(8,128)(2,1)S(1)}) custom-call(s32[32]{0:T(128)S(1)} %fusion.26.order_ref, f32[8,1024]{1,0:T(8,128)S(1)} %slice.369.vec_ref, bf16[512,1024]{1,0:T(8,128)(2,1)S(1)} %bitcast.67, bf16[8,32,3200]{2,1,0:T(8,128)(2,1)S(1)} %constant_dynamic-update-slice_fusion.10.w0.f0, ...), custom_call_target="tpu_custom_call" | custom-call | tf_op jit(solution)/shard_map/project/pallas_call | solution.py:370
  87.4 2.8 collective-permute-done.11
  99.1 6.3 %attend.1 = (bf16[8,1024,256]{2,1,0:T(8,128)(2,1)S(1)}, bf16[512,1024]{1,0:T(8,128)(2,1)S(1)}) custom-call(bf16[512,3072]{1,0:T(8,128)(2,1)S(1)} %copy-done.4, s32[2,256]{1,0:T(2,128)S(1)} %copy-done.28, s32[512,1]{1,0:T(8,128)S(1)} %bitcast.69), custom_call_target="tpu_custom_call" | custom-call | tf_op jit(solution)/shard_map/attend/pallas_call | solution.py:412
  107.5 6.5 %collective-permute-done.14 = bf16[2,128,512]{2,1,0:T(8,128)(2,1)S(1)} collective-permute-done((bf16[2,128,512]{2,1,0:T(8,128)(2,1)S(1)}, bf16[2,128,512]{2,1,0:T(8,128)(2,1)S(1)}, u32[]{:S(2)}, u32[]{:S(2)}) %collective-permute-start.14) | collective-permute-done | bytes 262176 | tf_op jit(solution)/shard_map/gather_mlp_1/ppermute | solution.py:106
  114.0 4.7 %collective-permute-done.15 = bf16[4,128,512]{2,1,0:T(8,128)(2,1)} collective-permute-done((bf16[4,128,512]{2,1,0:T(8,128)(2,1)}, bf16[4,128,512]{2,1,0:T(8,128)(2,1)}, u32[]{:S(2)}, u32[]{:S(2)}) %collective-permute-start.15) | collective-permute-done | bytes 524320 | tf_op jit(solution)/shard_map/gather_late_2/ppermute | solution.py:106
  118.7 6.3 %collective-permute-done.12.w1 = bf16[8,32,5120]{2,1,0:T(8,128)(2,1)} collective-permute-done((bf16[8,32,5120]{2,1,0:T(8,128)(2,1)S(1)}, bf16[8,32,5120]{2,1,0:T(8,128)(2,1)}, u32[]{:S(2)}, u32[]{:S(2)}) %collective-permute-start.12) | collective-permute-done | bytes 2621472 | tf_op jit(solution)/shard_map/gather_in_3/ppermute | solution.py:106
  126.6 3.5 %collective-permute-done.16.w3 = bf16[8,32,5120]{2,1,0:T(8,128)(2,1)S(1)} collective-permute-done((bf16[8,32,5120]{2,1,0:T(8,128)(2,1)}, bf16[8,32,5120]{2,1,0:T(8,128)(2,1)S(1)}, u32[]{:S(2)}, u32[]{:S(2)}) %collective-permute-start.16) | collective-permute-done | bytes 2621472 | tf_op jit(solution)/shard_map/gather_in_swap_second/ppermute | solution.py:106
  130.1 5.2 %settle.1 = (f32[512,1024]{1,0:T(8,128)S(1)}, bf16[512,1024]{1,0:T(8,128)(2,1)S(1)}) custom-call(s32[32]{0:T(128)S(1)} %fusion.26.order_ref, f32[8,1024]{1,0:T(8,128)S(1)} %slice.369.vec_ref, bf16[512,1024]{1,0:T(8,128)(2,1)S(1)} %bitcast.68, bf16[512,1024]{1,0:T(8,128)(2,1)S(1)} %get-tuple-element.363.mixed_ref, ...), custom_call_target="tpu_custom_call" | custom-call | tf_op jit(solution)/shard_map/settle/pallas_call | solution.py:454
  141.3 18.4 %rise.1 = (bf16[512,4096]{1,0:T(8,128)(2,1)}, bf16[512,4096]{1,0:T(8,128)(2,1)}, bf16[8,128,1024]{2,1,0:T(8,128)(2,1)S(1)}, bf16[8,128,1024]{2,1,0:T(8,128)(2,1)...) custom-call(s32[32]{0:T(128)S(1)} %fusion.26.order_ref, f32[1,4096]{1,0:T(1,128)S(1)} %bitcast.70, ...), custom_call_target="tpu_custom_call" | custom-call | tf_op jit(solution)/shard_map/rise/pallas_call | solution.py:515
  159.7 5.2 %collective-permute-done.21.l1 = bf16[8,128,512]{2,1,0:T(8,128)(2,1)} collective-permute-done((bf16[8,128,512]{2,1,0:T(8,128)(2,1)S(1)}, bf16[8,128,512]{2,1,0:T(8,128)(2,1)}, u32[]{:S(2)}, u32[]{:S(2)}) %collective-permute-start.21) | collective-permute-done | bytes 1048608 | tf_op jit(solution)/shard_map/gather_late_3/ppermute | solution.py:106
  165.6 3.7 %collective-permute-done.25 = bf16[8,128,1024]{2,1,0:T(8,128)(2,1)S(1)} collective-permute-done((bf16[8,128,1024]{2,1,0:T(8,128)(2,1)}, bf16[8,128,1024]{2,1,0:T(8,128)(2,1)S(1)}, u32[]{:S(2)}, u32[]{:S(2)}) %collective-permute-start.25) | collective-permute-done | bytes 2097184 | tf_op jit(solution)/shard_map/sum_mlp_swap_high/ppermute | solution.py:106
  169.3 3.9 %add.197 = bf16[8,128,1024]{2,1,0:T(8,128)(2,1)} add(bf16[8,128,1024]{2,1,0:T(8,128)(2,1)} %get-tuple-element.317, bf16[8,128,1024]{2,1,0:T(8,128)(2,1)S(1)} %collective-permute-done.25) | non-fusion elementwise | flops 1048576 | bytes 6291456 | tf_op jit(solution)/shard_map/add | solution.py:152
  174.6 14.7 %fall.1 = (bf16[512,4096]{1,0:T(8,128)(2,1)}, f32[1,4096]{1,0:T(1,128)S(1)}, bf16[8,32,4096]{2,1,0:T(8,128)(2,1)S(1)}, bf16[8,32,4096]{2,1,0:T(8,128)(2,1)}, bf1...) custom-call(s32[32]{0:T(128)S(1)} %fusion.26.order_ref, s32[32]{0:T(128)S(1)} %select_reduce_fusion.spot_ref, ...), custom_call_target="tpu_custom_call" | custom-call | tf_op jit(solution)/shard_map/fall/pallas_call | solution.py:629
  191.3 13.1 %back.1 = (f32[512,1024]{1,0:T(8,128)}, bf16[512,1024]{1,0:T(8,128)(2,1)S(1)}, f32[8,1024]{1,0:T(8,128)S(1)}) custom-call(s32[32]{0:T(128)S(1)} %fusion.26.order_ref, f32[8,1024]{1,0:T(8,128)S(1)} %slice.369.vec_ref, bf16[512,4096]{1,0:T(8,128)(2,1)} %get-tuple-element.340.ghidden_ref, bf16[512,1024]{1,0:T(8,128)(2,1)} %copy-done.2, f32[512,1024]{1,0:T(8,128)} %copy-done.8, ...), custom_call_target="tpu_custom_call" | custom-call | tf_op jit(solution)/shard_map/back/pallas_call | solution.py:700
  207.3 3.2 add_convert_fusion.2
  211.3 25.8 %unattend.1 = (f32[512,1024]{1,0:T(8,128)}, f32[8,1024]{1,0:T(8,128)}, bf16[8,32,4096]{2,1,0:T(8,128)(2,1)}, bf16[8,32,4096]{2,1,0:T(8,128)(2,1)}, bf16[8,32,409...) custom-call(s32[32]{0:T(128)} %copy-done.26, f32[8,1024]{1,0:T(8,128)} %copy-done.22, bf16[512,1024]{1,0:T(8,128)(2,1)} %bitcast.66, ...), custom_call_target="tpu_custom_call" | custom-call | tf_op jit(solution)/shard_map/unattend/pallas_call | solution.py:828
  238.0 2.7 add_convert_fusion.4
  240.7 3.4 %collective-permute-done.30 = bf16[8,32,4096]{2,1,0:T(8,128)(2,1)} collective-permute-done((bf16[8,32,4096]{2,1,0:T(8,128)(2,1)}, bf16[8,32,4096]{2,1,0:T(8,128)(2,1)}, u32[]{:S(2)}, u32[]{:S(2)}) %collective-permute-start.30) | collective-permute-done | bytes 2097184 | tf_op jit(solution)/shard_map/sum_in_3/ppermute | solution.py:106
  252.2 6.9 %collective-permute-done.29 = bf16[2,128,1024]{2,1,0:T(8,128)(2,1)S(1)} collective-permute-done((bf16[2,128,1024]{2,1,0:T(8,128)(2,1)}, bf16[2,128,1024]{2,1,0:T(8,128)(2,1)S(1)}, u32[]{:S(2)}, u32[]{:S(2)}) %collective-permute-start.29) | collective-permute-done | bytes 524320 | tf_op jit(solution)/shard_map/sum_mlp_1/ppermute | solution.py:106
  262.7 8.6 %finish.1 = bf16[512,1024]{1,0:T(8,128)(2,1)} custom-call(s32[32]{0:T(128)S(1)} %select_reduce_fusion.spot_ref, f32[8,1024]{1,0:T(8,128)S(1)} %copy-done.23, f32[512,1024]{1,0:T(8,128)S(1)} %copy-done.9, bf16[512,4096]{1,0:T(8,128)(2,1)S(1)} %copy-done.10, bf16[8,128,512]{2,1,0:T(8,128)(2,1)S(1)} %constant_dynamic-update-slice_fusion.22.m0, ...), custom_call_target="tpu_custom_call" | custom-call | tf_op jit(solution)/shard_map/finish/pallas_call | solution.py:886
  277.1 11.7 %collective-permute-done.38 = bf16[2,32,4096]{2,1,0:T(8,128)(2,1)S(1)} collective-permute-done((bf16[2,32,4096]{2,1,0:T(8,128)(2,1)S(1)}, bf16[2,32,4096]{2,1,0:T(8,128)(2,1)S(1)}, u32[]{:S(2)}, u32[]{:S(2)}) %collective-permute-start.38) | collective-permute-done | bytes 524320 | tf_op jit(solution)/shard_map/sum_in_1/ppermute | solution.py:106
  291.6 3.4 %collective-permute-start.40 = (bf16[1,32,4096]{2,1,0:T(8,128)(2,1)S(1)}, bf16[1,32,4096]{2,1,0:T(8,128)(2,1)S(1)}, u32[]{:S(2)}, u32[]{:S(2)}) collective-permute-start(bf16[1,32,4096]{2,1,0:T(8,128)(2,1)S(1)} %add_convert_fusion.8), channel_id=1, source_target_pairs={{0,4},{1,5},{2,6},{3,7},{4,0},{5,1},{6,2},{7,3},{8,12},{9,13},{10,... | collective-permute-start | bytes 786440 | tf_op jit(solution)/shard_map/sum_in_0/ppermute | solution.py:106
  297.8 7.0 %collective-permute-done.40 = bf16[1,32,4096]{2,1,0:T(8,128)(2,1)S(1)} collective-permute-done((bf16[1,32,4096]{2,1,0:T(8,128)(2,1)S(1)}, bf16[1,32,4096]{2,1,0:T(8,128)(2,1)S(1)}, u32[]{:S(2)}, u32[]{:S(2)}) %collective-permute-start.40) | collective-permute-done | bytes 262176 | tf_op jit(solution)/shard_map/sum_in_0/ppermute | solution.py:106
  305.4 3.4 %collective-permute-start.41 = (bf16[1,32,4224]{2,1,0:T(8,128)(2,1)S(1)}, bf16[1,32,4224]{2,1,0:T(8,128)(2,1)S(1)}, u32[]{:S(2)}, u32[]{:S(2)}) collective-permute-start(bf16[1,32,4224]{2,1,0:T(8,128)(2,1)S(1)} %get-tuple-element.436), channel_id=1, source_target_pairs={{0,4},{1,5},{2,6},{3,7},{4,0},{5,1},{6,2},{7,3},{8,12},{9,13},{10,... | collective-permute-start | bytes 811016 | tf_op jit(solution)/shard_map/sum_first_last_1/ppermute | solution.py:106
  312.9 11.6 %collective-permute-done.41 = bf16[1,32,4224]{2,1,0:T(8,128)(2,1)S(1)} collective-permute-done((bf16[1,32,4224]{2,1,0:T(8,128)(2,1)S(1)}, bf16[1,32,4224]{2,1,0:T(8,128)(2,1)S(1)}, u32[]{:S(2)}, u32[]{:S(2)}) %collective-permute-start.41) | collective-permute-done | bytes 270368 | tf_op jit(solution)/shard_map/sum_first_last_1/ppermute | solution.py:106
  324.5 6.6 %collective-permute-done.43 = bf16[1,32,4224]{2,1,0:T(8,128)(2,1)S(1)} collective-permute-done((bf16[1,32,4224]{2,1,0:T(8,128)(2,1)S(1)}, bf16[1,32,4224]{2,1,0:T(8,128)(2,1)S(1)}, u32[]{:S(2)}, u32[]{:S(2)}) %collective-permute-start.43) | collective-permute-done | bytes 270368 | tf_op jit(solution)/shard_map/sum_first_last_3/ppermute | solution.py:106
  (253 shorter events, 88.2 us)
Async XLA Ops:
  15.0 16.6 %collective-permute-start.2 = (bf16[2,32,3200]{2,1,0:T(8,128)(2,1)S(1)}, bf16[2,32,3200]{2,1,0:T(8,128)(2,1)S(1)}, u32[]{:S(2)}, u32[]{:S(2)}) collective-permute-start(bf16[2,32,3200]{2,1,0:T(8,128)(2,1)S(1)} %constant_dynamic-update-slice_fusion), channel_id=1, source_target_pairs={{0,2},{1,3},{2,0},{3,1},{4,6},{5,7},{6,4},{7,5},{8,10},{9,11},{10,... | collective-permute-start | bytes 1228808 | tf_op jit(solution)/shard_map/gather_qkv_1/ppermute | solution.py:106
  16.4 18.8 %collective-permute-start.3 = (bf16[2,128,512]{2,1,0:T(8,128)(2,1)S(1)}, bf16[2,128,512]{2,1,0:T(8,128)(2,1)S(1)}, u32[]{:S(2)}, u32[]{:S(2)}) collective-permute-start(bf16[2,128,512]{2,1,0:T(8,128)(2,1)S(1)} %constant_dynamic-update-slice_fusion.2), channel_id=1, source_target_pairs={{0,16},{1,17},{2,18},{3,19},{4,20},{5,21},{6,22},{7,23},{8,9},{9,8... | collective-permute-start | bytes 786440 | tf_op jit(solution)/shard_map/gather_late_1/ppermute | solution.py:106
  18.1 17.1 %collective-permute-start.4 = (bf16[1,32,5120]{2,1,0:T(8,128)(2,1)S(1)}, bf16[1,32,5120]{2,1,0:T(8,128)(2,1)S(1)}, u32[]{:S(2)}, u32[]{:S(2)}) collective-permute-start(bf16[1,32,5120]{2,1,0:T(8,128)(2,1)S(1)} %maximum_bitcast_fusion), channel_id=1, source_target_pairs={{0,4},{1,5},{2,6},{3,7},{4,0},{5,1},{6,2},{7,3},{8,12},{9,13},{10,... | collective-permute-start | bytes 983048 | tf_op jit(solution)/shard_map/gather_in_0/ppermute | solution.py:106
  49.2 21.3 %collective-permute-start.6 = (bf16[8,32,3200]{2,1,0:T(8,128)(2,1)S(1)}, bf16[8,32,3200]{2,1,0:T(8,128)(2,1)}, u32[]{:S(2)}, u32[]{:S(2)}) collective-permute-start(bf16[8,32,3200]{2,1,0:T(8,128)(2,1)S(1)} %constant_dynamic-update-slice_fusion.10.w0.f0), channel_id=1, source_target_pairs={{0,16},{1,17},{2,18},{3,19},{4,20},{5,21},{6,22},{7,23},{8,9},{9,8... | collective-permute-start | bytes 4915208 | tf_op jit(solution)/shard_map/gather_qkv_3/ppermute | solution.py:106
  50.8 15.0 %collective-permute-start.8 = (bf16[2,32,5120]{2,1,0:T(8,128)(2,1)S(1)}, bf16[2,32,5120]{2,1,0:T(8,128)(2,1)S(1)}, u32[]{:S(2)}, u32[]{:S(2)}) collective-permute-start(bf16[2,32,5120]{2,1,0:T(8,128)(2,1)S(1)} %constant_dynamic-update-slice_fusion.6), channel_id=1, source_target_pairs={{0,2},{1,3},{2,0},{3,1},{4,6},{5,7},{6,4},{7,5},{8,10},{9,11},{10,... | collective-permute-start | bytes 1966088 | tf_op jit(solution)/shard_map/gather_in_1/ppermute | solution.py:106
  50.8 24.9 %collective-permute-start.7 = (bf16[8,32,3200]{2,1,0:T(8,128)(2,1)S(1)}, bf16[8,32,3200]{2,1,0:T(8,128)(2,1)}, u32[]{:S(2)}, u32[]{:S(2)}) collective-permute-start(bf16[8,32,3200]{2,1,0:T(8,128)(2,1)S(1)} %constant_dynamic-update-slice_fusion.10.w0.f0), channel_id=1, source_target_pairs={{0,8},{1,9},{2,10},{3,11},{4,12},{5,13},{6,14},{7,15},{8,0},{9,1},... | collective-permute-start | bytes 4915208 | tf_op jit(solution)/shard_map/gather_qkv_swap_first/ppermute | solution.py:106
  72.3 17.9 %collective-permute-start.11 = (bf16[4,32,5120]{2,1,0:T(8,128)(2,1)}, bf16[4,32,5120]{2,1,0:T(8,128)(2,1)}, u32[]{:S(2)}, u32[]{:S(2)}) collective-permute-start(bf16[4,32,5120]{2,1,0:T(8,128)(2,1)} %constant_dynamic-update-slice_fusion.12), channel_id=1, source_target_pairs={{0,1},{1,0},{2,3},{3,2},{4,5},{5,4},{6,7},{7,6},{8,24},{9,25},{10,... | collective-permute-start | bytes 3932168 | tf_op jit(solution)/shard_map/gather_in_2/ppermute | solution.py:106
  73.8 13.6 %collective-permute-start.10 = (bf16[1,128,512]{2,1,0:T(8,128)(2,1)S(1)}, bf16[1,128,512]{2,1,0:T(8,128)(2,1)S(1)}, u32[]{:S(2)}, u32[]{:S(2)}) collective-permute-start(bf16[1,128,512]{2,1,0:T(8,128)(2,1)S(1)} %get-tuple-element.271), channel_id=1, source_target_pairs={{0,4},{1,5},{2,6},{3,7},{4,0},{5,1},{6,2},{7,3},{8,12},{9,13},{10,... | collective-permute-start | bytes 393224 | tf_op jit(solution)/shard_map/gather_mlp_0/ppermute | solution.py:106
  93.1 25.6 %collective-permute-start.13 = (bf16[8,32,5120]{2,1,0:T(8,128)(2,1)S(1)}, bf16[8,32,5120]{2,1,0:T(8,128)(2,1)}, u32[]{:S(2)}, u32[]{:S(2)}) collective-permute-start(bf16[8,32,5120]{2,1,0:T(8,128)(2,1)S(1)} %constant_dynamic-update-slice_fusion.14.w0), channel_id=1, source_target_pairs={{0,8},{1,9},{2,10},{3,11},{4,12},{5,13},{6,14},{7,15},{8,0},{9,1},... | collective-permute-start | bytes 7864328 | tf_op jit(solution)/shard_map/gather_in_swap_first/ppermute | solution.py:106
  93.1 31.8 %collective-permute-start.12 = (bf16[8,32,5120]{2,1,0:T(8,128)(2,1)S(1)}, bf16[8,32,5120]{2,1,0:T(8,128)(2,1)}, u32[]{:S(2)}, u32[]{:S(2)}) collective-permute-start(bf16[8,32,5120]{2,1,0:T(8,128)(2,1)S(1)} %constant_dynamic-update-slice_fusion.14.w0), channel_id=1, source_target_pairs={{0,16},{1,17},{2,18},{3,19},{4,20},{5,21},{6,22},{7,23},{8,9},{9,8... | collective-permute-start | bytes 7864328 | tf_op jit(solution)/shard_map/gather_in_3/ppermute | solution.py:106
  94.8 23.9 %collective-permute-start.15 = (bf16[4,128,512]{2,1,0:T(8,128)(2,1)}, bf16[4,128,512]{2,1,0:T(8,128)(2,1)}, u32[]{:S(2)}, u32[]{:S(2)}) collective-permute-start(bf16[4,128,512]{2,1,0:T(8,128)(2,1)} %constant_dynamic-update-slice_fusion.8), channel_id=1, source_target_pairs={{0,4},{1,5},{2,6},{3,7},{4,0},{5,1},{6,2},{7,3},{8,12},{9,13},{10,... | collective-permute-start | bytes 1572872 | tf_op jit(solution)/shard_map/gather_late_2/ppermute | solution.py:106
  97.1 17.0 %collective-permute-start.14 = (bf16[2,128,512]{2,1,0:T(8,128)(2,1)S(1)}, bf16[2,128,512]{2,1,0:T(8,128)(2,1)S(1)}, u32[]{:S(2)}, u32[]{:S(2)}) collective-permute-start(bf16[2,128,512]{2,1,0:T(8,128)(2,1)S(1)} %constant_dynamic-update-slice_fusion.16), channel_id=1, source_target_pairs={{0,2},{1,3},{2,0},{3,1},{4,6},{5,7},{6,4},{7,5},{8,10},{9,11},{10,... | collective-permute-start | bytes 786440 | tf_op jit(solution)/shard_map/gather_mlp_1/ppermute | solution.py:106
  138.0 21.8 %collective-permute-start.19 = (bf16[8,128,512]{2,1,0:T(8,128)(2,1)S(1)}, bf16[8,128,512]{2,1,0:T(8,128)(2,1)S(1)}, u32[]{:S(2)}, u32[]{:S(2)}) collective-permute-start(bf16[8,128,512]{2,1,0:T(8,128)(2,1)S(1)} %constant_dynamic-update-slice_fusion.22.m0), channel_id=1, source_target_pairs={{0,8},{1,9},{2,10},{3,11},{4,12},{5,13},{6,14},{7,15},{8,0},{9,1},... | collective-permute-start | bytes 3145736 | tf_op jit(solution)/shard_map/gather_mlp_swap_first/ppermute | solution.py:106
  138.2 21.6 %collective-permute-start.18 = (bf16[8,128,512]{2,1,0:T(8,128)(2,1)S(1)}, bf16[8,128,512]{2,1,0:T(8,128)(2,1)}, u32[]{:S(2)}, u32[]{:S(2)}) collective-permute-start(bf16[8,128,512]{2,1,0:T(8,128)(2,1)S(1)} %constant_dynamic-update-slice_fusion.22.m0), channel_id=1, source_target_pairs={{0,16},{1,17},{2,18},{3,19},{4,20},{5,21},{6,22},{7,23},{8,9},{9,8... | collective-permute-start | bytes 3145736 | tf_op jit(solution)/shard_map/gather_mlp_3/ppermute | solution.py:106
  139.7 25.2 %collective-permute-start.21 = (bf16[8,128,512]{2,1,0:T(8,128)(2,1)S(1)}, bf16[8,128,512]{2,1,0:T(8,128)(2,1)}, u32[]{:S(2)}, u32[]{:S(2)}) collective-permute-start(bf16[8,128,512]{2,1,0:T(8,128)(2,1)S(1)} %constant_dynamic-update-slice_fusion.20.l0), channel_id=1, source_target_pairs={{0,2},{1,3},{2,0},{3,1},{4,6},{5,7},{6,4},{7,5},{8,10},{9,11},{10,... | collective-permute-start | bytes 3145736 | tf_op jit(solution)/shard_map/gather_late_3/ppermute | solution.py:106
  139.7 25.2 %collective-permute-start.20 = (bf16[8,128,512]{2,1,0:T(8,128)(2,1)S(1)}, bf16[8,128,512]{2,1,0:T(8,128)(2,1)}, u32[]{:S(2)}, u32[]{:S(2)}) collective-permute-start(bf16[8,128,512]{2,1,0:T(8,128)(2,1)S(1)} %constant_dynamic-update-slice_fusion.20.l0), channel_id=1, source_target_pairs={{0,8},{1,9},{2,10},{3,11},{4,12},{5,13},{6,14},{7,15},{8,0},{9,1},... | collective-permute-start | bytes 3145736 | tf_op jit(solution)/shard_map/gather_late_swap_first/ppermute | solution.py:106
  173.3 31.2 %collective-permute-start.26 = (bf16[8,128,1024]{2,1,0:T(8,128)(2,1)}, bf16[8,128,1024]{2,1,0:T(8,128)(2,1)}, u32[]{:S(2)}, u32[]{:S(2)}) collective-permute-start(bf16[8,128,1024]{2,1,0:T(8,128)(2,1)} %add.197), channel_id=1, source_target_pairs={{0,16},{1,17},{2,18},{3,19},{4,20},{5,21},{6,22},{7,23},{8,9},{9,8... | collective-permute-start | bytes 6291464 | tf_op jit(solution)/shard_map/sum_mlp_3/ppermute | solution.py:106
  190.8 13.7 %collective-permute-start.27 = (bf16[8,32,4096]{2,1,0:T(8,128)(2,1)}, bf16[8,32,4096]{2,1,0:T(8,128)(2,1)S(1)}, u32[]{:S(2)}, u32[]{:S(2)}) collective-permute-start(bf16[8,32,4096]{2,1,0:T(8,128)(2,1)} %get-tuple-element.337), channel_id=1, source_target_pairs={{0,8},{1,9},{2,10},{3,11},{4,12},{5,13},{6,14},{7,15},{8,0},{9,1},... | collective-permute-start | bytes 6291464 | tf_op jit(solution)/shard_map/sum_in_swap_high/ppermute | solution.py:106
  190.8 16.5 %collective-permute-start.24 = (bf16[8,128,1024]{2,1,0:T(8,128)(2,1)}, bf16[8,128,1024]{2,1,0:T(8,128)(2,1)}, u32[]{:S(2)}, u32[]{:S(2)}) collective-permute-start(bf16[8,128,1024]{2,1,0:T(8,128)(2,1)} %get-tuple-element.313), channel_id=1, source_target_pairs={{0,8},{1,9},{2,10},{3,11},{4,12},{5,13},{6,14},{7,15},{8,0},{9,1},... | collective-permute-start | bytes 6291464 | tf_op jit(solution)/shard_map/sum_mlp_swap_low/ppermute | solution.py:106
  206.5 37.6 %collective-permute-start.30 = (bf16[8,32,4096]{2,1,0:T(8,128)(2,1)}, bf16[8,32,4096]{2,1,0:T(8,128)(2,1)}, u32[]{:S(2)}, u32[]{:S(2)}) collective-permute-start(bf16[8,32,4096]{2,1,0:T(8,128)(2,1)} %add.198), channel_id=1, source_target_pairs={{0,16},{1,17},{2,18},{3,19},{4,20},{5,21},{6,22},{7,23},{8,9},{9,8... | collective-permute-start | bytes 6291464 | tf_op jit(solution)/shard_map/sum_in_3/ppermute | solution.py:106
  210.4 27.6 %collective-permute-start.28 = (bf16[4,128,1024]{2,1,0:T(8,128)(2,1)}, bf16[4,128,1024]{2,1,0:T(8,128)(2,1)}, u32[]{:S(2)}, u32[]{:S(2)}) collective-permute-start(bf16[4,128,1024]{2,1,0:T(8,128)(2,1)} %add_convert_fusion.2), channel_id=1, source_target_pairs={{0,1},{1,0},{2,3},{3,2},{4,5},{5,4},{6,7},{7,6},{8,24},{9,25},{10,... | collective-permute-start | bytes 3145736 | tf_op jit(solution)/shard_map/sum_mlp_2/ppermute | solution.py:106
  211.1 33.5 %collective-permute-start.32 = (bf16[8,32,4096]{2,1,0:T(8,128)(2,1)}, bf16[8,32,4096]{2,1,0:T(8,128)(2,1)}, u32[]{:S(2)}, u32[]{:S(2)}) collective-permute-start(bf16[8,32,4096]{2,1,0:T(8,128)(2,1)} %get-tuple-element.384), channel_id=1, source_target_pairs={{0,8},{1,9},{2,10},{3,11},{4,12},{5,13},{6,14},{7,15},{8,0},{9,1},... | collective-permute-start | bytes 6291464 | tf_op jit(solution)/shard_map/sum_in_swap_low/ppermute | solution.py:106
  244.5 14.6 %collective-permute-start.29 = (bf16[2,128,1024]{2,1,0:T(8,128)(2,1)}, bf16[2,128,1024]{2,1,0:T(8,128)(2,1)S(1)}, u32[]{:S(2)}, u32[]{:S(2)}) collective-permute-start(bf16[2,128,1024]{2,1,0:T(8,128)(2,1)} %add_convert_fusion.4), channel_id=1, source_target_pairs={{0,2},{1,3},{2,0},{3,1},{4,6},{5,7},{6,4},{7,5},{8,10},{9,11},{10,... | collective-permute-start | bytes 1572872 | tf_op jit(solution)/shard_map/sum_mlp_1/ppermute | solution.py:106
  247.6 23.7 %collective-permute-start.36 = (bf16[4,32,4096]{2,1,0:T(8,128)(2,1)S(1)}, bf16[4,32,4096]{2,1,0:T(8,128)(2,1)S(1)}, u32[]{:S(2)}, u32[]{:S(2)}) collective-permute-start(bf16[4,32,4096]{2,1,0:T(8,128)(2,1)S(1)} %add_convert_fusion.1), channel_id=1, source_target_pairs={{0,1},{1,0},{2,3},{3,2},{4,5},{5,4},{6,7},{7,6},{8,24},{9,25},{10,... | collective-permute-start | bytes 3145736 | tf_op jit(solution)/shard_map/sum_in_2/ppermute | solution.py:106
  251.4 37.5 %collective-permute-start.35 = (bf16[8,32,4224]{2,1,0:T(8,128)(2,1)S(1)}, bf16[8,32,4224]{2,1,0:T(8,128)(2,1)S(1)}, u32[]{:S(2)}, u32[]{:S(2)}) collective-permute-start(bf16[8,32,4224]{2,1,0:T(8,128)(2,1)S(1)} %pad_maximum_fusion), channel_id=1, source_target_pairs={{0,16},{1,17},{2,18},{3,19},{4,20},{5,21},{6,22},{7,23},{8,9},{9,8... | collective-permute-start | bytes 6488072 | tf_op jit(solution)/shard_map/sum_first_3/ppermute | solution.py:106
  252.2 25.0 %collective-permute-start.34 = (bf16[8,32,4096]{2,1,0:T(8,128)(2,1)S(1)}, bf16[8,32,4096]{2,1,0:T(8,128)(2,1)S(1)}, u32[]{:S(2)}, u32[]{:S(2)}) collective-permute-start(bf16[8,32,4096]{2,1,0:T(8,128)(2,1)S(1)} %copy-done.38), channel_id=1, source_target_pairs={{0,8},{1,9},{2,10},{3,11},{4,12},{5,13},{6,14},{7,15},{8,0},{9,1},... | collective-permute-start | bytes 6291464 | tf_op jit(solution)/shard_map/sum_first_swap_low/ppermute | solution.py:106
  274.9 13.9 %collective-permute-start.38 = (bf16[2,32,4096]{2,1,0:T(8,128)(2,1)S(1)}, bf16[2,32,4096]{2,1,0:T(8,128)(2,1)S(1)}, u32[]{:S(2)}, u32[]{:S(2)}) collective-permute-start(bf16[2,32,4096]{2,1,0:T(8,128)(2,1)S(1)} %add_convert_fusion.3), channel_id=1, source_target_pairs={{0,2},{1,3},{2,0},{3,1},{4,6},{5,7},{6,4},{7,5},{8,10},{9,11},{10,... | collective-permute-start | bytes 1572872 | tf_op jit(solution)/shard_map/sum_in_1/ppermute | solution.py:106
  289.4 15.5 %collective-permute-start.39 = (bf16[4,32,4224]{2,1,0:T(8,128)(2,1)S(1)}, bf16[4,32,4224]{2,1,0:T(8,128)(2,1)S(1)}, u32[]{:S(2)}, u32[]{:S(2)}) collective-permute-start(bf16[4,32,4224]{2,1,0:T(8,128)(2,1)S(1)} %pad_maximum_fusion.1), channel_id=1, source_target_pairs={{0,1},{1,0},{2,3},{3,2},{4,5},{5,4},{6,7},{7,6},{8,24},{9,25},{10,... | collective-permute-start | bytes 3244040 | tf_op jit(solution)/shard_map/sum_first_2/ppermute | solution.py:106
  291.6 13.2 %collective-permute-start.40 = (bf16[1,32,4096]{2,1,0:T(8,128)(2,1)S(1)}, bf16[1,32,4096]{2,1,0:T(8,128)(2,1)S(1)}, u32[]{:S(2)}, u32[]{:S(2)}) collective-permute-start(bf16[1,32,4096]{2,1,0:T(8,128)(2,1)S(1)} %add_convert_fusion.8), channel_id=1, source_target_pairs={{0,4},{1,5},{2,6},{3,7},{4,0},{5,1},{6,2},{7,3},{8,12},{9,13},{10,... | collective-permute-start | bytes 786440 | tf_op jit(solution)/shard_map/sum_in_0/ppermute | solution.py:106
  305.4 19.2 %collective-permute-start.41 = (bf16[1,32,4224]{2,1,0:T(8,128)(2,1)S(1)}, bf16[1,32,4224]{2,1,0:T(8,128)(2,1)S(1)}, u32[]{:S(2)}, u32[]{:S(2)}) collective-permute-start(bf16[1,32,4224]{2,1,0:T(8,128)(2,1)S(1)} %get-tuple-element.436), channel_id=1, source_target_pairs={{0,4},{1,5},{2,6},{3,7},{4,0},{5,1},{6,2},{7,3},{8,12},{9,13},{10,... | collective-permute-start | bytes 811016 | tf_op jit(solution)/shard_map/sum_first_last_1/ppermute | solution.py:106
  308.8 22.3 %collective-permute-start.43 = (bf16[1,32,4224]{2,1,0:T(8,128)(2,1)S(1)}, bf16[1,32,4224]{2,1,0:T(8,128)(2,1)S(1)}, u32[]{:S(2)}, u32[]{:S(2)}) collective-permute-start(bf16[1,32,4224]{2,1,0:T(8,128)(2,1)S(1)} %pad_maximum_fusion.4), channel_id=1, source_target_pairs={{0,6},{1,7},{2,4},{3,5},{4,2},{5,3},{6,0},{7,1},{8,14},{9,15},{10,... | collective-permute-start | bytes 811016 | tf_op jit(solution)/shard_map/sum_first_last_3/ppermute | solution.py:106
  308.8 22.3 %collective-permute-start.42 = (bf16[1,32,4224]{2,1,0:T(8,128)(2,1)S(1)}, bf16[1,32,4224]{2,1,0:T(8,128)(2,1)S(1)}, u32[]{:S(2)}, u32[]{:S(2)}) collective-permute-start(bf16[1,32,4224]{2,1,0:T(8,128)(2,1)S(1)} %get-tuple-element.437), channel_id=1, source_target_pairs={{0,2},{1,3},{2,0},{3,1},{4,6},{5,7},{6,4},{7,5},{8,10},{9,11},{10,... | collective-permute-start | bytes 811016 | tf_op jit(solution)/shard_map/sum_first_last_2/ppermute | solution.py:106
  (51 other events, 862.4 us)
